TPU v7x, 32 devices: a whole 2x2x4 slice. The times are simulated.
32 devices in a mesh: dp: 8 (over y, x, core), tensor: 4 (over z).
Axes of the slice: x: 2, y: 2, z: 4, core: 2. Of those that a mesh axis runs over, the one named last changes fastest.
Arguments:
- inputs: bfloat16 [16384, 768], P(('dp', 'tensor')), may hold values from -6 to 6
- attention_gain: float32 [768], replicated, may hold values from 0.5 to 1.5
- feedforward_gain: float32 [768], replicated, may hold values from 0.5 to 1.5
- query_weight: bfloat16 [768, 768], P('dp', 'tensor'), may hold values from -0.109375 to 0.109375
- key_weight: bfloat16 [768, 768], P('dp', 'tensor'), may hold values from -0.109375 to 0.109375
- value_weight: bfloat16 [768, 768], P('dp', 'tensor'), may hold values from -0.21875 to 0.21875
- output_weight: bfloat16 [768, 768], P('tensor', 'dp'), may hold values from -1.75 to 1.75
- inner_weight: bfloat16 [768, 3072], P('dp', 'tensor'), may hold values from -0.21875 to 0.21875
- outer_weight: bfloat16 [3072, 768], P('tensor', 'dp'), may hold values from -0.15625 to 0.15625
- bias_table: float32 [32, 12], P(None, 'tensor'), may hold values from -6 to 6
- block_index: int32 [8, 2048], P('dp'), may hold values from 0 to 7, never falling along the last dimension, each value on 1 to 512 neighbouring positions
- position_bucket: int32 [4095], replicated, may hold values from 0 to 31
- cotangent: bfloat16 [16384, 768], P(('dp', 'tensor')), may hold values from -6 to 6
Outputs:
- layer_output: bfloat16 [16384, 768], P(('dp', 'tensor'))
- input_grad: bfloat16 [16384, 768], P(('dp', 'tensor'))
- attention_gain_grad: float32 [768], replicated
- feedforward_gain_grad: float32 [768], replicated
- query_grad: float32 [768, 768], P('dp', 'tensor')
- key_grad: float32 [768, 768], P('dp', 'tensor')
- value_grad: float32 [768, 768], P('dp', 'tensor')
- output_grad: float32 [768, 768], P('tensor', 'dp')
- inner_grad: float32 [768, 3072], P('dp', 'tensor')
- outer_grad: float32 [3072, 768], P('tensor', 'dp')
- table_grad: float32 [32, 12], replicated
Inputs may be any that keep to these rules, and one draw needn't show every extreme that they name: `block_index`: in each sequence's row of 2048 positions the block numbers never fall; a block holds 1 to 512 positions, and some block holds exactly 512.
All inputs are finite; a program needn't handle non-finite values.
Results may differ from a plain program's by a relative error of at most 0.018.
Values may be sent and summed in bfloat16 or wider, within the bound.
No kernel may reach another device: no remote copies, remote signals or barrier semaphores. Data moves between devices by JAX's collectives and lax.ppermute only.
A program may use at most 192 MiB of HBM per device.

v0:
```python
import math

import jax
import jax.numpy as jnp
from jax import lax
from jax.experimental import pallas as pl
from jax.experimental.pallas import tpu as pltpu
from jax.sharding import PartitionSpec as P

H = 12
EPSILON = 1e-06
MASKED = -1e30
TILE = 256
AHEAD = 2
BLOCKS = 8
VMEM_LIMIT = 60 * 1024 * 1024
f32, bf16 = jnp.float32, jnp.bfloat16


def dot(left, right, contract=((1,), (0,))):
    return lax.dot_general(left, right, (contract, ((), ())), preferred_element_type=f32)


def norm_forward(values, gain):
    inverse = lax.rsqrt(jnp.mean(values * values, axis=-1, keepdims=True) + EPSILON)
    scaled = values * inverse
    return scaled, inverse, (scaled * gain).astype(bf16)


def norm_backward(grad_normed, scaled, inverse, gain):
    grad_scaled = grad_normed * gain
    return inverse * (
        grad_scaled - scaled * jnp.mean(grad_scaled * scaled, axis=-1, keepdims=True)
    )


def gelu_parts(values):
    cumulative = 0.5 * (1.0 + lax.erf(values * (1.0 / math.sqrt(2.0))))
    density = jnp.exp(-0.5 * values * values) * (1.0 / math.sqrt(2.0 * math.pi))
    return values * cumulative, cumulative + values * density


def whole(shape):
    return pl.BlockSpec(shape, lambda *_: (0,) * len(shape), pipeline_mode=pl.Buffered(1))


def params():
    return pltpu.CompilerParams(vmem_limit_bytes=VMEM_LIMIT)


def bias_rows(bias_table, position_bucket):
    bucket = jnp.concatenate([position_bucket, jnp.zeros((1,), jnp.int32)])[::-1]
    names = jnp.arange(bias_table.shape[0], dtype=jnp.int32)
    onehot = (bucket[None, :] == names[:, None]).astype(f32)
    rows = lax.dot_general(
        bias_table, onehot, (((0,), (0,)), ((), ())), precision=lax.Precision.HIGHEST
    )
    return rows[:, None, :], onehot


def bias_kernel(row_ref, out_ref):
    tiles = out_ref.shape[1]

    def one(place, _):
        start = pl.multiple_of((tiles - 1 - place) * TILE, TILE)
        piece = row_ref[0, :, pl.ds(start, 2 * TILE)]
        spread = jnp.broadcast_to(piece, (TILE, 2 * TILE))
        out_ref[0, place] = pltpu.roll(spread, 0, 1, stride=1, stride_axis=0)[:, TILE:]
        return 0

    lax.fori_loop(0, tiles, one, 0)


def bias_tiles(rows, length):
    heads = rows.shape[0]
    count = length // TILE
    rows = rows[:, :, (count - 1 - AHEAD) * TILE :]
    tiles = count + AHEAD
    return pl.pallas_call(
        bias_kernel,
        grid=(heads,),
        in_specs=[pl.BlockSpec((1, 1, rows.shape[2]), lambda h: (h, 0, 0))],
        out_specs=pl.BlockSpec((1, tiles, TILE, TILE), lambda h: (h, 0, 0, 0)),
        out_shape=jax.ShapeDtypeStruct((heads, tiles, TILE, TILE), f32),
        compiler_params=params(),
        name="bias_tiles",
    )(rows)


def table_part(bands, onehot, length):
    heads, tiles = bands.shape[:2]
    pieces = bands[:, ::-1, 0, :]
    pad = jnp.zeros((heads, 1, TILE), f32)
    line = jnp.concatenate([pieces[:, :, :TILE], pad], 1) + jnp.concatenate(
        [pad, pieces[:, :, TILE:]], 1
    )
    line = line.reshape(heads, (tiles + 1) * TILE)
    base = (length // TILE - 1 - AHEAD) * TILE
    return lax.dot_general(
        onehot[:, base : base + line.shape[1]],
        line,
        (((1,), (1,)), ((), ())),
        precision=lax.Precision.HIGHEST,
    )


def spans(block_row):
    length = block_row.shape[0]
    names = jnp.arange(BLOCKS, dtype=jnp.int32)[:, None]
    upto = jnp.sum(block_row[None, :] <= names, axis=1, dtype=jnp.int32)
    end = jnp.sum(jnp.where(block_row[None, :] == names, upto[:, None], 0), axis=0, dtype=jnp.int32)
    by_tile = end.reshape(length // TILE, TILE)
    full = by_tile[:, 0] // TILE
    most = (by_tile[:, TILE - 1] + TILE - 1) // TILE
    places = jnp.arange(length // TILE, dtype=jnp.int32)[:, None]
    least = jnp.sum(most[None, :] <= places, axis=1, dtype=jnp.int32)
    clear = jnp.sum(full[None, :] <= places, axis=1, dtype=jnp.int32)
    return end.reshape(1, length), full, most, least, clear


def forward_kernel(full_ref, most_ref, qt_ref, kt_ref, vt_ref, bias_ref, end_ref, ot_ref, lse_ref, k_ref, acc_ref, stat_ref):
    heads = qt_ref.shape[0]
    count = kt_ref.shape[2] // TILE
    query = pl.program_id(0)

    @pl.when(query == 0)
    def _():
        for h in range(heads):
            k_ref[h] = kt_ref[h].T

    acc_ref[...] = jnp.zeros_like(acc_ref)
    stat_ref[0] = jnp.full(stat_ref.shape[1:], -jnp.inf, f32)
    stat_ref[1] = jnp.zeros(stat_ref.shape[1:], f32)

    def step(key, masked):
        start = pl.multiple_of(key * TILE, TILE)
        if masked:
            keep = lax.broadcasted_iota(jnp.int32, (TILE, TILE), 0) + start < end_ref[...]
        for h in range(heads):
            scores = dot(k_ref[h, pl.ds(start, TILE), :], qt_ref[h])
            scores = scores + bias_ref[h, key - query + count - 1]
            if masked:
                scores = jnp.where(keep, scores, MASKED)
            old = stat_ref[0, h]
            new = jnp.maximum(old, jnp.max(scores, axis=0, keepdims=True))
            weights = jnp.exp(scores - new)
            scale = jnp.exp(old - new)
            stat_ref[0, h] = new
            stat_ref[1, h] = stat_ref[1, h] * scale + jnp.sum(weights, axis=0, keepdims=True)
            acc_ref[h] = acc_ref[h] * scale + dot(
                vt_ref[h, :, pl.ds(start, TILE)], weights.astype(bf16)
            )

    def full_step(key, _):
        step(key, False)
        return 0

    def edge_step(key, _):
        step(key, True)
        return 0

    lax.fori_loop(0, full_ref[query], full_step, 0)
    lax.fori_loop(full_ref[query], most_ref[query], edge_step, 0)
    for h in range(heads):
        total = stat_ref[1, h]
        ot_ref[0, h] = (acc_ref[h] * (1.0 / total)).astype(bf16)
        lse_ref[h] = stat_ref[0, h] + jnp.log(total)


def attend_forward(qt, kt, vt, bias, end, full, most, parts):
    heads, size, length = qt.shape
    count = length // TILE
    each = count // parts
    smem = pl.BlockSpec(memory_space=pltpu.SMEM)
    return pl.pallas_call(
        forward_kernel,
        grid=(count,),
        in_specs=[
            smem,
            smem,
            pl.BlockSpec((heads, size, TILE), lambda i: (0, 0, i)),
            whole(kt.shape),
            whole(vt.shape),
            whole(bias.shape),
            pl.BlockSpec((1, TILE), lambda i: (0, i)),
        ],
        out_specs=[
            pl.BlockSpec((1, heads, size, TILE), lambda i: (i // each, 0, 0, i % each)),
            pl.BlockSpec((heads, 1, TILE), lambda i: (0, 0, i)),
        ],
        out_shape=[
            jax.ShapeDtypeStruct((parts, heads, size, length // parts), bf16),
            jax.ShapeDtypeStruct((heads, 1, length), f32),
        ],
        scratch_shapes=[
            pltpu.VMEM((heads, length, size), bf16),
            pltpu.VMEM((heads, size, TILE), f32),
            pltpu.VMEM((2, heads, 1, TILE), f32),
        ],
        compiler_params=params(),
        name="attend_forward",
    )(full, most, qt, kt, vt, bias, end)


def backward_kernel(
    least_ref, clear_ref, qt_ref, kt_ref, vt_ref, ot_ref, got_ref, lse_ref, bias_ref, end_ref,
    out_ref, band_out_ref,
    q_ref, go_ref, dqt_acc, dk_acc, dv_acc, delta_ref, band_ref,
):
    heads, size, length = qt_ref.shape
    count = length // TILE
    parts = got_ref.shape[0]
    each = count // parts
    key = pl.program_id(0)
    key_cols = pl.ds(pl.multiple_of(key * TILE, TILE), TILE)

    @pl.when(key == 0)
    def _():
        dqt_acc[...] = jnp.zeros_like(dqt_acc)
        band_ref[...] = jnp.zeros_like(band_ref)
        for h in range(heads):
            q_ref[h] = qt_ref[h].T
            for part in range(parts):
                rows = pl.ds(part * (length // parts), length // parts)
                grad = got_ref[part, h]
                go_ref[h, rows, :] = grad.T
                delta_ref[h, :, rows] = jnp.sum(
                    ot_ref[part, h].astype(f32) * grad.astype(f32), axis=0, keepdims=True
                )

    dk_acc[...] = jnp.zeros_like(dk_acc)
    dv_acc[...] = jnp.zeros_like(dv_acc)
    kt = [kt_ref[h, :, key_cols] for h in range(heads)]
    k = [tile.T for tile in kt]
    v = [vt_ref[h, :, key_cols].T for h in range(heads)]

    def step(query, masked):
        cols = pl.ds(pl.multiple_of(query * TILE, TILE), TILE)
        part = query // each
        inner = pl.ds(pl.multiple_of((query % each) * TILE, TILE), TILE)
        if masked:
            keep = lax.broadcasted_iota(jnp.int32, (TILE, TILE), 0) + key * TILE < end_ref[:, cols]
        place = key - query + count - 1
        for h in range(heads):
            scores = dot(k[h], qt_ref[h, :, cols])
            scores = scores + bias_ref[h, place]
            if masked:
                scores = jnp.where(keep, scores, MASKED)
            weights = jnp.exp(scores - lse_ref[h, :, cols])
            grad_weights = dot(v[h], got_ref[part, h, :, inner])
            grad_scores = weights * (grad_weights - delta_ref[h, :, cols])
            rounded = grad_scores.astype(bf16)
            band_ref[h, place] += grad_scores
            dv_acc[h] += dot(weights.astype(bf16), go_ref[h, cols, :])
            dk_acc[h] += dot(rounded, q_ref[h, cols, :])
            dqt_acc[h, :, cols] += dot(kt[h], rounded)

    def edge_step(query, _):
        step(query, True)
        return 0

    def full_step(query, _):
        step(query, False)
        return 0

    lax.fori_loop(least_ref[key], clear_ref[key], edge_step, 0)
    lax.fori_loop(clear_ref[key], count, full_step, 0)
    for h in range(heads):
        out_ref[1, h, :, key_cols] = dk_acc[h].T.astype(bf16)
        out_ref[2, h, :, key_cols] = dv_acc[h].T.astype(bf16)

    @pl.when(key == count - 1)
    def _():
        out_ref[0] = dqt_acc[...].astype(bf16)

        def one(place, _):
            for h in range(heads):
                band = band_ref[h, place]
                zero = jnp.zeros((TILE // 2, TILE // 2), f32)
                upper, lower = band[: TILE // 2], band[TILE // 2 :]
                lines = jnp.concatenate([zero, zero, upper], axis=1) + jnp.concatenate(
                    [zero, lower, zero], axis=1
                )
                half = TILE // 4
                while half >= 8:
                    lines = lines[:half] + pltpu.roll(lines[half:], 2 * TILE - half, 1)
                    half //= 2
                total = lines[0:1]
                for row in range(1, 8):
                    total = total + pltpu.roll(lines[row : row + 1], 2 * TILE - row, 1)
                band_out_ref[h, place] = total
            return 0

        lax.fori_loop(0, band_ref.shape[1], one, 0)


def attend_backward(qt, kt, vt, ot, got, lse, bias, end, least, clear):
    heads, size, length = qt.shape
    count = length // TILE
    tiles = bias.shape[1]
    smem = pl.BlockSpec(memory_space=pltpu.SMEM)
    operands = (qt, kt, vt, ot, got, lse, bias, end)
    outs = [((3, heads, size, length), bf16), ((heads, tiles, 1, 2 * TILE), f32)]
    return pl.pallas_call(
        backward_kernel,
        grid=(count,),
        in_specs=[smem, smem] + [whole(a.shape) for a in operands],
        out_specs=[whole(shape) for shape, _ in outs],
        out_shape=[jax.ShapeDtypeStruct(shape, kind) for shape, kind in outs],
        scratch_shapes=[
            pltpu.VMEM((heads, length, size), bf16),
            pltpu.VMEM((heads, length, size), bf16),
            pltpu.VMEM((heads, size, length), f32),
            pltpu.VMEM((heads, TILE, size), f32),
            pltpu.VMEM((heads, TILE, size), f32),
            pltpu.VMEM((heads, 1, length), f32),
            pltpu.VMEM((heads, tiles, TILE, TILE), f32),
        ],
        compiler_params=params(),
        name="attend_backward",
    )(least, clear, *operands)


def feed_kernel(second_ref, grad_ref, weight_ref, out_ref, dsecond_ref, grads_ref):
    width = second_ref.shape[1]

    @pl.when(pl.program_id(0) == 0)
    def _():
        out_ref[...] = jnp.zeros_like(out_ref)
        dsecond_ref[...] = jnp.zeros_like(dsecond_ref)

    second = second_ref[...]
    grad = grad_ref[...]
    hidden = weight_ref.shape[2] // 2
    inner = weight_ref[0, :, :hidden]
    outer = weight_ref[0, :, hidden:]
    grad_active = dot(grad, outer).astype(bf16).astype(f32)
    units = dot(second, inner)
    active, slope = gelu_parts(units)
    active = active.astype(bf16)
    grad_units = (grad_active * slope).astype(bf16)
    out_ref[...] += dot(active, outer, ((1,), (1,)))
    dsecond_ref[...] += dot(grad_units, inner, ((1,), (1,)))
    grads_ref[0, :, :hidden] = dot(second, grad_units, ((0,), (0,))).astype(bf16)
    grads_ref[0, :, hidden:] = dot(grad, active, ((0,), (0,))).astype(bf16)


def feed_forward(second, grad, weights):
    rows, width = second.shape
    parts, _, columns = weights.shape
    return pl.pallas_call(
        feed_kernel,
        grid=(parts,),
        in_specs=[
            whole(second.shape),
            whole(grad.shape),
            pl.BlockSpec((1, width, columns), lambda i: (i, 0, 0)),
        ],
        out_specs=[
            whole((rows, width)),
            whole((rows, width)),
            pl.BlockSpec((1, width, columns), lambda i: (i, 0, 0)),
        ],
        out_shape=[
            jax.ShapeDtypeStruct((rows, width), f32),
            jax.ShapeDtypeStruct((rows, width), f32),
            jax.ShapeDtypeStruct(weights.shape, bf16),
        ],
        compiler_params=params(),
        name="feed_forward",
    )(second, grad, weights)


def body(
    inputs,
    attention_gain,
    feedforward_gain,
    query_weight,
    key_weight,
    value_weight,
    output_weight,
    inner_weight,
    outer_weight,
    bias_table,
    block_index,
    position_bucket,
    cotangent,
):
    length = block_index.shape[1]
    parts = lax.axis_size("tensor")
    groups = lax.axis_size("dp")
    factor = 1.0 / math.sqrt(block_index.shape[0] * length * groups)
    heads = bias_table.shape[1]
    width = inputs.shape[1]
    size = query_weight.shape[1] // heads
    columns = heads * size

    packed_attention = jnp.concatenate([query_weight, key_weight, value_weight], axis=1)
    packed_feed = jnp.concatenate([inner_weight, outer_weight.T], axis=1)
    attention_full = lax.all_gather(packed_attention, "dp", axis=0, tiled=True)
    output_full = lax.all_gather(output_weight.T, ("tensor", "dp"), axis=0, tiled=True).reshape(
        parts, width, columns
    )
    feed_full = lax.all_gather(packed_feed, ("tensor", "dp"), axis=0, tiled=True).reshape(
        parts, width, packed_feed.shape[1]
    )

    rows, onehot = bias_rows(bias_table, position_bucket)
    bias = bias_tiles(rows, length)
    end, full, most, least, clear = spans(block_index[0])

    inputs_wide = inputs.astype(f32)
    scaled_first, inverse_first, normed_local = norm_forward(inputs_wide, attention_gain)
    normed = lax.all_gather(normed_local, "tensor", axis=0, tiled=True)
    qkv = dot(attention_full, normed, ((0,), (1,))).astype(bf16).reshape(3, heads, size, length)
    qt, kt, vt = qkv[0], qkv[1], qkv[2]
    ot, lse = attend_forward(qt, kt, vt, bias, end, full, most, parts)
    mix = lax.all_to_all(ot.reshape(parts, columns, length // parts), "tensor", 0, 0)
    hidden = inputs_wide + sum(dot(mix[z], output_full[z], ((0,), (1,))) for z in range(parts))
    scaled_second, inverse_second, second = norm_forward(hidden, feedforward_gain)
    feed_out, grad_second, feed_grads = feed_forward(second, cotangent, feed_full)
    layer_output = (hidden + feed_out).astype(bf16)
    feedforward_part = jnp.sum(grad_second * scaled_second, axis=0)
    grad_hidden = cotangent.astype(f32) + norm_backward(
        grad_second, scaled_second, inverse_second, feedforward_gain
    )
    grad_mix_rows = grad_hidden.astype(bf16)
    output_grads = jnp.stack(
        [dot(grad_mix_rows, mix[z], ((0,), (1,))) for z in range(parts)]
    ).astype(bf16)
    grad_mix = jnp.stack(
        [dot(output_full[z], grad_mix_rows, ((0,), (1,))) for z in range(parts)]
    ).astype(bf16)
    got = lax.all_to_all(grad_mix, "tensor", 0, 0).reshape(ot.shape)
    dqkv, bands = attend_backward(qt, kt, vt, ot, got, lse, bias, end, least, clear)
    dqkv = dqkv.reshape(3 * columns, length)
    attention_grads = dot(normed, dqkv, ((0,), (1,)))
    grad_normed = dot(dqkv, attention_full, ((0,), (1,)))
    grad_first = lax.psum_scatter(
        grad_normed.astype(bf16), "tensor", scatter_dimension=0, tiled=True
    ).astype(f32)
    input_grad = (
        grad_hidden + norm_backward(grad_first, scaled_first, inverse_first, attention_gain)
    ).astype(bf16)
    attention_part = jnp.sum(grad_first * scaled_first, axis=0)

    table_local = table_part(bands, onehot, length)
    table_whole = lax.dynamic_update_slice(
        jnp.zeros((table_local.shape[0], H), f32),
        table_local,
        (jnp.zeros((), jnp.int32), lax.axis_index("tensor") * heads),
    )
    attention_gain_grad, feedforward_gain_grad, table_grad = lax.psum(
        (attention_part * factor, feedforward_part * factor, table_whole * factor), ("dp", "tensor")
    )

    attention_share = (
        lax.psum_scatter(attention_grads.astype(bf16), "dp", scatter_dimension=0, tiled=True)
        .astype(f32)
        * factor
    )
    output_share = (
        lax.psum_scatter(
            output_grads.reshape(parts * width, columns),
            ("tensor", "dp"),
            scatter_dimension=0,
            tiled=True,
        ).astype(f32)
        * factor
    )
    feed_share = (
        lax.psum_scatter(
            feed_grads.reshape(parts * width, packed_feed.shape[1]),
            ("tensor", "dp"),
            scatter_dimension=0,
            tiled=True,
        ).astype(f32)
        * factor
    )
    hidden_units = inner_weight.shape[1]
    return (
        layer_output,
        input_grad,
        attention_gain_grad,
        feedforward_gain_grad,
        attention_share[:, :columns],
        attention_share[:, columns : 2 * columns],
        attention_share[:, 2 * columns :],
        output_share.T,
        feed_share[:, :hidden_units],
        feed_share[:, hidden_units:].T,
        table_grad,
    )


def solution(mesh):
    tokens = P(("dp", "tensor"), None)
    by_rows = P("dp", "tensor")
    by_columns = P("tensor", "dp")
    placed = (
        tokens, P(), P(), by_rows, by_rows, by_rows, by_columns, by_rows, by_columns,
        P(None, "tensor"), P("dp", None), P(), tokens,
    )
    results = (
        tokens, tokens, P(), P(), by_rows, by_rows, by_rows, by_columns, by_rows, by_columns, P(),
    )
    return jax.shard_map(body, mesh=mesh, in_specs=placed, out_specs=results, check_vma=False)
```

profile of v0, /device:TPU:9, one launch (start us, length us, event | category | flops | bytes accessed | tf_op | source)
XLA Modules:
  0.0 602.1 jit_solution(6542364863052603783)
XLA Ops:
  7.3 1.5 fusion.11
  8.8 2.3 fusion.8
  14.7 6.5 %bias_tiles.1.bias_ref = f32[3,10,256,256]{3,2,1,0:T(8,128)} custom-call(f32[3,1,2816]{2,1,0:T(1,128)} %slice.108.row_ref), custom_call_target="tpu_custom_call" | custom-call | tf_op jit(solution)/shard_map/bias_tiles/pallas_call | solution.py:79
  21.5 11.4 %all_gather.12 = bf16[768,576]{1,0:T(8,128)(2,1)S(1)} all-gather(bf16[96,576]{1,0:T(8,128)(2,1)S(1)} %pad_maximum_fusion.3), channel_id=1, replica_groups=mesh['dp'=8,'tensor'=4] {'dp'}, dimensions={0}, use_global_device_ids=true | all-gather | bytes 995328 | tf_op jit(solution)/shard_map/all_gather | solution.py:400
  33.5 39.9 %all-gather.4.cloned.1.call-done = bf16[2048,768]{1,0:T(8,128)(2,1)} async-done(((bf16[512,768]{1,0:T(8,128)(2,1)}), bf16[2048,768]{1,0:T(8,128)(2,1)}) %all-gather.4.cloned.1.call-update) | async-done | bytes 3145744 | tf_op jit(solution)/shard_map/all_gather | solution.py:414
  73.4 4.3 convolution_convert_fusion.1
  77.7 1.5 fusion.35
  79.2 42.4 %attend_forward.1 = (bf16[4,3,64,512]{3,2,1,0:T(8,128)(2,1)}, f32[3,1,2048]{2,1,0:T(1,128)}) custom-call(s32[8]{0:T(128)} %get-tuple-element.49.full_ref, s32[8]{0:T(128)} %get-tuple-element.48.most_ref, bf16[3,64,2048]{2,1,0:T(8,128)(2,1)} %bitcast.88, bf16[3,64,2048]{2,1,0:T(8,128)(2,1)} %bitcast.86, bf16[3,64,2048]{2,1,0:T(8,128)(2,1)} %bitcast.84, ...), custom_call_target="tpu_custom_call" | custom-call | tf_op jit(solution)/shard_map/attend_forward/pallas_call | solution.py:175
  121.6 6.1 %all-to-all-start = ((bf16[4,192,512]{2,1,0:T(8,128)(2,1)}), bf16[4,192,512]{2,1,0:T(8,128)(2,1)S(1)}, u32[]{:S(2)}, u32[]{:S(2)}) async-start(bf16[4,192,512]{2,1,0:T(8,128)(2,1)} %bitcast.91), calls=%async_computation | async-start | bytes 1572864 | tf_op jit(solution)/shard_map/all_to_all | solution.py:418
  127.7 5.0 all-gather.6.cloned.1.call-done
  132.8 11.1 %all-to-all-done = bf16[4,192,512]{2,1,0:T(8,128)(2,1)S(1)} async-done(((bf16[4,192,512]{2,1,0:T(8,128)(2,1)}), bf16[4,192,512]{2,1,0:T(8,128)(2,1)S(1)}, u32[]{:S(2)}, u32[]{:S(2)}) %all-to-all-start) | async-done | bytes 786464 | tf_op jit(solution)/shard_map/all_to_all | solution.py:418
  143.9 1.7 fusion.25
  147.2 1.7 multiply_reduce_fusion.2
  149.0 1.1 multiply_convert_fusion.second_ref
  150.1 68.6 %all-gather.8.cloned.1.call-done = bf16[3072,1536]{1,0:T(8,128)(2,1)} async-done(((bf16[96,1536]{1,0:T(8,128)(2,1)}), bf16[3072,1536]{1,0:T(8,128)(2,1)}) %all-gather.8.cloned.1.call-update) | async-done | bytes 9437200 | tf_op jit(solution)/shard_map/all_gather | solution.py:404
  218.7 19.8 %feed_forward.1 = (f32[512,768]{1,0:T(8,128)}, f32[512,768]{1,0:T(8,128)}, bf16[4,768,1536]{2,1,0:T(8,128)(2,1)}) custom-call(bf16[512,768]{1,0:T(8,128)(2,1)} %multiply_convert_fusion.second_ref, bf16[512,768]{1,0:T(8,128)(2,1)} %grad_ref.1, bf16[4,768,1536]{2,1,0:T(8,128)(2,1)} %bitcast.83), custom_call_target="tpu_custom_call" | custom-call | tf_op jit(solution)/shard_map/feed_forward/pallas_call | solution.py:351
  238.5 2.7 multiply_reduce_fusion
  245.4 4.5 all-to-all-start.1
  249.8 1.3 fusion.12
  251.2 1.3 fusion.13
  253.3 1.6 copy.36
  256.7 10.1 %all-to-all-done.1 = bf16[4,192,512]{2,1,0:T(8,128)(2,1)} async-done(((bf16[4,192,512]{2,1,0:T(8,128)(2,1)}), bf16[4,192,512]{2,1,0:T(8,128)(2,1)}, u32[]{:S(2)}, u32[]{:S(2)}) %all-to-all-start.1) | async-done | bytes 786464 | tf_op jit(solution)/shard_map/all_to_all | solution.py:434
  266.8 51.5 %attend_backward.1 = (bf16[3,3,64,2048]{3,2,1,0:T(8,128)(2,1)}, f32[3,10,1,512]{3,2,1,0:T(1,128)}) custom-call(s32[8]{0:T(128)} %convert_reduce_fusion.2.least_ref, s32[8]{0:T(128)} %convert_reduce_fusion.1.clear_ref, bf16[3,64,2048]{2,1,0:T(8,128)(2,1)} %bitcast.89, bf16[3,64,2048]{2,1,0:T(8,128)(2,1)} %bitcast.87, bf16[3,64,2048]{2,1,0:T(8,128)(2,1)} %bitcast.85, ...), custom_call_target="tpu_custom_call" | custom-call | tf_op jit(solution)/shard_map/attend_backward/pallas_call | solution.py:304
  318.3 6.3 %convolution_convert_fusion.2 = bf16[768,576]{1,0:T(8,128)(2,1)} fusion(bf16[2048,768]{1,0:T(8,128)(2,1)} %all-gather.4.cloned.1.call-done, bf16[576,2048]{1,0:T(8,128)(2,1)} %bitcast.100), kind=kOutput, calls=%fused_computation.25 | convolution fusion | flops 1812381696 | bytes 6389760 | tf_op jit(solution)/shard_map/dot_general | solution.py:21
  324.7 6.0 %convolution_convert_fusion = bf16[2048,768]{1,0:T(8,128)(2,1)} fusion(bf16[576,2048]{1,0:T(8,128)(2,1)} %bitcast.101, bf16[768,576]{1,0:T(8,128)(2,1)S(1)} %copy-done.11), kind=kOutput, calls=%fused_computation.1 | convolution fusion | flops 1813512192 | bytes 6389760 | tf_op jit(solution)/shard_map/dot_general | solution.py:21
  332.2 18.5 %reduce-scatter.13.cloned.1.call-done = bf16[96,192]{1,0:T(8,128)(2,1)} async-done(((bf16[3072,192]{1,0:T(8,128)(2,1)}), bf16[96,192]{1,0:T(8,128)(2,1)}) %reduce-scatter.13.cloned.1.call-update) | async-done | bytes 36880
  352.3 37.9 %reduce-scatter.9.cloned.1.call-done = bf16[96,576]{1,0:T(8,128)(2,1)} async-done(((bf16[768,576]{1,0:T(8,128)(2,1)}), bf16[96,576]{1,0:T(8,128)(2,1)}) %reduce-scatter.9.cloned.1.call-update) | async-done | bytes 110608 | tf_op jit(solution)/shard_map/reduce_scatter | solution.py:458
  391.9 60.5 %reduce-scatter.7.cloned.1.call-done = bf16[512,768]{1,0:T(8,128)(2,1)} async-done(((bf16[2048,768]{1,0:T(8,128)(2,1)}), bf16[512,768]{1,0:T(8,128)(2,1)}) %reduce-scatter.7.cloned.1.call-update) | async-done | bytes 786448 | tf_op jit(solution)/shard_map/reduce_scatter | solution.py:439
  452.4 1.8 fusion.10
  454.3 39.7 %all-reduce.2 = (f32[768]{0:T(1024)}, f32[768]{0:T(1024)}, f32[32,12]{0,1:T(8,128)}) all-reduce(f32[768]{0:T(1024)S(1)} %broadcast_multiply_fusion.2, f32[768]{0:T(1024)S(1)} %broadcast_multiply_fusion.1, f32[32,12]{0,1:T(8,128)S(1)} %broadcast_multiply_fusion), channel_id=1, replica_groups=mesh['dp'=8,'tensor'=4] {'dp','tensor'}, use_global_device_ids=true, to_apply=%region_10.11 | all-reduce | flops 1920 | bytes 15360 | tf_op jit(solution)/shard_map/psum | solution.py:453
  494.0 4.4 fusion.7
  498.4 95.0 %reduce-scatter.11.cloned.1.call-done = bf16[96,1536]{1,0:T(8,128)(2,1)} async-done(((bf16[3072,1536]{1,0:T(8,128)(2,1)}), bf16[96,1536]{1,0:T(8,128)(2,1)}) %reduce-scatter.11.cloned.1.call-update) | async-done | bytes 294928 | tf_op jit(solution)/shard_map/reduce_scatter | solution.py:472
  (123 shorter events, 19.3 us)
Async XLA Ops:
  7.2 6.6 %copy-start = (f32[32,3]{0,1:T(4,128)S(1)}, f32[32,3]{0,1:T(4,128)}, u32[]{:S(2)}) copy-start(f32[32,3]{0,1:T(4,128)} %param.22) | copy-start | bytes 1156
  7.2 3.9 copy-start.19
  7.2 4.7 copy-start.12
  7.2 4.7 copy-start.13
  7.2 66.2 %all-gather.4.cloned.1.call-start = ((), (), s32[]{:S(2)}) async-start(), calls=%async_computation.6 | async-start | bytes 3932160 | tf_op jit(solution)/shard_map/all_gather | solution.py:414
  8.7 4.0 copy-start.24
  8.7 4.2 copy-start.28
  11.1 121.7 %all-gather.6.cloned.1.call-start = ((), (), s32[]{:S(2)}) async-start(), calls=%async_computation.7 | async-start | bytes 1622016 | tf_op jit(solution)/shard_map/all_gather | solution.py:401
  11.9 206.8 %all-gather.8.cloned.1.call-start = ((), (), s32[]{:S(2)}) async-start(), calls=%async_computation.8 | async-start | bytes 9732096 | tf_op jit(solution)/shard_map/all_gather | solution.py:404
  12.9 8.3 %copy-start.14 = (s32[2048]{0:T(1024)}, s32[2048]{0:T(1024)S(1)}, u32[]{:S(2)}) copy-start(s32[2048]{0:T(1024)S(1)} %select_reduce_fusion) | copy-start | bytes 24580
  14.7 6.7 %copy-start.20 = (bf16[96,192]{1,0:T(8,128)(2,1)S(1)}, bf16[96,192]{1,0:T(8,128)(2,1)}, u32[]{:S(2)}) copy-start(bf16[96,192]{1,0:T(8,128)(2,1)} %param.18) | copy-start | bytes 110596
  14.7 6.7 %copy-start.21 = (bf16[96,192]{1,0:T(8,128)(2,1)S(1)}, bf16[96,192]{1,0:T(8,128)(2,1)}, u32[]{:S(2)}) copy-start(bf16[96,192]{1,0:T(8,128)(2,1)} %param.17) | copy-start | bytes 110596
  14.7 6.7 %copy-start.22 = (bf16[96,192]{1,0:T(8,128)(2,1)S(1)}, bf16[96,192]{1,0:T(8,128)(2,1)}, u32[]{:S(2)}) copy-start(bf16[96,192]{1,0:T(8,128)(2,1)} %param.16) | copy-start | bytes 110596
  32.9 44.8 %copy-start.10 = (bf16[768,576]{1,0:T(8,128)(2,1)}, bf16[768,576]{1,0:T(8,128)(2,1)S(1)}, u32[]{:S(2)}) copy-start(bf16[768,576]{1,0:T(8,128)(2,1)S(1)} %all_gather.12) | copy-start | bytes 2654212
  121.6 22.3 %all-to-all-start = ((bf16[4,192,512]{2,1,0:T(8,128)(2,1)}), bf16[4,192,512]{2,1,0:T(8,128)(2,1)S(1)}, u32[]{:S(2)}, u32[]{:S(2)}) async-start(bf16[4,192,512]{2,1,0:T(8,128)(2,1)} %bitcast.91), calls=%async_computation | async-start | bytes 1572864 | tf_op jit(solution)/shard_map/all_to_all | solution.py:418
  132.8 12.9 %copy-start.8 = (bf16[3072,192]{1,0:T(8,128)(2,1)S(1)}, bf16[3072,192]{1,0:T(8,128)(2,1)}, u32[]{:S(2)}) copy-start(bf16[3072,192]{1,0:T(8,128)(2,1)} %all-gather.6.cloned.1.call-done) | copy-start | bytes 3538948
  143.9 2.6 copy-start.4
  147.2 1.8 copy-start.15
  238.5 2.7 copy-start.3
  238.5 2.7 copy-start.6
  245.4 21.5 %all-to-all-start.1 = ((bf16[4,192,512]{2,1,0:T(8,128)(2,1)}), bf16[4,192,512]{2,1,0:T(8,128)(2,1)}, u32[]{:S(2)}, u32[]{:S(2)}) async-start(bf16[4,192,512]{2,1,0:T(8,128)(2,1)} %pad_maximum_fusion.1), calls=%async_computation.1 | async-start | bytes 1572864 | tf_op jit(solution)/shard_map/all_to_all | solution.py:434
  249.8 100.9 %reduce-scatter.13.cloned.1.call-start = ((), (), s32[]{:S(2)}) async-start(), calls=%async_computation.12 | async-start | bytes 1622016
  249.8 2.6 copy-start.5
  253.3 2.9 copy-start.29
  254.9 135.3 %reduce-scatter.9.cloned.1.call-start = ((), (), s32[]{:S(2)}) async-start(), calls=%async_computation.10 | async-start | bytes 1105920 | tf_op jit(solution)/shard_map/reduce_scatter | solution.py:458
  318.3 6.4 %copy-start.11 = (bf16[768,576]{1,0:T(8,128)(2,1)S(1)}, bf16[768,576]{1,0:T(8,128)(2,1)}, u32[]{:S(2)}) copy-start(bf16[768,576]{1,0:T(8,128)(2,1)} %copy-done.10) | copy-start | bytes 2654212
  324.7 127.8 %reduce-scatter.7.cloned.1.call-start = ((), (), s32[]{:S(2)}) async-start(), calls=%async_computation.9 | async-start | bytes 3932160 | tf_op jit(solution)/shard_map/reduce_scatter | solution.py:439
  330.8 262.6 %reduce-scatter.11.cloned.1.call-start = ((), (), s32[]{:S(2)}) async-start(), calls=%async_computation.11 | async-start | bytes 9732096 | tf_op jit(solution)/shard_map/reduce_scatter | solution.py:472
  331.5 120.9 %copy-start.23 = (f32[768]{0:T(1024)S(1)}, f32[768]{0:T(1024)}, u32[]{:S(2)}) copy-start(f32[768]{0:T(1024)} %param.14) | copy-start | bytes 9220
  331.8 162.1 %copy-start.7 = (bf16[512,768]{1,0:T(8,128)(2,1)S(1)}, bf16[512,768]{1,0:T(8,128)(2,1)}, u32[]{:S(2)}) copy-start(bf16[512,768]{1,0:T(8,128)(2,1)} %grad_ref.1) | copy-start | bytes 2359300
  331.8 162.1 %copy-start.26 = (f32[512]{0:T(512)S(1)}, f32[512]{0:T(512)}, u32[]{:S(2)}) copy-start(f32[512]{0:T(512)} %copy-done.25) | copy-start | bytes 6148
  493.9 101.3 %copy-start.1 = (f32[32,3]{0,1:T(4,128)S(1)}, f32[32,3]{0,1:T(4,128)}, u32[]{:S(2)}) copy-start(f32[32,3]{0,1:T(4,128)} %param.22) | copy-start | bytes 1156
  (8 other events, 6.7 us)
Sparse Core Ops, SparseCore 0:
  11.2 62.2 all-gather.3
  76.9 55.8 all-gather.5
  136.3 82.4 all-gather.7
  255.6 95.0 reduce-scatter.12
  353.8 36.3 reduce-scatter.8
  392.5 59.9 reduce-scatter.6
  459.3 133.9 reduce-scatter.10
where the time goes:
time: 606 us; the launch traced here: 602 us
  waiting for transfers between devices  348 us (57%)
  Pallas kernels  120 us (20%)
  blocking collectives  51.1 us (8%)
  matrix products  26.4 us (4%)
  other arithmetic  21.2 us (3%)
  between operations  14.6 us (2%)
  starting transfers between devices  11.1 us (2%)
  local copies, waits for them, and re-layouts  9.94 us (2%)
    reduce_scatter x1, waiting for transfers between devices, body(): lax.psum_scatter(feed_grads.reshape(parts * width, packed_feed.shape[1]),...  95 us
    all_gather x1, waiting for transfers between devices, body(): lax.all_gather(packed_feed, ('tensor', 'dp'), axis=0, tiled=True)  68.6 us
    reduce_scatter x1, waiting for transfers between devices, body(): lax.psum_scatter(grad_normed.astype(bf16), 'tensor', scatter_dimension=0,...  60.5 us
    pallas_call x1, Pallas kernels, attend_backward(): pl.pallas_call(backward_kernel, grid=(count,), in_specs=[smem, smem] + [w...  51.5 us
    pallas_call x1, Pallas kernels, attend_forward(): pl.pallas_call(forward_kernel, grid=(count,), in_specs=[smem, smem, pl.Bl...  42.4 us
    all_gather x1, waiting for transfers between devices, body(): normed = lax.all_gather(normed_local, 'tensor', axis=0, tiled=True)  39.9 us
    psum x1, blocking collectives, body(): lax.psum((attention_part * factor, feedforward_part * factor, table_whole...  39.7 us
    reduce_scatter x1, waiting for transfers between devices, body(): lax.psum_scatter(attention_grads.astype(bf16), 'dp', scatter_dimension=0,...  37.9 us
  transfers between devices with their start and end apart: 9, of which 9 were waited for; matrix products, arithmetic and copies ran while one was open for 7% of the time, Pallas kernels for 17%

commit v1 on v0

v1 whole, which is shorter than its diff:
```python
import math

import jax
import jax.numpy as jnp
from jax import lax
from jax.experimental import pallas as pl
from jax.experimental.pallas import tpu as pltpu
from jax.sharding import Mesh, PartitionSpec as P

H = 12
EPSILON = 1e-06
MASKED = -1e30
TILE = 256
AHEAD = 2
BLOCKS = 8
VMEM_LIMIT = 60 * 1024 * 1024
f32, bf16 = jnp.float32, jnp.bfloat16


def dot(left, right, contract=((1,), (0,))):
    return lax.dot_general(left, right, (contract, ((), ())), preferred_element_type=f32)


def norm_forward(values, gain):
    inverse = lax.rsqrt(jnp.mean(values * values, axis=-1, keepdims=True) + EPSILON)
    scaled = values * inverse
    return scaled, inverse, (scaled * gain).astype(bf16)


def norm_backward(grad_normed, scaled, inverse, gain):
    grad_scaled = grad_normed * gain
    return inverse * (
        grad_scaled - scaled * jnp.mean(grad_scaled * scaled, axis=-1, keepdims=True)
    )


def gelu_parts(values):
    cumulative = 0.5 * (1.0 + lax.erf(values * (1.0 / math.sqrt(2.0))))
    density = jnp.exp(-0.5 * values * values) * (1.0 / math.sqrt(2.0 * math.pi))
    return values * cumulative, cumulative + values * density


def whole(shape):
    return pl.BlockSpec(shape, lambda *_: (0,) * len(shape), pipeline_mode=pl.Buffered(1))


def params():
    return pltpu.CompilerParams(vmem_limit_bytes=VMEM_LIMIT)


def bias_rows(bias_table, position_bucket):
    bucket = jnp.concatenate([position_bucket, jnp.zeros((1,), jnp.int32)])[::-1]
    names = jnp.arange(bias_table.shape[0], dtype=jnp.int32)
    onehot = (bucket[None, :] == names[:, None]).astype(f32)
    rows = lax.dot_general(
        bias_table, onehot, (((0,), (0,)), ((), ())), precision=lax.Precision.HIGHEST
    )
    return rows[:, None, :], onehot


def bias_kernel(row_ref, out_ref):
    tiles = out_ref.shape[1]

    def one(place, _):
        start = pl.multiple_of((tiles - 1 - place) * TILE, TILE)
        piece = row_ref[0, :, pl.ds(start, 2 * TILE)]
        spread = jnp.broadcast_to(piece, (TILE, 2 * TILE))
        out_ref[0, place] = pltpu.roll(spread, 0, 1, stride=1, stride_axis=0)[:, TILE:]
        return 0

    lax.fori_loop(0, tiles, one, 0)


def bias_tiles(rows, length):
    heads = rows.shape[0]
    count = length // TILE
    rows = rows[:, :, (count - 1 - AHEAD) * TILE :]
    tiles = count + AHEAD
    return pl.pallas_call(
        bias_kernel,
        grid=(heads,),
        in_specs=[pl.BlockSpec((1, 1, rows.shape[2]), lambda h: (h, 0, 0))],
        out_specs=pl.BlockSpec((1, tiles, TILE, TILE), lambda h: (h, 0, 0, 0)),
        out_shape=jax.ShapeDtypeStruct((heads, tiles, TILE, TILE), f32),
        compiler_params=params(),
        name="bias_tiles",
    )(rows)


def table_part(bands, onehot, length):
    heads, tiles = bands.shape[:2]
    pieces = bands[:, ::-1, 0, :]
    pad = jnp.zeros((heads, 1, TILE), f32)
    line = jnp.concatenate([pieces[:, :, :TILE], pad], 1) + jnp.concatenate(
        [pad, pieces[:, :, TILE:]], 1
    )
    line = line.reshape(heads, (tiles + 1) * TILE)
    base = (length // TILE - 1 - AHEAD) * TILE
    return lax.dot_general(
        onehot[:, base : base + line.shape[1]],
        line,
        (((1,), (1,)), ((), ())),
        precision=lax.Precision.HIGHEST,
    )


def spans(block_row):
    length = block_row.shape[0]
    names = jnp.arange(BLOCKS, dtype=jnp.int32)[:, None]
    upto = jnp.sum(block_row[None, :] <= names, axis=1, dtype=jnp.int32)
    end = jnp.sum(jnp.where(block_row[None, :] == names, upto[:, None], 0), axis=0, dtype=jnp.int32)
    by_tile = end.reshape(length // TILE, TILE)
    full = by_tile[:, 0] // TILE
    most = (by_tile[:, TILE - 1] + TILE - 1) // TILE
    places = jnp.arange(length // TILE, dtype=jnp.int32)[:, None]
    least = jnp.sum(most[None, :] <= places, axis=1, dtype=jnp.int32)
    clear = jnp.sum(full[None, :] <= places, axis=1, dtype=jnp.int32)
    return end.reshape(1, length), full, most, least, clear


def forward_kernel(full_ref, most_ref, slot_ref, group_ref, *refs):
    parts = slot_ref.shape[0]
    pieces = refs[:parts]
    bias_ref, end_ref, ot_ref, lse_ref, qt_ref, k_ref, vt_ref, acc_ref, stat_ref = refs[parts:]
    heads, size, length = qt_ref.shape
    count = length // TILE
    each = count // parts
    query = pl.program_id(0)

    @pl.when(query == 0)
    def _():
        for i, piece in enumerate(pieces):
            places = pl.ds(pl.multiple_of(slot_ref[i] * (length // parts), TILE), length // parts)
            for h in range(heads):
                qt_ref[h, :, places] = piece[h]
                k_ref[h, places, :] = piece[heads + h].T
                vt_ref[h, :, places] = piece[2 * heads + h]

    own = pl.ds(pl.multiple_of(query * TILE, TILE), TILE)
    acc_ref[...] = jnp.zeros_like(acc_ref)
    stat_ref[0] = jnp.full(stat_ref.shape[1:], -jnp.inf, f32)
    stat_ref[1] = jnp.zeros(stat_ref.shape[1:], f32)

    def step(key, masked):
        start = pl.multiple_of(key * TILE, TILE)
        if masked:
            keep = lax.broadcasted_iota(jnp.int32, (TILE, TILE), 0) + start < end_ref[...]
        for h in range(heads):
            scores = dot(k_ref[h, pl.ds(start, TILE), :], qt_ref[h, :, own])
            scores = scores + bias_ref[h, key - query + count - 1]
            if masked:
                scores = jnp.where(keep, scores, MASKED)
            old = stat_ref[0, h]
            new = jnp.maximum(old, jnp.max(scores, axis=0, keepdims=True))
            weights = jnp.exp(scores - new)
            scale = jnp.exp(old - new)
            stat_ref[0, h] = new
            stat_ref[1, h] = stat_ref[1, h] * scale + jnp.sum(weights, axis=0, keepdims=True)
            acc_ref[h] = acc_ref[h] * scale + dot(
                vt_ref[h, :, pl.ds(start, TILE)], weights.astype(bf16)
            )

    def full_step(key, _):
        step(key, False)
        return 0

    def edge_step(key, _):
        step(key, True)
        return 0

    lax.fori_loop(0, full_ref[query], full_step, 0)
    lax.fori_loop(full_ref[query], most_ref[query], edge_step, 0)
    turn = lax.rem(query // each - group_ref[0] + parts, parts)
    inner = pl.ds(pl.multiple_of(lax.rem(query, each) * TILE, TILE), TILE)
    for h in range(heads):
        total = stat_ref[1, h]
        ot_ref[turn, h, :, inner] = (acc_ref[h] * (1.0 / total)).astype(bf16)
        lse_ref[h] = stat_ref[0, h] + jnp.log(total)


def attend_forward(pieces, bias, end, full, most, slots, group):
    parts = len(pieces)
    triple, size, part_length = pieces[0].shape
    heads, length = triple // 3, parts * part_length
    count = length // TILE
    smem = pl.BlockSpec(memory_space=pltpu.SMEM)
    return pl.pallas_call(
        forward_kernel,
        grid=(count,),
        in_specs=[smem] * 4
        + [whole(piece.shape) for piece in pieces]
        + [whole(bias.shape), pl.BlockSpec((1, TILE), lambda i: (0, i))],
        out_specs=[
            whole((parts, heads, size, part_length)),
            pl.BlockSpec((heads, 1, TILE), lambda i: (0, 0, i)),
        ],
        out_shape=[
            jax.ShapeDtypeStruct((parts, heads, size, part_length), bf16),
            jax.ShapeDtypeStruct((heads, 1, length), f32),
        ],
        scratch_shapes=[
            pltpu.VMEM((heads, size, length), bf16),
            pltpu.VMEM((heads, length, size), bf16),
            pltpu.VMEM((heads, size, length), bf16),
            pltpu.VMEM((heads, size, TILE), f32),
            pltpu.VMEM((2, heads, 1, TILE), f32),
        ],
        compiler_params=params(),
        name="attend_forward",
    )(full, most, slots, group, *pieces, bias, end)


def backward_kernel(least_ref, clear_ref, slot_ref, group_ref, *refs):
    parts = slot_ref.shape[0]
    pieces, grads = refs[:parts], refs[parts : 2 * parts]
    (
        ot_ref, lse_ref, bias_ref, end_ref, out_ref, band_out_ref,
        qt_ref, kt_ref, vt_ref, got_ref, q_ref, go_ref,
        dqt_acc, dk_acc, dv_acc, delta_ref, band_ref,
    ) = refs[2 * parts :]
    heads, size, length = qt_ref.shape
    count = length // TILE
    each = count // parts
    part_length = length // parts
    key = pl.program_id(0)
    key_cols = pl.ds(pl.multiple_of(key * TILE, TILE), TILE)

    @pl.when(key == 0)
    def _():
        dqt_acc[...] = jnp.zeros_like(dqt_acc)
        band_ref[...] = jnp.zeros_like(band_ref)
        for i, piece in enumerate(pieces):
            places = pl.ds(pl.multiple_of(slot_ref[i] * part_length, TILE), part_length)
            for h in range(heads):
                qt_ref[h, :, places] = piece[h]
                q_ref[h, places, :] = piece[h].T
                kt_ref[h, :, places] = piece[heads + h]
                vt_ref[h, :, places] = piece[2 * heads + h]
        for turn, grad_piece in enumerate(grads):
            part = lax.rem(group_ref[0] + turn, parts)
            places = pl.ds(pl.multiple_of(part * part_length, TILE), part_length)
            for h in range(heads):
                grad = grad_piece[h]
                got_ref[h, :, places] = grad
                go_ref[h, places, :] = grad.T
                delta_ref[h, :, places] = jnp.sum(
                    ot_ref[turn, h].astype(f32) * grad.astype(f32), axis=0, keepdims=True
                )

    dk_acc[...] = jnp.zeros_like(dk_acc)
    dv_acc[...] = jnp.zeros_like(dv_acc)
    kt = [kt_ref[h, :, key_cols] for h in range(heads)]
    k = [tile.T for tile in kt]
    v = [vt_ref[h, :, key_cols].T for h in range(heads)]

    def step(query, masked):
        cols = pl.ds(pl.multiple_of(query * TILE, TILE), TILE)
        if masked:
            keep = lax.broadcasted_iota(jnp.int32, (TILE, TILE), 0) + key * TILE < end_ref[:, cols]
        place = key - query + count - 1
        for h in range(heads):
            scores = dot(k[h], qt_ref[h, :, cols])
            scores = scores + bias_ref[h, place]
            if masked:
                scores = jnp.where(keep, scores, MASKED)
            weights = jnp.exp(scores - lse_ref[h, :, cols])
            grad_weights = dot(v[h], got_ref[h, :, cols])
            grad_scores = weights * (grad_weights - delta_ref[h, :, cols])
            rounded = grad_scores.astype(bf16)
            band_ref[h, place] += grad_scores
            dv_acc[h] += dot(weights.astype(bf16), go_ref[h, cols, :])
            dk_acc[h] += dot(rounded, q_ref[h, cols, :])
            dqt_acc[h, :, cols] += dot(kt[h], rounded)

    def edge_step(query, _):
        step(query, True)
        return 0

    def full_step(query, _):
        step(query, False)
        return 0

    lax.fori_loop(least_ref[key], clear_ref[key], edge_step, 0)
    lax.fori_loop(clear_ref[key], count, full_step, 0)
    slot = jnp.int32(0)
    for i in range(parts):
        slot = jnp.where(slot_ref[i] == key // each, i, slot)
    inner = pl.ds(pl.multiple_of(lax.rem(key, each) * TILE, TILE), TILE)
    for h in range(heads):
        out_ref[slot, heads + h, :, inner] = dk_acc[h].T.astype(bf16)
        out_ref[slot, 2 * heads + h, :, inner] = dv_acc[h].T.astype(bf16)

    @pl.when(key == count - 1)
    def _():
        for i in range(parts):
            places = pl.ds(pl.multiple_of(slot_ref[i] * part_length, TILE), part_length)
            for h in range(heads):
                out_ref[i, h] = dqt_acc[h, :, places].astype(bf16)

        def one(place, _):
            for h in range(heads):
                band = band_ref[h, place]
                zero = jnp.zeros((TILE // 2, TILE // 2), f32)
                upper, lower = band[: TILE // 2], band[TILE // 2 :]
                lines = jnp.concatenate([zero, zero, upper], axis=1) + jnp.concatenate(
                    [zero, lower, zero], axis=1
                )
                half = TILE // 4
                while half >= 8:
                    lines = lines[:half] + pltpu.roll(lines[half:], 2 * TILE - half, 1)
                    half //= 2
                total = lines[0:1]
                for row in range(1, 8):
                    total = total + pltpu.roll(lines[row : row + 1], 2 * TILE - row, 1)
                band_out_ref[h, place] = total
            return 0

        lax.fori_loop(0, band_ref.shape[1], one, 0)


def attend_backward(pieces, grads, ot, lse, bias, end, least, clear, slots, group):
    parts = len(pieces)
    triple, size, part_length = pieces[0].shape
    heads, length = triple // 3, parts * part_length
    count = length // TILE
    tiles = bias.shape[1]
    smem = pl.BlockSpec(memory_space=pltpu.SMEM)
    operands = (*pieces, *grads, ot, lse, bias, end)
    outs = [((parts, triple, size, part_length), bf16), ((heads, tiles, 1, 2 * TILE), f32)]
    by_columns = pltpu.VMEM((heads, size, length), bf16)
    by_rows = pltpu.VMEM((heads, length, size), bf16)
    return pl.pallas_call(
        backward_kernel,
        grid=(count,),
        in_specs=[smem] * 4 + [whole(a.shape) for a in operands],
        out_specs=[whole(shape) for shape, _ in outs],
        out_shape=[jax.ShapeDtypeStruct(shape, kind) for shape, kind in outs],
        scratch_shapes=[by_columns] * 4
        + [by_rows] * 2
        + [
            pltpu.VMEM((heads, size, length), f32),
            pltpu.VMEM((heads, TILE, size), f32),
            pltpu.VMEM((heads, TILE, size), f32),
            pltpu.VMEM((heads, 1, length), f32),
            pltpu.VMEM((heads, tiles, TILE, TILE), f32),
        ],
        compiler_params=params(),
        name="attend_backward",
    )(least, clear, slots, group, *operands)


def middle_kernel(place_ref, *refs):
    parts = place_ref.shape[0] - 1
    mixes = refs[:parts]
    x_ref, g_ref, gain_ref, own_ref, other_ref, out_ref, gh_ref, gain_grad_ref = refs[
        parts : parts + 8
    ]
    gots = refs[parts + 8 : 2 * parts + 8]
    keep_ref, send_ref, w_ref, grad_ref, second_ref, acc_ref, back_ref, load_sem, store_sem = refs[
        2 * parts + 8 :
    ]
    core = place_ref[parts]
    width = x_ref.shape[1]
    columns = mixes[0].shape[0]
    feed = own_ref.shape[3] - 256
    hidden_units = feed // 2
    late, early = pl.ds(feed, 256), pl.ds(0, feed)

    def loads(z, which, cols):
        pairs = [(own_ref, core), (other_ref, 1 - core)]
        return [
            pltpu.make_async_copy(
                src.at[z, :, :, cols], w_ref.at[z, :, at, :, cols], load_sem.at[z, which, i]
            )
            for i, (src, at) in enumerate(pairs)
        ]

    def stores(z, which, cols):
        pairs = [(keep_ref, core), (send_ref, 1 - core)]
        return [
            pltpu.make_async_copy(
                grad_ref.at[z, :, at, :, cols], dst.at[z, :, :, cols], store_sem.at[z, which, i]
            )
            for i, (dst, at) in enumerate(pairs)
        ]

    for z in range(parts):
        for copy in loads(z, 0, late):
            copy.start()
    for z in range(parts):
        for copy in loads(z, 1, early):
            copy.start()
    for z in range(parts):
        for copy in loads(z, 0, late):
            copy.wait()

    def output_rows(turn):
        return w_ref[place_ref[turn], :, :, :, feed : feed + columns].reshape(width, columns)

    hidden = x_ref[...].astype(f32)
    for turn in range(parts):
        hidden = hidden + dot(mixes[turn][...], output_rows(turn), ((0,), (1,)))
    inverse = lax.rsqrt(jnp.mean(hidden * hidden, axis=-1, keepdims=True) + EPSILON)
    second_ref[...] = (hidden * inverse * gain_ref[...]).astype(bf16)
    acc_ref[...] = hidden
    back_ref[...] = jnp.zeros_like(back_ref)
    gh_ref[...] = hidden * inverse

    def hidden_part(z, _):
        for copy in loads(z, 1, early):
            copy.wait()
        inner = w_ref[z, :, :, :, :hidden_units].reshape(width, hidden_units)
        outer = w_ref[z, :, :, :, hidden_units:feed].reshape(width, hidden_units)
        second = second_ref[...]
        grad = g_ref[...]
        grad_active = dot(grad, outer).astype(bf16).astype(f32)
        active, slope = gelu_parts(dot(second, inner))
        active = active.astype(bf16)
        grad_units = (grad_active * slope).astype(bf16)
        acc_ref[...] += dot(active, outer, ((1,), (1,)))
        back_ref[...] += dot(grad_units, inner, ((1,), (1,)))
        shape = (*grad_ref.shape[1:4], hidden_units)
        grad_ref[z, :, :, :, :hidden_units] = (
            dot(second, grad_units, ((0,), (0,))).astype(bf16).reshape(shape)
        )
        grad_ref[z, :, :, :, hidden_units:feed] = (
            dot(grad, active, ((0,), (0,))).astype(bf16).reshape(shape)
        )
        for copy in stores(z, 1, early):
            copy.start()
        return 0

    lax.fori_loop(0, parts, hidden_part, 0)
    out_ref[...] = acc_ref[...].astype(bf16)
    scaled = gh_ref[...]
    grad_second = back_ref[...]
    gain_grad_ref[...] = jnp.sum(grad_second * scaled, axis=0, keepdims=True)
    grad_scaled = grad_second * gain_ref[...]
    grad_hidden = g_ref[...].astype(f32) + inverse * (
        grad_scaled - scaled * jnp.mean(grad_scaled * scaled, axis=-1, keepdims=True)
    )
    gh_ref[...] = grad_hidden
    rounded = grad_hidden.astype(bf16)
    for turn in range(parts):
        gots[turn][...] = dot(output_rows(turn), rounded, ((0,), (1,))).astype(bf16)
        grads = dot(rounded, mixes[turn][...], ((0,), (1,))).astype(bf16)
        grad_ref[place_ref[turn], :, :, :, feed : feed + columns] = grads.reshape(
            *grad_ref.shape[1:4], columns
        )
        grad_ref[place_ref[turn], :, :, :, feed + columns :] = jnp.zeros(
            (*grad_ref.shape[1:4], 256 - columns), bf16
        )
    for z in range(parts):
        for copy in stores(z, 0, late):
            copy.start()
    for z in range(parts):
        for copy in stores(z, 0, late) + stores(z, 1, early):
            copy.wait()


def middle(place, mixes, inputs, cotangent, gain, own, other):
    rows, width = inputs.shape
    parts, planes, each, columns = own.shape
    smem = pl.BlockSpec(memory_space=pltpu.SMEM)
    hbm = pl.BlockSpec(memory_space=pl.ANY)
    held = pltpu.VMEM((parts, planes, 2, each, columns), bf16)
    token_shape = jax.ShapeDtypeStruct((rows, width), f32)
    gain = gain.reshape(1, width)
    dense = [*mixes, inputs, cotangent, gain]
    outs = [
        jax.ShapeDtypeStruct((rows, width), bf16),
        token_shape,
        jax.ShapeDtypeStruct((1, width), f32),
        *[jax.ShapeDtypeStruct(mix.shape, bf16) for mix in mixes],
    ]
    return pl.pallas_call(
        middle_kernel,
        in_specs=[smem] + [whole(a.shape) for a in dense] + [hbm, hbm],
        out_specs=[whole(a.shape) for a in outs] + [hbm, hbm],
        out_shape=outs + [jax.ShapeDtypeStruct(own.shape, bf16)] * 2,
        scratch_shapes=[
            held,
            held,
            pltpu.VMEM((rows, width), bf16),
            pltpu.VMEM((rows, width), f32),
            pltpu.VMEM((rows, width), f32),
            pltpu.SemaphoreType.DMA((parts, 2, 2)),
            pltpu.SemaphoreType.DMA((parts, 2, 2)),
        ],
        compiler_params=params(),
        name="middle",
    )(place, *dense, own, other)


def flat(pairs, parts):
    return [(c * parts + z, d * parts + y) for (c, z), (d, y) in pairs]


def routes(parts):
    half = parts // 2
    devices = [(c, z) for c in range(2) for z in range(parts)]

    def group(c, z):
        return (z % half) * 2 + c

    gather = [
        flat([((0, z), (0, z - 1)) for z in (1, 2, 3)] + [((1, z), (1, z + 1)) for z in (0, 1, 2)], parts),
        flat([((0, z), (0, z - 1)) for z in (1, 2)] + [((1, z), (1, z + 1)) for z in (1, 2)], parts),
        flat([((0, 1), (0, 0)), ((0, 0), (0, 1)), ((1, 2), (1, 3)), ((1, 3), (1, 2))], parts),
    ]
    rounds = [
        flat([((c, z), (z // half, (group(c, z) + r) % parts)) for c, z in devices], parts)
        for r in range(parts)
    ]
    weights = [
        flat([((z // half ^ flip, group(c, z)), (c, z)) for c, z in devices], parts)
        for flip in range(2)
    ]
    return gather, rounds, weights


def back(pairs):
    return [(target, source) for source, target in pairs]


SWAP = [(0, 1), (1, 0)]
LINE = ("core", "tensor")
EVERY = ("tensor", "plane")


def body(
    inputs,
    attention_gain,
    feedforward_gain,
    query_weight,
    key_weight,
    value_weight,
    output_weight,
    inner_weight,
    outer_weight,
    bias_table,
    block_index,
    position_bucket,
    cotangent,
):
    length = block_index.shape[1]
    parts = lax.axis_size("tensor")
    planes = lax.axis_size("plane")
    factor = 1.0 / math.sqrt(block_index.shape[0] * length * planes * 2)
    heads = bias_table.shape[1]
    width = inputs.shape[1]
    size = query_weight.shape[1] // heads
    columns = heads * size
    each = query_weight.shape[0]
    hidden_units = inner_weight.shape[1]
    core, z = lax.axis_index("core"), lax.axis_index("tensor")
    half = parts // 2
    lower = z < half
    owner = core == z // half
    outer_chip = (z == 0) | (z == parts - 1)
    group = (z % half) * 2 + core
    gather, rounds, weight_routes = routes(parts)
    slots = jnp.array([[0, 1, 2, 3], [1, 2, 3, 0], [2, 1, 0, 3], [3, 2, 1, 0]], jnp.int32)[z]

    def swap(value):
        return lax.ppermute(value, "core", SWAP)

    inputs_wide = inputs.astype(f32)
    scaled_first, inverse_first, normed_own = norm_forward(inputs_wide, attention_gain)
    first = lax.ppermute(normed_own, LINE, gather[0])
    second = lax.ppermute(first, LINE, gather[1])
    third = lax.ppermute(jnp.where(outer_chip, normed_own, second), LINE, gather[2])
    normed = [jnp.where(owner, piece, swap(piece)) for piece in (normed_own, first, second, third)]

    packed = jnp.concatenate([query_weight, key_weight, value_weight], axis=1)
    one, two = (lax.ppermute(packed, LINE, route) for route in weight_routes)
    mine = jnp.concatenate([jnp.where(lower, one, two), jnp.where(lower, two, one)], axis=0)
    attention_full = lax.all_gather(mine, "plane", axis=0, tiled=True)
    table = lax.ppermute(bias_table, LINE, weight_routes[0])
    block_row = jnp.where(owner, block_index, swap(block_index))[0]

    pad = jnp.zeros((each, 256 - columns), bf16)
    packed_rest = jnp.concatenate([inner_weight, outer_weight.T, output_weight.T, pad], axis=1)
    own_rest = lax.all_gather(packed_rest, EVERY, axis=0).reshape(parts, planes, each, -1)
    other_rest = swap(own_rest)

    rows, onehot = bias_rows(table, position_bucket)
    bias = bias_tiles(rows, length)
    end, full, most, least, clear = spans(block_row)
    group_ref = group.reshape(1)

    pieces = [
        dot(attention_full, piece, ((0,), (1,))).astype(bf16).reshape(3 * heads, size, -1)
        for piece in normed
    ]
    ot, lse = attend_forward(pieces, bias, end, full, most, slots, group_ref)
    mixes = [
        lax.ppermute(ot[r].reshape(columns, -1), LINE, rounds[r]) for r in range(parts)
    ]
    place = jnp.stack([(z - r) % parts for r in range(parts)] + [core]).astype(jnp.int32)
    aligned = each % 16 == 0
    if aligned:
        outs = middle(place, mixes, inputs, cotangent, feedforward_gain, own_rest, other_rest)
        layer_output, grad_hidden, feedforward_part, *gots, keep, send = outs
    else:
        low, high = jnp.where(core == 0, own_rest, other_rest), jnp.where(core == 0, other_rest, own_rest)
        both = jnp.stack([low, high], axis=2).reshape(parts, 2, width // 2, -1)
        lone = place.at[parts].set(0)
        outs = middle(lone, mixes, inputs, cotangent, feedforward_gain, both[:, :1], both[:, 1:])
        layer_output, grad_hidden, feedforward_part, *gots, keep, send = outs
        grads = jnp.concatenate([keep, send], axis=1).reshape(parts, planes, 2, each, -1)
        keep, send = (
            lax.dynamic_index_in_dim(grads, at, 2, False) for at in (core, 1 - core)
        )
    rest = (keep + swap(send)).reshape(parts * planes, each, -1)
    rest_share = lax.psum_scatter(rest, EVERY, scatter_dimension=0).astype(f32) * factor

    gots = [lax.ppermute(got, LINE, back(rounds[r])) for r, got in enumerate(gots)]
    gots = [got.reshape(heads, size, -1) for got in gots]
    dqkv, bands = attend_backward(
        pieces, gots, ot, lse, bias, end, least, clear, slots, group_ref
    )
    dqkv = dqkv.reshape(parts, 3 * columns, length // parts)

    def normed_part(i):
        part = dot(dqkv[i], attention_full, ((0,), (1,))).astype(bf16)
        return part + swap(part)

    third, second, first, own = (normed_part(i) for i in (3, 2, 1, 0))
    none = jnp.zeros_like(own)
    got = lax.ppermute(third, LINE, back(gather[2]))
    own = jnp.where(owner, jnp.where(outer_chip, own + got, own), none)
    second = jnp.where(outer_chip, second, second + got)
    got = lax.ppermute(second, LINE, back(gather[1]))
    first = jnp.where(owner, first, none) + got
    got = lax.ppermute(first, LINE, back(gather[0]))
    grad_first = (own + got).astype(f32)
    input_grad = (
        grad_hidden + norm_backward(grad_first, scaled_first, inverse_first, attention_gain)
    ).astype(bf16)

    attention_grads = sum(dot(normed[i], dqkv[i], ((0,), (1,))) for i in range(parts))
    attention_part = (
        jnp.sum(attention_grads * attention_full.astype(f32), axis=1) / attention_gain
    )
    shared = lax.psum_scatter(
        attention_grads.astype(bf16), "plane", scatter_dimension=0, tiled=True
    )
    low, high = shared[:each], shared[each:]
    attention_share = (
        lax.ppermute(jnp.where(lower, low, high), LINE, back(weight_routes[0]))
        + lax.ppermute(jnp.where(lower, high, low), LINE, back(weight_routes[1]))
    ).astype(f32) * factor

    table_local = table_part(bands, onehot, length)
    buckets = table_local.shape[0]
    table_whole = lax.dynamic_update_slice(
        jnp.zeros((buckets, H), f32), table_local, (jnp.zeros((), jnp.int32), group * heads)
    )
    small = jnp.concatenate(
        [attention_part, feedforward_part.reshape(width), table_whole.reshape(buckets * H)]
    )
    for axis, count in (("core", 2), ("tensor", parts), ("plane", planes)):
        step = 1
        while step < count:
            small = small + lax.ppermute(small, axis, [(i, i ^ step) for i in range(count)])
            step *= 2
    small = small * factor

    return (
        layer_output,
        input_grad,
        small[:width],
        small[width : 2 * width],
        attention_share[:, :columns],
        attention_share[:, columns : 2 * columns],
        attention_share[:, 2 * columns :],
        rest_share[:, 2 * hidden_units : 2 * hidden_units + columns].T,
        rest_share[:, :hidden_units],
        rest_share[:, hidden_units : 2 * hidden_units].T,
        small[2 * width :].reshape(buckets, H),
    )


def solution(mesh):
    groups, parts = mesh.devices.shape
    fine = Mesh(mesh.devices.reshape(groups // 2, 2, parts), ("plane", "core", "tensor"))
    dp = ("plane", "core")
    tokens = P(("plane", "core", "tensor"), None)
    by_rows = P(dp, "tensor")
    by_columns = P("tensor", dp)
    placed = (
        tokens, P(), P(), by_rows, by_rows, by_rows, by_columns, by_rows, by_columns,
        P(None, "tensor"), P(dp, None), P(), tokens,
    )
    results = (
        tokens, tokens, P(), P(), by_rows, by_rows, by_rows, by_columns, by_rows, by_columns, P(),
    )
    return jax.shard_map(body, mesh=fine, in_specs=placed, out_specs=results, check_vma=False)
```

time: 606 us -> 527 us (0.87)
  waiting for transfers between devices: 348 us -> 224 us
  starting transfers between devices: 11.1 us -> 83.5 us
  blocking collectives: 51.1 us -> 11.8 us
  Pallas kernels: 120 us -> 132 us
  matrix products: 26.4 us -> 16.3 us
  local copies, waits for them, and re-layouts: 9.94 us -> 17.8 us
    reduce_scatter x3 -> x2, waiting for transfers between devices: 193 us -> 79 us  [the longest x1 79 us: body(): lax.psum_scatter(rest, EVERY, scatter_dimension=0).astype(f32) * factor]
    ppermute x0 -> x35, starting transfers between devices: none -> 83.4 us  [the longest x11 24.5 us: swap(): return lax.ppermute(value, 'core', SWAP)]
    ppermute x0 -> x35, waiting for transfers between devices: none -> 57.2 us  [the longest x1 24.8 us: body(): lax.ppermute(jnp.where(lower, low, high), LINE, back(weight_routes[0]))]
    psum x1 -> x0, blocking collectives: 39.7 us -> none  [body(): lax.psum((attention_part * factor, feedforward_part * factor, table_whole...]
    all_gather x3 -> x1, waiting for transfers between devices: 114 us -> 88.1 us  [body(): lax.all_gather(packed_rest, EVERY, axis=0).reshape(parts, planes, each, -1)]
    all_to_all x2 -> x0, waiting for transfers between devices: 21.2 us -> none  [the longest x1 11.1 us: body(): lax.all_to_all(ot.reshape(parts, columns, length // parts), 'tensor', 0, 0)]
    unnamed x8 -> x3, waiting for transfers between devices: 19.3 us -> 0.05 us
    pallas_call x3, Pallas kernels: 114 us -> 125 us  [the longest x1 53.8 us: attend_backward(): pl.pallas_call(backward_kernel, grid=(count,), in_specs=[smem] * 4 + [who...]
  transfers between devices with their start and end apart: 9 -> 38, of which waited for: 9 -> 13; matrix products, arithmetic and copies ran while one was open for 7% -> 9% of each run, Pallas kernels for 17% -> 20%
where the time goes in v1:
time: 527 us; the launch traced here: 522 us
  waiting for transfers between devices  224 us (43%)
  Pallas kernels  132 us (25%)
  starting transfers between devices  83.5 us (16%)
  other arithmetic  22.1 us (4%)
  local copies, waits for them, and re-layouts  17.8 us (3%)
  matrix products  16.3 us (3%)
  between operations  14.6 us (3%)
  blocking collectives  11.8 us (2%)
    all_gather x1, waiting for transfers between devices, body(): lax.all_gather(packed_rest, EVERY, axis=0).reshape(parts, planes, each, -1)  88.1 us
    reduce_scatter x1, waiting for transfers between devices, body(): lax.psum_scatter(rest, EVERY, scatter_dimension=0).astype(f32) * factor  79 us
    pallas_call x1, Pallas kernels, attend_backward(): pl.pallas_call(backward_kernel, grid=(count,), in_specs=[smem] * 4 + [who...  53.8 us
    pallas_call x1, Pallas kernels, attend_forward(): pl.pallas_call(forward_kernel, grid=(count,), in_specs=[smem] * 4 + [whol...  45.6 us
    pallas_call x1, Pallas kernels, middle(): pl.pallas_call(middle_kernel, in_specs=[smem] + [whole(a.shape) for a in...  26 us
    ppermute x1, waiting for transfers between devices, body(): lax.ppermute(jnp.where(lower, low, high), LINE, back(weight_routes[0]))  24.8 us
    ppermute x11, starting transfers between devices, swap(): return lax.ppermute(value, 'core', SWAP)  24.5 us
    ppermute x5, starting transfers between devices, body(): lax.ppermute(small, axis, [(i, i ^ step) for i in range(count)])  18.9 us
  transfers between devices with their start and end apart: 38, of which 13 were waited for; matrix products, arithmetic and copies ran while one was open for 9% of the time, Pallas kernels for 20%

profile of v1, /device:TPU:9, one launch (start us, length us, event | category | flops | bytes accessed | tf_op | source)
XLA Modules:
  0.0 522.4 jit_solution(12382500380529276712)
XLA Ops:
  10.1 88.1 %all-gather.3.cloned.1.call-done = bf16[1536,1792]{1,0:T(8,128)(2,1)} async-done(((bf16[96,1792]{1,0:T(8,128)(2,1)}), bf16[1536,1792]{1,0:T(8,128)(2,1)}) %all-gather.3.cloned.1.call-update) | async-done | bytes 5505040 | tf_op jit(solution)/shard_map/all_gather | solution.py:584
  98.2 2.0 collective-permute-start.15
  100.7 2.8 collective-permute-start.4
  103.6 2.2 collective-permute-start.1
  107.5 3.2 collective-permute-start.10
  112.2 5.6 %collective-permute-done.10 = f32[32,3]{0,1:T(4,128)S(1)} collective-permute-done((f32[32,3]{0,1:T(4,128)S(1)}, f32[32,3]{0,1:T(4,128)S(1)}, u32[]{:S(2)}, u32[]{:S(2)}) %collective-permute-start.10) | collective-permute-done | bytes 416 | tf_op jit(solution)/shard_map/ppermute | solution.py:579
  117.7 2.2 collective-permute-start
  122.5 6.5 %bias_tiles.1.refs_4_.refs_10_ = f32[3,10,256,256]{3,2,1,0:T(8,128)} custom-call(f32[3,1,2816]{2,1,0:T(1,128)} %slice.121.row_ref), custom_call_target="tpu_custom_call" | custom-call | tf_op jit(solution)/shard_map/bias_tiles/pallas_call | solution.py:79
  132.6 4.4 collective-permute-start.5
  137.2 11.8 %all_gather.9 = bf16[768,576]{1,0:T(8,128)(2,1)S(1)} all-gather(bf16[192,576]{1,0:T(8,128)(2,1)S(1)} %pad_maximum_fusion), channel_id=1, replica_groups=mesh['plane'=4,'core'=2,'tensor'=4] {'plane'}, dimensions={0}, use_global_device_ids=true | all-gather | bytes 1105920 | tf_op jit(solution)/shard_map/all_gather | solution.py:578
  149.0 2.0 collective-permute-start.9
  151.1 2.7 convolution_convert_fusion.7
  158.7 45.6 %attend_forward.1 = (bf16[4,3,64,512]{3,2,1,0:T(8,128)(2,1)}, f32[3,1,2048]{2,1,0:T(1,128)}) custom-call(s32[8]{0:T(128)} %get-tuple-element.120.full_ref, s32[8]{0:T(128)} %get-tuple-element.119.most_ref, s32[4]{0:T(128)} %dynamic-slice_bitcast_fusion.slot_ref, s32[1]{0:T(128)} %bitcast.7.group_ref, bf16[9,64,512]{2,1,0:T(8,128)(2,1)} %bitcast.64, ...), custom_call_target="tpu_custom_call" | custom-call | tf_op jit(solution)/shard_map/attend_forward/pallas_call | solution.py:187
  205.6 3.7 collective-permute-start.11
  212.1 3.0 collective-permute-start.14
  216.4 10.3 %collective-permute-done.12.refs_1_ = bf16[192,512]{1,0:T(8,128)(2,1)} collective-permute-done((bf16[192,512]{1,0:T(8,128)(2,1)S(1)}, bf16[192,512]{1,0:T(8,128)(2,1)}, u32[]{:S(2)}, u32[]{:S(2)}) %collective-permute-start.12) | collective-permute-done | bytes 196640 | tf_op jit(solution)/shard_map/ppermute | solution.py:598
  226.8 26.0 %middle.1 = (bf16[512,768]{1,0:T(8,128)(2,1)}, f32[512,768]{1,0:T(8,128)}, f32[1,768]{1,0:T(1,128)}, bf16[192,512]{1,0:T(8,128)(2,1)}, bf16[192,512]{1,0:T(8,128...) custom-call(s32[5]{0:T(128)} %stack.23.place_ref, ...), custom_call_target="tpu_custom_call" | custom-call | tf_op jit(solution)/shard_map/middle/pallas_call | solution.py:476
  252.9 3.8 collective-permute-start.16
  256.8 2.1 collective-permute-start.17
  259.6 5.4 %collective-permute-start.19 = (bf16[192,512]{1,0:T(8,128)(2,1)}, bf16[192,512]{1,0:T(8,128)(2,1)}, u32[]{:S(2)}, u32[]{:S(2)}) collective-permute-start(bf16[192,512]{1,0:T(8,128)(2,1)} %get-tuple-element.30), channel_id=1, source_target_pairs={{3,0},{1,1},{7,2},{5,3},{0,4},{2,5},{4,6},{6,7},{11,8},{9,9},{15,1... | collective-permute-start | bytes 589832 | tf_op jit(solution)/shard_map/ppermute | solution.py:618
  267.0 5.3 %collective-permute-done.18 = bf16[192,512]{1,0:T(8,128)(2,1)} collective-permute-done((bf16[192,512]{1,0:T(8,128)(2,1)}, bf16[192,512]{1,0:T(8,128)(2,1)}, u32[]{:S(2)}, u32[]{:S(2)}) %collective-permute-start.18) | collective-permute-done | bytes 196640 | tf_op jit(solution)/shard_map/ppermute | solution.py:618
  272.3 3.0 collective-permute-done.19
  275.4 53.8 %attend_backward.1 = (bf16[4,9,64,512]{3,2,1,0:T(8,128)(2,1)}, f32[3,10,1,512]{3,2,1,0:T(1,128)}) custom-call(s32[8]{0:T(128)} %convert_reduce_fusion.2.least_ref, s32[8]{0:T(128)} %convert_reduce_fusion.1.clear_ref, s32[4]{0:T(128)} %dynamic-slice_bitcast_fusion.slot_ref, s32[1]{0:T(128)} %bitcast.7.group_ref, bf16[9,64,512]{2,1,0:T(8,128)(2,1)} %bitcast.65, ...), custom_call_target="tpu_custom_call" | custom-call | tf_op jit(solution)/shard_map/attend_backward/pallas_call | solution.py:332
  337.8 8.2 %add.159 = bf16[4,4,96,1792]{3,2,1,0:T(8,128)(2,1)} add(bf16[4,4,96,1792]{3,2,1,0:T(8,128)(2,1)} %get-tuple-element.35, bf16[4,4,96,1792]{3,2,1,0:T(8,128)(2,1)} %collective-permute-done.34) | non-fusion elementwise | flops 2752512 | bytes 16515072 | tf_op jit(solution)/shard_map/add | solution.py:615
  359.1 10.6 %collective-permute-start.27 = (f32[1920]{0:T(1024)S(1)}, f32[1920]{0:T(1024)S(1)}, u32[]{:S(2)}, u32[]{:S(2)}) collective-permute-start(f32[1920]{0:T(1024)S(1)} %pad_maximum_fusion.2), channel_id=1, source_target_pairs={{0,4},{4,0},{1,5},{5,1},{2,6},{6,2},{3,7},{7,3},{8,12},{12,8},{9,1... | collective-permute-start | bytes 23048 | tf_op jit(solution)/shard_map/ppermute | solution.py:666
  373.8 6.5 %collective-permute-start.29 = (f32[1920]{0:T(1024)S(1)}, f32[1920]{0:T(1024)S(1)}, u32[]{:S(2)}, u32[]{:S(2)}) collective-permute-start(f32[1920]{0:T(1024)S(1)} %add.154), channel_id=1, source_target_pairs={{0,2},{1,3},{2,0},{3,1},{4,6},{5,7},{6,4},{7,5},{8,10},{9,11},{10,... | collective-permute-start | bytes 23048 | tf_op jit(solution)/shard_map/ppermute | solution.py:666
  381.8 2.9 collective-permute-done.30
  385.6 11.2 %collective-permute-start.20 = (bf16[512,768]{1,0:T(8,128)(2,1)S(1)}, bf16[512,768]{1,0:T(8,128)(2,1)S(1)}, u32[]{:S(2)}, u32[]{:S(2)}) collective-permute-start(bf16[512,768]{1,0:T(8,128)(2,1)S(1)} %convolution_convert_fusion.3), channel_id=1, source_target_pairs={{0,4},{4,0},{1,5},{5,1},{2,6},{6,2},{3,7},{7,3},{8,12},{12,8},{9,1... | collective-permute-start | bytes 2359304 | tf_op jit(solution)/shard_map/ppermute | solution.py:566
  397.7 2.0 collective-permute-start.26
  404.2 24.8 %collective-permute-done.32 = bf16[96,576]{1,0:T(8,128)(2,1)} collective-permute-done((bf16[96,576]{1,0:T(8,128)(2,1)S(1)}, bf16[96,576]{1,0:T(8,128)(2,1)}, u32[]{:S(2)}, u32[]{:S(2)}) %collective-permute-start.32) | collective-permute-done | bytes 110624 | tf_op jit(solution)/shard_map/ppermute | solution.py:651
  430.8 2.1 fusion.4
  434.2 79.0 %reduce-scatter.5.cloned.1.call-done = bf16[1,96,1792]{2,1,0:T(8,128)(2,1)} async-done(((bf16[16,96,1792]{2,1,0:T(8,128)(2,1)}), bf16[1,96,1792]{2,1,0:T(8,128)(2,1)}) %reduce-scatter.5.cloned.1.call-update) | async-done | bytes 344080 | tf_op jit(solution)/shard_map/reduce_scatter | solution.py:616
  (199 shorter events, 65.1 us)
Async XLA Ops:
  7.2 91.0 %all-gather.3.cloned.1.call-start = ((), (), s32[]{:S(2)}) async-start(), calls=%async_computation.3 | async-start | bytes 5849088 | tf_op jit(solution)/shard_map/all_gather | solution.py:584
  10.1 389.7 %reduce-scatter.7.cloned.1.call-start = ((), (), s32[]{:S(2)}) async-start(), calls=%async_computation.4 | async-start | bytes 1228800 | tf_op jit(solution)/shard_map/reduce_scatter | solution.py:646
  98.2 128.6 %collective-permute-start.15 = (bf16[4,4,96,1792]{3,2,1,0:T(8,128)(2,1)}, bf16[4,4,96,1792]{3,2,1,0:T(8,128)(2,1)}, u32[]{:S(2)}, u32[]{:S(2)}) collective-permute-start(bf16[4,4,96,1792]{3,2,1,0:T(8,128)(2,1)} %bitcast.62), channel_id=1, source_target_pairs={{0,4},{4,0},{1,5},{5,1},{2,6},{6,2},{3,7},{7,3},{8,12},{12,8},{9,1... | collective-permute-start | bytes 16515080 | tf_op jit(solution)/shard_map/ppermute | solution.py:566
  100.7 19.2 %collective-permute-start.4 = (bf16[512,768]{1,0:T(8,128)(2,1)S(1)}, bf16[512,768]{1,0:T(8,128)(2,1)}, u32[]{:S(2)}, u32[]{:S(2)}) collective-permute-start(bf16[512,768]{1,0:T(8,128)(2,1)S(1)} %fusion.3), channel_id=1, source_target_pairs={{1,0},{2,1},{3,2},{4,5},{5,6},{6,7},{9,8},{10,9},{11,10},{12,13},{... | collective-permute-start | bytes 2359304 | tf_op jit(solution)/shard_map/ppermute | solution.py:570
  103.6 29.0 %collective-permute-start.1 = (bf16[96,576]{1,0:T(8,128)(2,1)S(1)}, bf16[96,576]{1,0:T(8,128)(2,1)S(1)}, u32[]{:S(2)}, u32[]{:S(2)}) collective-permute-start(bf16[96,576]{1,0:T(8,128)(2,1)S(1)} %pad_maximum_fusion.1), channel_id=1, source_target_pairs={{0,0},{2,1},{4,2},{6,3},{1,4},{3,5},{5,6},{7,7},{8,8},{10,9},{12,1... | collective-permute-start | bytes 331784 | tf_op jit(solution)/shard_map/ppermute | solution.py:576
  105.8 31.2 %collective-permute-start.2 = (bf16[96,576]{1,0:T(8,128)(2,1)S(1)}, bf16[96,576]{1,0:T(8,128)(2,1)S(1)}, u32[]{:S(2)}, u32[]{:S(2)}) collective-permute-start(bf16[96,576]{1,0:T(8,128)(2,1)S(1)} %pad_maximum_fusion.1), channel_id=1, source_target_pairs={{4,0},{6,1},{0,2},{2,3},{5,4},{7,5},{1,6},{3,7},{12,8},{14,9},{8,1... | collective-permute-start | bytes 331784 | tf_op jit(solution)/shard_map/ppermute | solution.py:576
  107.5 10.2 %collective-permute-start.10 = (f32[32,3]{0,1:T(4,128)S(1)}, f32[32,3]{0,1:T(4,128)S(1)}, u32[]{:S(2)}, u32[]{:S(2)}) collective-permute-start(f32[32,3]{0,1:T(4,128)S(1)} %copy-done.34), channel_id=1, source_target_pairs={{0,0},{2,1},{4,2},{6,3},{1,4},{3,5},{5,6},{7,7},{8,8},{10,9},{12,1... | collective-permute-start | bytes 1160 | tf_op jit(solution)/shard_map/ppermute | solution.py:579
  117.7 11.3 %collective-permute-start = (s32[1,2048]{1,0:T(1,128)S(1)}, s32[1,2048]{1,0:T(1,128)S(1)}, u32[]{:S(2)}, u32[]{:S(2)}) collective-permute-start(s32[1,2048]{1,0:T(1,128)S(1)} %copy-done.29), channel_id=1, source_target_pairs={{0,4},{4,0},{1,5},{5,1},{2,6},{6,2},{3,7},{7,3},{8,12},{12,8},{9,1... | collective-permute-start | bytes 24584 | tf_op jit(solution)/shard_map/ppermute | solution.py:566
  119.9 10.9 %collective-permute-start.6 = (bf16[512,768]{1,0:T(8,128)(2,1)}, bf16[512,768]{1,0:T(8,128)(2,1)S(1)}, u32[]{:S(2)}, u32[]{:S(2)}) collective-permute-start(bf16[512,768]{1,0:T(8,128)(2,1)} %collective-permute-done.4), channel_id=1, source_target_pairs={{1,0},{2,1},{5,6},{6,7},{9,8},{10,9},{13,14},{14,15},{17,16},{18,1... | collective-permute-start | bytes 2359304 | tf_op jit(solution)/shard_map/ppermute | solution.py:571
  129.0 22.1 %collective-permute-start.3 = (bf16[512,768]{1,0:T(8,128)(2,1)S(1)}, bf16[512,768]{1,0:T(8,128)(2,1)}, u32[]{:S(2)}, u32[]{:S(2)}) collective-permute-start(bf16[512,768]{1,0:T(8,128)(2,1)S(1)} %fusion.3), channel_id=1, source_target_pairs={{0,4},{4,0},{1,5},{5,1},{2,6},{6,2},{3,7},{7,3},{8,12},{12,8},{9,1... | collective-permute-start | bytes 2359304 | tf_op jit(solution)/shard_map/ppermute | solution.py:566
  131.1 17.9 %collective-permute-start.8 = (bf16[512,768]{1,0:T(8,128)(2,1)S(1)}, bf16[512,768]{1,0:T(8,128)(2,1)S(1)}, u32[]{:S(2)}, u32[]{:S(2)}) collective-permute-start(bf16[512,768]{1,0:T(8,128)(2,1)S(1)} %broadcast_select_fusion), channel_id=1, source_target_pairs={{1,0},{0,1},{6,7},{7,6},{9,8},{8,9},{14,15},{15,14},{17,16},{16,17... | collective-permute-start | bytes 2359304 | tf_op jit(solution)/shard_map/ppermute | solution.py:572
  132.6 21.2 %collective-permute-start.5 = (bf16[512,768]{1,0:T(8,128)(2,1)}, bf16[512,768]{1,0:T(8,128)(2,1)S(1)}, u32[]{:S(2)}, u32[]{:S(2)}) collective-permute-start(bf16[512,768]{1,0:T(8,128)(2,1)} %collective-permute-done.4), channel_id=1, source_target_pairs={{0,4},{4,0},{1,5},{5,1},{2,6},{6,2},{3,7},{7,3},{8,12},{12,8},{9,1... | collective-permute-start | bytes 2359304 | tf_op jit(solution)/shard_map/ppermute | solution.py:566
  137.1 18.4 %collective-permute-start.7 = (bf16[512,768]{1,0:T(8,128)(2,1)S(1)}, bf16[512,768]{1,0:T(8,128)(2,1)S(1)}, u32[]{:S(2)}, u32[]{:S(2)}) collective-permute-start(bf16[512,768]{1,0:T(8,128)(2,1)S(1)} %collective-permute-done.6), channel_id=1, source_target_pairs={{0,4},{4,0},{1,5},{5,1},{2,6},{6,2},{3,7},{7,3},{8,12},{12,8},{9,1... | collective-permute-start | bytes 2359304 | tf_op jit(solution)/shard_map/ppermute | solution.py:566
  149.0 8.0 %collective-permute-start.9 = (bf16[512,768]{1,0:T(8,128)(2,1)S(1)}, bf16[512,768]{1,0:T(8,128)(2,1)S(1)}, u32[]{:S(2)}, u32[]{:S(2)}) collective-permute-start(bf16[512,768]{1,0:T(8,128)(2,1)S(1)} %collective-permute-done.8), channel_id=1, source_target_pairs={{0,4},{4,0},{1,5},{5,1},{2,6},{6,2},{3,7},{7,3},{8,12},{12,8},{9,1... | collective-permute-start | bytes 2359304 | tf_op jit(solution)/shard_map/ppermute | solution.py:566
  205.6 10.8 %collective-permute-start.11 = (bf16[192,512]{1,0:T(8,128)(2,1)S(1)}, bf16[192,512]{1,0:T(8,128)(2,1)}, u32[]{:S(2)}, u32[]{:S(2)}) collective-permute-start(bf16[192,512]{1,0:T(8,128)(2,1)S(1)} %bitcast.84), channel_id=1, source_target_pairs={{0,0},{1,2},{2,4},{3,6},{4,1},{5,3},{6,5},{7,7},{8,8},{9,10},{10,1... | collective-permute-start | bytes 589832 | tf_op jit(solution)/shard_map/ppermute | solution.py:598
  209.3 17.5 %collective-permute-start.12 = (bf16[192,512]{1,0:T(8,128)(2,1)S(1)}, bf16[192,512]{1,0:T(8,128)(2,1)}, u32[]{:S(2)}, u32[]{:S(2)}) collective-permute-start(bf16[192,512]{1,0:T(8,128)(2,1)S(1)} %bitcast.83), channel_id=1, source_target_pairs={{0,1},{1,3},{2,5},{3,7},{4,2},{5,0},{6,6},{7,4},{8,9},{9,11},{10,1... | collective-permute-start | bytes 589832 | tf_op jit(solution)/shard_map/ppermute | solution.py:598
  211.2 15.6 %collective-permute-start.13 = (bf16[192,512]{1,0:T(8,128)(2,1)S(1)}, bf16[192,512]{1,0:T(8,128)(2,1)}, u32[]{:S(2)}, u32[]{:S(2)}) collective-permute-start(bf16[192,512]{1,0:T(8,128)(2,1)S(1)} %bitcast.82), channel_id=1, source_target_pairs={{0,2},{1,0},{2,6},{3,4},{4,3},{5,1},{6,7},{7,5},{8,10},{9,8},{10,1... | collective-permute-start | bytes 589832 | tf_op jit(solution)/shard_map/ppermute | solution.py:598
  212.1 14.6 %collective-permute-start.14 = (bf16[192,512]{1,0:T(8,128)(2,1)S(1)}, bf16[192,512]{1,0:T(8,128)(2,1)}, u32[]{:S(2)}, u32[]{:S(2)}) collective-permute-start(bf16[192,512]{1,0:T(8,128)(2,1)S(1)} %bitcast.81), channel_id=1, source_target_pairs={{0,3},{1,1},{2,7},{3,5},{4,0},{5,2},{6,4},{7,6},{8,11},{9,9},{10,1... | collective-permute-start | bytes 589832 | tf_op jit(solution)/shard_map/ppermute | solution.py:598
  252.8 84.9 %collective-permute-start.34 = (bf16[4,4,96,1792]{3,2,1,0:T(8,128)(2,1)}, bf16[4,4,96,1792]{3,2,1,0:T(8,128)(2,1)}, u32[]{:S(2)}, u32[]{:S(2)}) collective-permute-start(bf16[4,4,96,1792]{3,2,1,0:T(8,128)(2,1)} %get-tuple-element.36), channel_id=1, source_target_pairs={{0,4},{4,0},{1,5},{5,1},{2,6},{6,2},{3,7},{7,3},{8,12},{12,8},{9,1... | collective-permute-start | bytes 16515080 | tf_op jit(solution)/shard_map/ppermute | solution.py:566
  252.9 13.9 %collective-permute-start.16 = (bf16[192,512]{1,0:T(8,128)(2,1)}, bf16[192,512]{1,0:T(8,128)(2,1)}, u32[]{:S(2)}, u32[]{:S(2)}) collective-permute-start(bf16[192,512]{1,0:T(8,128)(2,1)} %get-tuple-element.27), channel_id=1, source_target_pairs={{0,0},{2,1},{4,2},{6,3},{1,4},{3,5},{5,6},{7,7},{8,8},{10,9},{12,1... | collective-permute-start | bytes 589832 | tf_op jit(solution)/shard_map/ppermute | solution.py:618
  256.8 10.2 %collective-permute-start.17 = (bf16[192,512]{1,0:T(8,128)(2,1)}, bf16[192,512]{1,0:T(8,128)(2,1)}, u32[]{:S(2)}, u32[]{:S(2)}) collective-permute-start(bf16[192,512]{1,0:T(8,128)(2,1)} %get-tuple-element.28), channel_id=1, source_target_pairs={{1,0},{3,1},{5,2},{7,3},{2,4},{0,5},{6,6},{4,7},{9,8},{11,9},{13,1... | collective-permute-start | bytes 589832 | tf_op jit(solution)/shard_map/ppermute | solution.py:618
  258.9 13.4 %collective-permute-start.18 = (bf16[192,512]{1,0:T(8,128)(2,1)}, bf16[192,512]{1,0:T(8,128)(2,1)}, u32[]{:S(2)}, u32[]{:S(2)}) collective-permute-start(bf16[192,512]{1,0:T(8,128)(2,1)} %get-tuple-element.29), channel_id=1, source_target_pairs={{2,0},{0,1},{6,2},{4,3},{3,4},{1,5},{7,6},{5,7},{10,8},{8,9},{14,1... | collective-permute-start | bytes 589832 | tf_op jit(solution)/shard_map/ppermute | solution.py:618
  259.6 15.8 %collective-permute-start.19 = (bf16[192,512]{1,0:T(8,128)(2,1)}, bf16[192,512]{1,0:T(8,128)(2,1)}, u32[]{:S(2)}, u32[]{:S(2)}) collective-permute-start(bf16[192,512]{1,0:T(8,128)(2,1)} %get-tuple-element.30), channel_id=1, source_target_pairs={{3,0},{1,1},{7,2},{5,3},{0,4},{2,5},{4,6},{6,7},{11,8},{9,9},{15,1... | collective-permute-start | bytes 589832 | tf_op jit(solution)/shard_map/ppermute | solution.py:618
  337.7 175.5 %reduce-scatter.5.cloned.1.call-start = ((), (), s32[]{:S(2)}) async-start(), calls=%async_computation.2 | async-start | bytes 5849088 | tf_op jit(solution)/shard_map/reduce_scatter | solution.py:616
  354.3 42.4 %collective-permute-start.23 = (bf16[512,768]{1,0:T(8,128)(2,1)S(1)}, bf16[512,768]{1,0:T(8,128)(2,1)S(1)}, u32[]{:S(2)}, u32[]{:S(2)}) collective-permute-start(bf16[512,768]{1,0:T(8,128)(2,1)S(1)} %convolution_convert_fusion.1), channel_id=1, source_target_pairs={{0,4},{4,0},{1,5},{5,1},{2,6},{6,2},{3,7},{7,3},{8,12},{12,8},{9,1... | collective-permute-start | bytes 2359304 | tf_op jit(solution)/shard_map/ppermute | solution.py:566
  357.6 39.2 %collective-permute-start.25 = (bf16[512,768]{1,0:T(8,128)(2,1)S(1)}, bf16[512,768]{1,0:T(8,128)(2,1)S(1)}, u32[]{:S(2)}, u32[]{:S(2)}) collective-permute-start(bf16[512,768]{1,0:T(8,128)(2,1)S(1)} %add_select_fusion), channel_id=1, source_target_pairs={{0,1},{1,2},{6,5},{7,6},{8,9},{9,10},{14,13},{15,14},{16,17},{17,1... | collective-permute-start | bytes 2359304 | tf_op jit(solution)/shard_map/ppermute | solution.py:634
  359.1 11.4 %collective-permute-start.27 = (f32[1920]{0:T(1024)S(1)}, f32[1920]{0:T(1024)S(1)}, u32[]{:S(2)}, u32[]{:S(2)}) collective-permute-start(f32[1920]{0:T(1024)S(1)} %pad_maximum_fusion.2), channel_id=1, source_target_pairs={{0,4},{4,0},{1,5},{5,1},{2,6},{6,2},{3,7},{7,3},{8,12},{12,8},{9,1... | collective-permute-start | bytes 23048 | tf_op jit(solution)/shard_map/ppermute | solution.py:666
  384.7 12.0 %collective-permute-start.31 = (f32[1920]{0:T(1024)S(1)}, f32[1920]{0:T(1024)S(1)}, u32[]{:S(2)}, u32[]{:S(2)}) collective-permute-start(f32[1920]{0:T(1024)S(1)} %add.156), channel_id=1, source_target_pairs={{0,16},{8,24},{16,0},{24,8},{1,17},{9,25},{17,1},{25,9},{2,18},{10... | collective-permute-start | bytes 23048 | tf_op jit(solution)/shard_map/ppermute | solution.py:666
  385.6 45.2 %collective-permute-start.20 = (bf16[512,768]{1,0:T(8,128)(2,1)S(1)}, bf16[512,768]{1,0:T(8,128)(2,1)S(1)}, u32[]{:S(2)}, u32[]{:S(2)}) collective-permute-start(bf16[512,768]{1,0:T(8,128)(2,1)S(1)} %convolution_convert_fusion.3), channel_id=1, source_target_pairs={{0,4},{4,0},{1,5},{5,1},{2,6},{6,2},{3,7},{7,3},{8,12},{12,8},{9,1... | collective-permute-start | bytes 2359304 | tf_op jit(solution)/shard_map/ppermute | solution.py:566
  397.7 33.0 %collective-permute-start.26 = (bf16[512,768]{1,0:T(8,128)(2,1)}, bf16[512,768]{1,0:T(8,128)(2,1)}, u32[]{:S(2)}, u32[]{:S(2)}) collective-permute-start(bf16[512,768]{1,0:T(8,128)(2,1)} %select_add_fusion), channel_id=1, source_target_pairs={{0,1},{1,2},{2,3},{5,4},{6,5},{7,6},{8,9},{9,10},{10,11},{13,12},{... | collective-permute-start | bytes 2359304 | tf_op jit(solution)/shard_map/ppermute | solution.py:636
  400.8 28.1 %collective-permute-start.32 = (bf16[96,576]{1,0:T(8,128)(2,1)S(1)}, bf16[96,576]{1,0:T(8,128)(2,1)}, u32[]{:S(2)}, u32[]{:S(2)}) collective-permute-start(bf16[96,576]{1,0:T(8,128)(2,1)S(1)} %get-tuple-element.112), channel_id=1, source_target_pairs={{0,0},{1,2},{2,4},{3,6},{4,1},{5,3},{6,5},{7,7},{8,8},{9,10},{10,1... | collective-permute-start | bytes 331784 | tf_op jit(solution)/shard_map/ppermute | solution.py:651
  402.7 26.2 %collective-permute-start.33 = (bf16[96,576]{1,0:T(8,128)(2,1)S(1)}, bf16[96,576]{1,0:T(8,128)(2,1)}, u32[]{:S(2)}, u32[]{:S(2)}) collective-permute-start(bf16[96,576]{1,0:T(8,128)(2,1)S(1)} %get-tuple-element.111), channel_id=1, source_target_pairs={{0,4},{1,6},{2,0},{3,2},{4,5},{5,7},{6,1},{7,3},{8,12},{9,14},{10,... | collective-permute-start | bytes 331784 | tf_op jit(solution)/shard_map/ppermute | solution.py:652
  (41 other events, 1047.3 us)
Sparse Core Ops, SparseCore 0:
  11.4 86.7 all-gather.2
  337.8 26.9 reduce-scatter.6
  370.1 143.0 reduce-scatter.4

commit v2 on v1

--- a/solution.py
+++ b/solution.py
@@ -349,53 +349,39 @@
     )(least, clear, slots, group, *operands)
 
 
-def middle_kernel(place_ref, *refs):
-    parts = place_ref.shape[0] - 1
+def middle_kernel(turn_ref, *refs):
+    parts = turn_ref.shape[0]
     mixes = refs[:parts]
-    x_ref, g_ref, gain_ref, own_ref, other_ref, out_ref, gh_ref, gain_grad_ref = refs[
-        parts : parts + 8
+    x_ref, g_ref, gain_ref, weight_ref, out_ref, gh_ref, gain_grad_ref = refs[parts : parts + 7]
+    gots = refs[parts + 7 : 2 * parts + 7]
+    grads_ref, w_ref, grad_ref, second_ref, acc_ref, back_ref, load_sem, store_sem = refs[
+        2 * parts + 7 :
     ]
-    gots = refs[parts + 8 : 2 * parts + 8]
-    keep_ref, send_ref, w_ref, grad_ref, second_ref, acc_ref, back_ref, load_sem, store_sem = refs[
-        2 * parts + 8 :
-    ]
-    core = place_ref[parts]
     width = x_ref.shape[1]
     columns = mixes[0].shape[0]
-    feed = own_ref.shape[3] - 256
+    feed = weight_ref.shape[3] - 256
     hidden_units = feed // 2
     late, early = pl.ds(feed, 256), pl.ds(0, feed)
 
-    def loads(z, which, cols):
-        pairs = [(own_ref, core), (other_ref, 1 - core)]
-        return [
-            pltpu.make_async_copy(
-                src.at[z, :, :, cols], w_ref.at[z, :, at, :, cols], load_sem.at[z, which, i]
-            )
-            for i, (src, at) in enumerate(pairs)
-        ]
-
-    def stores(z, which, cols):
-        pairs = [(keep_ref, core), (send_ref, 1 - core)]
-        return [
-            pltpu.make_async_copy(
-                grad_ref.at[z, :, at, :, cols], dst.at[z, :, :, cols], store_sem.at[z, which, i]
-            )
-            for i, (dst, at) in enumerate(pairs)
-        ]
+    def load(z, which, cols):
+        return pltpu.make_async_copy(
+            weight_ref.at[:, z, :, cols], w_ref.at[z, :, :, cols], load_sem.at[z, which]
+        )
+
+    def store(z, which, cols):
+        return pltpu.make_async_copy(
+            grad_ref.at[z, :, :, cols], grads_ref.at[:, z, :, cols], store_sem.at[z, which]
+        )
 
     for z in range(parts):
-        for copy in loads(z, 0, late):
-            copy.start()
+        load(z, 0, late).start()
     for z in range(parts):
-        for copy in loads(z, 1, early):
-            copy.start()
+        load(z, 1, early).start()
     for z in range(parts):
-        for copy in loads(z, 0, late):
-            copy.wait()
+        load(z, 0, late).wait()
 
     def output_rows(turn):
-        return w_ref[place_ref[turn], :, :, :, feed : feed + columns].reshape(width, columns)
+        return w_ref[turn_ref[turn], :, :, feed : feed + columns].reshape(width, columns)
 
     hidden = x_ref[...].astype(f32)
     for turn in range(parts):
@@ -407,10 +393,9 @@
     gh_ref[...] = hidden * inverse
 
     def hidden_part(z, _):
-        for copy in loads(z, 1, early):
-            copy.wait()
-        inner = w_ref[z, :, :, :, :hidden_units].reshape(width, hidden_units)
-        outer = w_ref[z, :, :, :, hidden_units:feed].reshape(width, hidden_units)
+        load(z, 1, early).wait()
+        inner = w_ref[z, :, :, :hidden_units].reshape(width, hidden_units)
+        outer = w_ref[z, :, :, hidden_units:feed].reshape(width, hidden_units)
         second = second_ref[...]
         grad = g_ref[...]
         grad_active = dot(grad, outer).astype(bf16).astype(f32)
@@ -419,15 +404,14 @@
         grad_units = (grad_active * slope).astype(bf16)
         acc_ref[...] += dot(active, outer, ((1,), (1,)))
         back_ref[...] += dot(grad_units, inner, ((1,), (1,)))
-        shape = (*grad_ref.shape[1:4], hidden_units)
-        grad_ref[z, :, :, :, :hidden_units] = (
+        shape = (*grad_ref.shape[1:3], hidden_units)
+        grad_ref[z, :, :, :hidden_units] = (
             dot(second, grad_units, ((0,), (0,))).astype(bf16).reshape(shape)
         )
-        grad_ref[z, :, :, :, hidden_units:feed] = (
+        grad_ref[z, :, :, hidden_units:feed] = (
             dot(grad, active, ((0,), (0,))).astype(bf16).reshape(shape)
         )
-        for copy in stores(z, 1, early):
-            copy.start()
+        store(z, 1, early).start()
         return 0
 
     lax.fori_loop(0, parts, hidden_part, 0)
@@ -444,52 +428,49 @@
     for turn in range(parts):
         gots[turn][...] = dot(output_rows(turn), rounded, ((0,), (1,))).astype(bf16)
         grads = dot(rounded, mixes[turn][...], ((0,), (1,))).astype(bf16)
-        grad_ref[place_ref[turn], :, :, :, feed : feed + columns] = grads.reshape(
-            *grad_ref.shape[1:4], columns
+        grad_ref[turn_ref[turn], :, :, feed : feed + columns] = grads.reshape(
+            *grad_ref.shape[1:3], columns
         )
-        grad_ref[place_ref[turn], :, :, :, feed + columns :] = jnp.zeros(
-            (*grad_ref.shape[1:4], 256 - columns), bf16
+        grad_ref[turn_ref[turn], :, :, feed + columns :] = jnp.zeros(
+            (*grad_ref.shape[1:3], 256 - columns), bf16
         )
     for z in range(parts):
-        for copy in stores(z, 0, late):
-            copy.start()
+        store(z, 0, late).start()
     for z in range(parts):
-        for copy in stores(z, 0, late) + stores(z, 1, early):
-            copy.wait()
-
-
-def middle(place, mixes, inputs, cotangent, gain, own, other):
+        store(z, 0, late).wait()
+        store(z, 1, early).wait()
+
+
+def middle(turns, mixes, inputs, cotangent, gain, weights):
     rows, width = inputs.shape
-    parts, planes, each, columns = own.shape
+    owners, parts, each, columns = weights.shape
     smem = pl.BlockSpec(memory_space=pltpu.SMEM)
     hbm = pl.BlockSpec(memory_space=pl.ANY)
-    held = pltpu.VMEM((parts, planes, 2, each, columns), bf16)
-    token_shape = jax.ShapeDtypeStruct((rows, width), f32)
-    gain = gain.reshape(1, width)
-    dense = [*mixes, inputs, cotangent, gain]
+    held = pltpu.VMEM((parts, owners, each, columns), bf16)
+    dense = [*mixes, inputs, cotangent, gain.reshape(1, width)]
     outs = [
         jax.ShapeDtypeStruct((rows, width), bf16),
-        token_shape,
+        jax.ShapeDtypeStruct((rows, width), f32),
         jax.ShapeDtypeStruct((1, width), f32),
         *[jax.ShapeDtypeStruct(mix.shape, bf16) for mix in mixes],
     ]
     return pl.pallas_call(
         middle_kernel,
-        in_specs=[smem] + [whole(a.shape) for a in dense] + [hbm, hbm],
-        out_specs=[whole(a.shape) for a in outs] + [hbm, hbm],
-        out_shape=outs + [jax.ShapeDtypeStruct(own.shape, bf16)] * 2,
+        in_specs=[smem] + [whole(a.shape) for a in dense] + [hbm],
+        out_specs=[whole(a.shape) for a in outs] + [hbm],
+        out_shape=outs + [jax.ShapeDtypeStruct(weights.shape, bf16)],
         scratch_shapes=[
             held,
             held,
             pltpu.VMEM((rows, width), bf16),
             pltpu.VMEM((rows, width), f32),
             pltpu.VMEM((rows, width), f32),
-            pltpu.SemaphoreType.DMA((parts, 2, 2)),
-            pltpu.SemaphoreType.DMA((parts, 2, 2)),
+            pltpu.SemaphoreType.DMA((parts, 2)),
+            pltpu.SemaphoreType.DMA((parts, 2)),
         ],
         compiler_params=params(),
         name="middle",
-    )(place, *dense, own, other)
+    )(turns, *dense, weights)
 
 
 def flat(pairs, parts):
@@ -525,7 +506,27 @@
 
 SWAP = [(0, 1), (1, 0)]
 LINE = ("core", "tensor")
-EVERY = ("tensor", "plane")
+
+
+def after(value, *earlier):
+    return lax.optimization_barrier((value, *earlier))[0]
+
+
+def across(value, step):
+    return lax.ppermute(value, "plane", [(i, i ^ step) for i in range(lax.axis_size("plane"))])
+
+
+def planes_gathered(low, high):
+    planes = lax.axis_size("plane")
+    if planes != 4:
+        return lax.all_gather(jnp.stack([low, high]), "plane", axis=0)
+    low_x, high_y = across(low, 1), across(high, 2)
+    low_y, high_x = across(low, 2), across(high, 1)
+    low_xy, high_xy = across(low_x, 2), across(high_y, 1)
+    pairs = jnp.stack(
+        [jnp.stack(pair) for pair in ((low, high), (low_x, high_x), (low_y, high_y), (low_xy, high_xy))]
+    )
+    return pairs[jnp.arange(planes) ^ lax.axis_index("plane")]
 
 
 def body(
@@ -565,24 +566,26 @@
     def swap(value):
         return lax.ppermute(value, "core", SWAP)
 
+    pad = jnp.zeros((each, 256 - columns), bf16)
+    packed_rest = jnp.concatenate([inner_weight, outer_weight.T, output_weight.T, pad], axis=1)
+    line_rest = lax.all_gather(packed_rest, "tensor", axis=0)
+
     inputs_wide = inputs.astype(f32)
     scaled_first, inverse_first, normed_own = norm_forward(inputs_wide, attention_gain)
+    packed = jnp.concatenate([query_weight, key_weight, value_weight], axis=1)
     first = lax.ppermute(normed_own, LINE, gather[0])
+    one, two = (lax.ppermute(packed, LINE, route) for route in weight_routes)
+    table = lax.ppermute(bias_table, LINE, weight_routes[0])
+    block_row = jnp.where(owner, block_index, swap(block_index))[0]
+    first, one, two, table, block_row = lax.optimization_barrier((first, one, two, table, block_row))
     second = lax.ppermute(first, LINE, gather[1])
+    attention_full = planes_gathered(
+        jnp.where(lower, one, two), jnp.where(lower, two, one)
+    ).reshape(width, 3 * columns)
+    second, attention_full = lax.optimization_barrier((second, attention_full))
     third = lax.ppermute(jnp.where(outer_chip, normed_own, second), LINE, gather[2])
     normed = [jnp.where(owner, piece, swap(piece)) for piece in (normed_own, first, second, third)]
-
-    packed = jnp.concatenate([query_weight, key_weight, value_weight], axis=1)
-    one, two = (lax.ppermute(packed, LINE, route) for route in weight_routes)
-    mine = jnp.concatenate([jnp.where(lower, one, two), jnp.where(lower, two, one)], axis=0)
-    attention_full = lax.all_gather(mine, "plane", axis=0, tiled=True)
-    table = lax.ppermute(bias_table, LINE, weight_routes[0])
-    block_row = jnp.where(owner, block_index, swap(block_index))[0]
-
-    pad = jnp.zeros((each, 256 - columns), bf16)
-    packed_rest = jnp.concatenate([inner_weight, outer_weight.T, output_weight.T, pad], axis=1)
-    own_rest = lax.all_gather(packed_rest, EVERY, axis=0).reshape(parts, planes, each, -1)
-    other_rest = swap(own_rest)
+    all_rest = lax.all_gather(after(line_rest, second), ("plane", "core"), axis=0)
 
     rows, onehot = bias_rows(table, position_bucket)
     bias = bias_tiles(rows, length)
@@ -594,32 +597,23 @@
         for piece in normed
     ]
     ot, lse = attend_forward(pieces, bias, end, full, most, slots, group_ref)
-    mixes = [
-        lax.ppermute(ot[r].reshape(columns, -1), LINE, rounds[r]) for r in range(parts)
-    ]
-    place = jnp.stack([(z - r) % parts for r in range(parts)] + [core]).astype(jnp.int32)
-    aligned = each % 16 == 0
-    if aligned:
-        outs = middle(place, mixes, inputs, cotangent, feedforward_gain, own_rest, other_rest)
-        layer_output, grad_hidden, feedforward_part, *gots, keep, send = outs
-    else:
-        low, high = jnp.where(core == 0, own_rest, other_rest), jnp.where(core == 0, other_rest, own_rest)
-        both = jnp.stack([low, high], axis=2).reshape(parts, 2, width // 2, -1)
-        lone = place.at[parts].set(0)
-        outs = middle(lone, mixes, inputs, cotangent, feedforward_gain, both[:, :1], both[:, 1:])
-        layer_output, grad_hidden, feedforward_part, *gots, keep, send = outs
-        grads = jnp.concatenate([keep, send], axis=1).reshape(parts, planes, 2, each, -1)
-        keep, send = (
-            lax.dynamic_index_in_dim(grads, at, 2, False) for at in (core, 1 - core)
-        )
-    rest = (keep + swap(send)).reshape(parts * planes, each, -1)
-    rest_share = lax.psum_scatter(rest, EVERY, scatter_dimension=0).astype(f32) * factor
-
+    mixes = [lax.ppermute(ot[r].reshape(columns, -1), LINE, rounds[r]) for r in range(parts)]
+    turns = jnp.stack([(z - r) % parts for r in range(parts)]).astype(jnp.int32)
+    if each % 16:
+        all_rest = jnp.swapaxes(all_rest, 0, 1).reshape(1, parts, width, -1)
+    layer_output, grad_hidden, feedforward_part, *gots, grads = middle(
+        turns, mixes, inputs, cotangent, feedforward_gain, all_rest
+    )
+    if each % 16:
+        grads = jnp.swapaxes(grads.reshape(parts, planes * 2, each, -1), 0, 1)
     gots = [lax.ppermute(got, LINE, back(rounds[r])) for r, got in enumerate(gots)]
     gots = [got.reshape(heads, size, -1) for got in gots]
-    dqkv, bands = attend_backward(
-        pieces, gots, ot, lse, bias, end, least, clear, slots, group_ref
-    )
+
+    rest = lax.psum_scatter(grads, ("plane", "core"), scatter_dimension=0)
+    rest = lax.psum_scatter(rest, "tensor", scatter_dimension=0)
+    rest_share = rest.astype(f32) * factor
+
+    dqkv, bands = attend_backward(pieces, gots, ot, lse, bias, end, least, clear, slots, group_ref)
     dqkv = dqkv.reshape(parts, 3 * columns, length // parts)
 
     def normed_part(i):
@@ -627,45 +621,62 @@
         return part + swap(part)
 
     third, second, first, own = (normed_part(i) for i in (3, 2, 1, 0))
+
+    attention_grads = sum(dot(normed[i], dqkv[i], ((0,), (1,))) for i in range(parts))
+    attention_part = (
+        jnp.sum(attention_grads * attention_full.astype(f32), axis=1) / attention_gain
+    )
+    attention_grads = attention_grads.astype(bf16).reshape(planes, 2, each, 3 * columns)
+
+    table_local = table_part(bands, onehot, length)
+    buckets = table_local.shape[0]
+    table_whole = lax.dynamic_update_slice(
+        jnp.zeros((buckets, H), f32), table_local, (jnp.zeros((), jnp.int32), group * heads)
+    )
+    small = jnp.concatenate(
+        [attention_part, feedforward_part.reshape(width), table_whole.reshape(buckets * H)]
+    )
+
+    def small_step(small, axis, step):
+        count = lax.axis_size(axis)
+        return small + lax.ppermute(small, axis, [(i, i ^ step) for i in range(count)])
+
     none = jnp.zeros_like(own)
     got = lax.ppermute(third, LINE, back(gather[2]))
+    if planes == 4:
+        relative = attention_grads[jnp.arange(planes) ^ lax.axis_index("plane")]
+        low, high = relative[:, 0], relative[:, 1]
+        low, high = low[0::2] + across(low[1::2], 1), high[:2] + across(high[2:], 2)
+    small = small_step(small, "core", 1)
+    small = small_step(small, "tensor", 1)
+    if planes == 4:
+        got, low, high, small = lax.optimization_barrier((got, low, high, small))
     own = jnp.where(owner, jnp.where(outer_chip, own + got, own), none)
     second = jnp.where(outer_chip, second, second + got)
     got = lax.ppermute(second, LINE, back(gather[1]))
+    if planes == 4:
+        low, high = low[0] + across(low[1], 2), high[0] + across(high[1], 1)
+    else:
+        shared = lax.psum_scatter(attention_grads, "plane", scatter_dimension=0)
+        low, high = shared[0], shared[1]
+    small = small_step(small, "tensor", 2)
+    small = small_step(small, "plane", 1)
+    got, low, high, small = lax.optimization_barrier((got, low, high, small))
     first = jnp.where(owner, first, none) + got
     got = lax.ppermute(first, LINE, back(gather[0]))
+    attention_share = (
+        lax.ppermute(jnp.where(lower, low, high), LINE, back(weight_routes[0]))
+        + lax.ppermute(jnp.where(lower, high, low), LINE, back(weight_routes[1]))
+    ).astype(f32) * factor
+    step = 2
+    while step < planes:
+        small = small_step(small, "plane", step)
+        step *= 2
+    small = small * factor
     grad_first = (own + got).astype(f32)
     input_grad = (
         grad_hidden + norm_backward(grad_first, scaled_first, inverse_first, attention_gain)
     ).astype(bf16)
-
-    attention_grads = sum(dot(normed[i], dqkv[i], ((0,), (1,))) for i in range(parts))
-    attention_part = (
-        jnp.sum(attention_grads * attention_full.astype(f32), axis=1) / attention_gain
-    )
-    shared = lax.psum_scatter(
-        attention_grads.astype(bf16), "plane", scatter_dimension=0, tiled=True
-    )
-    low, high = shared[:each], shared[each:]
-    attention_share = (
-        lax.ppermute(jnp.where(lower, low, high), LINE, back(weight_routes[0]))
-        + lax.ppermute(jnp.where(lower, high, low), LINE, back(weight_routes[1]))
-    ).astype(f32) * factor
-
-    table_local = table_part(bands, onehot, length)
-    buckets = table_local.shape[0]
-    table_whole = lax.dynamic_update_slice(
-        jnp.zeros((buckets, H), f32), table_local, (jnp.zeros((), jnp.int32), group * heads)
-    )
-    small = jnp.concatenate(
-        [attention_part, feedforward_part.reshape(width), table_whole.reshape(buckets * H)]
-    )
-    for axis, count in (("core", 2), ("tensor", parts), ("plane", planes)):
-        step = 1
-        while step < count:
-            small = small + lax.ppermute(small, axis, [(i, i ^ step) for i in range(count)])
-            step *= 2
-    small = small * factor
 
     return (
         layer_output,

time: 527 us -> 370 us (0.70)
  waiting for transfers between devices: 224 us -> 84.1 us
  blocking collectives: 11.8 us -> 0 us
  other arithmetic: 22.1 us -> 16.5 us
    all_gather x1 -> x2, waiting for transfers between devices: 88.1 us -> 0.04 us  [the longest x1 0.02 us: body(): lax.all_gather(after(line_rest, second), ('plane', 'core'), axis=0)]
    reduce_scatter x2, waiting for transfers between devices: 79 us -> 0.01 us  [the longest x1 0.01 us: body(): rest = lax.psum_scatter(grads, ('plane', 'core'), scatter_dimension=0)]
    ppermute x1, waiting for transfers between devices: 24.8 us -> 0.01 us  [body(): lax.ppermute(jnp.where(lower, low, high), LINE, back(weight_routes[0]))]
    ppermute x1, waiting for transfers between devices: 5.55 us -> 26.1 us  [body(): table = lax.ppermute(bias_table, LINE, weight_routes[0])]
    ppermute x1, waiting for transfers between devices: 0.01 us -> 17.6 us  [body(): got = lax.ppermute(first, LINE, back(gather[0]))]
    all_gather x1 -> x0, blocking collectives: 11.8 us -> none  [body(): attention_full = lax.all_gather(mine, 'plane', axis=0, tiled=True)]
    add x5 -> x8, other arithmetic: 8.19 us -> 0.12 us  [the longest x2 0.04 us: body(): low, high = (low[0] + across(low[1], 2), high[0] + across(high[1], 1))]
    ppermute x1, waiting for transfers between devices: 0.01 us -> 6.92 us  [body(): lax.ppermute(jnp.where(lower, high, low), LINE, back(weight_routes[1]))]
  transfers between devices with their start and end apart: 38 -> 47, of which waited for: 13 -> 15; matrix products, arithmetic and copies ran while one was open for 9% -> 13% of each run, Pallas kernels for 20% -> 28%
where the time goes in v2:
time: 370 us; the launch traced here: 368 us
  Pallas kernels  128 us (35%)
  starting transfers between devices  84.4 us (23%)
  waiting for transfers between devices  84.1 us (23%)
  local copies, waits for them, and re-layouts  20.8 us (6%)
  matrix products  19.2 us (5%)
  other arithmetic  16.5 us (4%)
  between operations  14.8 us (4%)
    pallas_call x1, Pallas kernels, attend_backward(): pl.pallas_call(backward_kernel, grid=(count,), in_specs=[smem] * 4 + [who...  52.1 us
    pallas_call x1, Pallas kernels, attend_forward(): pl.pallas_call(forward_kernel, grid=(count,), in_specs=[smem] * 4 + [whol...  43.8 us
    ppermute x1, waiting for transfers between devices, body(): table = lax.ppermute(bias_table, LINE, weight_routes[0])  26.1 us
    pallas_call x1, Pallas kernels, middle(): pl.pallas_call(middle_kernel, in_specs=[smem] + [whole(a.shape) for a in...  25.8 us
    ppermute x9, starting transfers between devices, swap(): return lax.ppermute(value, 'core', SWAP)  21.8 us
    dot_general x12, matrix products, dot(): lax.dot_general(left, right, (contract, ((), ())), preferred_element_type...  17.8 us
    ppermute x1, waiting for transfers between devices, body(): got = lax.ppermute(first, LINE, back(gather[0]))  17.6 us
    ppermute x10, starting transfers between devices, across(): lax.ppermute(value, 'plane', [(i, i ^ step) for i in range(lax.axis_size(...  12.7 us
  transfers between devices with their start and end apart: 47, of which 15 were waited for; matrix products, arithmetic and copies ran while one was open for 13% of the time, Pallas kernels for 28%

profile of v2, /device:TPU:9, one launch (start us, length us, event | category | flops | bytes accessed | tf_op | source)
XLA Modules:
  0.0 368.1 jit_solution(6125799669366482314)
XLA Ops:
  10.7 3.2 collective-permute-start
  14.0 3.2 collective-permute-start.1
  22.1 26.1 %collective-permute-done.3 = f32[32,3]{0,1:T(4,128)S(1)} collective-permute-done((f32[32,3]{0,1:T(4,128)S(1)}, f32[32,3]{0,1:T(4,128)S(1)}, u32[]{:S(2)}, u32[]{:S(2)}) %collective-permute-start.3) | collective-permute-done | bytes 416 | tf_op jit(solution)/shard_map/ppermute | solution.py:578
  48.8 5.1 %collective-permute-start.5 = (bf16[512,768]{1,0:T(8,128)(2,1)}, bf16[512,768]{1,0:T(8,128)(2,1)}, u32[]{:S(2)}, u32[]{:S(2)}) collective-permute-start(bf16[512,768]{1,0:T(8,128)(2,1)} %collective-permute-done), channel_id=1, source_target_pairs={{1,0},{2,1},{5,6},{6,7},{9,8},{10,9},{13,14},{14,15},{17,16},{18,1... | collective-permute-start | bytes 2359304 | tf_op jit(solution)/shard_map/ppermute | solution.py:581
  66.2 3.8 %collective-permute-start.12 = (bf16[512,768]{1,0:T(8,128)(2,1)S(1)}, bf16[512,768]{1,0:T(8,128)(2,1)}, u32[]{:S(2)}, u32[]{:S(2)}) collective-permute-start(bf16[512,768]{1,0:T(8,128)(2,1)S(1)} %fusion.3), channel_id=1, source_target_pairs={{0,4},{4,0},{1,5},{5,1},{2,6},{6,2},{3,7},{7,3},{8,12},{12,8},{9,1... | collective-permute-start | bytes 2359304 | tf_op jit(solution)/shard_map/ppermute | solution.py:567
  75.4 6.6 %bias_tiles.1.refs_4_.refs_10_ = f32[3,10,256,256]{3,2,1,0:T(8,128)} custom-call(f32[3,1,2816]{2,1,0:T(1,128)} %slice.164.row_ref), custom_call_target="tpu_custom_call" | custom-call | tf_op jit(solution)/shard_map/bias_tiles/pallas_call | solution.py:79
  84.4 3.4 collective-permute-start.16
  87.8 2.7 convolution_convert_fusion.6
  90.6 2.7 convolution_convert_fusion.7
  96.5 43.8 %attend_forward.1 = (bf16[4,3,64,512]{3,2,1,0:T(8,128)(2,1)}, f32[3,1,2048]{2,1,0:T(1,128)}) custom-call(s32[8]{0:T(128)} %get-tuple-element.150.full_ref, s32[8]{0:T(128)} %get-tuple-element.149.most_ref, s32[4]{0:T(128)} %dynamic-slice_bitcast_fusion.slot_ref, s32[1]{0:T(128)} %bitcast.6.group_ref, bf16[9,64,512]{2,1,0:T(8,128)(2,1)} %bitcast.111, ...), custom_call_target="tpu_custom_call" | custom-call | tf_op jit(solution)/shard_map/attend_forward/pallas_call | solution.py:187
  141.7 3.4 collective-permute-start.17
  147.0 2.4 collective-permute-start.19
  152.8 4.6 %collective-permute-done.17.refs_0_ = bf16[192,512]{1,0:T(8,128)(2,1)S(1)} collective-permute-done((bf16[192,512]{1,0:T(8,128)(2,1)S(1)}, bf16[192,512]{1,0:T(8,128)(2,1)S(1)}, u32[]{:S(2)}, u32[]{:S(2)}) %collective-permute-start.17) | collective-permute-done | bytes 196640 | tf_op jit(solution)/shard_map/ppermute | solution.py:600
  157.4 6.0 %collective-permute-done.18.refs_1_ = bf16[192,512]{1,0:T(8,128)(2,1)S(1)} collective-permute-done((bf16[192,512]{1,0:T(8,128)(2,1)S(1)}, bf16[192,512]{1,0:T(8,128)(2,1)S(1)}, u32[]{:S(2)}, u32[]{:S(2)}) %collective-permute-start.18) | collective-permute-done | bytes 196640 | tf_op jit(solution)/shard_map/ppermute | solution.py:600
  164.1 25.8 %middle.1 = (bf16[512,768]{1,0:T(8,128)(2,1)}, f32[512,768]{1,0:T(8,128)}, f32[1,768]{1,0:T(1,128)}, bf16[192,512]{1,0:T(8,128)(2,1)}, bf16[192,512]{1,0:T(8,128...) custom-call(s32[4]{0:T(128)} %pad_add_fusion.2.turn_ref, ...), custom_call_target="tpu_custom_call" | custom-call | tf_op jit(solution)/shard_map/middle/pallas_call | solution.py:457
  192.7 3.4 collective-permute-start.22
  197.4 4.4 %collective-permute-start.24 = (bf16[192,512]{1,0:T(8,128)(2,1)}, bf16[192,512]{1,0:T(8,128)(2,1)S(1)}, u32[]{:S(2)}, u32[]{:S(2)}) collective-permute-start(bf16[192,512]{1,0:T(8,128)(2,1)} %get-tuple-element.53), channel_id=1, source_target_pairs={{3,0},{1,1},{7,2},{5,3},{0,4},{2,5},{4,6},{6,7},{11,8},{9,9},{15,1... | collective-permute-start | bytes 589832 | tf_op jit(solution)/shard_map/ppermute | solution.py:609
  205.6 7.0 %collective-permute-done.24 = bf16[192,512]{1,0:T(8,128)(2,1)S(1)} collective-permute-done((bf16[192,512]{1,0:T(8,128)(2,1)}, bf16[192,512]{1,0:T(8,128)(2,1)S(1)}, u32[]{:S(2)}, u32[]{:S(2)}) %collective-permute-start.24) | collective-permute-done | bytes 196640 | tf_op jit(solution)/shard_map/ppermute | solution.py:609
  213.3 52.1 %attend_backward.1 = (bf16[4,9,64,512]{3,2,1,0:T(8,128)(2,1)}, f32[3,10,1,512]{3,2,1,0:T(1,128)}) custom-call(s32[8]{0:T(128)} %convert_reduce_fusion.2.least_ref, s32[8]{0:T(128)} %convert_reduce_fusion.1.clear_ref, s32[4]{0:T(128)} %dynamic-slice_bitcast_fusion.slot_ref, s32[1]{0:T(128)} %bitcast.6.group_ref, bf16[9,64,512]{2,1,0:T(8,128)(2,1)} %bitcast.112, ...), custom_call_target="tpu_custom_call" | custom-call | tf_op jit(solution)/shard_map/attend_backward/pallas_call | solution.py:332
  270.3 2.5 fusion.15
  283.4 2.2 collective-permute-start.29
  287.1 2.4 collective-permute-start.28
  289.8 10.4 %collective-permute-start.32 = (bf16[512,768]{1,0:T(8,128)(2,1)S(1)}, bf16[512,768]{1,0:T(8,128)(2,1)}, u32[]{:S(2)}, u32[]{:S(2)}) collective-permute-start(bf16[512,768]{1,0:T(8,128)(2,1)S(1)} %convolution_convert_fusion.1), channel_id=1, source_target_pairs={{0,4},{4,0},{1,5},{5,1},{2,6},{6,2},{3,7},{7,3},{8,12},{12,8},{9,1... | collective-permute-start | bytes 2359304 | tf_op jit(solution)/shard_map/ppermute | solution.py:567
  303.6 2.2 collective-permute-start.36
  306.6 2.2 collective-permute-done.38
  310.2 2.7 collective-permute-done.35
  312.9 2.5 collective-permute-done.34
  315.4 5.2 %collective-permute-start.41 = (bf16[96,576]{1,0:T(8,128)(2,1)S(1)}, bf16[96,576]{1,0:T(8,128)(2,1)}, u32[]{:S(2)}, u32[]{:S(2)}) collective-permute-start(bf16[96,576]{1,0:T(8,128)(2,1)S(1)} %get-tuple-element.142), channel_id=1, source_target_pairs={{0,0},{1,2},{2,4},{3,6},{4,1},{5,3},{6,5},{7,7},{8,8},{9,10},{10,1... | collective-permute-start | bytes 331784 | tf_op jit(solution)/shard_map/ppermute | solution.py:668
  322.2 2.4 select_add_fusion
  324.5 3.3 collective-permute-start.39
  329.2 6.9 %collective-permute-done.42 = bf16[96,576]{1,0:T(8,128)(2,1)} collective-permute-done((bf16[96,576]{1,0:T(8,128)(2,1)S(1)}, bf16[96,576]{1,0:T(8,128)(2,1)}, u32[]{:S(2)}, u32[]{:S(2)}) %collective-permute-start.42) | collective-permute-done | bytes 110624 | tf_op jit(solution)/shard_map/ppermute | solution.py:669
  337.9 17.6 %collective-permute-done.39 = bf16[512,768]{1,0:T(8,128)(2,1)S(1)} collective-permute-done((bf16[512,768]{1,0:T(8,128)(2,1)}, bf16[512,768]{1,0:T(8,128)(2,1)S(1)}, u32[]{:S(2)}, u32[]{:S(2)}) %collective-permute-start.39) | collective-permute-done | bytes 786464 | tf_op jit(solution)/shard_map/ppermute | solution.py:666
  (243 shorter events, 81.1 us)
Async XLA Ops:
  7.2 58.9 %all-gather.5.cloned.1.call-start = ((), (), s32[]{:S(2)}) async-start(), calls=%async_computation.4 | async-start | bytes 1720320 | tf_op jit(solution)/shard_map/all_gather | solution.py:571
  10.1 153.3 %all-gather.7.cloned.1.call-start = ((), (), s32[]{:S(2)}) async-start(), calls=%async_computation.5 | async-start | bytes 12386304 | tf_op jit(solution)/shard_map/all_gather | solution.py:588
  10.7 37.6 %collective-permute-start = (bf16[512,768]{1,0:T(8,128)(2,1)S(1)}, bf16[512,768]{1,0:T(8,128)(2,1)}, u32[]{:S(2)}, u32[]{:S(2)}) collective-permute-start(bf16[512,768]{1,0:T(8,128)(2,1)S(1)} %fusion.3), channel_id=1, source_target_pairs={{1,0},{2,1},{3,2},{4,5},{5,6},{6,7},{9,8},{10,9},{11,10},{12,13},{... | collective-permute-start | bytes 2359304 | tf_op jit(solution)/shard_map/ppermute | solution.py:576
  14.0 34.2 %collective-permute-start.1 = (bf16[96,576]{1,0:T(8,128)(2,1)S(1)}, bf16[96,576]{1,0:T(8,128)(2,1)S(1)}, u32[]{:S(2)}, u32[]{:S(2)}) collective-permute-start(bf16[96,576]{1,0:T(8,128)(2,1)S(1)} %pad_maximum_fusion.1), channel_id=1, source_target_pairs={{0,0},{2,1},{4,2},{6,3},{1,4},{3,5},{5,6},{7,7},{8,8},{10,9},{12,1... | collective-permute-start | bytes 331784 | tf_op jit(solution)/shard_map/ppermute | solution.py:577
  17.2 31.0 %collective-permute-start.2 = (bf16[96,576]{1,0:T(8,128)(2,1)S(1)}, bf16[96,576]{1,0:T(8,128)(2,1)S(1)}, u32[]{:S(2)}, u32[]{:S(2)}) collective-permute-start(bf16[96,576]{1,0:T(8,128)(2,1)S(1)} %pad_maximum_fusion.1), channel_id=1, source_target_pairs={{4,0},{6,1},{0,2},{2,3},{5,4},{7,5},{1,6},{3,7},{12,8},{14,9},{8,1... | collective-permute-start | bytes 331784 | tf_op jit(solution)/shard_map/ppermute | solution.py:577
  19.6 28.6 %collective-permute-start.3 = (f32[32,3]{0,1:T(4,128)S(1)}, f32[32,3]{0,1:T(4,128)S(1)}, u32[]{:S(2)}, u32[]{:S(2)}) collective-permute-start(f32[32,3]{0,1:T(4,128)S(1)} %copy-done.37), channel_id=1, source_target_pairs={{0,0},{2,1},{4,2},{6,3},{1,4},{3,5},{5,6},{7,7},{8,8},{10,9},{12,1... | collective-permute-start | bytes 1160 | tf_op jit(solution)/shard_map/ppermute | solution.py:578
  48.8 17.2 %collective-permute-start.5 = (bf16[512,768]{1,0:T(8,128)(2,1)}, bf16[512,768]{1,0:T(8,128)(2,1)}, u32[]{:S(2)}, u32[]{:S(2)}) collective-permute-start(bf16[512,768]{1,0:T(8,128)(2,1)} %collective-permute-done), channel_id=1, source_target_pairs={{1,0},{2,1},{5,6},{6,7},{9,8},{10,9},{13,14},{14,15},{17,16},{18,1... | collective-permute-start | bytes 2359304 | tf_op jit(solution)/shard_map/ppermute | solution.py:581
  66.1 244.0 %reduce-scatter.3.cloned.1.call-start = ((), (), s32[]{:S(2)}) async-start(), calls=%async_computation.2 | async-start | bytes 12386304 | tf_op jit(solution)/shard_map/reduce_scatter | solution.py:612
  66.2 24.4 %collective-permute-start.12 = (bf16[512,768]{1,0:T(8,128)(2,1)S(1)}, bf16[512,768]{1,0:T(8,128)(2,1)}, u32[]{:S(2)}, u32[]{:S(2)}) collective-permute-start(bf16[512,768]{1,0:T(8,128)(2,1)S(1)} %fusion.3), channel_id=1, source_target_pairs={{0,4},{4,0},{1,5},{5,1},{2,6},{6,2},{3,7},{7,3},{8,12},{12,8},{9,1... | collective-permute-start | bytes 2359304 | tf_op jit(solution)/shard_map/ppermute | solution.py:567
  71.9 15.9 %collective-permute-start.13 = (bf16[512,768]{1,0:T(8,128)(2,1)}, bf16[512,768]{1,0:T(8,128)(2,1)}, u32[]{:S(2)}, u32[]{:S(2)}) collective-permute-start(bf16[512,768]{1,0:T(8,128)(2,1)} %collective-permute-done), channel_id=1, source_target_pairs={{0,4},{4,0},{1,5},{5,1},{2,6},{6,2},{3,7},{7,3},{8,12},{12,8},{9,1... | collective-permute-start | bytes 2359304 | tf_op jit(solution)/shard_map/ppermute | solution.py:567
  73.5 11.0 %collective-permute-start.15 = (bf16[512,768]{1,0:T(8,128)(2,1)S(1)}, bf16[512,768]{1,0:T(8,128)(2,1)S(1)}, u32[]{:S(2)}, u32[]{:S(2)}) collective-permute-start(bf16[512,768]{1,0:T(8,128)(2,1)S(1)} %broadcast_select_fusion), channel_id=1, source_target_pairs={{1,0},{0,1},{6,7},{7,6},{9,8},{8,9},{14,15},{15,14},{17,16},{16,17... | collective-permute-start | bytes 2359304 | tf_op jit(solution)/shard_map/ppermute | solution.py:586
  82.2 11.1 %collective-permute-start.14 = (bf16[512,768]{1,0:T(8,128)(2,1)}, bf16[512,768]{1,0:T(8,128)(2,1)S(1)}, u32[]{:S(2)}, u32[]{:S(2)}) collective-permute-start(bf16[512,768]{1,0:T(8,128)(2,1)} %collective-permute-done.5), channel_id=1, source_target_pairs={{0,4},{4,0},{1,5},{5,1},{2,6},{6,2},{3,7},{7,3},{8,12},{12,8},{9,1... | collective-permute-start | bytes 2359304 | tf_op jit(solution)/shard_map/ppermute | solution.py:567
  84.4 10.4 %collective-permute-start.16 = (bf16[512,768]{1,0:T(8,128)(2,1)S(1)}, bf16[512,768]{1,0:T(8,128)(2,1)S(1)}, u32[]{:S(2)}, u32[]{:S(2)}) collective-permute-start(bf16[512,768]{1,0:T(8,128)(2,1)S(1)} %collective-permute-done.15), channel_id=1, source_target_pairs={{0,4},{4,0},{1,5},{5,1},{2,6},{6,2},{3,7},{7,3},{8,12},{12,8},{9,1... | collective-permute-start | bytes 2359304 | tf_op jit(solution)/shard_map/ppermute | solution.py:567
  141.7 15.7 %collective-permute-start.17 = (bf16[192,512]{1,0:T(8,128)(2,1)S(1)}, bf16[192,512]{1,0:T(8,128)(2,1)S(1)}, u32[]{:S(2)}, u32[]{:S(2)}) collective-permute-start(bf16[192,512]{1,0:T(8,128)(2,1)S(1)} %bitcast.133), channel_id=1, source_target_pairs={{0,0},{1,2},{2,4},{3,6},{4,1},{5,3},{6,5},{7,7},{8,8},{9,10},{10,1... | collective-permute-start | bytes 589832 | tf_op jit(solution)/shard_map/ppermute | solution.py:600
  145.1 18.2 %collective-permute-start.18 = (bf16[192,512]{1,0:T(8,128)(2,1)S(1)}, bf16[192,512]{1,0:T(8,128)(2,1)S(1)}, u32[]{:S(2)}, u32[]{:S(2)}) collective-permute-start(bf16[192,512]{1,0:T(8,128)(2,1)S(1)} %bitcast.132), channel_id=1, source_target_pairs={{0,1},{1,3},{2,5},{3,7},{4,2},{5,0},{6,6},{7,4},{8,9},{9,11},{10,1... | collective-permute-start | bytes 589832 | tf_op jit(solution)/shard_map/ppermute | solution.py:600
  147.0 16.3 %collective-permute-start.19 = (bf16[192,512]{1,0:T(8,128)(2,1)S(1)}, bf16[192,512]{1,0:T(8,128)(2,1)S(1)}, u32[]{:S(2)}, u32[]{:S(2)}) collective-permute-start(bf16[192,512]{1,0:T(8,128)(2,1)S(1)} %bitcast.131), channel_id=1, source_target_pairs={{0,2},{1,0},{2,6},{3,4},{4,3},{5,1},{6,7},{7,5},{8,10},{9,8},{10,1... | collective-permute-start | bytes 589832 | tf_op jit(solution)/shard_map/ppermute | solution.py:600
  149.4 14.0 %collective-permute-start.20 = (bf16[192,512]{1,0:T(8,128)(2,1)S(1)}, bf16[192,512]{1,0:T(8,128)(2,1)S(1)}, u32[]{:S(2)}, u32[]{:S(2)}) collective-permute-start(bf16[192,512]{1,0:T(8,128)(2,1)S(1)} %bitcast.130), channel_id=1, source_target_pairs={{0,3},{1,1},{2,7},{3,5},{4,0},{5,2},{6,4},{7,6},{8,11},{9,9},{10,1... | collective-permute-start | bytes 589832 | tf_op jit(solution)/shard_map/ppermute | solution.py:600
  190.0 168.9 %reduce-scatter.5.cloned.1.call-start = ((), (), s32[]{:S(2)}) async-start(), calls=%async_computation.3 | async-start | bytes 1720320 | tf_op jit(solution)/shard_map/reduce_scatter | solution.py:613
  190.8 12.9 %collective-permute-start.21 = (bf16[192,512]{1,0:T(8,128)(2,1)}, bf16[192,512]{1,0:T(8,128)(2,1)S(1)}, u32[]{:S(2)}, u32[]{:S(2)}) collective-permute-start(bf16[192,512]{1,0:T(8,128)(2,1)} %get-tuple-element.50), channel_id=1, source_target_pairs={{0,0},{2,1},{4,2},{6,3},{1,4},{3,5},{5,6},{7,7},{8,8},{10,9},{12,1... | collective-permute-start | bytes 589832 | tf_op jit(solution)/shard_map/ppermute | solution.py:609
  192.7 11.0 %collective-permute-start.22 = (bf16[192,512]{1,0:T(8,128)(2,1)}, bf16[192,512]{1,0:T(8,128)(2,1)S(1)}, u32[]{:S(2)}, u32[]{:S(2)}) collective-permute-start(bf16[192,512]{1,0:T(8,128)(2,1)} %get-tuple-element.51), channel_id=1, source_target_pairs={{1,0},{3,1},{5,2},{7,3},{2,4},{0,5},{6,6},{4,7},{9,8},{11,9},{13,1... | collective-permute-start | bytes 589832 | tf_op jit(solution)/shard_map/ppermute | solution.py:609
  197.4 15.2 %collective-permute-start.24 = (bf16[192,512]{1,0:T(8,128)(2,1)}, bf16[192,512]{1,0:T(8,128)(2,1)S(1)}, u32[]{:S(2)}, u32[]{:S(2)}) collective-permute-start(bf16[192,512]{1,0:T(8,128)(2,1)} %get-tuple-element.53), channel_id=1, source_target_pairs={{3,0},{1,1},{7,2},{5,3},{0,4},{2,5},{4,6},{6,7},{11,8},{9,9},{15,1... | collective-permute-start | bytes 589832 | tf_op jit(solution)/shard_map/ppermute | solution.py:609
  276.4 10.6 %collective-permute-start.30 = (f32[1920]{0:T(1024)S(1)}, f32[1920]{0:T(1024)S(1)}, u32[]{:S(2)}, u32[]{:S(2)}) collective-permute-start(f32[1920]{0:T(1024)S(1)} %pad_maximum_fusion.2), channel_id=1, source_target_pairs={{0,4},{4,0},{1,5},{5,1},{2,6},{6,2},{3,7},{7,3},{8,12},{12,8},{9,1... | collective-permute-start | bytes 23048 | tf_op jit(solution)/shard_map/ppermute | solution.py:642
  283.4 16.8 %collective-permute-start.29 = (bf16[2,96,576]{2,1,0:T(8,128)(2,1)S(1)}, bf16[2,96,576]{2,1,0:T(8,128)(2,1)S(1)}, u32[]{:S(2)}, u32[]{:S(2)}) collective-permute-start(bf16[2,96,576]{2,1,0:T(8,128)(2,1)S(1)} %slice_bitcast_fusion.2), channel_id=1, source_target_pairs={{0,16},{8,24},{16,0},{24,8},{1,17},{9,25},{17,1},{25,9},{2,18},{10... | collective-permute-start | bytes 663560 | tf_op jit(solution)/shard_map/ppermute | solution.py:516
  285.6 15.4 %collective-permute-start.33 = (bf16[512,768]{1,0:T(8,128)(2,1)S(1)}, bf16[512,768]{1,0:T(8,128)(2,1)S(1)}, u32[]{:S(2)}, u32[]{:S(2)}) collective-permute-start(bf16[512,768]{1,0:T(8,128)(2,1)S(1)} %convolution_convert_fusion), channel_id=1, source_target_pairs={{0,4},{4,0},{1,5},{5,1},{2,6},{6,2},{3,7},{7,3},{8,12},{12,8},{9,1... | collective-permute-start | bytes 2359304 | tf_op jit(solution)/shard_map/ppermute | solution.py:567
  286.2 14.2 %collective-permute-start.27 = (bf16[512,768]{1,0:T(8,128)(2,1)S(1)}, bf16[512,768]{1,0:T(8,128)(2,1)S(1)}, u32[]{:S(2)}, u32[]{:S(2)}) collective-permute-start(bf16[512,768]{1,0:T(8,128)(2,1)S(1)} %add.161), channel_id=1, source_target_pairs={{0,1},{1,0},{7,6},{6,7},{8,9},{9,8},{15,14},{14,15},{16,17},{17,16... | collective-permute-start | bytes 2359304 | tf_op jit(solution)/shard_map/ppermute | solution.py:645
  287.1 13.2 %collective-permute-start.28 = (bf16[2,96,576]{2,1,0:T(8,128)(2,1)S(1)}, bf16[2,96,576]{2,1,0:T(8,128)(2,1)S(1)}, u32[]{:S(2)}, u32[]{:S(2)}) collective-permute-start(bf16[2,96,576]{2,1,0:T(8,128)(2,1)S(1)} %slice.136), channel_id=1, source_target_pairs={{0,8},{8,0},{16,24},{24,16},{1,9},{9,1},{17,25},{25,17},{2,10},{10... | collective-permute-start | bytes 663560 | tf_op jit(solution)/shard_map/ppermute | solution.py:516
  289.8 32.3 %collective-permute-start.32 = (bf16[512,768]{1,0:T(8,128)(2,1)S(1)}, bf16[512,768]{1,0:T(8,128)(2,1)}, u32[]{:S(2)}, u32[]{:S(2)}) collective-permute-start(bf16[512,768]{1,0:T(8,128)(2,1)S(1)} %convolution_convert_fusion.1), channel_id=1, source_target_pairs={{0,4},{4,0},{1,5},{5,1},{2,6},{6,2},{3,7},{7,3},{8,12},{12,8},{9,1... | collective-permute-start | bytes 2359304 | tf_op jit(solution)/shard_map/ppermute | solution.py:567
  300.3 37.7 %collective-permute-start.25 = (bf16[512,768]{1,0:T(8,128)(2,1)S(1)}, bf16[512,768]{1,0:T(8,128)(2,1)}, u32[]{:S(2)}, u32[]{:S(2)}) collective-permute-start(bf16[512,768]{1,0:T(8,128)(2,1)S(1)} %convolution_convert_fusion.3), channel_id=1, source_target_pairs={{0,4},{4,0},{1,5},{5,1},{2,6},{6,2},{3,7},{7,3},{8,12},{12,8},{9,1... | collective-permute-start | bytes 2359304 | tf_op jit(solution)/shard_map/ppermute | solution.py:567
  302.0 13.3 %collective-permute-start.34 = (bf16[512,768]{1,0:T(8,128)(2,1)}, bf16[512,768]{1,0:T(8,128)(2,1)}, u32[]{:S(2)}, u32[]{:S(2)}) collective-permute-start(bf16[512,768]{1,0:T(8,128)(2,1)} %add_select_fusion), channel_id=1, source_target_pairs={{0,1},{1,2},{6,5},{7,6},{8,9},{9,10},{14,13},{15,14},{16,17},{17,1... | collective-permute-start | bytes 2359304 | tf_op jit(solution)/shard_map/ppermute | solution.py:656
  315.4 13.9 %collective-permute-start.41 = (bf16[96,576]{1,0:T(8,128)(2,1)S(1)}, bf16[96,576]{1,0:T(8,128)(2,1)}, u32[]{:S(2)}, u32[]{:S(2)}) collective-permute-start(bf16[96,576]{1,0:T(8,128)(2,1)S(1)} %get-tuple-element.142), channel_id=1, source_target_pairs={{0,0},{1,2},{2,4},{3,6},{4,1},{5,3},{6,5},{7,7},{8,8},{9,10},{10,1... | collective-permute-start | bytes 331784 | tf_op jit(solution)/shard_map/ppermute | solution.py:668
  320.6 15.5 %collective-permute-start.42 = (bf16[96,576]{1,0:T(8,128)(2,1)S(1)}, bf16[96,576]{1,0:T(8,128)(2,1)}, u32[]{:S(2)}, u32[]{:S(2)}) collective-permute-start(bf16[96,576]{1,0:T(8,128)(2,1)S(1)} %get-tuple-element.141), channel_id=1, source_target_pairs={{0,4},{1,6},{2,0},{3,2},{4,5},{5,7},{6,1},{7,3},{8,12},{9,14},{10,... | collective-permute-start | bytes 331784 | tf_op jit(solution)/shard_map/ppermute | solution.py:669
  324.5 31.0 %collective-permute-start.39 = (bf16[512,768]{1,0:T(8,128)(2,1)}, bf16[512,768]{1,0:T(8,128)(2,1)S(1)}, u32[]{:S(2)}, u32[]{:S(2)}) collective-permute-start(bf16[512,768]{1,0:T(8,128)(2,1)} %select_add_fusion), channel_id=1, source_target_pairs={{0,1},{1,2},{2,3},{5,4},{6,5},{7,6},{8,9},{9,10},{10,11},{13,12},{... | collective-permute-start | bytes 2359304 | tf_op jit(solution)/shard_map/ppermute | solution.py:666
  (55 other events, 319.3 us)
Sparse Core Ops, SparseCore 0:
  10.2 40.0 all-gather.4
  66.2 68.5 all-gather.6
  190.1 84.2 reduce-scatter.2
  310.2 41.6 reduce-scatter.4

commit v3 on v2

v3 whole, which is shorter than its diff:
```python
import math

import jax
import jax.numpy as jnp
from jax import lax
from jax.experimental import pallas as pl
from jax.experimental.pallas import tpu as pltpu
from jax.sharding import Mesh, PartitionSpec as P

H = 12
EPSILON = 1e-06
MASKED = -1e30
TILE = 256
AHEAD = 2
BLOCKS = 8
VMEM_LIMIT = 60 * 1024 * 1024
f32, bf16 = jnp.float32, jnp.bfloat16


def dot(left, right, contract=((1,), (0,))):
    return lax.dot_general(left, right, (contract, ((), ())), preferred_element_type=f32)


def norm_forward(values, gain):
    inverse = lax.rsqrt(jnp.mean(values * values, axis=-1, keepdims=True) + EPSILON)
    scaled = values * inverse
    return scaled, inverse, (scaled * gain).astype(bf16)


def norm_backward(grad_normed, scaled, inverse, gain):
    grad_scaled = grad_normed * gain
    return inverse * (
        grad_scaled - scaled * jnp.mean(grad_scaled * scaled, axis=-1, keepdims=True)
    )


def gelu_parts(values):
    cumulative = 0.5 * (1.0 + lax.erf(values * (1.0 / math.sqrt(2.0))))
    density = jnp.exp(-0.5 * values * values) * (1.0 / math.sqrt(2.0 * math.pi))
    return values * cumulative, cumulative + values * density


def whole(shape):
    return pl.BlockSpec(shape, lambda *_: (0,) * len(shape), pipeline_mode=pl.Buffered(1))


def params():
    return pltpu.CompilerParams(vmem_limit_bytes=VMEM_LIMIT)


def cost(microseconds):
    return pl.CostEstimate(flops=microseconds * 10**9, bytes_accessed=0, transcendentals=0)


def bias_rows(bias_table, position_bucket):
    length = (position_bucket.shape[0] + 1) // 2
    bucket = jnp.concatenate([position_bucket, jnp.zeros((1,), jnp.int32)])[::-1]
    bucket = bucket[(length // TILE - 1 - AHEAD) * TILE :]
    names = jnp.arange(bias_table.shape[0], dtype=jnp.int32)
    onehot = (bucket[None, :] == names[:, None]).astype(f32)
    rows = lax.dot_general(
        bias_table, onehot, (((0,), (0,)), ((), ())), precision=lax.Precision.HIGHEST
    )
    return rows[:, None, :], bucket[None, :]


def bias_kernel(row_ref, out_ref):
    tiles = out_ref.shape[1]

    def one(place, _):
        start = pl.multiple_of((tiles - 1 - place) * TILE, TILE)
        piece = row_ref[0, :, pl.ds(start, 2 * TILE)]
        spread = jnp.broadcast_to(piece, (TILE, 2 * TILE))
        out_ref[0, place] = pltpu.roll(spread, 0, 1, stride=1, stride_axis=0)[:, TILE:]
        return 0

    lax.fori_loop(0, tiles, one, 0)


def bias_tiles(rows, length):
    heads = rows.shape[0]
    tiles = length // TILE + AHEAD
    return pl.pallas_call(
        bias_kernel,
        grid=(heads,),
        in_specs=[pl.BlockSpec((1, 1, rows.shape[2]), lambda h: (h, 0, 0))],
        out_specs=pl.BlockSpec((1, tiles, TILE, TILE), lambda h: (h, 0, 0, 0)),
        out_shape=jax.ShapeDtypeStruct((heads, tiles, TILE, TILE), f32),
        compiler_params=params(),
        cost_estimate=cost(6),
        name="bias_tiles",
    )(rows)


def spans(block_row):
    length = block_row.shape[0]
    names = jnp.arange(BLOCKS, dtype=jnp.int32)[:, None]
    upto = jnp.sum(block_row[None, :] <= names, axis=1, dtype=jnp.int32)
    end = jnp.sum(jnp.where(block_row[None, :] == names, upto[:, None], 0), axis=0, dtype=jnp.int32)
    by_tile = end.reshape(length // TILE, TILE)
    full = by_tile[:, 0] // TILE
    most = (by_tile[:, TILE - 1] + TILE - 1) // TILE
    places = jnp.arange(length // TILE, dtype=jnp.int32)[:, None]
    least = jnp.sum(most[None, :] <= places, axis=1, dtype=jnp.int32)
    clear = jnp.sum(full[None, :] <= places, axis=1, dtype=jnp.int32)
    return end.reshape(1, length), full, most, least, clear


def forward_kernel(full_ref, most_ref, slot_ref, group_ref, place_ref, *refs):
    parts, rows_in = slot_ref.shape[0], place_ref.shape[0]
    pieces, weights = refs[:parts], refs[parts : parts + rows_in]
    gain_ref, bias_ref, end_ref = refs[parts + rows_in : parts + rows_in + 3]
    rest = refs[parts + rows_in + 3 :]
    ots = rest[:parts]
    (
        lse_ref, qkv_ref, normed_ref, weight_ref,
        qt_ref, k_ref, vt_ref, bias_held, scores_ref, rows_held, bias_sem,
    ) = rest[parts:]
    heads, size, length = qt_ref.shape
    count = length // TILE
    each = count // parts
    part_length = length // parts
    query = pl.program_id(0)
    load = pltpu.make_async_copy(bias_ref, bias_held, bias_sem)

    @pl.when(query == 0)
    def _():
        load.start()
        for i, piece in enumerate(weights):
            rows = piece.shape[0]
            rows_held[pl.ds(pl.multiple_of(place_ref[i] * rows, rows), rows), :] = piece[...]
        by_columns = rows_held[...].T
        weight_ref[...] = by_columns
        for i, piece in enumerate(pieces):
            tokens = piece[...].astype(f32)
            inverse = lax.rsqrt(jnp.mean(tokens * tokens, axis=-1, keepdims=True) + EPSILON)
            normed = (tokens * inverse * gain_ref[...]).astype(bf16)
            normed_ref[i] = normed
            qkv = dot(by_columns, normed, ((1,), (1,))).astype(bf16)
            qkv = qkv.reshape(3 * heads, size, part_length)
            qkv_ref[i] = qkv
            places = pl.ds(pl.multiple_of(slot_ref[i] * part_length, TILE), part_length)
            for h in range(heads):
                qt_ref[h, :, places] = qkv[h]
                k_ref[h, places, :] = qkv[heads + h].T
                vt_ref[h, :, places] = qkv[2 * heads + h]
        load.wait()

    own = pl.ds(pl.multiple_of(query * TILE, TILE), TILE)
    queries = [qt_ref[h, :, own] for h in range(heads)]
    last = most_ref[query] - 1

    def scores(key):
        rows = pl.ds(pl.multiple_of(key * TILE, TILE), TILE)
        place = key - query + count - 1
        return [
            dot(k_ref[h, rows, :], queries[h]) + bias_held[h, place] for h in range(heads)
        ]

    def step(key, state, masked):
        slot = lax.rem(key, 2)
        ahead = scores(jnp.minimum(key + 1, last))
        current = [scores_ref[slot, h] for h in range(heads)]
        start = pl.multiple_of(key * TILE, TILE)
        if masked:
            keep = lax.broadcasted_iota(jnp.int32, (TILE, TILE), 0) + start < end_ref[...]
            current = [jnp.where(keep, tile, MASKED) for tile in current]
        tops = [
            jnp.maximum(state[h][0], jnp.max(current[h], axis=0, keepdims=True))
            for h in range(heads)
        ]
        weights = [jnp.exp(current[h] - tops[h]) for h in range(heads)]
        result = []
        for h in range(heads):
            top, total, mix = state[h]
            scale = jnp.exp(top - tops[h])
            total = total * scale + jnp.sum(weights[h], axis=0, keepdims=True)
            mix = mix * scale + dot(vt_ref[h, :, pl.ds(start, TILE)], weights[h].astype(bf16))
            result.append((tops[h], total, mix))
        for h in range(heads):
            scores_ref[1 - slot, h] = ahead[h]
        return tuple(result)

    for h, tile in enumerate(scores(0)):
        scores_ref[0, h] = tile
    state = tuple(
        (jnp.full((1, TILE), -jnp.inf, f32), jnp.zeros((1, TILE), f32), jnp.zeros((size, TILE), f32))
        for _ in range(heads)
    )
    state = lax.fori_loop(0, full_ref[query], lambda key, s: step(key, s, False), state)
    state = lax.fori_loop(full_ref[query], most_ref[query], lambda key, s: step(key, s, True), state)
    turn = lax.rem(query // each - group_ref[0] + parts, parts)
    inner = pl.ds(pl.multiple_of(lax.rem(query, each) * TILE, TILE), TILE)
    mixes = [(mix * (1.0 / total)).astype(bf16) for _, total, mix in state]
    for h, (top, total, _) in enumerate(state):
        lse_ref[h] = top + jnp.log(total)
    for r in range(parts):

        @pl.when(turn == r)
        def _():
            for h in range(heads):
                ots[r][h * size : (h + 1) * size, inner] = mixes[h]


def attend_forward(pieces, weights, places, gain, bias, end, full, most, slots, group):
    parts = len(pieces)
    part_length, width = pieces[0].shape
    columns = weights[0].shape[1]
    heads = bias.shape[0]
    size = columns // (3 * heads)
    length = parts * part_length
    smem = pl.BlockSpec(memory_space=pltpu.SMEM)
    outs = [
        *[jax.ShapeDtypeStruct((heads * size, part_length), bf16)] * parts,
        jax.ShapeDtypeStruct((heads, 1, length), f32),
        jax.ShapeDtypeStruct((parts, 3 * heads, size, part_length), bf16),
        jax.ShapeDtypeStruct((parts, part_length, width), bf16),
        jax.ShapeDtypeStruct((columns, width), bf16),
    ]
    out_specs = [whole(a.shape) for a in outs]
    out_specs[parts] = pl.BlockSpec((heads, 1, TILE), lambda i: (0, 0, i))
    return pl.pallas_call(
        forward_kernel,
        grid=(length // TILE,),
        in_specs=[smem] * 5
        + [whole(a.shape) for a in (*pieces, *weights)]
        + [
            whole((1, width)),
            pl.BlockSpec(memory_space=pl.ANY),
            pl.BlockSpec((1, TILE), lambda i: (0, i)),
        ],
        out_specs=out_specs,
        out_shape=outs,
        scratch_shapes=[
            pltpu.VMEM((heads, size, length), bf16),
            pltpu.VMEM((heads, length, size), bf16),
            pltpu.VMEM((heads, size, length), bf16),
            pltpu.VMEM(bias.shape, f32),
            pltpu.VMEM((2, heads, TILE, TILE), f32),
            pltpu.VMEM((width, columns), bf16),
            pltpu.SemaphoreType.DMA,
        ],
        compiler_params=params(),
        cost_estimate=cost(30),
        name="attend_forward",
    )(full, most, slots, group, places, *pieces, *weights, gain.reshape(1, width), bias, end)


def backward_kernel(least_ref, clear_ref, slot_ref, group_ref, place_ref, *refs):
    parts = slot_ref.shape[0]
    grads, ots = refs[:parts], refs[parts : 2 * parts]
    (
        qkv_ref, lse_ref, end_ref, normed_ref, weight_ref, gain_ref, feed_gain_ref, bucket_ref, bias_ref,
    ) = refs[2 * parts : 2 * parts + 9]
    outs = refs[2 * parts + 9 : 3 * parts + 9]
    small_ref = refs[3 * parts + 9]
    scratch = 16
    share_refs = refs[3 * parts + 10 : len(refs) - scratch]
    (
        qt_ref, kt_ref, vt_ref, got_ref, q_ref, go_ref, dqkv_ref,
        dqt_acc, dk_acc, dv_acc, delta_ref, band_ref, bias_held, sum_ref, line_ref, bias_sem,
    ) = refs[len(refs) - scratch :]
    heads, size, length = qt_ref.shape
    columns = heads * size
    count = length // TILE
    each = count // parts
    part_length = length // parts
    key = pl.program_id(0)
    key_cols = pl.ds(pl.multiple_of(key * TILE, TILE), TILE)
    load = pltpu.make_async_copy(bias_ref, bias_held, bias_sem)
    every = range(heads)

    @pl.when(key == 0)
    def _():
        load.start()
        dqt_acc[...] = jnp.zeros_like(dqt_acc)
        band_ref[...] = jnp.zeros_like(band_ref)
        for i in range(parts):
            places = pl.ds(pl.multiple_of(slot_ref[i] * part_length, TILE), part_length)
            for h in every:
                qt_ref[h, :, places] = qkv_ref[i, h]
                q_ref[h, places, :] = qkv_ref[i, h].T
                kt_ref[h, :, places] = qkv_ref[i, heads + h]
                vt_ref[h, :, places] = qkv_ref[i, 2 * heads + h]
        for turn in range(parts):
            part = lax.rem(group_ref[0] + turn, parts)
            places = pl.ds(pl.multiple_of(part * part_length, TILE), part_length)
            for h in every:
                rows = slice(h * size, (h + 1) * size)
                grad = grads[turn][rows, :]
                got_ref[h, :, places] = grad
                go_ref[h, places, :] = grad.T
                delta_ref[h, :, places] = jnp.sum(
                    ots[turn][rows, :].astype(f32) * grad.astype(f32), axis=0, keepdims=True
                )
        load.wait()

    dk_acc[...] = jnp.zeros_like(dk_acc)
    dv_acc[...] = jnp.zeros_like(dv_acc)
    kt = [kt_ref[h, :, key_cols] for h in every]
    k = [tile.T for tile in kt]
    v = [vt_ref[h, :, key_cols].T for h in every]

    def step(query, masked):
        cols = pl.ds(pl.multiple_of(query * TILE, TILE), TILE)
        place = key - query + count - 1
        scores = [dot(k[h], qt_ref[h, :, cols]) + bias_held[h, place] for h in every]
        if masked:
            keep = lax.broadcasted_iota(jnp.int32, (TILE, TILE), 0) + key * TILE < end_ref[:, cols]
            scores = [jnp.where(keep, tile, MASKED) for tile in scores]
        grad_weights = [dot(v[h], got_ref[h, :, cols]) for h in every]
        weights = [jnp.exp(scores[h] - lse_ref[h, :, cols]) for h in every]
        grad_scores = [weights[h] * (grad_weights[h] - delta_ref[h, :, cols]) for h in every]
        for h in every:
            band_ref[h, place] += grad_scores[h]
        rounded = [tile.astype(bf16) for tile in grad_scores]
        weights = [tile.astype(bf16) for tile in weights]
        for h in every:
            dv_acc[h] += dot(weights[h], go_ref[h, cols, :])
        for h in every:
            dk_acc[h] += dot(rounded[h], q_ref[h, cols, :])
        for h in every:
            dqt_acc[h, :, cols] += dot(kt[h], rounded[h])

    def edge_step(query, _):
        step(query, True)
        return 0

    def full_step(query, _):
        step(query, False)
        return 0

    lax.fori_loop(least_ref[key], clear_ref[key], edge_step, 0)
    lax.fori_loop(clear_ref[key], count, full_step, 0)
    slot = jnp.int32(0)
    for i in range(parts):
        slot = jnp.where(slot_ref[i] == key // each, i, slot)
    inner = pl.ds(pl.multiple_of(lax.rem(key, each) * TILE, TILE), TILE)
    for h in every:
        dqkv_ref[slot, columns + h * size : columns + (h + 1) * size, inner] = dk_acc[h].T.astype(bf16)
        dqkv_ref[slot, 2 * columns + h * size : 2 * columns + (h + 1) * size, inner] = (
            dv_acc[h].T.astype(bf16)
        )

    @pl.when(key == count - 1)
    def _():
        for i in range(parts):
            places = pl.ds(pl.multiple_of(slot_ref[i] * part_length, TILE), part_length)
            for h in every:
                dqkv_ref[i, h * size : (h + 1) * size, :] = dqt_acc[h, :, places].astype(bf16)
        weight = weight_ref[...]
        for i in range(parts):
            outs[i][...] = dot(dqkv_ref[i], weight, ((0,), (0,))).astype(bf16)
        total = dot(dqkv_ref[0], normed_ref[0])
        for i in range(1, parts):
            total = total + dot(dqkv_ref[i], normed_ref[i])
        sum_ref[...] = total.T
        place = 0
        for share in share_refs:
            for i in range(share.shape[0]):
                rows = share.shape[1]
                at = pl.ds(pl.multiple_of(place_ref[place] * rows, rows), rows)
                share[i] = sum_ref[at, :].astype(bf16)
                place += 1

        small_ref[...] = jnp.zeros_like(small_ref)
        gain_grad = jnp.sum(total * weight.astype(f32), axis=0, keepdims=True) / gain_ref[...]
        lanes = small_ref.shape[1]
        each_gain = weight.shape[1] // lanes
        for row in range(each_gain):
            cut = slice(row * lanes, (row + 1) * lanes)
            small_ref[row : row + 1, :] = gain_grad[:, cut]
            small_ref[each_gain + row : each_gain + row + 1, :] = feed_gain_ref[:, cut]

        line_ref[...] = jnp.zeros_like(line_ref)
        tiles = band_ref.shape[1]

        def one(pair, _):
            bands = [(place, h) for place in (2 * pair, 2 * pair + 1) for h in every]
            zero = jnp.zeros((TILE // 2, TILE // 2), f32)
            lines = []
            for place, h in bands:
                upper, lower = band_ref[h, place, : TILE // 2], band_ref[h, place, TILE // 2 :]
                lines.append(
                    jnp.concatenate([zero, zero, upper], axis=1)
                    + jnp.concatenate([zero, lower, zero], axis=1)
                )
            half = TILE // 4
            while half >= 1:
                turned = [pltpu.roll(line[half:], 2 * TILE - half, 1) for line in lines]
                lines = [line[:half] + turn for line, turn in zip(lines, turned)]
                half //= 2
            for (place, h), line in zip(bands, lines):
                start = pl.multiple_of((tiles - 1 - place) * TILE, TILE)
                line_ref[h : h + 1, pl.ds(start, 2 * TILE)] += line
            return 0

        lax.fori_loop(0, tiles // 2, one, 0)
        line = line_ref[0:8, :]
        terms = []
        for _ in range(3):
            term = line.astype(bf16)
            terms.append(term)
            line = line - term.astype(f32)
        names = lax.broadcasted_iota(jnp.int32, (lanes, line_ref.shape[1]), 0)
        onehot = jnp.where(lax.rem(names, lanes // 4) == bucket_ref[...], 1.0, 0.0).astype(bf16)
        sums = [dot(term, onehot, ((1,), (1,))) for term in terms]
        sums = sums[0] + sums[1] + sums[2]
        lane = lax.broadcasted_iota(jnp.int32, (1, lanes), 1)
        table = jnp.zeros((1, lanes), f32)
        for h in every:
            mine = (lane >= h * (lanes // 4)) & (lane < (h + 1) * (lanes // 4))
            table = jnp.where(mine, sums[h : h + 1], table)
        small_ref[pl.ds(2 * each_gain + group_ref[0], 1), :] = table


def attend_backward(
    grads, ots, qkv, lse, end, normed, weight, gain, feed_gain_grad, bucket, bias,
    least, clear, slots, group, places, shares,
):
    parts, triple, size, part_length = qkv.shape
    heads, length = triple // 3, parts * part_length
    columns, width = weight.shape
    tiles = bias.shape[1]
    smem = pl.BlockSpec(memory_space=pltpu.SMEM)
    dense = [*grads, *ots, qkv, lse, end, normed, weight, gain.reshape(1, width), feed_gain_grad, bucket]
    small = jax.ShapeDtypeStruct((2 * (width // 128) + parts, 128), f32)
    outs = [jax.ShapeDtypeStruct((part_length, width), bf16)] * parts + [small]
    outs += [jax.ShapeDtypeStruct((number, rows, columns), bf16) for number, rows in shares]
    by_columns = pltpu.VMEM((heads, size, length), bf16)
    by_rows = pltpu.VMEM((heads, length, size), bf16)
    return pl.pallas_call(
        backward_kernel,
        grid=(length // TILE,),
        in_specs=[smem] * 5
        + [whole(a.shape) for a in dense]
        + [pl.BlockSpec(memory_space=pl.ANY)],
        out_specs=[whole(a.shape) for a in outs],
        out_shape=outs,
        scratch_shapes=[by_columns] * 4
        + [by_rows] * 2
        + [
            pltpu.VMEM((parts, columns, part_length), bf16),
            pltpu.VMEM((heads, size, length), f32),
            pltpu.VMEM((heads, TILE, size), f32),
            pltpu.VMEM((heads, TILE, size), f32),
            pltpu.VMEM((heads, 1, length), f32),
            pltpu.VMEM((heads, tiles, TILE, TILE), f32),
            pltpu.VMEM(bias.shape, f32),
            pltpu.VMEM((width, columns), f32),
            pltpu.VMEM((8, bucket.shape[1]), f32),
            pltpu.SemaphoreType.DMA,
        ],
        compiler_params=params(),
        cost_estimate=cost(50),
        name="attend_backward",
    )(least, clear, slots, group, places, *dense, bias)


def middle_kernel(turn_ref, *refs):
    parts = turn_ref.shape[0]
    mixes = refs[:parts]
    x_ref, g_ref, gain_ref, weight_ref, out_ref, gh_ref, gain_grad_ref = refs[parts : parts + 7]
    gots = refs[parts + 7 : 2 * parts + 7]
    grads_ref, w_ref, grad_ref, second_ref, acc_ref, back_ref, load_sem, store_sem = refs[
        2 * parts + 7 :
    ]
    width = x_ref.shape[1]
    columns = mixes[0].shape[0]
    feed = weight_ref.shape[3] - 256
    hidden_units = feed // 2
    late, early = pl.ds(feed, 256), pl.ds(0, feed)

    def load(z, which, cols):
        return pltpu.make_async_copy(
            weight_ref.at[:, z, :, cols], w_ref.at[z, :, :, cols], load_sem.at[z, which]
        )

    def store(z, which, cols):
        return pltpu.make_async_copy(
            grad_ref.at[z, :, :, cols], grads_ref.at[:, z, :, cols], store_sem.at[z, which]
        )

    for z in range(parts):
        load(z, 0, late).start()
    for z in range(parts):
        load(z, 1, early).start()
    for z in range(parts):
        load(z, 0, late).wait()

    def output_rows(turn):
        return w_ref[turn_ref[turn], :, :, feed : feed + columns].reshape(width, columns)

    hidden = x_ref[...].astype(f32)
    for turn in range(parts):
        hidden = hidden + dot(mixes[turn][...], output_rows(turn), ((0,), (1,)))
    inverse = lax.rsqrt(jnp.mean(hidden * hidden, axis=-1, keepdims=True) + EPSILON)
    second_ref[...] = (hidden * inverse * gain_ref[...]).astype(bf16)
    acc_ref[...] = hidden
    back_ref[...] = jnp.zeros_like(back_ref)
    gh_ref[...] = hidden * inverse

    def hidden_part(z, _):
        load(z, 1, early).wait()
        inner = w_ref[z, :, :, :hidden_units].reshape(width, hidden_units)
        outer = w_ref[z, :, :, hidden_units:feed].reshape(width, hidden_units)
        second = second_ref[...]
        grad = g_ref[...]
        grad_active = dot(grad, outer).astype(bf16).astype(f32)
        active, slope = gelu_parts(dot(second, inner))
        active = active.astype(bf16)
        grad_units = (grad_active * slope).astype(bf16)
        acc_ref[...] += dot(active, outer, ((1,), (1,)))
        back_ref[...] += dot(grad_units, inner, ((1,), (1,)))
        shape = (*grad_ref.shape[1:3], hidden_units)
        grad_ref[z, :, :, :hidden_units] = (
            dot(second, grad_units, ((0,), (0,))).astype(bf16).reshape(shape)
        )
        grad_ref[z, :, :, hidden_units:feed] = (
            dot(grad, active, ((0,), (0,))).astype(bf16).reshape(shape)
        )
        store(z, 1, early).start()
        return 0

    lax.fori_loop(0, parts, hidden_part, 0)
    out_ref[...] = acc_ref[...].astype(bf16)
    scaled = gh_ref[...]
    grad_second = back_ref[...]
    gain_grad_ref[...] = jnp.sum(grad_second * scaled, axis=0, keepdims=True)
    grad_scaled = grad_second * gain_ref[...]
    grad_hidden = g_ref[...].astype(f32) + inverse * (
        grad_scaled - scaled * jnp.mean(grad_scaled * scaled, axis=-1, keepdims=True)
    )
    gh_ref[...] = grad_hidden
    rounded = grad_hidden.astype(bf16)
    for turn in range(parts):
        gots[turn][...] = dot(output_rows(turn), rounded, ((0,), (1,))).astype(bf16)
        grads = dot(rounded, mixes[turn][...], ((0,), (1,))).astype(bf16)
        grad_ref[turn_ref[turn], :, :, feed : feed + columns] = grads.reshape(
            *grad_ref.shape[1:3], columns
        )
        grad_ref[turn_ref[turn], :, :, feed + columns :] = jnp.zeros(
            (*grad_ref.shape[1:3], 256 - columns), bf16
        )
    for z in range(parts):
        store(z, 0, late).start()
    for z in range(parts):
        store(z, 0, late).wait()
        store(z, 1, early).wait()


def middle(turns, mixes, inputs, cotangent, gain, weights):
    rows, width = inputs.shape
    owners, parts, each, columns = weights.shape
    smem = pl.BlockSpec(memory_space=pltpu.SMEM)
    hbm = pl.BlockSpec(memory_space=pl.ANY)
    held = pltpu.VMEM((parts, owners, each, columns), bf16)
    dense = [*mixes, inputs, cotangent, gain.reshape(1, width)]
    outs = [
        jax.ShapeDtypeStruct((rows, width), bf16),
        jax.ShapeDtypeStruct((rows, width), f32),
        jax.ShapeDtypeStruct((1, width), f32),
        *[jax.ShapeDtypeStruct(mix.shape, bf16) for mix in mixes],
    ]
    return pl.pallas_call(
        middle_kernel,
        in_specs=[smem] + [whole(a.shape) for a in dense] + [hbm],
        out_specs=[whole(a.shape) for a in outs] + [hbm],
        out_shape=outs + [jax.ShapeDtypeStruct(weights.shape, bf16)],
        scratch_shapes=[
            held,
            held,
            pltpu.VMEM((rows, width), bf16),
            pltpu.VMEM((rows, width), f32),
            pltpu.VMEM((rows, width), f32),
            pltpu.SemaphoreType.DMA((parts, 2)),
            pltpu.SemaphoreType.DMA((parts, 2)),
        ],
        compiler_params=params(),
        cost_estimate=cost(25),
        name="middle",
    )(turns, *dense, weights)


def flat(pairs, parts):
    return [(c * parts + z, d * parts + y) for (c, z), (d, y) in pairs]


def routes(parts):
    half = parts // 2
    devices = [(c, z) for c in range(2) for z in range(parts)]

    def group(c, z):
        return (z % half) * 2 + c

    gather = [
        flat([((0, z), (0, z - 1)) for z in (1, 2, 3)] + [((1, z), (1, z + 1)) for z in (0, 1, 2)], parts),
        flat([((0, z), (0, z - 1)) for z in (1, 2)] + [((1, z), (1, z + 1)) for z in (1, 2)], parts),
        flat([((0, 1), (0, 0)), ((0, 0), (0, 1)), ((1, 2), (1, 3)), ((1, 3), (1, 2))], parts),
    ]
    rounds = [
        flat([((c, z), (z // half, (group(c, z) + r) % parts)) for c, z in devices], parts)
        for r in range(parts)
    ]
    weights = [
        flat([((z // half ^ flip, group(c, z)), (c, z)) for c, z in devices], parts)
        for flip in range(2)
    ]
    return gather, rounds, weights


def back(pairs):
    return [(target, source) for source, target in pairs]


SWAP = [(0, 1), (1, 0)]
LINE = ("core", "tensor")


def after(value, *earlier):
    return lax.optimization_barrier((value, *earlier))[0]


def across(value, step):
    return lax.ppermute(value, "plane", [(i, i ^ step) for i in range(lax.axis_size("plane"))])


def body(
    inputs,
    attention_gain,
    feedforward_gain,
    query_weight,
    key_weight,
    value_weight,
    output_weight,
    inner_weight,
    outer_weight,
    bias_table,
    block_index,
    position_bucket,
    cotangent,
):
    length = block_index.shape[1]
    parts = lax.axis_size("tensor")
    planes = lax.axis_size("plane")
    factor = 1.0 / math.sqrt(block_index.shape[0] * length * planes * 2)
    heads = bias_table.shape[1]
    buckets = bias_table.shape[0]
    width = inputs.shape[1]
    size = query_weight.shape[1] // heads
    columns = heads * size
    each = query_weight.shape[0]
    hidden_units = inner_weight.shape[1]
    core, z, plane = lax.axis_index("core"), lax.axis_index("tensor"), lax.axis_index("plane")
    half = parts // 2
    lower = z < half
    owner = core == z // half
    outer_chip = (z == 0) | (z == parts - 1)
    group = (z % half) * 2 + core
    group_ref = group.reshape(1)
    square = planes == 4 and each % 16 == 0
    gather, rounds, weight_routes = routes(parts)
    slots = jnp.array([[0, 1, 2, 3], [1, 2, 3, 0], [2, 1, 0, 3], [3, 2, 1, 0]], jnp.int32)[z]

    def swap(value):
        return lax.ppermute(value, "core", SWAP)

    pad = jnp.zeros((each, 256 - columns), bf16)
    packed_rest = jnp.concatenate([inner_weight, outer_weight.T, output_weight.T, pad], axis=1)
    line_rest = lax.all_gather(packed_rest, "tensor", axis=0)

    packed = jnp.concatenate([query_weight, key_weight, value_weight], axis=1)
    first = lax.ppermute(inputs, LINE, gather[0])
    one, two = (lax.ppermute(packed, LINE, route) for route in weight_routes)
    table = lax.ppermute(bias_table, LINE, weight_routes[0])
    block_row = jnp.where(owner, block_index, swap(block_index))[0]
    first, one, two, table, block_row = lax.optimization_barrier((first, one, two, table, block_row))
    second = lax.ppermute(first, LINE, gather[1])
    low, high = jnp.where(lower, one, two), jnp.where(lower, two, one)
    if square:
        low_x, high_y = across(low, 1), across(high, 2)
        low_y, high_x = across(low, 2), across(high, 1)
        low_xy, high_xy = across(low_x, 2), across(high_y, 1)
        weights = [low, high, low_x, high_x, low_y, high_y, low_xy, high_xy]
        order = plane ^ jnp.arange(planes, dtype=jnp.int32)
        places = jnp.stack([order * 2, order * 2 + 1], axis=1).reshape(-1)
    else:
        both = lax.all_gather(jnp.stack([low, high]), "plane", axis=0)
        weights = [both.reshape(width, 3 * columns)]
        places = jnp.zeros((1,), jnp.int32)
    rows, bucket = bias_rows(table, position_bucket)
    bias = bias_tiles(rows, length)
    second, bias, *weights = lax.optimization_barrier((second, bias, *weights))
    third = lax.ppermute(jnp.where(outer_chip, inputs, second), LINE, gather[2])
    pieces = [jnp.where(owner, piece, swap(piece)) for piece in (inputs, first, second, third)]
    all_rest = lax.all_gather(after(line_rest, second), ("plane", "core"), axis=0)

    end, full, most, least, clear = spans(block_row)

    *ots, lse, qkv, normed, weight = attend_forward(
        pieces, weights, places, attention_gain, bias, end, full, most, slots, group_ref
    )
    mixes = [lax.ppermute(ot, LINE, rounds[r]) for r, ot in enumerate(ots)]
    turns = jnp.stack([(z - r) % parts for r in range(parts)]).astype(jnp.int32)
    if each % 16:
        all_rest = jnp.swapaxes(all_rest, 0, 1).reshape(1, parts, width, -1)
    layer_output, grad_hidden, feedforward_part, *gots, grads = middle(
        turns, mixes, inputs, cotangent, feedforward_gain, all_rest
    )
    if each % 16:
        grads = jnp.swapaxes(grads.reshape(parts, planes * 2, each, -1), 0, 1)
    gots = [lax.ppermute(got, LINE, back(rounds[r])) for r, got in enumerate(gots)]

    rest = lax.psum_scatter(grads, ("plane", "core"), scatter_dimension=0)

    if square:
        order = plane ^ jnp.array([1, 3, 0, 2, 2, 3, 0, 1], jnp.int32)
        places = order * 2 + jnp.array([0, 0, 0, 0, 1, 1, 1, 1], jnp.int32)
        shares = [(2, each)] * 4
    else:
        places, shares = jnp.zeros((1,), jnp.int32), [(1, width)]
    back_outs = attend_backward(
        gots, ots, qkv, lse, end, normed, weight, attention_gain, feedforward_part, bucket, bias,
        least, clear, slots, group_ref, places, shares,
    )

    def small_step(small, axis, step):
        count = lax.axis_size(axis)
        return small + lax.ppermute(small, axis, [(i, i ^ step) for i in range(count)])

    own, first, second, third, small, *weight_grads = back_outs
    third = third + swap(third)
    got = lax.ppermute(third, LINE, back(gather[2]))
    own, first, second = (part + swap(part) for part in (own, first, second))
    none = jnp.zeros_like(own)
    if square:
        low_send, low, high_send, high = weight_grads
        low, high = low + across(low_send, 1), high + across(high_send, 2)
    else:
        attention_grads = weight_grads[0].reshape(planes, 2, each, 3 * columns)
        low = high = attention_grads
    small = small_step(small, "core", 1)
    small = small_step(small, "tensor", 1)
    got, low, high, small, rest = lax.optimization_barrier((got, low, high, small, rest))
    rest = lax.psum_scatter(rest, "tensor", scatter_dimension=0)
    own = jnp.where(owner, jnp.where(outer_chip, own + got, own), none)
    second = jnp.where(outer_chip, second, second + got)
    got = lax.ppermute(second, LINE, back(gather[1]))
    if square:
        low, high = low[0] + across(low[1], 2), high[0] + across(high[1], 1)
    else:
        shared = lax.psum_scatter(low, "plane", scatter_dimension=0)
        low, high = shared[0], shared[1]
    small = small_step(small, "tensor", 2)
    small = small_step(small, "plane", 1)
    got, low, high, small = lax.optimization_barrier((got, low, high, small))
    first = jnp.where(owner, first, none) + got
    got = lax.ppermute(first, LINE, back(gather[0]))
    attention_share = (
        lax.ppermute(jnp.where(lower, low, high), LINE, back(weight_routes[0]))
        + lax.ppermute(jnp.where(lower, high, low), LINE, back(weight_routes[1]))
    ).astype(f32) * factor
    step = 2
    while step < planes:
        small = small_step(small, "plane", step)
        step *= 2
    small = small * factor
    rest_share = rest.astype(f32) * factor
    grad_first = (own + got).astype(f32)
    scaled_first, inverse_first, _ = norm_forward(inputs.astype(f32), attention_gain)
    input_grad = (
        grad_hidden + norm_backward(grad_first, scaled_first, inverse_first, attention_gain)
    ).astype(bf16)
    gain_rows = width // 128
    table_grad = small[2 * gain_rows :, : heads * 32].reshape(parts * heads, 32)[:, :buckets].T

    return (
        layer_output,
        input_grad,
        small[:gain_rows].reshape(width),
        small[gain_rows : 2 * gain_rows].reshape(width),
        attention_share[:, :columns],
        attention_share[:, columns : 2 * columns],
        attention_share[:, 2 * columns :],
        rest_share[:, 2 * hidden_units : 2 * hidden_units + columns].T,
        rest_share[:, :hidden_units],
        rest_share[:, hidden_units : 2 * hidden_units].T,
        table_grad,
    )


def solution(mesh):
    groups, parts = mesh.devices.shape
    fine = Mesh(mesh.devices.reshape(groups // 2, 2, parts), ("plane", "core", "tensor"))
    dp = ("plane", "core")
    tokens = P(("plane", "core", "tensor"), None)
    by_rows = P(dp, "tensor")
    by_columns = P("tensor", dp)
    placed = (
        tokens, P(), P(), by_rows, by_rows, by_rows, by_columns, by_rows, by_columns,
        P(None, "tensor"), P(dp, None), P(), tokens,
    )
    results = (
        tokens, tokens, P(), P(), by_rows, by_rows, by_rows, by_columns, by_rows, by_columns, P(),
    )
    return jax.shard_map(body, mesh=fine, in_specs=placed, out_specs=results, check_vma=False)
```

time: 370 us -> 333 us (0.900)
  matrix products: 19.2 us -> 0.22 us
  Pallas kernels: 128 us -> 118 us
  waiting for transfers between devices: 84.1 us -> 75.9 us
  local copies, waits for them, and re-layouts: 20.8 us -> 15.7 us
  other arithmetic: 16.5 us -> 20.5 us
    dot_general x13 -> x0, matrix products: 18.9 us -> none  [the longest x12 17.8 us: dot(): lax.dot_general(left, right, (contract, ((), ())), preferred_element_type...]
    pallas_call x2, Pallas kernels: 95.9 us -> 85.2 us  [the longest x1 53.1 us: attend_backward(): pl.pallas_call(backward_kernel, grid=(length // TILE,), in_specs=[smem] *...]
    ppermute x1, starting transfers between devices: 3.28 us -> 12.8 us  [body(): got = lax.ppermute(first, LINE, back(gather[0]))]
    ppermute x1, waiting for transfers between devices: 6.92 us -> 0.01 us  [body(): lax.ppermute(jnp.where(lower, high, low), LINE, back(weight_routes[1]))]
    ppermute x1, waiting for transfers between devices: 17.6 us -> 12.2 us  [body(): got = lax.ppermute(first, LINE, back(gather[0]))]
    ppermute x10, waiting for transfers between devices: 8.99 us -> 3.9 us  [across(): lax.ppermute(value, 'plane', [(i, i ^ step) for i in range(lax.axis_size(...]
    ppermute x9, waiting for transfers between devices: 0.02 us -> 4.75 us  [swap(): return lax.ppermute(value, 'core', SWAP)]
    ppermute x1, waiting for transfers between devices: 2.47 us -> 6.22 us  [body(): got = lax.ppermute(second, LINE, back(gather[1]))]
  transfers between devices with their start and end apart: 47 -> 47, of which waited for: 15 -> 11; matrix products, arithmetic and copies ran while one was open for 13% -> 8% of each run, Pallas kernels for 28% -> 28%
where the time goes in v3:
time: 333 us; the launch traced here: 331 us
  Pallas kernels  118 us (35%)
  starting transfers between devices  86.7 us (26%)
  waiting for transfers between devices  75.9 us (23%)
  other arithmetic  20.5 us (6%)
  local copies, waits for them, and re-layouts  15.7 us (5%)
  between operations  14.5 us (4%)
    pallas_call x1, Pallas kernels, attend_backward(): pl.pallas_call(backward_kernel, grid=(length // TILE,), in_specs=[smem] *...  53.1 us
    pallas_call x1, Pallas kernels, attend_forward(): pl.pallas_call(forward_kernel, grid=(length // TILE,), in_specs=[smem] *...  32.1 us
    pallas_call x1, Pallas kernels, middle(): pl.pallas_call(middle_kernel, in_specs=[smem] + [whole(a.shape) for a in...  25.8 us
    ppermute x1, waiting for transfers between devices, body(): table = lax.ppermute(bias_table, LINE, weight_routes[0])  23.6 us
    ppermute x9, starting transfers between devices, swap(): return lax.ppermute(value, 'core', SWAP)  22.1 us
    ppermute x1, starting transfers between devices, body(): got = lax.ppermute(first, LINE, back(gather[0]))  12.8 us
    ppermute x1, waiting for transfers between devices, body(): got = lax.ppermute(first, LINE, back(gather[0]))  12.2 us
    ppermute x4, waiting for transfers between devices, body(): mixes = [lax.ppermute(ot, LINE, rounds[r]) for r, ot in enumerate(ots)]  11.1 us
  transfers between devices with their start and end apart: 47, of which 11 were waited for; matrix products, arithmetic and copies ran while one was open for 8% of the time, Pallas kernels for 28%

profile of v3, /device:TPU:9, one launch (start us, length us, event | category | flops | bytes accessed | tf_op | source)
XLA Modules:
  0.0 331.1 jit_solution(12162310835074482469)
XLA Ops:
  10.0 3.2 collective-permute-start
  14.2 3.2 collective-permute-start.1
  21.8 23.6 %collective-permute-done.3 = f32[32,3]{0,1:T(4,128)S(1)} collective-permute-done((f32[32,3]{0,1:T(4,128)}, f32[32,3]{0,1:T(4,128)S(1)}, u32[]{:S(2)}, u32[]{:S(2)}) %collective-permute-start.3) | collective-permute-done | bytes 416 | tf_op jit(solution)/shard_map/ppermute | solution.py:675
  48.5 5.2 %collective-permute-start.7 = (bf16[512,768]{1,0:T(8,128)(2,1)S(1)}, bf16[512,768]{1,0:T(8,128)(2,1)S(1)}, u32[]{:S(2)}, u32[]{:S(2)}) collective-permute-start(bf16[512,768]{1,0:T(8,128)(2,1)S(1)} %collective-permute-done), channel_id=1, source_target_pairs={{1,0},{2,1},{5,6},{6,7},{9,8},{10,9},{13,14},{14,15},{17,16},{18,1... | collective-permute-start | bytes 2359304 | tf_op jit(solution)/shard_map/ppermute | solution.py:678
  57.0 6.6 %bias_tiles.1.refs_13_.refs_16_ = f32[3,10,256,256]{3,2,1,0:T(8,128)} custom-call(f32[3,1,2816]{2,1,0:T(1,128)} %broadcast_in_dim.22.row_ref), custom_call_target="tpu_custom_call" | custom-call | flops 6000000000 | tf_op jit(solution)/shard_map/bias_tiles/pallas_call | solution.py:83
  65.5 3.9 %collective-permute-start.5 = (bf16[512,768]{1,0:T(8,128)(2,1)S(1)}, bf16[512,768]{1,0:T(8,128)(2,1)S(1)}, u32[]{:S(2)}, u32[]{:S(2)}) collective-permute-start(bf16[512,768]{1,0:T(8,128)(2,1)S(1)} %copy-done), channel_id=1, source_target_pairs={{0,4},{4,0},{1,5},{5,1},{2,6},{6,2},{3,7},{7,3},{8,12},{12,8},{9,1... | collective-permute-start | bytes 2359304 | tf_op jit(solution)/shard_map/ppermute | solution.py:666
  69.6 2.3 collective-permute-done.5
  72.7 2.7 broadcast_select_fusion
  78.9 9.4 %collective-permute-start.16 = (bf16[512,768]{1,0:T(8,128)(2,1)S(1)}, bf16[512,768]{1,0:T(8,128)(2,1)S(1)}, u32[]{:S(2)}, u32[]{:S(2)}) collective-permute-start(bf16[512,768]{1,0:T(8,128)(2,1)S(1)} %collective-permute-done.15), channel_id=1, source_target_pairs={{0,4},{4,0},{1,5},{5,1},{2,6},{6,2},{3,7},{7,3},{8,12},{12,8},{9,1... | collective-permute-start | bytes 2359304 | tf_op jit(solution)/shard_map/ppermute | solution.py:666
  91.2 32.1 %attend_forward.1 = (bf16[192,512]{1,0:T(8,128)(2,1)}, bf16[192,512]{1,0:T(8,128)(2,1)}, bf16[192,512]{1,0:T(8,128)(2,1)}, bf16[192,512]{1,0:T(8,128)(2,1)}, f32...) custom-call(s32[8]{0:T(128)} %get-tuple-element.185.full_ref, ...), custom_call_target="tpu_custom_call" | custom-call | flops 30000001024 | tf_op jit(solution)/shard_map/attend_forward/pallas_call | solution.py:222
  123.3 2.7 collective-permute-start.17
  128.0 2.1 collective-permute-start.19
  130.1 2.1 collective-permute-start.20
  133.5 11.1 %collective-permute-done.18.refs_1_ = bf16[192,512]{1,0:T(8,128)(2,1)S(1)} collective-permute-done((bf16[192,512]{1,0:T(8,128)(2,1)}, bf16[192,512]{1,0:T(8,128)(2,1)S(1)}, u32[]{:S(2)}, u32[]{:S(2)}) %collective-permute-start.18) | collective-permute-done | bytes 196640 | tf_op jit(solution)/shard_map/ppermute | solution.py:703
  145.4 25.8 %middle.1 = (bf16[512,768]{1,0:T(8,128)(2,1)}, f32[512,768]{1,0:T(8,128)}, f32[1,768]{1,0:T(1,128)}, bf16[192,512]{1,0:T(8,128)(2,1)}, bf16[192,512]{1,0:T(8,128...) custom-call(s32[4]{0:T(128)} %pad_add_fusion.1.turn_ref, ...), custom_call_target="tpu_custom_call" | custom-call | flops 24999999488 | tf_op jit(solution)/shard_map/middle/pallas_call | solution.py:565
  174.4 3.3 collective-permute-start.22
  179.2 4.3 %collective-permute-start.24 = (bf16[192,512]{1,0:T(8,128)(2,1)S(1)}, bf16[192,512]{1,0:T(8,128)(2,1)S(1)}, u32[]{:S(2)}, u32[]{:S(2)}) collective-permute-start(bf16[192,512]{1,0:T(8,128)(2,1)S(1)} %copy-done.23), channel_id=1, source_target_pairs={{3,0},{1,1},{7,2},{5,3},{0,4},{2,5},{4,6},{6,7},{11,8},{9,9},{15,1... | collective-permute-start | bytes 589832 | tf_op jit(solution)/shard_map/ppermute | solution.py:712
  184.7 2.3 collective-permute-done.23.refs_2_
  187.0 7.2 %collective-permute-done.24.refs_3_ = bf16[192,512]{1,0:T(8,128)(2,1)S(1)} collective-permute-done((bf16[192,512]{1,0:T(8,128)(2,1)S(1)}, bf16[192,512]{1,0:T(8,128)(2,1)S(1)}, u32[]{:S(2)}, u32[]{:S(2)}) %collective-permute-start.24) | collective-permute-done | bytes 196640 | tf_op jit(solution)/shard_map/ppermute | solution.py:712
  194.8 53.1 %attend_backward.1 = (bf16[512,768]{1,0:T(8,128)(2,1)}, bf16[512,768]{1,0:T(8,128)(2,1)}, bf16[512,768]{1,0:T(8,128)(2,1)}, bf16[512,768]{1,0:T(8,128)(2,1)}, f3...) custom-call(s32[8]{0:T(128)} %convert_reduce_fusion.2.least_ref, ...), custom_call_target="tpu_custom_call" | custom-call | flops 49999998976 | tf_op jit(solution)/shard_map/attend_backward/pallas_call | solution.py:432
  248.1 2.5 collective-permute-done.26
  259.4 6.8 %collective-permute-start.32 = (bf16[512,768]{1,0:T(8,128)(2,1)}, bf16[512,768]{1,0:T(8,128)(2,1)}, u32[]{:S(2)}, u32[]{:S(2)}) collective-permute-start(bf16[512,768]{1,0:T(8,128)(2,1)} %get-tuple-element.101), channel_id=1, source_target_pairs={{0,4},{4,0},{1,5},{5,1},{2,6},{6,2},{3,7},{7,3},{8,12},{12,8},{9,1... | collective-permute-start | bytes 2359304 | tf_op jit(solution)/shard_map/ppermute | solution.py:666
  266.8 2.4 add_select_fusion
  270.5 2.0 collective-permute-start.36
  272.6 2.8 collective-permute-done.38
  275.6 3.9 %collective-permute-done.35 = bf16[96,576]{1,0:T(8,128)(2,1)S(1)} collective-permute-done((bf16[96,576]{1,0:T(8,128)(2,1)S(1)}, bf16[96,576]{1,0:T(8,128)(2,1)S(1)}, u32[]{:S(2)}, u32[]{:S(2)}) %collective-permute-start.35) | collective-permute-done | bytes 110624 | tf_op jit(solution)/shard_map/ppermute | solution.py:625
  279.5 6.2 %collective-permute-done.34 = bf16[512,768]{1,0:T(8,128)(2,1)} collective-permute-done((bf16[512,768]{1,0:T(8,128)(2,1)}, bf16[512,768]{1,0:T(8,128)(2,1)}, u32[]{:S(2)}, u32[]{:S(2)}) %collective-permute-start.34) | collective-permute-done | bytes 786464 | tf_op jit(solution)/shard_map/ppermute | solution.py:748
  285.7 1.9 collective-permute-start.41
  288.5 2.6 select_add_fusion
  291.1 12.8 %collective-permute-start.39 = (bf16[512,768]{1,0:T(8,128)(2,1)}, bf16[512,768]{1,0:T(8,128)(2,1)}, u32[]{:S(2)}, u32[]{:S(2)}) collective-permute-start(bf16[512,768]{1,0:T(8,128)(2,1)} %select_add_fusion), channel_id=1, source_target_pairs={{0,1},{1,2},{2,3},{5,4},{6,5},{7,6},{8,9},{9,10},{10,11},{13,12},{... | collective-permute-start | bytes 2359304 | tf_op jit(solution)/shard_map/ppermute | solution.py:758
  306.1 12.2 %collective-permute-done.39 = bf16[512,768]{1,0:T(8,128)(2,1)} collective-permute-done((bf16[512,768]{1,0:T(8,128)(2,1)}, bf16[512,768]{1,0:T(8,128)(2,1)}, u32[]{:S(2)}, u32[]{:S(2)}) %collective-permute-start.39) | collective-permute-done | bytes 786464 | tf_op jit(solution)/shard_map/ppermute | solution.py:758
  318.3 2.2 fusion.2
  (202 shorter events, 52.3 us)
Async XLA Ops:
  7.2 57.7 %all-gather.5.cloned.1.call-start = ((), (), s32[]{:S(2)}) async-start(), calls=%async_computation.4 | async-start | bytes 1720320 | tf_op jit(solution)/shard_map/all_gather | solution.py:670
  10.0 134.7 %all-gather.7.cloned.1.call-start = ((), (), s32[]{:S(2)}) async-start(), calls=%async_computation.5 | async-start | bytes 12386304 | tf_op jit(solution)/shard_map/all_gather | solution.py:696
  10.0 35.4 %collective-permute-start = (bf16[512,768]{1,0:T(8,128)(2,1)}, bf16[512,768]{1,0:T(8,128)(2,1)S(1)}, u32[]{:S(2)}, u32[]{:S(2)}) collective-permute-start(bf16[512,768]{1,0:T(8,128)(2,1)} %refs_4_.1), channel_id=1, source_target_pairs={{1,0},{2,1},{3,2},{4,5},{5,6},{6,7},{9,8},{10,9},{11,10},{12,13},{... | collective-permute-start | bytes 2359304 | tf_op jit(solution)/shard_map/ppermute | solution.py:673
  14.2 31.2 %collective-permute-start.1 = (bf16[96,576]{1,0:T(8,128)(2,1)S(1)}, bf16[96,576]{1,0:T(8,128)(2,1)S(1)}, u32[]{:S(2)}, u32[]{:S(2)}) collective-permute-start(bf16[96,576]{1,0:T(8,128)(2,1)S(1)} %pad_maximum_fusion), channel_id=1, source_target_pairs={{0,0},{2,1},{4,2},{6,3},{1,4},{3,5},{5,6},{7,7},{8,8},{10,9},{12,1... | collective-permute-start | bytes 331784 | tf_op jit(solution)/shard_map/ppermute | solution.py:674
  17.5 28.0 %collective-permute-start.2 = (bf16[96,576]{1,0:T(8,128)(2,1)S(1)}, bf16[96,576]{1,0:T(8,128)(2,1)S(1)}, u32[]{:S(2)}, u32[]{:S(2)}) collective-permute-start(bf16[96,576]{1,0:T(8,128)(2,1)S(1)} %pad_maximum_fusion), channel_id=1, source_target_pairs={{4,0},{6,1},{0,2},{2,3},{5,4},{7,5},{1,6},{3,7},{12,8},{14,9},{8,1... | collective-permute-start | bytes 331784 | tf_op jit(solution)/shard_map/ppermute | solution.py:674
  19.1 26.4 %collective-permute-start.3 = (f32[32,3]{0,1:T(4,128)}, f32[32,3]{0,1:T(4,128)S(1)}, u32[]{:S(2)}, u32[]{:S(2)}) collective-permute-start(f32[32,3]{0,1:T(4,128)} %param.25), channel_id=1, source_target_pairs={{0,0},{2,1},{4,2},{6,3},{1,4},{3,5},{5,6},{7,7},{8,8},{10,9},{12,1... | collective-permute-start | bytes 1160 | tf_op jit(solution)/shard_map/ppermute | solution.py:675
  46.7 16.9 %collective-permute-start.10 = (bf16[96,576]{1,0:T(8,128)(2,1)S(1)}, bf16[96,576]{1,0:T(8,128)(2,1)S(1)}, u32[]{:S(2)}, u32[]{:S(2)}) collective-permute-start(bf16[96,576]{1,0:T(8,128)(2,1)S(1)} %get-tuple-element.67.refs_4_), channel_id=1, source_target_pairs={{0,16},{8,24},{16,0},{24,8},{1,17},{9,25},{17,1},{25,9},{2,18},{10... | collective-permute-start | bytes 331784 | tf_op jit(solution)/shard_map/ppermute | solution.py:625
  48.2 15.4 %collective-permute-start.9 = (bf16[96,576]{1,0:T(8,128)(2,1)S(1)}, bf16[96,576]{1,0:T(8,128)(2,1)S(1)}, u32[]{:S(2)}, u32[]{:S(2)}) collective-permute-start(bf16[96,576]{1,0:T(8,128)(2,1)S(1)} %get-tuple-element.68.refs_5_), channel_id=1, source_target_pairs={{0,8},{8,0},{16,24},{24,16},{1,9},{9,1},{17,25},{25,17},{2,10},{10... | collective-permute-start | bytes 331784 | tf_op jit(solution)/shard_map/ppermute | solution.py:625
  48.5 16.4 %collective-permute-start.7 = (bf16[512,768]{1,0:T(8,128)(2,1)S(1)}, bf16[512,768]{1,0:T(8,128)(2,1)S(1)}, u32[]{:S(2)}, u32[]{:S(2)}) collective-permute-start(bf16[512,768]{1,0:T(8,128)(2,1)S(1)} %collective-permute-done), channel_id=1, source_target_pairs={{1,0},{2,1},{5,6},{6,7},{9,8},{10,9},{13,14},{14,15},{17,16},{18,1... | collective-permute-start | bytes 2359304 | tf_op jit(solution)/shard_map/ppermute | solution.py:678
  65.5 200.9 %reduce-scatter.3.cloned.1.call-start = ((), (), s32[]{:S(2)}) async-start(), calls=%async_computation.2 | async-start | bytes 12386304 | tf_op jit(solution)/shard_map/reduce_scatter | solution.py:714
  76.1 13.1 %collective-permute-start.6 = (bf16[512,768]{1,0:T(8,128)(2,1)S(1)}, bf16[512,768]{1,0:T(8,128)(2,1)S(1)}, u32[]{:S(2)}, u32[]{:S(2)}) collective-permute-start(bf16[512,768]{1,0:T(8,128)(2,1)S(1)} %collective-permute-done), channel_id=1, source_target_pairs={{0,4},{4,0},{1,5},{5,1},{2,6},{6,2},{3,7},{7,3},{8,12},{12,8},{9,1... | collective-permute-start | bytes 2359304 | tf_op jit(solution)/shard_map/ppermute | solution.py:666
  78.9 11.4 %collective-permute-start.16 = (bf16[512,768]{1,0:T(8,128)(2,1)S(1)}, bf16[512,768]{1,0:T(8,128)(2,1)S(1)}, u32[]{:S(2)}, u32[]{:S(2)}) collective-permute-start(bf16[512,768]{1,0:T(8,128)(2,1)S(1)} %collective-permute-done.15), channel_id=1, source_target_pairs={{0,4},{4,0},{1,5},{5,1},{2,6},{6,2},{3,7},{7,3},{8,12},{12,8},{9,1... | collective-permute-start | bytes 2359304 | tf_op jit(solution)/shard_map/ppermute | solution.py:666
  123.3 10.1 %collective-permute-start.17 = (bf16[192,512]{1,0:T(8,128)(2,1)}, bf16[192,512]{1,0:T(8,128)(2,1)S(1)}, u32[]{:S(2)}, u32[]{:S(2)}) collective-permute-start(bf16[192,512]{1,0:T(8,128)(2,1)} %get-tuple-element.76.refs_4_), channel_id=1, source_target_pairs={{0,0},{1,2},{2,4},{3,6},{4,1},{5,3},{6,5},{7,7},{8,8},{9,10},{10,1... | collective-permute-start | bytes 589832 | tf_op jit(solution)/shard_map/ppermute | solution.py:703
  126.1 18.5 %collective-permute-start.18 = (bf16[192,512]{1,0:T(8,128)(2,1)}, bf16[192,512]{1,0:T(8,128)(2,1)S(1)}, u32[]{:S(2)}, u32[]{:S(2)}) collective-permute-start(bf16[192,512]{1,0:T(8,128)(2,1)} %get-tuple-element.77.refs_5_), channel_id=1, source_target_pairs={{0,1},{1,3},{2,5},{3,7},{4,2},{5,0},{6,6},{7,4},{8,9},{9,11},{10,1... | collective-permute-start | bytes 589832 | tf_op jit(solution)/shard_map/ppermute | solution.py:703
  128.0 16.6 %collective-permute-start.19 = (bf16[192,512]{1,0:T(8,128)(2,1)}, bf16[192,512]{1,0:T(8,128)(2,1)S(1)}, u32[]{:S(2)}, u32[]{:S(2)}) collective-permute-start(bf16[192,512]{1,0:T(8,128)(2,1)} %get-tuple-element.78.refs_6_), channel_id=1, source_target_pairs={{0,2},{1,0},{2,6},{3,4},{4,3},{5,1},{6,7},{7,5},{8,10},{9,8},{10,1... | collective-permute-start | bytes 589832 | tf_op jit(solution)/shard_map/ppermute | solution.py:703
  130.1 14.5 %collective-permute-start.20 = (bf16[192,512]{1,0:T(8,128)(2,1)}, bf16[192,512]{1,0:T(8,128)(2,1)S(1)}, u32[]{:S(2)}, u32[]{:S(2)}) collective-permute-start(bf16[192,512]{1,0:T(8,128)(2,1)} %get-tuple-element.79.refs_7_), channel_id=1, source_target_pairs={{0,3},{1,1},{2,7},{3,5},{4,0},{5,2},{6,4},{7,6},{8,11},{9,9},{10,1... | collective-permute-start | bytes 589832 | tf_op jit(solution)/shard_map/ppermute | solution.py:703
  171.3 150.6 %reduce-scatter.5.cloned.1.call-start = ((), (), s32[]{:S(2)}) async-start(), calls=%async_computation.3 | async-start | bytes 1720320 | tf_op jit(solution)/shard_map/reduce_scatter | solution.py:745
  172.5 12.2 %collective-permute-start.21 = (bf16[192,512]{1,0:T(8,128)(2,1)S(1)}, bf16[192,512]{1,0:T(8,128)(2,1)S(1)}, u32[]{:S(2)}, u32[]{:S(2)}) collective-permute-start(bf16[192,512]{1,0:T(8,128)(2,1)S(1)} %copy-done.29), channel_id=1, source_target_pairs={{0,0},{2,1},{4,2},{6,3},{1,4},{3,5},{5,6},{7,7},{8,8},{10,9},{12,1... | collective-permute-start | bytes 589832 | tf_op jit(solution)/shard_map/ppermute | solution.py:712
  174.4 10.3 %collective-permute-start.22 = (bf16[192,512]{1,0:T(8,128)(2,1)S(1)}, bf16[192,512]{1,0:T(8,128)(2,1)S(1)}, u32[]{:S(2)}, u32[]{:S(2)}) collective-permute-start(bf16[192,512]{1,0:T(8,128)(2,1)S(1)} %copy-done.27), channel_id=1, source_target_pairs={{1,0},{3,1},{5,2},{7,3},{2,4},{0,5},{6,6},{4,7},{9,8},{11,9},{13,1... | collective-permute-start | bytes 589832 | tf_op jit(solution)/shard_map/ppermute | solution.py:712
  177.7 9.3 %collective-permute-start.23 = (bf16[192,512]{1,0:T(8,128)(2,1)S(1)}, bf16[192,512]{1,0:T(8,128)(2,1)S(1)}, u32[]{:S(2)}, u32[]{:S(2)}) collective-permute-start(bf16[192,512]{1,0:T(8,128)(2,1)S(1)} %copy-done.25), channel_id=1, source_target_pairs={{2,0},{0,1},{6,2},{4,3},{3,4},{1,5},{7,6},{5,7},{10,8},{8,9},{14,1... | collective-permute-start | bytes 589832 | tf_op jit(solution)/shard_map/ppermute | solution.py:712
  179.2 15.0 %collective-permute-start.24 = (bf16[192,512]{1,0:T(8,128)(2,1)S(1)}, bf16[192,512]{1,0:T(8,128)(2,1)S(1)}, u32[]{:S(2)}, u32[]{:S(2)}) collective-permute-start(bf16[192,512]{1,0:T(8,128)(2,1)S(1)} %copy-done.23), channel_id=1, source_target_pairs={{3,0},{1,1},{7,2},{5,3},{0,4},{2,5},{4,6},{6,7},{11,8},{9,9},{15,1... | collective-permute-start | bytes 589832 | tf_op jit(solution)/shard_map/ppermute | solution.py:712
  251.9 14.5 %collective-permute-start.27 = (bf16[512,768]{1,0:T(8,128)(2,1)S(1)}, bf16[512,768]{1,0:T(8,128)(2,1)S(1)}, u32[]{:S(2)}, u32[]{:S(2)}) collective-permute-start(bf16[512,768]{1,0:T(8,128)(2,1)S(1)} %add.145), channel_id=1, source_target_pairs={{0,1},{1,0},{7,6},{6,7},{8,9},{9,8},{15,14},{14,15},{16,17},{17,16... | collective-permute-start | bytes 2359304 | tf_op jit(solution)/shard_map/ppermute | solution.py:733
  252.6 14.2 %collective-permute-start.33 = (bf16[512,768]{1,0:T(8,128)(2,1)}, bf16[512,768]{1,0:T(8,128)(2,1)}, u32[]{:S(2)}, u32[]{:S(2)}) collective-permute-start(bf16[512,768]{1,0:T(8,128)(2,1)} %get-tuple-element.102), channel_id=1, source_target_pairs={{0,4},{4,0},{1,5},{5,1},{2,6},{6,2},{3,7},{7,3},{8,12},{12,8},{9,1... | collective-permute-start | bytes 2359304 | tf_op jit(solution)/shard_map/ppermute | solution.py:666
  254.4 11.7 %collective-permute-start.29 = (bf16[2,96,576]{2,1,0:T(8,128)(2,1)S(1)}, bf16[2,96,576]{2,1,0:T(8,128)(2,1)S(1)}, u32[]{:S(2)}, u32[]{:S(2)}) collective-permute-start(bf16[2,96,576]{2,1,0:T(8,128)(2,1)S(1)} %copy-done.18), channel_id=1, source_target_pairs={{0,16},{8,24},{16,0},{24,8},{1,17},{9,25},{17,1},{25,9},{2,18},{10... | collective-permute-start | bytes 663560 | tf_op jit(solution)/shard_map/ppermute | solution.py:625
  256.1 10.2 %collective-permute-start.28 = (bf16[2,96,576]{2,1,0:T(8,128)(2,1)S(1)}, bf16[2,96,576]{2,1,0:T(8,128)(2,1)S(1)}, u32[]{:S(2)}, u32[]{:S(2)}) collective-permute-start(bf16[2,96,576]{2,1,0:T(8,128)(2,1)S(1)} %copy-done.17), channel_id=1, source_target_pairs={{0,8},{8,0},{16,24},{24,16},{1,9},{9,1},{17,25},{25,17},{2,10},{10... | collective-permute-start | bytes 663560 | tf_op jit(solution)/shard_map/ppermute | solution.py:625
  259.4 29.2 %collective-permute-start.32 = (bf16[512,768]{1,0:T(8,128)(2,1)}, bf16[512,768]{1,0:T(8,128)(2,1)}, u32[]{:S(2)}, u32[]{:S(2)}) collective-permute-start(bf16[512,768]{1,0:T(8,128)(2,1)} %get-tuple-element.101), channel_id=1, source_target_pairs={{0,4},{4,0},{1,5},{5,1},{2,6},{6,2},{3,7},{7,3},{8,12},{12,8},{9,1... | collective-permute-start | bytes 2359304 | tf_op jit(solution)/shard_map/ppermute | solution.py:666
  266.1 40.0 %collective-permute-start.25 = (bf16[512,768]{1,0:T(8,128)(2,1)S(1)}, bf16[512,768]{1,0:T(8,128)(2,1)}, u32[]{:S(2)}, u32[]{:S(2)}) collective-permute-start(bf16[512,768]{1,0:T(8,128)(2,1)S(1)} %copy-done.3), channel_id=1, source_target_pairs={{0,4},{4,0},{1,5},{5,1},{2,6},{6,2},{3,7},{7,3},{8,12},{12,8},{9,1... | collective-permute-start | bytes 2359304 | tf_op jit(solution)/shard_map/ppermute | solution.py:666
  269.2 16.6 %collective-permute-start.34 = (bf16[512,768]{1,0:T(8,128)(2,1)}, bf16[512,768]{1,0:T(8,128)(2,1)}, u32[]{:S(2)}, u32[]{:S(2)}) collective-permute-start(bf16[512,768]{1,0:T(8,128)(2,1)} %add_select_fusion), channel_id=1, source_target_pairs={{0,1},{1,2},{6,5},{7,6},{8,9},{9,10},{14,13},{15,14},{16,17},{17,1... | collective-permute-start | bytes 2359304 | tf_op jit(solution)/shard_map/ppermute | solution.py:748
  285.7 19.6 %collective-permute-start.41 = (bf16[96,576]{1,0:T(8,128)(2,1)S(1)}, bf16[96,576]{1,0:T(8,128)(2,1)S(1)}, u32[]{:S(2)}, u32[]{:S(2)}) collective-permute-start(bf16[96,576]{1,0:T(8,128)(2,1)S(1)} %get-tuple-element.179), channel_id=1, source_target_pairs={{0,0},{1,2},{2,4},{3,6},{4,1},{5,3},{6,5},{7,7},{8,8},{9,10},{10,1... | collective-permute-start | bytes 331784 | tf_op jit(solution)/shard_map/ppermute | solution.py:760
  287.7 17.6 %collective-permute-start.42 = (bf16[96,576]{1,0:T(8,128)(2,1)S(1)}, bf16[96,576]{1,0:T(8,128)(2,1)S(1)}, u32[]{:S(2)}, u32[]{:S(2)}) collective-permute-start(bf16[96,576]{1,0:T(8,128)(2,1)S(1)} %get-tuple-element.178), channel_id=1, source_target_pairs={{0,4},{1,6},{2,0},{3,2},{4,5},{5,7},{6,1},{7,3},{8,12},{9,14},{10,... | collective-permute-start | bytes 331784 | tf_op jit(solution)/shard_map/ppermute | solution.py:761
  287.7 16.3 %collective-permute-start.40 = (f32[16,128]{1,0:T(8,128)S(1)}, f32[16,128]{1,0:T(8,128)S(1)}, u32[]{:S(2)}, u32[]{:S(2)}) collective-permute-start(f32[16,128]{1,0:T(8,128)S(1)} %add.157), channel_id=1, source_target_pairs={{0,16},{8,24},{16,0},{24,8},{1,17},{9,25},{17,1},{25,9},{2,18},{10... | collective-permute-start | bytes 24584 | tf_op jit(solution)/shard_map/ppermute | solution.py:729
  291.1 27.2 %collective-permute-start.39 = (bf16[512,768]{1,0:T(8,128)(2,1)}, bf16[512,768]{1,0:T(8,128)(2,1)}, u32[]{:S(2)}, u32[]{:S(2)}) collective-permute-start(bf16[512,768]{1,0:T(8,128)(2,1)} %select_add_fusion), channel_id=1, source_target_pairs={{0,1},{1,2},{2,3},{5,4},{6,5},{7,6},{8,9},{9,10},{10,11},{13,12},{... | collective-permute-start | bytes 2359304 | tf_op jit(solution)/shard_map/ppermute | solution.py:758
  (52 other events, 382.0 us)
Sparse Core Ops, SparseCore 0:
  10.2 39.6 all-gather.4
  65.0 68.4 all-gather.6
  171.4 82.9 reduce-scatter.2
  272.7 37.3 reduce-scatter.4

commit v4 on v3

--- a/solution.py
+++ b/solution.py
@@ -113,7 +113,7 @@
     rest = refs[parts + rows_in + 3 :]
     ots = rest[:parts]
     (
-        lse_ref, qkv_ref, normed_ref, weight_ref,
+        lse_ref, qkv_ref, normed_ref, weight_ref, own_ref,
         qt_ref, k_ref, vt_ref, bias_held, scores_ref, rows_held, bias_sem,
     ) = rest[parts:]
     heads, size, length = qt_ref.shape
@@ -132,6 +132,10 @@
         by_columns = rows_held[...].T
         weight_ref[...] = by_columns
         for i, piece in enumerate(pieces):
+            @pl.when(slot_ref[i] == group_ref[0])
+            def _():
+                own_ref[...] = piece[...]
+
             tokens = piece[...].astype(f32)
             inverse = lax.rsqrt(jnp.mean(tokens * tokens, axis=-1, keepdims=True) + EPSILON)
             normed = (tokens * inverse * gain_ref[...]).astype(bf16)
@@ -189,7 +193,7 @@
     )
     state = lax.fori_loop(0, full_ref[query], lambda key, s: step(key, s, False), state)
     state = lax.fori_loop(full_ref[query], most_ref[query], lambda key, s: step(key, s, True), state)
-    turn = lax.rem(query // each - group_ref[0] + parts, parts)
+    turn = (query // each) ^ group_ref[0]
     inner = pl.ds(pl.multiple_of(lax.rem(query, each) * TILE, TILE), TILE)
     mixes = [(mix * (1.0 / total)).astype(bf16) for _, total, mix in state]
     for h, (top, total, _) in enumerate(state):
@@ -216,6 +220,7 @@
         jax.ShapeDtypeStruct((parts, 3 * heads, size, part_length), bf16),
         jax.ShapeDtypeStruct((parts, part_length, width), bf16),
         jax.ShapeDtypeStruct((columns, width), bf16),
+        jax.ShapeDtypeStruct((part_length, width), bf16),
     ]
     out_specs = [whole(a.shape) for a in outs]
     out_specs[parts] = pl.BlockSpec((heads, 1, TILE), lambda i: (0, 0, i))
@@ -283,7 +288,7 @@
                 kt_ref[h, :, places] = qkv_ref[i, heads + h]
                 vt_ref[h, :, places] = qkv_ref[i, 2 * heads + h]
         for turn in range(parts):
-            part = lax.rem(group_ref[0] + turn, parts)
+            part = group_ref[0] ^ turn
             places = pl.ds(pl.multiple_of(part * part_length, TILE), part_length)
             for h in every:
                 rows = slice(h * size, (h + 1) * size)
@@ -460,11 +465,11 @@
 def middle_kernel(turn_ref, *refs):
     parts = turn_ref.shape[0]
     mixes = refs[:parts]
-    x_ref, g_ref, gain_ref, weight_ref, out_ref, gh_ref, gain_grad_ref = refs[parts : parts + 7]
-    gots = refs[parts + 7 : 2 * parts + 7]
-    grads_ref, w_ref, grad_ref, second_ref, acc_ref, back_ref, load_sem, store_sem = refs[
-        2 * parts + 7 :
-    ]
+    x_ref, g_ref, gain_ref, weight_ref, out_ref, gain_grad_ref = refs[parts : parts + 6]
+    gots = refs[parts + 6 : 2 * parts + 6]
+    (
+        grads_ref, w_ref, grad_ref, second_ref, acc_ref, back_ref, gh_ref, load_sem, store_sem,
+    ) = refs[2 * parts + 6 :]
     width = x_ref.shape[1]
     columns = mixes[0].shape[0]
     feed = weight_ref.shape[3] - 256
@@ -523,7 +528,7 @@
         return 0
 
     lax.fori_loop(0, parts, hidden_part, 0)
-    out_ref[...] = acc_ref[...].astype(bf16)
+    out_ref[0] = acc_ref[...].astype(bf16)
     scaled = gh_ref[...]
     grad_second = back_ref[...]
     gain_grad_ref[...] = jnp.sum(grad_second * scaled, axis=0, keepdims=True)
@@ -531,8 +536,8 @@
     grad_hidden = g_ref[...].astype(f32) + inverse * (
         grad_scaled - scaled * jnp.mean(grad_scaled * scaled, axis=-1, keepdims=True)
     )
-    gh_ref[...] = grad_hidden
     rounded = grad_hidden.astype(bf16)
+    out_ref[1] = rounded
     for turn in range(parts):
         gots[turn][...] = dot(output_rows(turn), rounded, ((0,), (1,))).astype(bf16)
         grads = dot(rounded, mixes[turn][...], ((0,), (1,))).astype(bf16)
@@ -557,8 +562,7 @@
     held = pltpu.VMEM((parts, owners, each, columns), bf16)
     dense = [*mixes, inputs, cotangent, gain.reshape(1, width)]
     outs = [
-        jax.ShapeDtypeStruct((rows, width), bf16),
-        jax.ShapeDtypeStruct((rows, width), f32),
+        jax.ShapeDtypeStruct((2, rows, width), bf16),
         jax.ShapeDtypeStruct((1, width), f32),
         *[jax.ShapeDtypeStruct(mix.shape, bf16) for mix in mixes],
     ]
@@ -573,11 +577,11 @@
             pltpu.VMEM((rows, width), bf16),
             pltpu.VMEM((rows, width), f32),
             pltpu.VMEM((rows, width), f32),
+            pltpu.VMEM((rows, width), f32),
             pltpu.SemaphoreType.DMA((parts, 2)),
             pltpu.SemaphoreType.DMA((parts, 2)),
         ],
         compiler_params=params(),
-        cost_estimate=cost(25),
         name="middle",
     )(turns, *dense, weights)
 
@@ -599,14 +603,15 @@
         flat([((0, 1), (0, 0)), ((0, 0), (0, 1)), ((1, 2), (1, 3)), ((1, 3), (1, 2))], parts),
     ]
     rounds = [
-        flat([((c, z), (z // half, (group(c, z) + r) % parts)) for c, z in devices], parts)
+        flat([((c, z), (c ^ (r % half), z ^ (r // half))) for c, z in devices], parts)
         for r in range(parts)
     ]
+    owners = flat([((c, z), (z // half, group(c, z))) for c, z in devices], parts)
     weights = [
         flat([((z // half ^ flip, group(c, z)), (c, z)) for c, z in devices], parts)
         for flip in range(2)
     ]
-    return gather, rounds, weights
+    return gather, rounds, owners, weights
 
 
 def back(pairs):
@@ -659,7 +664,7 @@
     group = (z % half) * 2 + core
     group_ref = group.reshape(1)
     square = planes == 4 and each % 16 == 0
-    gather, rounds, weight_routes = routes(parts)
+    gather, rounds, owners, weight_routes = routes(parts)
     slots = jnp.array([[0, 1, 2, 3], [1, 2, 3, 0], [2, 1, 0, 3], [3, 2, 1, 0]], jnp.int32)[z]
 
     def swap(value):
@@ -667,15 +672,20 @@
 
     pad = jnp.zeros((each, 256 - columns), bf16)
     packed_rest = jnp.concatenate([inner_weight, outer_weight.T, output_weight.T, pad], axis=1)
-    line_rest = lax.all_gather(packed_rest, "tensor", axis=0)
 
     packed = jnp.concatenate([query_weight, key_weight, value_weight], axis=1)
     first = lax.ppermute(inputs, LINE, gather[0])
-    one, two = (lax.ppermute(packed, LINE, route) for route in weight_routes)
     table = lax.ppermute(bias_table, LINE, weight_routes[0])
     block_row = jnp.where(owner, block_index, swap(block_index))[0]
-    first, one, two, table, block_row = lax.optimization_barrier((first, one, two, table, block_row))
+    first, table, block_row, packed, packed_rest = lax.optimization_barrier(
+        (first, table, block_row, packed, packed_rest)
+    )
+    one, two = (lax.ppermute(packed, LINE, route) for route in weight_routes)
+    line_rest = lax.all_gather(packed_rest, "tensor", axis=0)
     second = lax.ppermute(first, LINE, gather[1])
+    rows, bucket = bias_rows(table, position_bucket)
+    bias = bias_tiles(rows, length)
+    one, two = after((one, two), bias)
     low, high = jnp.where(lower, one, two), jnp.where(lower, two, one)
     if square:
         low_x, high_y = across(low, 1), across(high, 2)
@@ -688,28 +698,30 @@
         both = lax.all_gather(jnp.stack([low, high]), "plane", axis=0)
         weights = [both.reshape(width, 3 * columns)]
         places = jnp.zeros((1,), jnp.int32)
-    rows, bucket = bias_rows(table, position_bucket)
-    bias = bias_tiles(rows, length)
-    second, bias, *weights = lax.optimization_barrier((second, bias, *weights))
+    second, *weights = lax.optimization_barrier((second, *weights))
     third = lax.ppermute(jnp.where(outer_chip, inputs, second), LINE, gather[2])
     pieces = [jnp.where(owner, piece, swap(piece)) for piece in (inputs, first, second, third)]
     all_rest = lax.all_gather(after(line_rest, second), ("plane", "core"), axis=0)
 
     end, full, most, least, clear = spans(block_row)
 
-    *ots, lse, qkv, normed, weight = attend_forward(
+    grad = lax.ppermute(after(cotangent, third), LINE, back(owners))
+    *ots, lse, qkv, normed, weight, own_tokens = attend_forward(
         pieces, weights, places, attention_gain, bias, end, full, most, slots, group_ref
     )
-    mixes = [lax.ppermute(ot, LINE, rounds[r]) for r, ot in enumerate(ots)]
-    turns = jnp.stack([(z - r) % parts for r in range(parts)]).astype(jnp.int32)
+    mixes = [ots[0]] + [lax.ppermute(ots[r], LINE, rounds[r]) for r in range(1, parts)]
+    turns = (group ^ jnp.arange(parts)).astype(jnp.int32)
     if each % 16:
         all_rest = jnp.swapaxes(all_rest, 0, 1).reshape(1, parts, width, -1)
-    layer_output, grad_hidden, feedforward_part, *gots, grads = middle(
-        turns, mixes, inputs, cotangent, feedforward_gain, all_rest
+    results, feedforward_part, *gots, grads = middle(
+        turns, mixes, own_tokens, grad, feedforward_gain, all_rest
     )
     if each % 16:
         grads = jnp.swapaxes(grads.reshape(parts, planes * 2, each, -1), 0, 1)
-    gots = [lax.ppermute(got, LINE, back(rounds[r])) for r, got in enumerate(gots)]
+    gots = [gots[0]] + [lax.ppermute(gots[r], LINE, rounds[r]) for r in range(1, parts)]
+    gots, results = lax.optimization_barrier((gots, results))
+    results = lax.ppermute(results, LINE, owners)
+    layer_output, grad_hidden = results[0], results[1].astype(f32)
 
     rest = lax.psum_scatter(grads, ("plane", "core"), scatter_dimension=0)
 

time: 333 us -> 323 us (0.970)
  starting transfers between devices: 86.7 us -> 71.3 us
  other arithmetic: 20.5 us -> 24.6 us
    ppermute x1, waiting for transfers between devices: 23.6 us -> 4.9 us  [body(): table = lax.ppermute(bias_table, LINE, weight_routes[0])]
    ppermute x1, waiting for transfers between devices: 0.01 us -> 16 us  [body(): second = lax.ppermute(first, LINE, gather[1])]
    ppermute x1, starting transfers between devices: 12.8 us -> 3.28 us  [body(): got = lax.ppermute(first, LINE, back(gather[0]))]
    ppermute x10, waiting for transfers between devices: 3.9 us -> 12.4 us  [across(): lax.ppermute(value, 'plane', [(i, i ^ step) for i in range(lax.axis_size(...]
    ppermute x8, starting transfers between devices: 19.7 us -> 11.5 us  [the longest x1 5.08 us: body(): results = lax.ppermute(results, LINE, owners)]
    ppermute x1, waiting for transfers between devices: 0.01 us -> 7.78 us  [body(): lax.ppermute(jnp.where(lower, high, low), LINE, back(weight_routes[1]))]
    ppermute x8, waiting for transfers between devices: 20.6 us -> 15.4 us  [the longest x3 7.87 us: body(): lax.ppermute(ots[r], LINE, rounds[r])]
    ppermute x1, waiting for transfers between devices: 6.22 us -> 1.18 us  [body(): got = lax.ppermute(second, LINE, back(gather[1]))]
  transfers between devices with their start and end apart: 47 -> 47, of which waited for: 11 -> 21; matrix products, arithmetic and copies ran while one was open for 8% -> 11% of each run, Pallas kernels for 28% -> 29%
where the time goes in v4:
time: 323 us; the launch traced here: 322 us
  Pallas kernels  118 us (37%)
  waiting for transfers between devices  79 us (24%)
  starting transfers between devices  71.3 us (22%)
  other arithmetic  24.6 us (8%)
  local copies, waits for them, and re-layouts  14.5 us (4%)
  between operations  14.4 us (4%)
    pallas_call x1, Pallas kernels, attend_backward(): pl.pallas_call(backward_kernel, grid=(length // TILE,), in_specs=[smem] *...  54.6 us
    pallas_call x1, Pallas kernels, attend_forward(): pl.pallas_call(forward_kernel, grid=(length // TILE,), in_specs=[smem] *...  30.9 us
    pallas_call x1, Pallas kernels, middle(): pl.pallas_call(middle_kernel, in_specs=[smem] + [whole(a.shape) for a in...  25.6 us
    ppermute x9, starting transfers between devices, swap(): return lax.ppermute(value, 'core', SWAP)  20.3 us
    ppermute x1, waiting for transfers between devices, body(): second = lax.ppermute(first, LINE, gather[1])  16 us
    ppermute x10, waiting for transfers between devices, across(): lax.ppermute(value, 'plane', [(i, i ^ step) for i in range(lax.axis_size(...  12.4 us
    ppermute x1, waiting for transfers between devices, body(): got = lax.ppermute(first, LINE, back(gather[0]))  11.7 us
    ppermute x10, starting transfers between devices, across(): lax.ppermute(value, 'plane', [(i, i ^ step) for i in range(lax.axis_size(...  10.6 us
  transfers between devices with their start and end apart: 47, of which 21 were waited for; matrix products, arithmetic and copies ran while one was open for 11% of the time, Pallas kernels for 29%

profile of v4, /device:TPU:9, one launch (start us, length us, event | category | flops | bytes accessed | tf_op | source)
XLA Modules:
  0.0 321.8 jit_solution(16916697356209675085)
XLA Ops:
  7.2 3.2 collective-permute-start
  10.5 3.2 collective-permute-start.1
  17.4 4.9 %collective-permute-done.1 = f32[32,3]{0,1:T(4,128)S(1)} collective-permute-done((f32[32,3]{0,1:T(4,128)}, f32[32,3]{0,1:T(4,128)S(1)}, u32[]{:S(2)}, u32[]{:S(2)}) %collective-permute-start.1) | collective-permute-done | bytes 416 | tf_op jit(solution)/shard_map/ppermute | solution.py:678
  25.1 2.1 collective-permute-start.7
  29.4 6.6 %bias_tiles.1.refs_13_.refs_16_ = f32[3,10,256,256]{3,2,1,0:T(8,128)} custom-call(f32[3,1,2816]{2,1,0:T(1,128)} %broadcast_in_dim.23.row_ref), custom_call_target="tpu_custom_call" | custom-call | flops 6000000000 | tf_op jit(solution)/shard_map/bias_tiles/pallas_call | solution.py:83
  43.2 2.1 collective-permute-done.12.refs_10_
  45.8 16.0 %collective-permute-done.5 = bf16[512,768]{1,0:T(8,128)(2,1)S(1)} collective-permute-done((bf16[512,768]{1,0:T(8,128)(2,1)S(1)}, bf16[512,768]{1,0:T(8,128)(2,1)S(1)}, u32[]{:S(2)}, u32[]{:S(2)}) %collective-permute-start.5) | collective-permute-done | bytes 786464 | tf_op jit(solution)/shard_map/ppermute | solution.py:685
  64.0 2.2 collective-permute-done.3
  67.0 2.6 broadcast_select_fusion
  73.5 9.5 %collective-permute-start.16 = (bf16[512,768]{1,0:T(8,128)(2,1)S(1)}, bf16[512,768]{1,0:T(8,128)(2,1)}, u32[]{:S(2)}, u32[]{:S(2)}) collective-permute-start(bf16[512,768]{1,0:T(8,128)(2,1)S(1)} %collective-permute-done.15), channel_id=1, source_target_pairs={{0,4},{4,0},{1,5},{5,1},{2,6},{6,2},{3,7},{7,3},{8,12},{12,8},{9,1... | collective-permute-start | bytes 2359304 | tf_op jit(solution)/shard_map/ppermute | solution.py:671
  85.0 2.1 collective-permute-start.20
  87.1 2.2 broadcast_select_fusion.1.refs_3_
  89.3 30.9 %attend_forward.1 = (bf16[192,512]{1,0:T(8,128)(2,1)}, bf16[192,512]{1,0:T(8,128)(2,1)}, bf16[192,512]{1,0:T(8,128)(2,1)}, bf16[192,512]{1,0:T(8,128)(2,1)}, f32...) custom-call(s32[8]{0:T(128)} %get-tuple-element.199.full_ref, ...), custom_call_target="tpu_custom_call" | custom-call | flops 30000001024 | tf_op jit(solution)/shard_map/attend_forward/pallas_call | solution.py:227
  123.6 3.1 collective-permute-done.18.refs_2_
  126.7 4.8 %collective-permute-done.19.refs_3_ = bf16[192,512]{1,0:T(8,128)(2,1)S(1)} collective-permute-done((bf16[192,512]{1,0:T(8,128)(2,1)}, bf16[192,512]{1,0:T(8,128)(2,1)S(1)}, u32[]{:S(2)}, u32[]{:S(2)}) %collective-permute-start.19) | collective-permute-done | bytes 196640 | tf_op jit(solution)/shard_map/ppermute | solution.py:712
  132.1 25.6 %middle.1 = (bf16[2,512,768]{2,1,0:T(8,128)(2,1)}, f32[1,768]{1,0:T(1,128)}, bf16[192,512]{1,0:T(8,128)(2,1)}, bf16[192,512]{1,0:T(8,128)(2,1)}, bf16[192,512]{1...) custom-call(s32[4]{0:T(128)} %iota_xor_fusion.turn_ref, ...), custom_call_target="tpu_custom_call" | custom-call | tf_op jit(solution)/shard_map/middle/pallas_call | solution.py:569
  162.7 2.7 collective-permute-done.22.refs_2_
  165.4 4.8 %collective-permute-done.23.refs_3_ = bf16[192,512]{1,0:T(8,128)(2,1)S(1)} collective-permute-done((bf16[192,512]{1,0:T(8,128)(2,1)S(1)}, bf16[192,512]{1,0:T(8,128)(2,1)S(1)}, u32[]{:S(2)}, u32[]{:S(2)}) %collective-permute-start.23) | collective-permute-done | bytes 196640 | tf_op jit(solution)/shard_map/ppermute | solution.py:721
  170.2 5.1 %collective-permute-start.24 = (bf16[2,512,768]{2,1,0:T(8,128)(2,1)}, bf16[2,512,768]{2,1,0:T(8,128)(2,1)S(1)}, u32[]{:S(2)}, u32[]{:S(2)}) collective-permute-start(bf16[2,512,768]{2,1,0:T(8,128)(2,1)} %get-tuple-element.96), channel_id=1, source_target_pairs={{0,0},{1,2},{2,4},{3,6},{4,1},{5,3},{6,5},{7,7},{8,8},{9,10},{10,1... | collective-permute-start | bytes 4718600 | tf_op jit(solution)/shard_map/ppermute | solution.py:723
  175.3 54.6 %attend_backward.1 = (bf16[512,768]{1,0:T(8,128)(2,1)}, bf16[512,768]{1,0:T(8,128)(2,1)}, bf16[512,768]{1,0:T(8,128)(2,1)}, bf16[512,768]{1,0:T(8,128)(2,1)}, f3...) custom-call(s32[8]{0:T(128)} %convert_reduce_fusion.2.least_ref, ...), custom_call_target="tpu_custom_call" | custom-call | flops 49999998976 | tf_op jit(solution)/shard_map/attend_backward/pallas_call | solution.py:437
  230.1 2.5 collective-permute-done.26
  242.5 5.3 %collective-permute-done.29 = bf16[2,96,576]{2,1,0:T(8,128)(2,1)S(1)} collective-permute-done((bf16[2,96,576]{2,1,0:T(8,128)(2,1)S(1)}, bf16[2,96,576]{2,1,0:T(8,128)(2,1)S(1)}, u32[]{:S(2)}, u32[]{:S(2)}) %collective-permute-start.29) | collective-permute-done | bytes 221216 | tf_op jit(solution)/shard_map/ppermute | solution.py:630
  249.3 5.1 %collective-permute-start.25 = (bf16[512,768]{1,0:T(8,128)(2,1)}, bf16[512,768]{1,0:T(8,128)(2,1)}, u32[]{:S(2)}, u32[]{:S(2)}) collective-permute-start(bf16[512,768]{1,0:T(8,128)(2,1)} %get-tuple-element.106), channel_id=1, source_target_pairs={{0,4},{4,0},{1,5},{5,1},{2,6},{6,2},{3,7},{7,3},{8,12},{12,8},{9,1... | collective-permute-start | bytes 2359304 | tf_op jit(solution)/shard_map/ppermute | solution.py:671
  256.1 2.5 add_select_fusion
  262.7 2.3 collective-permute-done.38
  267.0 2.8 collective-permute-done.35
  272.0 6.6 %collective-permute-start.41 = (bf16[96,576]{1,0:T(8,128)(2,1)S(1)}, bf16[96,576]{1,0:T(8,128)(2,1)S(1)}, u32[]{:S(2)}, u32[]{:S(2)}) collective-permute-start(bf16[96,576]{1,0:T(8,128)(2,1)S(1)} %get-tuple-element.193), channel_id=1, source_target_pairs={{0,0},{1,2},{2,4},{3,6},{4,1},{5,3},{6,5},{7,7},{8,8},{9,10},{10,1... | collective-permute-start | bytes 331784 | tf_op jit(solution)/shard_map/ppermute | solution.py:772
  280.2 2.6 select_add_fusion
  282.8 3.3 %collective-permute-start.39 = (bf16[512,768]{1,0:T(8,128)(2,1)}, bf16[512,768]{1,0:T(8,128)(2,1)}, u32[]{:S(2)}, u32[]{:S(2)}) collective-permute-start(bf16[512,768]{1,0:T(8,128)(2,1)} %select_add_fusion), channel_id=1, source_target_pairs={{0,1},{1,2},{2,3},{5,4},{6,5},{7,6},{8,9},{9,10},{10,11},{13,12},{... | collective-permute-start | bytes 2359304 | tf_op jit(solution)/shard_map/ppermute | solution.py:770
  287.4 7.8 %collective-permute-done.42 = bf16[96,576]{1,0:T(8,128)(2,1)} collective-permute-done((bf16[96,576]{1,0:T(8,128)(2,1)S(1)}, bf16[96,576]{1,0:T(8,128)(2,1)}, u32[]{:S(2)}, u32[]{:S(2)}) %collective-permute-start.42) | collective-permute-done | bytes 110624 | tf_op jit(solution)/shard_map/ppermute | solution.py:773
  296.9 11.7 %collective-permute-done.39 = bf16[512,768]{1,0:T(8,128)(2,1)} collective-permute-done((bf16[512,768]{1,0:T(8,128)(2,1)}, bf16[512,768]{1,0:T(8,128)(2,1)}, u32[]{:S(2)}, u32[]{:S(2)}) %collective-permute-start.39) | collective-permute-done | bytes 786464 | tf_op jit(solution)/shard_map/ppermute | solution.py:770
  308.7 2.5 fusion.2
  (193 shorter events, 64.1 us)
Async XLA Ops:
  7.2 54.6 %all-gather.5.cloned.1.call-start = ((), (), s32[]{:S(2)}) async-start(), calls=%async_computation.4 | async-start | bytes 1720320 | tf_op jit(solution)/shard_map/all_gather | solution.py:684
  7.2 15.1 %collective-permute-start = (bf16[512,768]{1,0:T(8,128)(2,1)}, bf16[512,768]{1,0:T(8,128)(2,1)S(1)}, u32[]{:S(2)}, u32[]{:S(2)}) collective-permute-start(bf16[512,768]{1,0:T(8,128)(2,1)} %param.16), channel_id=1, source_target_pairs={{1,0},{2,1},{3,2},{4,5},{5,6},{6,7},{9,8},{10,9},{11,10},{12,13},{... | collective-permute-start | bytes 2359304 | tf_op jit(solution)/shard_map/ppermute | solution.py:677
  10.4 7.0 %collective-permute-start.2 = (s32[1,2048]{1,0:T(1,128)}, s32[1,2048]{1,0:T(1,128)S(1)}, u32[]{:S(2)}, u32[]{:S(2)}) collective-permute-start(s32[1,2048]{1,0:T(1,128)} %param.26), channel_id=1, source_target_pairs={{0,4},{4,0},{1,5},{5,1},{2,6},{6,2},{3,7},{7,3},{8,12},{12,8},{9,1... | collective-permute-start | bytes 24584 | tf_op jit(solution)/shard_map/ppermute | solution.py:671
  10.5 11.8 %collective-permute-start.1 = (f32[32,3]{0,1:T(4,128)}, f32[32,3]{0,1:T(4,128)S(1)}, u32[]{:S(2)}, u32[]{:S(2)}) collective-permute-start(f32[32,3]{0,1:T(4,128)} %param.25), channel_id=1, source_target_pairs={{0,0},{2,1},{4,2},{6,3},{1,4},{3,5},{5,6},{7,7},{8,8},{10,9},{12,1... | collective-permute-start | bytes 1160 | tf_op jit(solution)/shard_map/ppermute | solution.py:678
  22.4 109.1 %all-gather.7.cloned.1.call-start = ((), (), s32[]{:S(2)}) async-start(), calls=%async_computation.5 | async-start | bytes 12386304 | tf_op jit(solution)/shard_map/all_gather | solution.py:704
  23.2 12.8 %collective-permute-start.6 = (bf16[96,576]{1,0:T(8,128)(2,1)S(1)}, bf16[96,576]{1,0:T(8,128)(2,1)S(1)}, u32[]{:S(2)}, u32[]{:S(2)}) collective-permute-start(bf16[96,576]{1,0:T(8,128)(2,1)S(1)} %pad_maximum_fusion), channel_id=1, source_target_pairs={{0,0},{2,1},{4,2},{6,3},{1,4},{3,5},{5,6},{7,7},{8,8},{10,9},{12,1... | collective-permute-start | bytes 331784 | tf_op jit(solution)/shard_map/ppermute | solution.py:683
  25.1 10.8 %collective-permute-start.7 = (bf16[96,576]{1,0:T(8,128)(2,1)S(1)}, bf16[96,576]{1,0:T(8,128)(2,1)S(1)}, u32[]{:S(2)}, u32[]{:S(2)}) collective-permute-start(bf16[96,576]{1,0:T(8,128)(2,1)S(1)} %pad_maximum_fusion), channel_id=1, source_target_pairs={{4,0},{6,1},{0,2},{2,3},{5,4},{7,5},{1,6},{3,7},{12,8},{14,9},{8,1... | collective-permute-start | bytes 331784 | tf_op jit(solution)/shard_map/ppermute | solution.py:683
  28.1 33.7 %collective-permute-start.5 = (bf16[512,768]{1,0:T(8,128)(2,1)S(1)}, bf16[512,768]{1,0:T(8,128)(2,1)S(1)}, u32[]{:S(2)}, u32[]{:S(2)}) collective-permute-start(bf16[512,768]{1,0:T(8,128)(2,1)S(1)} %collective-permute-done), channel_id=1, source_target_pairs={{1,0},{2,1},{5,6},{6,7},{9,8},{10,9},{13,14},{14,15},{17,16},{18,1... | collective-permute-start | bytes 2359304 | tf_op jit(solution)/shard_map/ppermute | solution.py:685
  40.2 5.1 %collective-permute-start.12 = (bf16[96,576]{1,0:T(8,128)(2,1)S(1)}, bf16[96,576]{1,0:T(8,128)(2,1)S(1)}, u32[]{:S(2)}, u32[]{:S(2)}) collective-permute-start(bf16[96,576]{1,0:T(8,128)(2,1)S(1)} %collective-permute-done.8.refs_6_), channel_id=1, source_target_pairs={{0,16},{8,24},{16,0},{24,8},{1,17},{9,25},{17,1},{25,9},{2,18},{10... | collective-permute-start | bytes 331784 | tf_op jit(solution)/shard_map/ppermute | solution.py:630
  61.9 194.2 %reduce-scatter.3.cloned.1.call-start = ((), (), s32[]{:S(2)}) async-start(), calls=%async_computation.2 | async-start | bytes 12386304 | tf_op jit(solution)/shard_map/reduce_scatter | solution.py:726
  70.4 13.6 %collective-permute-start.4 = (bf16[512,768]{1,0:T(8,128)(2,1)S(1)}, bf16[512,768]{1,0:T(8,128)(2,1)S(1)}, u32[]{:S(2)}, u32[]{:S(2)}) collective-permute-start(bf16[512,768]{1,0:T(8,128)(2,1)S(1)} %collective-permute-done), channel_id=1, source_target_pairs={{0,4},{4,0},{1,5},{5,1},{2,6},{6,2},{3,7},{7,3},{8,12},{12,8},{9,1... | collective-permute-start | bytes 2359304 | tf_op jit(solution)/shard_map/ppermute | solution.py:671
  73.5 13.7 %collective-permute-start.16 = (bf16[512,768]{1,0:T(8,128)(2,1)S(1)}, bf16[512,768]{1,0:T(8,128)(2,1)}, u32[]{:S(2)}, u32[]{:S(2)}) collective-permute-start(bf16[512,768]{1,0:T(8,128)(2,1)S(1)} %collective-permute-done.15), channel_id=1, source_target_pairs={{0,4},{4,0},{1,5},{5,1},{2,6},{6,2},{3,7},{7,3},{8,12},{12,8},{9,1... | collective-permute-start | bytes 2359304 | tf_op jit(solution)/shard_map/ppermute | solution.py:671
  85.0 38.5 %collective-permute-start.20 = (bf16[512,768]{1,0:T(8,128)(2,1)}, bf16[512,768]{1,0:T(8,128)(2,1)S(1)}, u32[]{:S(2)}, u32[]{:S(2)}) collective-permute-start(bf16[512,768]{1,0:T(8,128)(2,1)} %param.28), channel_id=1, source_target_pairs={{0,0},{2,1},{4,2},{6,3},{1,4},{3,5},{5,6},{7,7},{8,8},{10,9},{12,1... | collective-permute-start | bytes 2359304 | tf_op jit(solution)/shard_map/ppermute | solution.py:708
  120.3 6.3 %collective-permute-start.18 = (bf16[192,512]{1,0:T(8,128)(2,1)}, bf16[192,512]{1,0:T(8,128)(2,1)S(1)}, u32[]{:S(2)}, u32[]{:S(2)}) collective-permute-start(bf16[192,512]{1,0:T(8,128)(2,1)} %get-tuple-element.85.refs_6_), channel_id=1, source_target_pairs={{0,1},{1,0},{2,3},{3,2},{4,5},{5,4},{6,7},{7,6},{8,9},{9,8},{10,11... | collective-permute-start | bytes 589832 | tf_op jit(solution)/shard_map/ppermute | solution.py:712
  121.2 10.2 %collective-permute-start.19 = (bf16[192,512]{1,0:T(8,128)(2,1)}, bf16[192,512]{1,0:T(8,128)(2,1)S(1)}, u32[]{:S(2)}, u32[]{:S(2)}) collective-permute-start(bf16[192,512]{1,0:T(8,128)(2,1)} %get-tuple-element.86.refs_7_), channel_id=1, source_target_pairs={{0,5},{1,4},{2,7},{3,6},{4,1},{5,0},{6,3},{7,2},{8,13},{9,12},{10,... | collective-permute-start | bytes 589832 | tf_op jit(solution)/shard_map/ppermute | solution.py:712
  157.9 154.7 %reduce-scatter.5.cloned.1.call-start = ((), (), s32[]{:S(2)}) async-start(), calls=%async_computation.3 | async-start | bytes 1720320 | tf_op jit(solution)/shard_map/reduce_scatter | solution.py:757
  159.3 6.1 %collective-permute-start.22 = (bf16[192,512]{1,0:T(8,128)(2,1)S(1)}, bf16[192,512]{1,0:T(8,128)(2,1)S(1)}, u32[]{:S(2)}, u32[]{:S(2)}) collective-permute-start(bf16[192,512]{1,0:T(8,128)(2,1)S(1)} %copy-done.24), channel_id=1, source_target_pairs={{0,1},{1,0},{2,3},{3,2},{4,5},{5,4},{6,7},{7,6},{8,9},{9,8},{10,11... | collective-permute-start | bytes 589832 | tf_op jit(solution)/shard_map/ppermute | solution.py:721
  160.2 10.0 %collective-permute-start.23 = (bf16[192,512]{1,0:T(8,128)(2,1)S(1)}, bf16[192,512]{1,0:T(8,128)(2,1)S(1)}, u32[]{:S(2)}, u32[]{:S(2)}) collective-permute-start(bf16[192,512]{1,0:T(8,128)(2,1)S(1)} %copy-done.22), channel_id=1, source_target_pairs={{0,5},{1,4},{2,7},{3,6},{4,1},{5,0},{6,3},{7,2},{8,13},{9,12},{10,... | collective-permute-start | bytes 589832 | tf_op jit(solution)/shard_map/ppermute | solution.py:721
  170.2 84.9 %collective-permute-start.24 = (bf16[2,512,768]{2,1,0:T(8,128)(2,1)}, bf16[2,512,768]{2,1,0:T(8,128)(2,1)S(1)}, u32[]{:S(2)}, u32[]{:S(2)}) collective-permute-start(bf16[2,512,768]{2,1,0:T(8,128)(2,1)} %get-tuple-element.96), channel_id=1, source_target_pairs={{0,0},{1,2},{2,4},{3,6},{4,1},{5,3},{6,5},{7,7},{8,8},{9,10},{10,1... | collective-permute-start | bytes 4718600 | tf_op jit(solution)/shard_map/ppermute | solution.py:723
  234.0 22.1 %collective-permute-start.27 = (bf16[512,768]{1,0:T(8,128)(2,1)S(1)}, bf16[512,768]{1,0:T(8,128)(2,1)S(1)}, u32[]{:S(2)}, u32[]{:S(2)}) collective-permute-start(bf16[512,768]{1,0:T(8,128)(2,1)S(1)} %add.126), channel_id=1, source_target_pairs={{0,1},{1,0},{7,6},{6,7},{8,9},{9,8},{15,14},{14,15},{16,17},{17,16... | collective-permute-start | bytes 2359304 | tf_op jit(solution)/shard_map/ppermute | solution.py:745
  234.7 21.4 %collective-permute-start.33 = (bf16[512,768]{1,0:T(8,128)(2,1)}, bf16[512,768]{1,0:T(8,128)(2,1)}, u32[]{:S(2)}, u32[]{:S(2)}) collective-permute-start(bf16[512,768]{1,0:T(8,128)(2,1)} %get-tuple-element.116), channel_id=1, source_target_pairs={{0,4},{4,0},{1,5},{5,1},{2,6},{6,2},{3,7},{7,3},{8,12},{12,8},{9,1... | collective-permute-start | bytes 2359304 | tf_op jit(solution)/shard_map/ppermute | solution.py:671
  239.9 7.8 %collective-permute-start.29 = (bf16[2,96,576]{2,1,0:T(8,128)(2,1)S(1)}, bf16[2,96,576]{2,1,0:T(8,128)(2,1)S(1)}, u32[]{:S(2)}, u32[]{:S(2)}) collective-permute-start(bf16[2,96,576]{2,1,0:T(8,128)(2,1)S(1)} %copy-done.19), channel_id=1, source_target_pairs={{0,16},{8,24},{16,0},{24,8},{1,17},{9,25},{17,1},{25,9},{2,18},{10... | collective-permute-start | bytes 663560 | tf_op jit(solution)/shard_map/ppermute | solution.py:630
  241.9 7.3 %collective-permute-start.28 = (bf16[2,96,576]{2,1,0:T(8,128)(2,1)S(1)}, bf16[2,96,576]{2,1,0:T(8,128)(2,1)S(1)}, u32[]{:S(2)}, u32[]{:S(2)}) collective-permute-start(bf16[2,96,576]{2,1,0:T(8,128)(2,1)S(1)} %copy-done.18), channel_id=1, source_target_pairs={{0,8},{8,0},{16,24},{24,16},{1,9},{9,1},{17,25},{25,17},{2,10},{10... | collective-permute-start | bytes 663560 | tf_op jit(solution)/shard_map/ppermute | solution.py:630
  247.7 32.5 %collective-permute-start.32 = (bf16[512,768]{1,0:T(8,128)(2,1)}, bf16[512,768]{1,0:T(8,128)(2,1)}, u32[]{:S(2)}, u32[]{:S(2)}) collective-permute-start(bf16[512,768]{1,0:T(8,128)(2,1)} %get-tuple-element.115), channel_id=1, source_target_pairs={{0,4},{4,0},{1,5},{5,1},{2,6},{6,2},{3,7},{7,3},{8,12},{12,8},{9,1... | collective-permute-start | bytes 2359304 | tf_op jit(solution)/shard_map/ppermute | solution.py:671
  249.3 47.7 %collective-permute-start.25 = (bf16[512,768]{1,0:T(8,128)(2,1)}, bf16[512,768]{1,0:T(8,128)(2,1)}, u32[]{:S(2)}, u32[]{:S(2)}) collective-permute-start(bf16[512,768]{1,0:T(8,128)(2,1)} %get-tuple-element.106), channel_id=1, source_target_pairs={{0,4},{4,0},{1,5},{5,1},{2,6},{6,2},{3,7},{7,3},{8,12},{12,8},{9,1... | collective-permute-start | bytes 2359304 | tf_op jit(solution)/shard_map/ppermute | solution.py:671
  256.1 5.1 %collective-permute-start.37 = (f32[16,128]{1,0:T(8,128)S(1)}, f32[16,128]{1,0:T(8,128)S(1)}, u32[]{:S(2)}, u32[]{:S(2)}) collective-permute-start(f32[16,128]{1,0:T(8,128)S(1)} %add.130), channel_id=1, source_target_pairs={{0,2},{1,3},{2,0},{3,1},{4,6},{5,7},{6,4},{7,5},{8,10},{9,11},{10,... | collective-permute-start | bytes 24584 | tf_op jit(solution)/shard_map/ppermute | solution.py:741
  258.6 13.3 %collective-permute-start.34 = (bf16[512,768]{1,0:T(8,128)(2,1)}, bf16[512,768]{1,0:T(8,128)(2,1)}, u32[]{:S(2)}, u32[]{:S(2)}) collective-permute-start(bf16[512,768]{1,0:T(8,128)(2,1)} %add_select_fusion), channel_id=1, source_target_pairs={{0,1},{1,2},{6,5},{7,6},{8,9},{9,10},{14,13},{15,14},{16,17},{17,1... | collective-permute-start | bytes 2359304 | tf_op jit(solution)/shard_map/ppermute | solution.py:760
  260.6 6.4 %collective-permute-start.36 = (bf16[96,576]{1,0:T(8,128)(2,1)}, bf16[96,576]{1,0:T(8,128)(2,1)S(1)}, u32[]{:S(2)}, u32[]{:S(2)}) collective-permute-start(bf16[96,576]{1,0:T(8,128)(2,1)} %slice_bitcast_fusion.3), channel_id=1, source_target_pairs={{0,8},{8,0},{16,24},{24,16},{1,9},{9,1},{17,25},{25,17},{2,10},{10... | collective-permute-start | bytes 331784 | tf_op jit(solution)/shard_map/ppermute | solution.py:630
  272.0 15.4 %collective-permute-start.41 = (bf16[96,576]{1,0:T(8,128)(2,1)S(1)}, bf16[96,576]{1,0:T(8,128)(2,1)S(1)}, u32[]{:S(2)}, u32[]{:S(2)}) collective-permute-start(bf16[96,576]{1,0:T(8,128)(2,1)S(1)} %get-tuple-element.193), channel_id=1, source_target_pairs={{0,0},{1,2},{2,4},{3,6},{4,1},{5,3},{6,5},{7,7},{8,8},{9,10},{10,1... | collective-permute-start | bytes 331784 | tf_op jit(solution)/shard_map/ppermute | solution.py:772
  278.6 16.6 %collective-permute-start.42 = (bf16[96,576]{1,0:T(8,128)(2,1)S(1)}, bf16[96,576]{1,0:T(8,128)(2,1)}, u32[]{:S(2)}, u32[]{:S(2)}) collective-permute-start(bf16[96,576]{1,0:T(8,128)(2,1)S(1)} %get-tuple-element.192), channel_id=1, source_target_pairs={{0,4},{1,6},{2,0},{3,2},{4,5},{5,7},{6,1},{7,3},{8,12},{9,14},{10,... | collective-permute-start | bytes 331784 | tf_op jit(solution)/shard_map/ppermute | solution.py:773
  278.7 7.5 %collective-permute-start.40 = (f32[16,128]{1,0:T(8,128)S(1)}, f32[16,128]{1,0:T(8,128)S(1)}, u32[]{:S(2)}, u32[]{:S(2)}) collective-permute-start(f32[16,128]{1,0:T(8,128)S(1)} %add.138), channel_id=1, source_target_pairs={{0,16},{8,24},{16,0},{24,8},{1,17},{9,25},{17,1},{25,9},{2,18},{10... | collective-permute-start | bytes 24584 | tf_op jit(solution)/shard_map/ppermute | solution.py:741
  282.8 25.8 %collective-permute-start.39 = (bf16[512,768]{1,0:T(8,128)(2,1)}, bf16[512,768]{1,0:T(8,128)(2,1)}, u32[]{:S(2)}, u32[]{:S(2)}) collective-permute-start(bf16[512,768]{1,0:T(8,128)(2,1)} %select_add_fusion), channel_id=1, source_target_pairs={{0,1},{1,2},{2,3},{5,4},{6,5},{7,6},{8,9},{9,10},{10,11},{13,12},{... | collective-permute-start | bytes 2359304 | tf_op jit(solution)/shard_map/ppermute | solution.py:770
  (47 other events, 457.7 us)
Sparse Core Ops, SparseCore 0:
  22.5 36.4 all-gather.4
  61.9 66.8 all-gather.6
  158.0 85.7 reduce-scatter.2
  262.8 38.9 reduce-scatter.4

commit v5 on v4

--- a/solution.py
+++ b/solution.py
@@ -106,68 +106,30 @@
     return end.reshape(1, length), full, most, least, clear
 
 
-def forward_kernel(full_ref, most_ref, slot_ref, group_ref, place_ref, *refs):
-    parts, rows_in = slot_ref.shape[0], place_ref.shape[0]
-    pieces, weights = refs[:parts], refs[parts : parts + rows_in]
-    gain_ref, bias_ref, end_ref = refs[parts + rows_in : parts + rows_in + 3]
-    rest = refs[parts + rows_in + 3 :]
-    ots = rest[:parts]
-    (
-        lse_ref, qkv_ref, normed_ref, weight_ref, own_ref,
-        qt_ref, k_ref, vt_ref, bias_held, scores_ref, rows_held, bias_sem,
-    ) = rest[parts:]
-    heads, size, length = qt_ref.shape
-    count = length // TILE
-    each = count // parts
-    part_length = length // parts
-    query = pl.program_id(0)
-    load = pltpu.make_async_copy(bias_ref, bias_held, bias_sem)
-
-    @pl.when(query == 0)
-    def _():
-        load.start()
-        for i, piece in enumerate(weights):
-            rows = piece.shape[0]
-            rows_held[pl.ds(pl.multiple_of(place_ref[i] * rows, rows), rows), :] = piece[...]
-        by_columns = rows_held[...].T
-        weight_ref[...] = by_columns
-        for i, piece in enumerate(pieces):
-            @pl.when(slot_ref[i] == group_ref[0])
-            def _():
-                own_ref[...] = piece[...]
-
-            tokens = piece[...].astype(f32)
-            inverse = lax.rsqrt(jnp.mean(tokens * tokens, axis=-1, keepdims=True) + EPSILON)
-            normed = (tokens * inverse * gain_ref[...]).astype(bf16)
-            normed_ref[i] = normed
-            qkv = dot(by_columns, normed, ((1,), (1,))).astype(bf16)
-            qkv = qkv.reshape(3 * heads, size, part_length)
-            qkv_ref[i] = qkv
-            places = pl.ds(pl.multiple_of(slot_ref[i] * part_length, TILE), part_length)
-            for h in range(heads):
-                qt_ref[h, :, places] = qkv[h]
-                k_ref[h, places, :] = qkv[heads + h].T
-                vt_ref[h, :, places] = qkv[2 * heads + h]
-        load.wait()
-
-    own = pl.ds(pl.multiple_of(query * TILE, TILE), TILE)
-    queries = [qt_ref[h, :, own] for h in range(heads)]
-    last = most_ref[query] - 1
+def token_parts(piece, gain, by_columns, heads):
+    tokens = piece.astype(f32)
+    inverse = lax.rsqrt(jnp.mean(tokens * tokens, axis=-1, keepdims=True) + EPSILON)
+    normed = (tokens * inverse * gain).astype(bf16)
+    qkv = dot(by_columns, normed, ((1,), (1,))).astype(bf16)
+    return normed, qkv.reshape(3 * heads, -1, normed.shape[0])
+
+
+def attend_tiles(query, first, clear, last, state, end, queries, k_ref, vt_ref, bias_held, scores_ref):
+    heads = len(queries)
+    count = k_ref.shape[1] // TILE
 
     def scores(key):
         rows = pl.ds(pl.multiple_of(key * TILE, TILE), TILE)
-        place = key - query + count - 1
-        return [
-            dot(k_ref[h, rows, :], queries[h]) + bias_held[h, place] for h in range(heads)
-        ]
+        place = jnp.minimum(key - query + count - 1, bias_held.shape[1] - 1)
+        return [dot(k_ref[h, rows, :], queries[h]) + bias_held[h, place] for h in range(heads)]
 
     def step(key, state, masked):
         slot = lax.rem(key, 2)
-        ahead = scores(jnp.minimum(key + 1, last))
+        ahead = scores(jnp.minimum(key + 1, last - 1))
         current = [scores_ref[slot, h] for h in range(heads)]
         start = pl.multiple_of(key * TILE, TILE)
         if masked:
-            keep = lax.broadcasted_iota(jnp.int32, (TILE, TILE), 0) + start < end_ref[...]
+            keep = lax.broadcasted_iota(jnp.int32, (TILE, TILE), 0) + start < end
             current = [jnp.where(keep, tile, MASKED) for tile in current]
         tops = [
             jnp.maximum(state[h][0], jnp.max(current[h], axis=0, keepdims=True))
@@ -185,14 +147,122 @@
             scores_ref[1 - slot, h] = ahead[h]
         return tuple(result)
 
-    for h, tile in enumerate(scores(0)):
-        scores_ref[0, h] = tile
+    begin = jnp.minimum(first, count - 1)
+    for h, tile in enumerate(scores(begin)):
+        scores_ref[lax.rem(begin, 2), h] = tile
+    clear = jnp.clip(clear, first, jnp.maximum(first, last))
+    state = lax.fori_loop(first, clear, lambda key, s: step(key, s, False), state)
+    return lax.fori_loop(clear, last, lambda key, s: step(key, s, True), state)
+
+
+def empty_state(heads, size):
+    return tuple(
+        (jnp.full((1, TILE), MASKED, f32), jnp.zeros((1, TILE), f32), jnp.zeros((size, TILE), f32))
+        for _ in range(heads)
+    )
+
+
+def early_kernel(full_ref, most_ref, slot_ref, group_ref, range_ref, place_ref, *refs):
+    known, rows_in = slot_ref.shape[0] - 1, place_ref.shape[0]
+    pieces, weights = refs[:known], refs[known : known + rows_in]
+    (
+        gain_ref, end_ref, bias_ref,
+        qkv_ref, normed_ref, weight_ref, own_ref, top_ref, total_ref, mix_ref,
+        qt_ref, k_ref, vt_ref, bias_held, scores_ref, rows_held, bias_sem,
+    ) = refs[known + rows_in :]
+    heads, size, length = qt_ref.shape
+    part_length = length // (known + 1)
+    turn = pl.program_id(0)
+    load = pltpu.make_async_copy(bias_ref, bias_held, bias_sem)
+
+    @pl.when(turn == 0)
+    def _():
+        load.start()
+        for i, piece in enumerate(weights):
+            rows = piece.shape[0]
+            rows_held[pl.ds(pl.multiple_of(place_ref[i] * rows, rows), rows), :] = piece[...]
+        by_columns = rows_held[...].T
+        weight_ref[...] = by_columns
+        for i, piece in enumerate(pieces):
+
+            @pl.when(slot_ref[i] == group_ref[0])
+            def _():
+                own_ref[...] = piece[...]
+
+            normed, qkv = token_parts(piece[...], gain_ref[...], by_columns, heads)
+            normed_ref[i] = normed
+            qkv_ref[i] = qkv
+            places = pl.ds(pl.multiple_of(slot_ref[i] * part_length, TILE), part_length)
+            for h in range(heads):
+                qt_ref[h, :, places] = qkv[h]
+                k_ref[h, places, :] = qkv[heads + h].T
+                vt_ref[h, :, places] = qkv[2 * heads + h]
+        load.wait()
+
+    low, high = range_ref[0], range_ref[1]
+    query = low + turn
+    own = pl.ds(pl.multiple_of(query * TILE, TILE), TILE)
+    state = attend_tiles(
+        query, low, full_ref[query], jnp.minimum(most_ref[query], high), empty_state(heads, size),
+        end_ref[:, own], [qt_ref[h, :, own] for h in range(heads)],
+        k_ref, vt_ref, bias_held, scores_ref,
+    )
+    for h, (top, total, mix) in enumerate(state):
+        top_ref[h, :, own] = top
+        total_ref[h, :, own] = total
+        mix_ref[h, :, own] = mix
+
+
+def late_kernel(full_ref, most_ref, slot_ref, group_ref, range_ref, *refs):
+    parts = slot_ref.shape[0]
+    (
+        piece_ref, weight_ref, gain_ref, end_ref, before_ref, top_ref, total_ref, mix_ref, bias_ref,
+    ) = refs[:9]
+    ots = refs[9 : 9 + parts]
+    (
+        lse_ref, qkv_ref, normed_ref,
+        qt_ref, k_ref, vt_ref, bias_held, scores_ref, held_ref, bias_sem,
+    ) = refs[9 + parts :]
+    heads, size, length = qt_ref.shape
+    count = length // TILE
+    each = count // parts
+    part_length = length // parts
+    query = pl.program_id(0)
+    load = pltpu.make_async_copy(bias_ref, bias_held, bias_sem)
+
+    @pl.when(query == 0)
+    def _():
+        load.start()
+        normed, qkv = token_parts(piece_ref[...], gain_ref[...], weight_ref[...], heads)
+        normed_ref[0] = normed
+        qkv_ref[0] = qkv
+        for i in range(parts):
+            source = before_ref.at[i] if i < parts - 1 else qkv_ref.at[0]
+            places = pl.ds(pl.multiple_of(slot_ref[i] * part_length, TILE), part_length)
+            for h in range(heads):
+                qt_ref[h, :, places] = source[h]
+                k_ref[h, places, :] = source[heads + h].T
+                vt_ref[h, :, places] = source[2 * heads + h]
+        load.wait()
+
+    low, high = range_ref[0], range_ref[1]
+    own = pl.ds(pl.multiple_of(query * TILE, TILE), TILE)
+    begun = (query >= low) & (query < high)
+    for h in range(heads):
+        held_ref[h, 0:1, :] = jnp.where(begun, top_ref[h, :, own], MASKED)
+        held_ref[h, 1:2, :] = jnp.where(begun, total_ref[h, :, own], 0.0)
+        held_ref[h, 8:, :] = jnp.where(begun, mix_ref[h, :, own], 0.0)
     state = tuple(
-        (jnp.full((1, TILE), -jnp.inf, f32), jnp.zeros((1, TILE), f32), jnp.zeros((size, TILE), f32))
-        for _ in range(heads)
-    )
-    state = lax.fori_loop(0, full_ref[query], lambda key, s: step(key, s, False), state)
-    state = lax.fori_loop(full_ref[query], most_ref[query], lambda key, s: step(key, s, True), state)
+        (held_ref[h, 0:1, :], held_ref[h, 1:2, :], held_ref[h, 8:, :]) for h in range(heads)
+    )
+    most = most_ref[query]
+    first = jnp.where(begun & (low == 0), high, 0)
+    last = jnp.where(begun & (low > 0), jnp.minimum(low, most), most)
+    state = attend_tiles(
+        query, first, full_ref[query], last, state,
+        end_ref[:, own], [qt_ref[h, :, own] for h in range(heads)],
+        k_ref, vt_ref, bias_held, scores_ref,
+    )
     turn = (query // each) ^ group_ref[0]
     inner = pl.ds(pl.multiple_of(lax.rem(query, each) * TILE, TILE), TILE)
     mixes = [(mix * (1.0 / total)).astype(bf16) for _, total, mix in state]
@@ -206,65 +276,95 @@
                 ots[r][h * size : (h + 1) * size, inner] = mixes[h]
 
 
-def attend_forward(pieces, weights, places, gain, bias, end, full, most, slots, group):
-    parts = len(pieces)
+def shape(*dims, kind=bf16):
+    return jax.ShapeDtypeStruct(dims, kind)
+
+
+def sequence_held(heads, size, length, bias):
+    return [
+        pltpu.VMEM((heads, size, length), bf16),
+        pltpu.VMEM((heads, length, size), bf16),
+        pltpu.VMEM((heads, size, length), bf16),
+        pltpu.VMEM(bias.shape, f32),
+        pltpu.VMEM((2, heads, TILE, TILE), f32),
+    ]
+
+
+def attend_early(pieces, weights, places, gain, bias, end, full, most, slots, group, known):
+    parts = len(pieces) + 1
     part_length, width = pieces[0].shape
     columns = weights[0].shape[1]
     heads = bias.shape[0]
     size = columns // (3 * heads)
     length = parts * part_length
     smem = pl.BlockSpec(memory_space=pltpu.SMEM)
+    hbm = pl.BlockSpec(memory_space=pl.ANY)
     outs = [
-        *[jax.ShapeDtypeStruct((heads * size, part_length), bf16)] * parts,
-        jax.ShapeDtypeStruct((heads, 1, length), f32),
-        jax.ShapeDtypeStruct((parts, 3 * heads, size, part_length), bf16),
-        jax.ShapeDtypeStruct((parts, part_length, width), bf16),
-        jax.ShapeDtypeStruct((columns, width), bf16),
-        jax.ShapeDtypeStruct((part_length, width), bf16),
+        shape(parts - 1, 3 * heads, size, part_length),
+        shape(parts - 1, part_length, width),
+        shape(columns, width),
+        shape(part_length, width),
+        shape(heads, 1, length, kind=f32),
+        shape(heads, 1, length, kind=f32),
+        shape(heads, size, length, kind=f32),
+    ]
+    dense = (*pieces, *weights, gain, end)
+    return pl.pallas_call(
+        early_kernel,
+        grid=((parts - 1) * part_length // TILE,),
+        in_specs=[smem] * 6 + [whole(a.shape) for a in dense] + [hbm],
+        out_specs=[whole(a.shape) for a in outs],
+        out_shape=outs,
+        scratch_shapes=sequence_held(heads, size, length, bias)
+        + [pltpu.VMEM((width, columns), bf16), pltpu.SemaphoreType.DMA],
+        compiler_params=params(),
+        cost_estimate=cost(20),
+        name="attend_early",
+    )(full, most, slots, group, known, places, *dense, bias)
+
+
+def attend_late(piece, weight, gain, bias, end, full, most, slots, group, known, qkv, state):
+    part_length, width = piece.shape
+    parts, heads = qkv.shape[0] + 1, bias.shape[0]
+    size = qkv.shape[2]
+    length = parts * part_length
+    smem = pl.BlockSpec(memory_space=pltpu.SMEM)
+    hbm = pl.BlockSpec(memory_space=pl.ANY)
+    outs = [
+        *[shape(heads * size, part_length)] * parts,
+        shape(heads, 1, length, kind=f32),
+        shape(1, 3 * heads, size, part_length),
+        shape(1, part_length, width),
     ]
     out_specs = [whole(a.shape) for a in outs]
     out_specs[parts] = pl.BlockSpec((heads, 1, TILE), lambda i: (0, 0, i))
+    dense = (piece, weight, gain, end, qkv, *state)
     return pl.pallas_call(
-        forward_kernel,
+        late_kernel,
         grid=(length // TILE,),
-        in_specs=[smem] * 5
-        + [whole(a.shape) for a in (*pieces, *weights)]
-        + [
-            whole((1, width)),
-            pl.BlockSpec(memory_space=pl.ANY),
-            pl.BlockSpec((1, TILE), lambda i: (0, i)),
-        ],
+        in_specs=[smem] * 5 + [whole(a.shape) for a in dense] + [hbm],
         out_specs=out_specs,
         out_shape=outs,
-        scratch_shapes=[
-            pltpu.VMEM((heads, size, length), bf16),
-            pltpu.VMEM((heads, length, size), bf16),
-            pltpu.VMEM((heads, size, length), bf16),
-            pltpu.VMEM(bias.shape, f32),
-            pltpu.VMEM((2, heads, TILE, TILE), f32),
-            pltpu.VMEM((width, columns), bf16),
-            pltpu.SemaphoreType.DMA,
-        ],
+        scratch_shapes=sequence_held(heads, size, length, bias)
+        + [pltpu.VMEM((heads, size + 8, TILE), f32), pltpu.SemaphoreType.DMA],
         compiler_params=params(),
-        cost_estimate=cost(30),
-        name="attend_forward",
-    )(full, most, slots, group, places, *pieces, *weights, gain.reshape(1, width), bias, end)
-
-
-def backward_kernel(least_ref, clear_ref, slot_ref, group_ref, place_ref, *refs):
+        cost_estimate=cost(15),
+        name="attend_late",
+    )(full, most, slots, group, known, *dense, bias)
+
+def backward_kernel(least_ref, clear_ref, slot_ref, group_ref, *refs):
     parts = slot_ref.shape[0]
     grads, ots = refs[:parts], refs[parts : 2 * parts]
     (
-        qkv_ref, lse_ref, end_ref, normed_ref, weight_ref, gain_ref, feed_gain_ref, bucket_ref, bias_ref,
-    ) = refs[2 * parts : 2 * parts + 9]
-    outs = refs[2 * parts + 9 : 3 * parts + 9]
-    small_ref = refs[3 * parts + 9]
-    scratch = 16
-    share_refs = refs[3 * parts + 10 : len(refs) - scratch]
+        qkv_early, qkv_late, lse_ref, end_ref, weight_ref, bias_ref,
+    ) = refs[2 * parts : 2 * parts + 6]
+    outs = refs[2 * parts + 6 : 3 * parts + 6]
+    qkv_ref = [qkv_early.at[i] for i in range(parts - 1)] + [qkv_late.at[0]]
     (
-        qt_ref, kt_ref, vt_ref, got_ref, q_ref, go_ref, dqkv_ref,
-        dqt_acc, dk_acc, dv_acc, delta_ref, band_ref, bias_held, sum_ref, line_ref, bias_sem,
-    ) = refs[len(refs) - scratch :]
+        dqkv_ref, band_out,
+        qt_ref, kt_ref, vt_ref, got_ref,
+        dqt_acc, dk_acc, dv_acc, delta_ref, band_ref, bias_held, bias_sem, band_sem,
+    ) = refs[3 * parts + 6 :]
     heads, size, length = qt_ref.shape
     columns = heads * size
     count = length // TILE
@@ -273,6 +373,7 @@
     key = pl.program_id(0)
     key_cols = pl.ds(pl.multiple_of(key * TILE, TILE), TILE)
     load = pltpu.make_async_copy(bias_ref, bias_held, bias_sem)
+    store = pltpu.make_async_copy(band_ref, band_out, band_sem)
     every = range(heads)
 
     @pl.when(key == 0)
@@ -283,10 +384,9 @@
         for i in range(parts):
             places = pl.ds(pl.multiple_of(slot_ref[i] * part_length, TILE), part_length)
             for h in every:
-                qt_ref[h, :, places] = qkv_ref[i, h]
-                q_ref[h, places, :] = qkv_ref[i, h].T
-                kt_ref[h, :, places] = qkv_ref[i, heads + h]
-                vt_ref[h, :, places] = qkv_ref[i, 2 * heads + h]
+                qt_ref[h, :, places] = qkv_ref[i][h]
+                kt_ref[h, :, places] = qkv_ref[i][heads + h]
+                vt_ref[h, :, places] = qkv_ref[i][2 * heads + h]
         for turn in range(parts):
             part = group_ref[0] ^ turn
             places = pl.ds(pl.multiple_of(part * part_length, TILE), part_length)
@@ -294,7 +394,6 @@
                 rows = slice(h * size, (h + 1) * size)
                 grad = grads[turn][rows, :]
                 got_ref[h, :, places] = grad
-                go_ref[h, places, :] = grad.T
                 delta_ref[h, :, places] = jnp.sum(
                     ots[turn][rows, :].astype(f32) * grad.astype(f32), axis=0, keepdims=True
                 )
@@ -321,9 +420,9 @@
         rounded = [tile.astype(bf16) for tile in grad_scores]
         weights = [tile.astype(bf16) for tile in weights]
         for h in every:
-            dv_acc[h] += dot(weights[h], go_ref[h, cols, :])
+            dv_acc[h] += dot(got_ref[h, :, cols], weights[h], ((1,), (1,)))
         for h in every:
-            dk_acc[h] += dot(rounded[h], q_ref[h, cols, :])
+            dk_acc[h] += dot(qt_ref[h, :, cols], rounded[h], ((1,), (1,)))
         for h in every:
             dqt_acc[h, :, cols] += dot(kt[h], rounded[h])
 
@@ -342,9 +441,9 @@
         slot = jnp.where(slot_ref[i] == key // each, i, slot)
     inner = pl.ds(pl.multiple_of(lax.rem(key, each) * TILE, TILE), TILE)
     for h in every:
-        dqkv_ref[slot, columns + h * size : columns + (h + 1) * size, inner] = dk_acc[h].T.astype(bf16)
+        dqkv_ref[slot, columns + h * size : columns + (h + 1) * size, inner] = dk_acc[h].astype(bf16)
         dqkv_ref[slot, 2 * columns + h * size : 2 * columns + (h + 1) * size, inner] = (
-            dv_acc[h].T.astype(bf16)
+            dv_acc[h].astype(bf16)
         )
 
     @pl.when(key == count - 1)
@@ -353,113 +452,146 @@
             places = pl.ds(pl.multiple_of(slot_ref[i] * part_length, TILE), part_length)
             for h in every:
                 dqkv_ref[i, h * size : (h + 1) * size, :] = dqt_acc[h, :, places].astype(bf16)
+        store.start()
         weight = weight_ref[...]
-        for i in range(parts):
+        for i in reversed(range(parts)):
             outs[i][...] = dot(dqkv_ref[i], weight, ((0,), (0,))).astype(bf16)
-        total = dot(dqkv_ref[0], normed_ref[0])
-        for i in range(1, parts):
-            total = total + dot(dqkv_ref[i], normed_ref[i])
-        sum_ref[...] = total.T
-        place = 0
-        for share in share_refs:
-            for i in range(share.shape[0]):
-                rows = share.shape[1]
-                at = pl.ds(pl.multiple_of(place_ref[place] * rows, rows), rows)
-                share[i] = sum_ref[at, :].astype(bf16)
-                place += 1
-
-        small_ref[...] = jnp.zeros_like(small_ref)
-        gain_grad = jnp.sum(total * weight.astype(f32), axis=0, keepdims=True) / gain_ref[...]
-        lanes = small_ref.shape[1]
-        each_gain = weight.shape[1] // lanes
-        for row in range(each_gain):
-            cut = slice(row * lanes, (row + 1) * lanes)
-            small_ref[row : row + 1, :] = gain_grad[:, cut]
-            small_ref[each_gain + row : each_gain + row + 1, :] = feed_gain_ref[:, cut]
-
-        line_ref[...] = jnp.zeros_like(line_ref)
-        tiles = band_ref.shape[1]
-
-        def one(pair, _):
-            bands = [(place, h) for place in (2 * pair, 2 * pair + 1) for h in every]
-            zero = jnp.zeros((TILE // 2, TILE // 2), f32)
-            lines = []
-            for place, h in bands:
-                upper, lower = band_ref[h, place, : TILE // 2], band_ref[h, place, TILE // 2 :]
-                lines.append(
-                    jnp.concatenate([zero, zero, upper], axis=1)
-                    + jnp.concatenate([zero, lower, zero], axis=1)
-                )
-            half = TILE // 4
-            while half >= 1:
-                turned = [pltpu.roll(line[half:], 2 * TILE - half, 1) for line in lines]
-                lines = [line[:half] + turn for line, turn in zip(lines, turned)]
-                half //= 2
-            for (place, h), line in zip(bands, lines):
-                start = pl.multiple_of((tiles - 1 - place) * TILE, TILE)
-                line_ref[h : h + 1, pl.ds(start, 2 * TILE)] += line
-            return 0
-
-        lax.fori_loop(0, tiles // 2, one, 0)
-        line = line_ref[0:8, :]
-        terms = []
-        for _ in range(3):
-            term = line.astype(bf16)
-            terms.append(term)
-            line = line - term.astype(f32)
-        names = lax.broadcasted_iota(jnp.int32, (lanes, line_ref.shape[1]), 0)
-        onehot = jnp.where(lax.rem(names, lanes // 4) == bucket_ref[...], 1.0, 0.0).astype(bf16)
-        sums = [dot(term, onehot, ((1,), (1,))) for term in terms]
-        sums = sums[0] + sums[1] + sums[2]
-        lane = lax.broadcasted_iota(jnp.int32, (1, lanes), 1)
-        table = jnp.zeros((1, lanes), f32)
-        for h in every:
-            mine = (lane >= h * (lanes // 4)) & (lane < (h + 1) * (lanes // 4))
-            table = jnp.where(mine, sums[h : h + 1], table)
-        small_ref[pl.ds(2 * each_gain + group_ref[0], 1), :] = table
-
-
-def attend_backward(
-    grads, ots, qkv, lse, end, normed, weight, gain, feed_gain_grad, bucket, bias,
-    least, clear, slots, group, places, shares,
-):
-    parts, triple, size, part_length = qkv.shape
+        store.wait()
+
+
+def sums_kernel(group_ref, place_ref, *refs):
+    (
+        dqkv_ref, normed_early, normed_late, weight_ref, gain_ref, feed_gain_ref, bucket_ref, band_in, small_ref,
+    ) = refs[:9]
+    share_refs = refs[9:-4]
+    band_ref, sum_ref, line_ref, band_sem = refs[-4:]
+    load = pltpu.make_async_copy(band_in, band_ref, band_sem)
+    load.start()
+    parts = dqkv_ref.shape[0]
+    every = range(band_ref.shape[0])
+    normed_ref = [normed_early.at[i] for i in range(parts - 1)] + [normed_late.at[0]]
+    weight = weight_ref[...]
+    total = dot(dqkv_ref[0], normed_ref[0][...])
+    for i in range(1, parts):
+        total = total + dot(dqkv_ref[i], normed_ref[i][...])
+    sum_ref[...] = total.T
+    place = 0
+    for share in share_refs:
+        for i in range(share.shape[0]):
+            rows = share.shape[1]
+            at = pl.ds(pl.multiple_of(place_ref[place] * rows, rows), rows)
+            share[i] = sum_ref[at, :].astype(bf16)
+            place += 1
+
+    small_ref[...] = jnp.zeros_like(small_ref)
+    gain_grad = jnp.sum(total * weight.astype(f32), axis=0, keepdims=True) / gain_ref[...]
+    lanes = small_ref.shape[1]
+    each_gain = weight.shape[1] // lanes
+    for row in range(each_gain):
+        cut = slice(row * lanes, (row + 1) * lanes)
+        small_ref[row : row + 1, :] = gain_grad[:, cut]
+        small_ref[each_gain + row : each_gain + row + 1, :] = feed_gain_ref[:, cut]
+
+    line_ref[...] = jnp.zeros_like(line_ref)
+    load.wait()
+    tiles = band_ref.shape[1]
+
+    def one(pair, _):
+        bands = [(place, h) for place in (2 * pair, 2 * pair + 1) for h in every]
+        zero = jnp.zeros((TILE // 2, TILE // 2), f32)
+        lines = []
+        for place, h in bands:
+            upper, lower = band_ref[h, place, : TILE // 2], band_ref[h, place, TILE // 2 :]
+            lines.append(
+                jnp.concatenate([zero, zero, upper], axis=1)
+                + jnp.concatenate([zero, lower, zero], axis=1)
+            )
+        half = TILE // 4
+        while half >= 1:
+            turned = [pltpu.roll(line[half:], 2 * TILE - half, 1) for line in lines]
+            lines = [line[:half] + turn for line, turn in zip(lines, turned)]
+            half //= 2
+        for (place, h), line in zip(bands, lines):
+            start = pl.multiple_of((tiles - 1 - place) * TILE, TILE)
+            line_ref[h : h + 1, pl.ds(start, 2 * TILE)] += line
+        return 0
+
+    lax.fori_loop(0, tiles // 2, one, 0)
+    line = line_ref[0:8, :]
+    terms = []
+    for _ in range(3):
+        term = line.astype(bf16)
+        terms.append(term)
+        line = line - term.astype(f32)
+    names = lax.broadcasted_iota(jnp.int32, (lanes, line_ref.shape[1]), 0)
+    onehot = jnp.where(lax.rem(names, lanes // 4) == bucket_ref[...], 1.0, 0.0).astype(bf16)
+    sums = [dot(term, onehot, ((1,), (1,))) for term in terms]
+    sums = sums[0] + sums[1] + sums[2]
+    lane = lax.broadcasted_iota(jnp.int32, (1, lanes), 1)
+    table = jnp.zeros((1, lanes), f32)
+    for h in every:
+        mine = (lane >= h * (lanes // 4)) & (lane < (h + 1) * (lanes // 4))
+        table = jnp.where(mine, sums[h : h + 1], table)
+    small_ref[pl.ds(2 * each_gain + group_ref[0], 1), :] = table
+
+
+def attend_backward(grads, ots, qkv, lse, end, weight, bias, least, clear, slots, group):
+    parts = len(grads)
+    _, triple, size, part_length = qkv[0].shape
     heads, length = triple // 3, parts * part_length
     columns, width = weight.shape
-    tiles = bias.shape[1]
     smem = pl.BlockSpec(memory_space=pltpu.SMEM)
-    dense = [*grads, *ots, qkv, lse, end, normed, weight, gain.reshape(1, width), feed_gain_grad, bucket]
-    small = jax.ShapeDtypeStruct((2 * (width // 128) + parts, 128), f32)
-    outs = [jax.ShapeDtypeStruct((part_length, width), bf16)] * parts + [small]
-    outs += [jax.ShapeDtypeStruct((number, rows, columns), bf16) for number, rows in shares]
+    hbm = pl.BlockSpec(memory_space=pl.ANY)
+    dense = [*grads, *ots, *qkv, lse, end, weight]
+    outs = [shape(part_length, width)] * parts + [shape(parts, columns, part_length)]
     by_columns = pltpu.VMEM((heads, size, length), bf16)
-    by_rows = pltpu.VMEM((heads, length, size), bf16)
     return pl.pallas_call(
         backward_kernel,
         grid=(length // TILE,),
-        in_specs=[smem] * 5
+        in_specs=[smem] * 4 + [whole(a.shape) for a in dense] + [hbm],
+        out_specs=[whole(a.shape) for a in outs] + [hbm],
+        out_shape=outs + [shape(*bias.shape, kind=f32)],
+        scratch_shapes=[by_columns] * 4
+        + [
+            pltpu.VMEM((heads, size, length), f32),
+            pltpu.VMEM((heads, size, TILE), f32),
+            pltpu.VMEM((heads, size, TILE), f32),
+            pltpu.VMEM((heads, 1, length), f32),
+            pltpu.VMEM(bias.shape, f32),
+            pltpu.VMEM(bias.shape, f32),
+            pltpu.SemaphoreType.DMA,
+            pltpu.SemaphoreType.DMA,
+        ],
+        compiler_params=params(),
+        cost_estimate=cost(45),
+        name="attend_backward",
+    )(least, clear, slots, group, *dense, bias)
+
+
+def attend_sums(dqkv, normed, weight, gain, feed_gain_grad, bucket, bands, group, places, shares):
+    parts, columns, _ = dqkv.shape
+    width = weight.shape[1]
+    smem = pl.BlockSpec(memory_space=pltpu.SMEM)
+    dense = [dqkv, *normed, weight, gain.reshape(1, width), feed_gain_grad, bucket]
+    outs = [shape(2 * (width // 128) + parts, 128, kind=f32)]
+    outs += [shape(number, rows, columns) for number, rows in shares]
+    return pl.pallas_call(
+        sums_kernel,
+        in_specs=[smem] * 2
         + [whole(a.shape) for a in dense]
         + [pl.BlockSpec(memory_space=pl.ANY)],
         out_specs=[whole(a.shape) for a in outs],
         out_shape=outs,
-        scratch_shapes=[by_columns] * 4
-        + [by_rows] * 2
-        + [
-            pltpu.VMEM((parts, columns, part_length), bf16),
-            pltpu.VMEM((heads, size, length), f32),
-            pltpu.VMEM((heads, TILE, size), f32),
-            pltpu.VMEM((heads, TILE, size), f32),
-            pltpu.VMEM((heads, 1, length), f32),
-            pltpu.VMEM((heads, tiles, TILE, TILE), f32),
-            pltpu.VMEM(bias.shape, f32),
+        scratch_shapes=[
+            pltpu.VMEM(bands.shape, f32),
             pltpu.VMEM((width, columns), f32),
             pltpu.VMEM((8, bucket.shape[1]), f32),
             pltpu.SemaphoreType.DMA,
         ],
         compiler_params=params(),
-        cost_estimate=cost(50),
-        name="attend_backward",
-    )(least, clear, slots, group, places, *dense, bias)
+        cost_estimate=cost(12),
+        name="attend_sums",
+    )(group, places, *dense, bands)
 
 
 def middle_kernel(turn_ref, *refs):
@@ -511,8 +643,9 @@
         outer = w_ref[z, :, :, hidden_units:feed].reshape(width, hidden_units)
         second = second_ref[...]
         grad = g_ref[...]
+        units = dot(second, inner)
         grad_active = dot(grad, outer).astype(bf16).astype(f32)
-        active, slope = gelu_parts(dot(second, inner))
+        active, slope = gelu_parts(units)
         active = active.astype(bf16)
         grad_units = (grad_active * slope).astype(bf16)
         acc_ref[...] += dot(active, outer, ((1,), (1,)))
@@ -665,6 +798,10 @@
     group_ref = group.reshape(1)
     square = planes == 4 and each % 16 == 0
     gather, rounds, owners, weight_routes = routes(parts)
+    tiles = length // TILE
+    at_start = (z == 0) | (z == half)
+    known = jnp.where(at_start, jnp.array([0, tiles - tiles // parts]), jnp.array([tiles // parts, tiles]))
+    known = known.astype(jnp.int32)
     slots = jnp.array([[0, 1, 2, 3], [1, 2, 3, 0], [2, 1, 0, 3], [3, 2, 1, 0]], jnp.int32)[z]
 
     def swap(value):
@@ -675,13 +812,13 @@
 
     packed = jnp.concatenate([query_weight, key_weight, value_weight], axis=1)
     first = lax.ppermute(inputs, LINE, gather[0])
-    table = lax.ppermute(bias_table, LINE, weight_routes[0])
-    block_row = jnp.where(owner, block_index, swap(block_index))[0]
     first, table, block_row, packed, packed_rest = lax.optimization_barrier(
-        (first, table, block_row, packed, packed_rest)
-    )
+        (first, bias_table, jnp.where(owner, block_index, swap(block_index)), packed, packed_rest)
+    )
+    table = lax.ppermute(table, LINE, weight_routes[0])
+    block_row = block_row[0]
+    line_rest = lax.all_gather(packed_rest, "tensor", axis=0)
     one, two = (lax.ppermute(packed, LINE, route) for route in weight_routes)
-    line_rest = lax.all_gather(packed_rest, "tensor", axis=0)
     second = lax.ppermute(first, LINE, gather[1])
     rows, bucket = bias_rows(table, position_bucket)
     bias = bias_tiles(rows, length)
@@ -698,17 +835,24 @@
         both = lax.all_gather(jnp.stack([low, high]), "plane", axis=0)
         weights = [both.reshape(width, 3 * columns)]
         places = jnp.zeros((1,), jnp.int32)
-    second, *weights = lax.optimization_barrier((second, *weights))
+    end, full, most, least, clear = spans(block_row)
+    marks = (attention_gain.reshape(1, width), bias, end, full, most, slots, group_ref, known)
+    pieces = [jnp.where(owner, piece, swap(piece)) for piece in (inputs, first)]
+    second, pieces, weights, places, marks, least, clear = lax.optimization_barrier(
+        (second, pieces, weights, places, marks, least, clear)
+    )
     third = lax.ppermute(jnp.where(outer_chip, inputs, second), LINE, gather[2])
-    pieces = [jnp.where(owner, piece, swap(piece)) for piece in (inputs, first, second, third)]
+    pieces = [*pieces, jnp.where(owner, second, swap(second))]
     all_rest = lax.all_gather(after(line_rest, second), ("plane", "core"), axis=0)
 
-    end, full, most, least, clear = spans(block_row)
-
-    grad = lax.ppermute(after(cotangent, third), LINE, back(owners))
-    *ots, lse, qkv, normed, weight, own_tokens = attend_forward(
-        pieces, weights, places, attention_gain, bias, end, full, most, slots, group_ref
-    )
+
+    _, bias, end, full, most, slots, group_ref, known = marks
+    qkv, normed, weight, own_tokens, *state = attend_early(pieces, weights, places, *marks)
+    third, state, cotangent = lax.optimization_barrier((third, state, cotangent))
+    grad = lax.ppermute(cotangent, LINE, back(owners))
+    third = jnp.where(owner, third, swap(third))
+    *ots, lse, late_qkv, late_normed = attend_late(third, weight, *marks, qkv, state)
+    qkv, normed = (qkv, late_qkv), (normed, late_normed)
     mixes = [ots[0]] + [lax.ppermute(ots[r], LINE, rounds[r]) for r in range(1, parts)]
     turns = (group ^ jnp.arange(parts)).astype(jnp.int32)
     if each % 16:
@@ -719,63 +863,64 @@
     if each % 16:
         grads = jnp.swapaxes(grads.reshape(parts, planes * 2, each, -1), 0, 1)
     gots = [gots[0]] + [lax.ppermute(gots[r], LINE, rounds[r]) for r in range(1, parts)]
-    gots, results = lax.optimization_barrier((gots, results))
-    results = lax.ppermute(results, LINE, owners)
-    layer_output, grad_hidden = results[0], results[1].astype(f32)
-
-    rest = lax.psum_scatter(grads, ("plane", "core"), scatter_dimension=0)
-
     if square:
         order = plane ^ jnp.array([1, 3, 0, 2, 2, 3, 0, 1], jnp.int32)
         places = order * 2 + jnp.array([0, 0, 0, 0, 1, 1, 1, 1], jnp.int32)
         shares = [(2, each)] * 4
     else:
         places, shares = jnp.zeros((1,), jnp.int32), [(1, width)]
-    back_outs = attend_backward(
-        gots, ots, qkv, lse, end, normed, weight, attention_gain, feedforward_part, bucket, bias,
-        least, clear, slots, group_ref, places, shares,
-    )
+    gots, results, places, bucket = lax.optimization_barrier((gots, results, places, bucket))
+    results = lax.ppermute(results, LINE, owners)
+
+    rest = lax.psum_scatter(grads, ("plane", "core"), scatter_dimension=0)
+
+    own, first, second, third, dqkv, bands = attend_backward(
+        gots, ots, qkv, lse, end, weight, bias, least, clear, slots, group_ref
+    )
+    third, results = lax.optimization_barrier((third, results))
+    layer_output, grad_hidden = results[0], results[1].astype(f32)
+    third = third + swap(third)
+    got = lax.ppermute(third, LINE, back(gather[2]))
+    own, first, second = (part + swap(part) for part in (own, first, second))
 
     def small_step(small, axis, step):
         count = lax.axis_size(axis)
         return small + lax.ppermute(small, axis, [(i, i ^ step) for i in range(count)])
 
-    own, first, second, third, small, *weight_grads = back_outs
-    third = third + swap(third)
-    got = lax.ppermute(third, LINE, back(gather[2]))
-    own, first, second = (part + swap(part) for part in (own, first, second))
+    dqkv, bands, third = lax.optimization_barrier((dqkv, bands, third))
+    small, *weight_grads = attend_sums(
+        dqkv, normed, weight, attention_gain, feedforward_part, bucket, bands, group_ref, places, shares
+    )
     none = jnp.zeros_like(own)
+    got, small, weight_grads, rest = lax.optimization_barrier((got, small, weight_grads, rest))
+    rest = lax.psum_scatter(rest, "tensor", scatter_dimension=0)
+    own = jnp.where(owner, jnp.where(outer_chip, own + got, own), none)
+    second = jnp.where(outer_chip, second, second + got)
+    got = lax.ppermute(second, LINE, back(gather[1]))
     if square:
         low_send, low, high_send, high = weight_grads
         low, high = low + across(low_send, 1), high + across(high_send, 2)
     else:
-        attention_grads = weight_grads[0].reshape(planes, 2, each, 3 * columns)
-        low = high = attention_grads
+        low = high = weight_grads[0].reshape(planes, 2, each, 3 * columns)
     small = small_step(small, "core", 1)
     small = small_step(small, "tensor", 1)
-    got, low, high, small, rest = lax.optimization_barrier((got, low, high, small, rest))
-    rest = lax.psum_scatter(rest, "tensor", scatter_dimension=0)
-    own = jnp.where(owner, jnp.where(outer_chip, own + got, own), none)
-    second = jnp.where(outer_chip, second, second + got)
-    got = lax.ppermute(second, LINE, back(gather[1]))
+    got, low, high, small = lax.optimization_barrier((got, low, high, small))
+    first = jnp.where(owner, first, none) + got
+    got = lax.ppermute(first, LINE, back(gather[0]))
     if square:
         low, high = low[0] + across(low[1], 2), high[0] + across(high[1], 1)
     else:
         shared = lax.psum_scatter(low, "plane", scatter_dimension=0)
         low, high = shared[0], shared[1]
     small = small_step(small, "tensor", 2)
-    small = small_step(small, "plane", 1)
-    got, low, high, small = lax.optimization_barrier((got, low, high, small))
-    first = jnp.where(owner, first, none) + got
-    got = lax.ppermute(first, LINE, back(gather[0]))
+    step = 1
+    while step < planes:
+        small = small_step(small, "plane", step)
+        step *= 2
     attention_share = (
         lax.ppermute(jnp.where(lower, low, high), LINE, back(weight_routes[0]))
         + lax.ppermute(jnp.where(lower, high, low), LINE, back(weight_routes[1]))
     ).astype(f32) * factor
-    step = 2
-    while step < planes:
-        small = small_step(small, "plane", step)
-        step *= 2
     small = small * factor
     rest_share = rest.astype(f32) * factor
     grad_first = (own + got).astype(f32)

time: 323 us -> 308 us (0.954)
  waiting for transfers between devices: 79 us -> 64.8 us
  starting transfers between devices: 71.3 us -> 59.2 us
  Pallas kernels: 118 us -> 129 us
    pallas_call x1 -> x3, Pallas kernels: 30.9 us -> 52.9 us  [the longest x1 22.7 us: attend_early(): pl.pallas_call(early_kernel, grid=((parts - 1) * part_length // TILE,), i...]
    ppermute x1, waiting for transfers between devices: 16 us -> 0.01 us  [body(): second = lax.ppermute(first, LINE, gather[1])]
    ppermute x1, waiting for transfers between devices: 0.01 us -> 13.9 us  [body(): lax.ppermute(jnp.where(lower, low, high), LINE, back(weight_routes[0]))]
    ppermute x1, waiting for transfers between devices: 11.7 us -> 0.01 us  [body(): got = lax.ppermute(first, LINE, back(gather[0]))]
    pallas_call x1, Pallas kernels: 54.6 us -> 44.1 us  [attend_backward(): pl.pallas_call(backward_kernel, grid=(length // TILE,), in_specs=[smem] *...]
    ppermute x10, waiting for transfers between devices: 12.4 us -> 4.47 us  [across(): lax.ppermute(value, 'plane', [(i, i ^ step) for i in range(lax.axis_size(...]
    ppermute x1, waiting for transfers between devices: 7.78 us -> 0.07 us  [body(): lax.ppermute(jnp.where(lower, high, low), LINE, back(weight_routes[1]))]
    reduce_scatter x1, waiting for transfers between devices: 0.01 us -> 6.38 us  [body(): rest = lax.psum_scatter(grads, ('plane', 'core'), scatter_dimension=0)]
  transfers between devices with their start and end apart: 47 -> 47, of which waited for: 21 -> 21; matrix products, arithmetic and copies ran while one was open for 11% -> 11% of each run, Pallas kernels for 29% -> 34%
where the time goes in v5:
time: 308 us; the launch traced here: 307 us
  Pallas kernels  129 us (42%)
  waiting for transfers between devices  64.8 us (21%)
  starting transfers between devices  59.2 us (19%)
  other arithmetic  26.4 us (9%)
  between operations  14.4 us (5%)
  local copies, waits for them, and re-layouts  13.3 us (4%)
    pallas_call x1, Pallas kernels, attend_backward(): pl.pallas_call(backward_kernel, grid=(length // TILE,), in_specs=[smem] *...  44.1 us
    pallas_call x1, Pallas kernels, middle(): pl.pallas_call(middle_kernel, in_specs=[smem] + [whole(a.shape) for a in...  25 us
    pallas_call x1, Pallas kernels, attend_early(): pl.pallas_call(early_kernel, grid=((parts - 1) * part_length // TILE,), i...  22.7 us
    pallas_call x1, Pallas kernels, attend_late(): pl.pallas_call(late_kernel, grid=(length // TILE,), in_specs=[smem] * 5 +...  18.9 us
    ppermute x9, starting transfers between devices, swap(): return lax.ppermute(value, 'core', SWAP)  14.7 us
    ppermute x1, waiting for transfers between devices, body(): lax.ppermute(jnp.where(lower, low, high), LINE, back(weight_routes[0]))  13.9 us
    pallas_call x1, Pallas kernels, attend_sums(): pl.pallas_call(sums_kernel, in_specs=[smem] * 2 + [whole(a.shape) for a i...  11.3 us
    ppermute x3, waiting for transfers between devices, body(): lax.ppermute(ots[r], LINE, rounds[r])  8.52 us
  transfers between devices with their start and end apart: 47, of which 21 were waited for; matrix products, arithmetic and copies ran while one was open for 11% of the time, Pallas kernels for 34%

profile of v5, /device:TPU:9, one launch (start us, length us, event | category | flops | bytes accessed | tf_op | source)
XLA Modules:
  0.0 306.9 jit_solution(7727887992968200146)
XLA Ops:
  8.0 3.2 %collective-permute-start = (bf16[512,768]{1,0:T(8,128)(2,1)}, bf16[512,768]{1,0:T(8,128)(2,1)S(1)}, u32[]{:S(2)}, u32[]{:S(2)}) collective-permute-start(bf16[512,768]{1,0:T(8,128)(2,1)} %param.18), channel_id=1, source_target_pairs={{1,0},{2,1},{3,2},{4,5},{5,6},{6,7},{9,8},{10,9},{11,10},{12,13},{... | collective-permute-start | bytes 2359304 | tf_op jit(solution)/shard_map/ppermute | solution.py:814
  21.2 4.3 %collective-permute-start.5 = (bf16[96,576]{1,0:T(8,128)(2,1)S(1)}, bf16[96,576]{1,0:T(8,128)(2,1)}, u32[]{:S(2)}, u32[]{:S(2)}) collective-permute-start(bf16[96,576]{1,0:T(8,128)(2,1)S(1)} %pad_maximum_fusion), channel_id=1, source_target_pairs={{0,0},{2,1},{4,2},{6,3},{1,4},{3,5},{5,6},{7,7},{8,8},{10,9},{12,1... | collective-permute-start | bytes 331784 | tf_op jit(solution)/shard_map/ppermute | solution.py:821
  25.6 3.9 %collective-permute-start.2 = (bf16[512,768]{1,0:T(8,128)(2,1)S(1)}, bf16[512,768]{1,0:T(8,128)(2,1)}, u32[]{:S(2)}, u32[]{:S(2)}) collective-permute-start(bf16[512,768]{1,0:T(8,128)(2,1)S(1)} %collective-permute-done), channel_id=1, source_target_pairs={{1,0},{2,1},{5,6},{6,7},{9,8},{10,9},{13,14},{14,15},{17,16},{18,1... | collective-permute-start | bytes 2359304 | tf_op jit(solution)/shard_map/ppermute | solution.py:822
  33.6 5.7 %collective-permute-done.7 = f32[32,3]{0,1:T(4,128)S(1)} collective-permute-done((f32[32,3]{0,1:T(4,128)S(1)}, f32[32,3]{0,1:T(4,128)S(1)}, u32[]{:S(2)}, u32[]{:S(2)}) %collective-permute-start.7) | collective-permute-done | bytes 416 | tf_op jit(solution)/shard_map/ppermute | solution.py:818
  40.2 6.6 %bias_tiles.1.refs_13_.refs_8_ = f32[3,10,256,256]{3,2,1,0:T(8,128)} custom-call(f32[3,1,2816]{2,1,0:T(1,128)} %broadcast_in_dim.21.row_ref), custom_call_target="tpu_custom_call" | custom-call | flops 6000000000 | tf_op jit(solution)/shard_map/bias_tiles/pallas_call | solution.py:83
  58.2 3.6 %all-gather.5.cloned.1.call-done = bf16[384,1792]{1,0:T(8,128)(2,1)} async-done(((bf16[96,1792]{1,0:T(8,128)(2,1)}), bf16[384,1792]{1,0:T(8,128)(2,1)}) %all-gather.5.cloned.1.call-update) | async-done | bytes 1376272 | tf_op jit(solution)/shard_map/all_gather | solution.py:820
  62.8 2.1 collective-permute-done.15
  65.0 2.1 broadcast_select_fusion.2
  67.9 22.7 %attend_early.1 = (bf16[3,9,64,512]{3,2,1,0:T(8,128)(2,1)}, bf16[3,512,768]{2,1,0:T(8,128)(2,1)}, bf16[576,768]{1,0:T(8,128)(2,1)}, bf16[512,768]{1,0:T(8,128)(2...) custom-call(s32[8]{0:T(128)} %copy-done.16, s32[8]{0:T(128)} %copy-done.15, ...), custom_call_target="tpu_custom_call" | custom-call | flops 20000000000 | tf_op jit(solution)/shard_map/attend_early/pallas_call | solution.py:312
  90.6 3.0 collective-permute-start.16
  93.6 2.1 collective-permute-start.20
  96.7 18.9 %attend_late.1 = (bf16[192,512]{1,0:T(8,128)(2,1)}, bf16[192,512]{1,0:T(8,128)(2,1)}, bf16[192,512]{1,0:T(8,128)(2,1)}, bf16[192,512]{1,0:T(8,128)(2,1)}, f32[3,...) custom-call(s32[8]{0:T(128)} %copy-done.16, s32[8]{0:T(128)} %copy-done.15, ...), custom_call_target="tpu_custom_call" | custom-call | flops 15000000512 | tf_op jit(solution)/shard_map/attend_late/pallas_call | solution.py:342
  118.9 3.7 %collective-permute-done.18.refs_2_ = bf16[192,512]{1,0:T(8,128)(2,1)S(1)} collective-permute-done((bf16[192,512]{1,0:T(8,128)(2,1)}, bf16[192,512]{1,0:T(8,128)(2,1)S(1)}, u32[]{:S(2)}, u32[]{:S(2)}) %collective-permute-start.18) | collective-permute-done | bytes 196640 | tf_op jit(solution)/shard_map/ppermute | solution.py:856
  122.6 4.8 %collective-permute-done.19.refs_3_ = bf16[192,512]{1,0:T(8,128)(2,1)S(1)} collective-permute-done((bf16[192,512]{1,0:T(8,128)(2,1)}, bf16[192,512]{1,0:T(8,128)(2,1)S(1)}, u32[]{:S(2)}, u32[]{:S(2)}) %collective-permute-start.19) | collective-permute-done | bytes 196640 | tf_op jit(solution)/shard_map/ppermute | solution.py:856
  127.4 2.4 all-gather.7.cloned.1.call-done
  129.8 25.0 %middle.1 = (bf16[2,512,768]{2,1,0:T(8,128)(2,1)}, f32[1,768]{1,0:T(1,128)}, bf16[192,512]{1,0:T(8,128)(2,1)}, bf16[192,512]{1,0:T(8,128)(2,1)}, bf16[192,512]{1...) custom-call(s32[4]{0:T(128)} %iota_xor_fusion.turn_ref, ...), custom_call_target="tpu_custom_call" | custom-call | tf_op jit(solution)/shard_map/middle/pallas_call | solution.py:702
  158.5 3.8 %collective-permute-done.22.refs_2_ = bf16[192,512]{1,0:T(8,128)(2,1)S(1)} collective-permute-done((bf16[192,512]{1,0:T(8,128)(2,1)S(1)}, bf16[192,512]{1,0:T(8,128)(2,1)S(1)}, u32[]{:S(2)}, u32[]{:S(2)}) %collective-permute-start.22) | collective-permute-done | bytes 196640 | tf_op jit(solution)/shard_map/ppermute | solution.py:865
  162.3 4.6 %collective-permute-done.23.refs_3_ = bf16[192,512]{1,0:T(8,128)(2,1)S(1)} collective-permute-done((bf16[192,512]{1,0:T(8,128)(2,1)S(1)}, bf16[192,512]{1,0:T(8,128)(2,1)S(1)}, u32[]{:S(2)}, u32[]{:S(2)}) %collective-permute-start.23) | collective-permute-done | bytes 196640 | tf_op jit(solution)/shard_map/ppermute | solution.py:865
  166.9 4.1 %collective-permute-start.24 = (bf16[2,512,768]{2,1,0:T(8,128)(2,1)}, bf16[2,512,768]{2,1,0:T(8,128)(2,1)S(1)}, u32[]{:S(2)}, u32[]{:S(2)}) collective-permute-start(bf16[2,512,768]{2,1,0:T(8,128)(2,1)} %get-tuple-element.157), channel_id=1, source_target_pairs={{0,0},{1,2},{2,4},{3,6},{4,1},{5,3},{6,5},{7,7},{8,8},{9,10},{10,1... | collective-permute-start | bytes 4718600 | tf_op jit(solution)/shard_map/ppermute | solution.py:873
  171.1 44.1 %attend_backward.1 = (bf16[512,768]{1,0:T(8,128)(2,1)}, bf16[512,768]{1,0:T(8,128)(2,1)}, bf16[512,768]{1,0:T(8,128)(2,1)}, bf16[512,768]{1,0:T(8,128)(2,1)}, bf...) custom-call(s32[8]{0:T(128)} %convert_reduce_fusion.2.least_ref, s32[8]{0:T(128)} %convert_reduce_fusion.1.clear_ref, ...), custom_call_target="tpu_custom_call" | custom-call | flops 44999999488 | tf_op jit(solution)/shard_map/attend_backward/pallas_call | solution.py:548
  215.7 2.3 collective-permute-done.26
  218.1 2.2 add.126
  221.0 11.3 %attend_sums.1 = (f32[16,128]{1,0:T(8,128)}, bf16[2,96,576]{2,1,0:T(8,128)(2,1)}, bf16[2,96,576]{2,1,0:T(8,128)(2,1)}, bf16[2,96,576]{2,1,0:T(8,128)(2,1)}, bf16[2,96,576]{2,1,0:T(8,128)(2,1)}) custom-call(s32[1]{0:T(128)} %bitcast.5.group_ref, s32[8]{0:T(128)} %multiply_add_fusion.place_ref, bf16[4,576,512]{2,1,0:T(8,128)(2,1)} %get-tuple-element.164.refs_0_, ...), custom_call_target="tpu_custom_call" | custom-call | flops 12000000000 | tf_op jit(solution)/shard_map/attend_sums/pallas_call | solution.py:578
  232.3 6.4 %reduce-scatter.3.cloned.1.call-done = bf16[1,4,96,1792]{3,2,1,0:T(8,128)(2,1)} async-done(((bf16[8,4,96,1792]{3,2,1,0:T(8,128)(2,1)}), bf16[1,4,96,1792]{3,2,1,0:T(8,128)(2,1)}) %reduce-scatter.3.cloned.1.call-update) | async-done | bytes 1376272 | tf_op jit(solution)/shard_map/reduce_scatter | solution.py:875
  238.7 2.4 add_select_fusion
  242.6 2.8 collective-permute-start.28
  250.3 6.4 %collective-permute-start.25 = (bf16[512,768]{1,0:T(8,128)(2,1)}, bf16[512,768]{1,0:T(8,128)(2,1)}, u32[]{:S(2)}, u32[]{:S(2)}) collective-permute-start(bf16[512,768]{1,0:T(8,128)(2,1)} %get-tuple-element.159), channel_id=1, source_target_pairs={{0,4},{4,0},{1,5},{5,1},{2,6},{6,2},{3,7},{7,3},{8,12},{12,8},{9,1... | collective-permute-start | bytes 2359304 | tf_op jit(solution)/shard_map/ppermute | solution.py:808
  259.0 3.6 %collective-permute-done.36 = f32[16,128]{1,0:T(8,128)S(1)} collective-permute-done((f32[16,128]{1,0:T(8,128)S(1)}, f32[16,128]{1,0:T(8,128)S(1)}, u32[]{:S(2)}, u32[]{:S(2)}) %collective-permute-start.36) | collective-permute-done | bytes 8224 | tf_op jit(solution)/shard_map/ppermute | solution.py:888
  265.9 2.7 select_add_fusion
  272.6 4.5 %collective-permute-start.41 = (bf16[96,576]{1,0:T(8,128)(2,1)S(1)}, bf16[96,576]{1,0:T(8,128)(2,1)}, u32[]{:S(2)}, u32[]{:S(2)}) collective-permute-start(bf16[96,576]{1,0:T(8,128)(2,1)S(1)} %get-tuple-element.251), channel_id=1, source_target_pairs={{0,0},{1,2},{2,4},{3,6},{4,1},{5,3},{6,5},{7,7},{8,8},{9,10},{10,1... | collective-permute-start | bytes 331784 | tf_op jit(solution)/shard_map/ppermute | solution.py:921
  278.5 13.9 %collective-permute-done.41 = bf16[96,576]{1,0:T(8,128)(2,1)} collective-permute-done((bf16[96,576]{1,0:T(8,128)(2,1)S(1)}, bf16[96,576]{1,0:T(8,128)(2,1)}, u32[]{:S(2)}, u32[]{:S(2)}) %collective-permute-start.41) | collective-permute-done | bytes 110624 | tf_op jit(solution)/shard_map/ppermute | solution.py:921
  294.1 2.2 fusion.2
  (193 shorter events, 61.0 us)
Async XLA Ops:
  7.2 54.6 %all-gather.5.cloned.1.call-start = ((), (), s32[]{:S(2)}) async-start(), calls=%async_computation.4 | async-start | bytes 1720320 | tf_op jit(solution)/shard_map/all_gather | solution.py:820
  7.2 22.8 %collective-permute-start.3 = (bf16[512,768]{1,0:T(8,128)(2,1)}, bf16[512,768]{1,0:T(8,128)(2,1)S(1)}, u32[]{:S(2)}, u32[]{:S(2)}) collective-permute-start(bf16[512,768]{1,0:T(8,128)(2,1)} %param.18), channel_id=1, source_target_pairs={{0,4},{4,0},{1,5},{5,1},{2,6},{6,2},{3,7},{7,3},{8,12},{12,8},{9,1... | collective-permute-start | bytes 2359304 | tf_op jit(solution)/shard_map/ppermute | solution.py:808
  8.0 13.2 %collective-permute-start = (bf16[512,768]{1,0:T(8,128)(2,1)}, bf16[512,768]{1,0:T(8,128)(2,1)S(1)}, u32[]{:S(2)}, u32[]{:S(2)}) collective-permute-start(bf16[512,768]{1,0:T(8,128)(2,1)} %param.18), channel_id=1, source_target_pairs={{1,0},{2,1},{3,2},{4,5},{5,6},{6,7},{9,8},{10,9},{11,10},{12,13},{... | collective-permute-start | bytes 2359304 | tf_op jit(solution)/shard_map/ppermute | solution.py:814
  11.2 8.9 %collective-permute-start.1 = (s32[1,2048]{1,0:T(1,128)}, s32[1,2048]{1,0:T(1,128)S(1)}, u32[]{:S(2)}, u32[]{:S(2)}) collective-permute-start(s32[1,2048]{1,0:T(1,128)} %param.28), channel_id=1, source_target_pairs={{0,4},{4,0},{1,5},{5,1},{2,6},{6,2},{3,7},{7,3},{8,12},{12,8},{9,1... | collective-permute-start | bytes 24584 | tf_op jit(solution)/shard_map/ppermute | solution.py:808
  21.2 25.6 %collective-permute-start.6 = (bf16[96,576]{1,0:T(8,128)(2,1)S(1)}, bf16[96,576]{1,0:T(8,128)(2,1)S(1)}, u32[]{:S(2)}, u32[]{:S(2)}) collective-permute-start(bf16[96,576]{1,0:T(8,128)(2,1)S(1)} %pad_maximum_fusion), channel_id=1, source_target_pairs={{4,0},{6,1},{0,2},{2,3},{5,4},{7,5},{1,6},{3,7},{12,8},{14,9},{8,1... | collective-permute-start | bytes 331784 | tf_op jit(solution)/shard_map/ppermute | solution.py:821
  21.2 25.6 %collective-permute-start.5 = (bf16[96,576]{1,0:T(8,128)(2,1)S(1)}, bf16[96,576]{1,0:T(8,128)(2,1)}, u32[]{:S(2)}, u32[]{:S(2)}) collective-permute-start(bf16[96,576]{1,0:T(8,128)(2,1)S(1)} %pad_maximum_fusion), channel_id=1, source_target_pairs={{0,0},{2,1},{4,2},{6,3},{1,4},{3,5},{5,6},{7,7},{8,8},{10,9},{12,1... | collective-permute-start | bytes 331784 | tf_op jit(solution)/shard_map/ppermute | solution.py:821
  25.5 28.3 %collective-permute-start.4 = (bf16[512,768]{1,0:T(8,128)(2,1)S(1)}, bf16[512,768]{1,0:T(8,128)(2,1)S(1)}, u32[]{:S(2)}, u32[]{:S(2)}) collective-permute-start(bf16[512,768]{1,0:T(8,128)(2,1)S(1)} %collective-permute-done), channel_id=1, source_target_pairs={{0,4},{4,0},{1,5},{5,1},{2,6},{6,2},{3,7},{7,3},{8,12},{12,8},{9,1... | collective-permute-start | bytes 2359304 | tf_op jit(solution)/shard_map/ppermute | solution.py:808
  25.6 32.6 %collective-permute-start.2 = (bf16[512,768]{1,0:T(8,128)(2,1)S(1)}, bf16[512,768]{1,0:T(8,128)(2,1)}, u32[]{:S(2)}, u32[]{:S(2)}) collective-permute-start(bf16[512,768]{1,0:T(8,128)(2,1)S(1)} %collective-permute-done), channel_id=1, source_target_pairs={{1,0},{2,1},{5,6},{6,7},{9,8},{10,9},{13,14},{14,15},{17,16},{18,1... | collective-permute-start | bytes 2359304 | tf_op jit(solution)/shard_map/ppermute | solution.py:822
  29.5 100.3 %all-gather.7.cloned.1.call-start = ((), (), s32[]{:S(2)}) async-start(), calls=%async_computation.5 | async-start | bytes 12386304 | tf_op jit(solution)/shard_map/all_gather | solution.py:846
  30.0 9.3 %collective-permute-start.7 = (f32[32,3]{0,1:T(4,128)S(1)}, f32[32,3]{0,1:T(4,128)S(1)}, u32[]{:S(2)}, u32[]{:S(2)}) collective-permute-start(f32[32,3]{0,1:T(4,128)S(1)} %copy-done.30), channel_id=1, source_target_pairs={{0,0},{2,1},{4,2},{6,3},{1,4},{3,5},{5,6},{7,7},{8,8},{10,9},{12,1... | collective-permute-start | bytes 1160 | tf_op jit(solution)/shard_map/ppermute | solution.py:818
  61.8 176.9 %reduce-scatter.3.cloned.1.call-start = ((), (), s32[]{:S(2)}) async-start(), calls=%async_computation.2 | async-start | bytes 12386304 | tf_op jit(solution)/shard_map/reduce_scatter | solution.py:875
  67.1 23.4 %collective-permute-start.14 = (bf16[512,768]{1,0:T(8,128)(2,1)S(1)}, bf16[512,768]{1,0:T(8,128)(2,1)S(1)}, u32[]{:S(2)}, u32[]{:S(2)}) collective-permute-start(bf16[512,768]{1,0:T(8,128)(2,1)S(1)} %get-tuple-element.249), channel_id=1, source_target_pairs={{1,0},{0,1},{6,7},{7,6},{9,8},{8,9},{14,15},{15,14},{17,16},{16,17... | collective-permute-start | bytes 2359304 | tf_op jit(solution)/shard_map/ppermute | solution.py:844
  90.6 5.1 %collective-permute-start.16 = (bf16[512,768]{1,0:T(8,128)(2,1)S(1)}, bf16[512,768]{1,0:T(8,128)(2,1)S(1)}, u32[]{:S(2)}, u32[]{:S(2)}) collective-permute-start(bf16[512,768]{1,0:T(8,128)(2,1)S(1)} %collective-permute-done.14), channel_id=1, source_target_pairs={{0,4},{4,0},{1,5},{5,1},{2,6},{6,2},{3,7},{7,3},{8,12},{12,8},{9,1... | collective-permute-start | bytes 2359304 | tf_op jit(solution)/shard_map/ppermute | solution.py:808
  93.6 25.2 %collective-permute-start.20 = (bf16[512,768]{1,0:T(8,128)(2,1)S(1)}, bf16[512,768]{1,0:T(8,128)(2,1)S(1)}, u32[]{:S(2)}, u32[]{:S(2)}) collective-permute-start(bf16[512,768]{1,0:T(8,128)(2,1)S(1)} %copy-done.17), channel_id=1, source_target_pairs={{0,0},{2,1},{4,2},{6,3},{1,4},{3,5},{5,6},{7,7},{8,8},{10,9},{12,1... | collective-permute-start | bytes 2359304 | tf_op jit(solution)/shard_map/ppermute | solution.py:852
  116.0 6.7 %collective-permute-start.18 = (bf16[192,512]{1,0:T(8,128)(2,1)}, bf16[192,512]{1,0:T(8,128)(2,1)S(1)}, u32[]{:S(2)}, u32[]{:S(2)}) collective-permute-start(bf16[192,512]{1,0:T(8,128)(2,1)} %get-tuple-element.139.refs_6_), channel_id=1, source_target_pairs={{0,1},{1,0},{2,3},{3,2},{4,5},{5,4},{6,7},{7,6},{8,9},{9,8},{10,11... | collective-permute-start | bytes 589832 | tf_op jit(solution)/shard_map/ppermute | solution.py:856
  116.4 11.0 %collective-permute-start.19 = (bf16[192,512]{1,0:T(8,128)(2,1)}, bf16[192,512]{1,0:T(8,128)(2,1)S(1)}, u32[]{:S(2)}, u32[]{:S(2)}) collective-permute-start(bf16[192,512]{1,0:T(8,128)(2,1)} %get-tuple-element.140.refs_7_), channel_id=1, source_target_pairs={{0,5},{1,4},{2,7},{3,6},{4,1},{5,0},{6,3},{7,2},{8,13},{9,12},{10,... | collective-permute-start | bytes 589832 | tf_op jit(solution)/shard_map/ppermute | solution.py:856
  154.9 142.8 %reduce-scatter.5.cloned.1.call-start = ((), (), s32[]{:S(2)}) async-start(), calls=%async_computation.3 | async-start | bytes 1720320 | tf_op jit(solution)/shard_map/reduce_scatter | solution.py:896
  156.0 6.2 %collective-permute-start.22 = (bf16[192,512]{1,0:T(8,128)(2,1)S(1)}, bf16[192,512]{1,0:T(8,128)(2,1)S(1)}, u32[]{:S(2)}, u32[]{:S(2)}) collective-permute-start(bf16[192,512]{1,0:T(8,128)(2,1)S(1)} %copy-done.20), channel_id=1, source_target_pairs={{0,1},{1,0},{2,3},{3,2},{4,5},{5,4},{6,7},{7,6},{8,9},{9,8},{10,11... | collective-permute-start | bytes 589832 | tf_op jit(solution)/shard_map/ppermute | solution.py:865
  156.3 10.6 %collective-permute-start.23 = (bf16[192,512]{1,0:T(8,128)(2,1)S(1)}, bf16[192,512]{1,0:T(8,128)(2,1)S(1)}, u32[]{:S(2)}, u32[]{:S(2)}) collective-permute-start(bf16[192,512]{1,0:T(8,128)(2,1)S(1)} %copy-done.18), channel_id=1, source_target_pairs={{0,5},{1,4},{2,7},{3,6},{4,1},{5,0},{6,3},{7,2},{8,13},{9,12},{10,... | collective-permute-start | bytes 589832 | tf_op jit(solution)/shard_map/ppermute | solution.py:865
  166.9 48.3 %collective-permute-start.24 = (bf16[2,512,768]{2,1,0:T(8,128)(2,1)}, bf16[2,512,768]{2,1,0:T(8,128)(2,1)S(1)}, u32[]{:S(2)}, u32[]{:S(2)}) collective-permute-start(bf16[2,512,768]{2,1,0:T(8,128)(2,1)} %get-tuple-element.157), channel_id=1, source_target_pairs={{0,0},{1,2},{2,4},{3,6},{4,1},{5,3},{6,5},{7,7},{8,8},{9,10},{10,1... | collective-permute-start | bytes 4718600 | tf_op jit(solution)/shard_map/ppermute | solution.py:873
  215.2 23.5 %collective-permute-start.29 = (bf16[512,768]{1,0:T(8,128)(2,1)}, bf16[512,768]{1,0:T(8,128)(2,1)}, u32[]{:S(2)}, u32[]{:S(2)}) collective-permute-start(bf16[512,768]{1,0:T(8,128)(2,1)} %get-tuple-element.178), channel_id=1, source_target_pairs={{0,4},{4,0},{1,5},{5,1},{2,6},{6,2},{3,7},{7,3},{8,12},{12,8},{9,1... | collective-permute-start | bytes 2359304 | tf_op jit(solution)/shard_map/ppermute | solution.py:808
  220.3 12.0 %collective-permute-start.27 = (bf16[512,768]{1,0:T(8,128)(2,1)}, bf16[512,768]{1,0:T(8,128)(2,1)S(1)}, u32[]{:S(2)}, u32[]{:S(2)}) collective-permute-start(bf16[512,768]{1,0:T(8,128)(2,1)} %add.126), channel_id=1, source_target_pairs={{0,1},{1,0},{7,6},{6,7},{8,9},{9,8},{15,14},{14,15},{16,17},{17,16... | collective-permute-start | bytes 2359304 | tf_op jit(solution)/shard_map/ppermute | solution.py:883
  241.1 17.8 %collective-permute-start.30 = (bf16[512,768]{1,0:T(8,128)(2,1)}, bf16[512,768]{1,0:T(8,128)(2,1)}, u32[]{:S(2)}, u32[]{:S(2)}) collective-permute-start(bf16[512,768]{1,0:T(8,128)(2,1)} %add_select_fusion), channel_id=1, source_target_pairs={{0,1},{1,2},{6,5},{7,6},{8,9},{9,10},{14,13},{15,14},{16,17},{17,1... | collective-permute-start | bytes 2359304 | tf_op jit(solution)/shard_map/ppermute | solution.py:899
  242.6 23.2 %collective-permute-start.28 = (bf16[512,768]{1,0:T(8,128)(2,1)}, bf16[512,768]{1,0:T(8,128)(2,1)}, u32[]{:S(2)}, u32[]{:S(2)}) collective-permute-start(bf16[512,768]{1,0:T(8,128)(2,1)} %get-tuple-element.177), channel_id=1, source_target_pairs={{0,4},{4,0},{1,5},{5,1},{2,6},{6,2},{3,7},{7,3},{8,12},{12,8},{9,1... | collective-permute-start | bytes 2359304 | tf_op jit(solution)/shard_map/ppermute | solution.py:808
  245.6 11.2 %collective-permute-start.31 = (bf16[2,96,576]{2,1,0:T(8,128)(2,1)}, bf16[2,96,576]{2,1,0:T(8,128)(2,1)}, u32[]{:S(2)}, u32[]{:S(2)}) collective-permute-start(bf16[2,96,576]{2,1,0:T(8,128)(2,1)} %get-tuple-element.180), channel_id=1, source_target_pairs={{0,8},{8,0},{16,24},{24,16},{1,9},{9,1},{17,25},{25,17},{2,10},{10... | collective-permute-start | bytes 663560 | tf_op jit(solution)/shard_map/ppermute | solution.py:763
  246.6 11.3 %collective-permute-start.32 = (bf16[2,96,576]{2,1,0:T(8,128)(2,1)}, bf16[2,96,576]{2,1,0:T(8,128)(2,1)}, u32[]{:S(2)}, u32[]{:S(2)}) collective-permute-start(bf16[2,96,576]{2,1,0:T(8,128)(2,1)} %get-tuple-element.182), channel_id=1, source_target_pairs={{0,16},{8,24},{16,0},{24,8},{1,17},{9,25},{17,1},{25,9},{2,18},{10... | collective-permute-start | bytes 663560 | tf_op jit(solution)/shard_map/ppermute | solution.py:763
  250.3 43.8 %collective-permute-start.25 = (bf16[512,768]{1,0:T(8,128)(2,1)}, bf16[512,768]{1,0:T(8,128)(2,1)}, u32[]{:S(2)}, u32[]{:S(2)}) collective-permute-start(bf16[512,768]{1,0:T(8,128)(2,1)} %get-tuple-element.159), channel_id=1, source_target_pairs={{0,4},{4,0},{1,5},{5,1},{2,6},{6,2},{3,7},{7,3},{8,12},{12,8},{9,1... | collective-permute-start | bytes 2359304 | tf_op jit(solution)/shard_map/ppermute | solution.py:808
  263.0 7.7 %collective-permute-start.40 = (bf16[96,576]{1,0:T(8,128)(2,1)S(1)}, bf16[96,576]{1,0:T(8,128)(2,1)S(1)}, u32[]{:S(2)}, u32[]{:S(2)}) collective-permute-start(bf16[96,576]{1,0:T(8,128)(2,1)S(1)} %slice_bitcast_fusion.2), channel_id=1, source_target_pairs={{0,8},{8,0},{16,24},{24,16},{1,9},{9,1},{17,25},{25,17},{2,10},{10... | collective-permute-start | bytes 331784 | tf_op jit(solution)/shard_map/ppermute | solution.py:763
  264.1 6.5 %collective-permute-start.39 = (bf16[96,576]{1,0:T(8,128)(2,1)S(1)}, bf16[96,576]{1,0:T(8,128)(2,1)S(1)}, u32[]{:S(2)}, u32[]{:S(2)}) collective-permute-start(bf16[96,576]{1,0:T(8,128)(2,1)S(1)} %slice_bitcast_fusion.3), channel_id=1, source_target_pairs={{0,16},{8,24},{16,0},{24,8},{1,17},{9,25},{17,1},{25,9},{2,18},{10... | collective-permute-start | bytes 331784 | tf_op jit(solution)/shard_map/ppermute | solution.py:763
  268.6 25.5 %collective-permute-start.35 = (bf16[512,768]{1,0:T(8,128)(2,1)}, bf16[512,768]{1,0:T(8,128)(2,1)}, u32[]{:S(2)}, u32[]{:S(2)}) collective-permute-start(bf16[512,768]{1,0:T(8,128)(2,1)} %select_add_fusion), channel_id=1, source_target_pairs={{0,1},{1,2},{2,3},{5,4},{6,5},{7,6},{8,9},{9,10},{10,11},{13,12},{... | collective-permute-start | bytes 2359304 | tf_op jit(solution)/shard_map/ppermute | solution.py:909
  270.7 7.8 %collective-permute-start.42 = (bf16[96,576]{1,0:T(8,128)(2,1)S(1)}, bf16[96,576]{1,0:T(8,128)(2,1)S(1)}, u32[]{:S(2)}, u32[]{:S(2)}) collective-permute-start(bf16[96,576]{1,0:T(8,128)(2,1)S(1)} %get-tuple-element.250), channel_id=1, source_target_pairs={{0,4},{1,6},{2,0},{3,2},{4,5},{5,7},{6,1},{7,3},{8,12},{9,14},{10,... | collective-permute-start | bytes 331784 | tf_op jit(solution)/shard_map/ppermute | solution.py:922
  272.6 19.7 %collective-permute-start.41 = (bf16[96,576]{1,0:T(8,128)(2,1)S(1)}, bf16[96,576]{1,0:T(8,128)(2,1)}, u32[]{:S(2)}, u32[]{:S(2)}) collective-permute-start(bf16[96,576]{1,0:T(8,128)(2,1)S(1)} %get-tuple-element.251), channel_id=1, source_target_pairs={{0,0},{1,2},{2,4},{3,6},{4,1},{5,3},{6,5},{7,7},{8,8},{9,10},{10,1... | collective-permute-start | bytes 331784 | tf_op jit(solution)/shard_map/ppermute | solution.py:921
  (46 other events, 412.4 us)
Sparse Core Ops, SparseCore 0:
  29.6 32.1 all-gather.4
  63.6 66.0 all-gather.6
  155.1 83.6 reduce-scatter.2
  249.5 31.0 reduce-scatter.4

commit v6 on v5

--- a/solution.py
+++ b/solution.py
@@ -10,6 +10,7 @@
 H = 12
 EPSILON = 1e-06
 MASKED = -1e30
+LOG2E = 1.4426950408889634
 TILE = 256
 AHEAD = 2
 BLOCKS = 8
@@ -61,7 +62,7 @@
     rows = lax.dot_general(
         bias_table, onehot, (((0,), (0,)), ((), ())), precision=lax.Precision.HIGHEST
     )
-    return rows[:, None, :], bucket[None, :]
+    return rows[:, None, :] * LOG2E, bucket[None, :]
 
 
 def bias_kernel(row_ref, out_ref):
@@ -106,6 +107,16 @@
     return end.reshape(1, length), full, most, least, clear
 
 
+def query_pair(queries):
+    scaled = queries.astype(f32) * LOG2E
+    high = scaled.astype(bf16)
+    return jnp.concatenate([high, (scaled - high.astype(f32)).astype(bf16)], axis=0)
+
+
+def key_pair(keys):
+    return jnp.concatenate([keys, keys], axis=0).T
+
+
 def token_parts(piece, gain, by_columns, heads):
     tokens = piece.astype(f32)
     inverse = lax.rsqrt(jnp.mean(tokens * tokens, axis=-1, keepdims=True) + EPSILON)
@@ -135,11 +146,11 @@
             jnp.maximum(state[h][0], jnp.max(current[h], axis=0, keepdims=True))
             for h in range(heads)
         ]
-        weights = [jnp.exp(current[h] - tops[h]) for h in range(heads)]
+        weights = [jnp.exp2(current[h] - tops[h]) for h in range(heads)]
         result = []
         for h in range(heads):
             top, total, mix = state[h]
-            scale = jnp.exp(top - tops[h])
+            scale = jnp.exp2(top - tops[h])
             total = total * scale + jnp.sum(weights[h], axis=0, keepdims=True)
             mix = mix * scale + dot(vt_ref[h, :, pl.ds(start, TILE)], weights[h].astype(bf16))
             result.append((tops[h], total, mix))
@@ -170,7 +181,7 @@
         qkv_ref, normed_ref, weight_ref, own_ref, top_ref, total_ref, mix_ref,
         qt_ref, k_ref, vt_ref, bias_held, scores_ref, rows_held, bias_sem,
     ) = refs[known + rows_in :]
-    heads, size, length = qt_ref.shape
+    heads, size, length = vt_ref.shape
     part_length = length // (known + 1)
     turn = pl.program_id(0)
     load = pltpu.make_async_copy(bias_ref, bias_held, bias_sem)
@@ -194,8 +205,8 @@
             qkv_ref[i] = qkv
             places = pl.ds(pl.multiple_of(slot_ref[i] * part_length, TILE), part_length)
             for h in range(heads):
-                qt_ref[h, :, places] = qkv[h]
-                k_ref[h, places, :] = qkv[heads + h].T
+                qt_ref[h, :, places] = query_pair(qkv[h])
+                k_ref[h, places, :] = key_pair(qkv[heads + h])
                 vt_ref[h, :, places] = qkv[2 * heads + h]
         load.wait()
 
@@ -223,7 +234,7 @@
         lse_ref, qkv_ref, normed_ref,
         qt_ref, k_ref, vt_ref, bias_held, scores_ref, held_ref, bias_sem,
     ) = refs[9 + parts :]
-    heads, size, length = qt_ref.shape
+    heads, size, length = vt_ref.shape
     count = length // TILE
     each = count // parts
     part_length = length // parts
@@ -240,8 +251,8 @@
             source = before_ref.at[i] if i < parts - 1 else qkv_ref.at[0]
             places = pl.ds(pl.multiple_of(slot_ref[i] * part_length, TILE), part_length)
             for h in range(heads):
-                qt_ref[h, :, places] = source[h]
-                k_ref[h, places, :] = source[heads + h].T
+                qt_ref[h, :, places] = query_pair(source[h])
+                k_ref[h, places, :] = key_pair(source[heads + h])
                 vt_ref[h, :, places] = source[2 * heads + h]
         load.wait()
 
@@ -267,7 +278,7 @@
     inner = pl.ds(pl.multiple_of(lax.rem(query, each) * TILE, TILE), TILE)
     mixes = [(mix * (1.0 / total)).astype(bf16) for _, total, mix in state]
     for h, (top, total, _) in enumerate(state):
-        lse_ref[h] = top + jnp.log(total)
+        lse_ref[h] = top + jnp.log(total) * LOG2E
     for r in range(parts):
 
         @pl.when(turn == r)
@@ -282,8 +293,8 @@
 
 def sequence_held(heads, size, length, bias):
     return [
-        pltpu.VMEM((heads, size, length), bf16),
-        pltpu.VMEM((heads, length, size), bf16),
+        pltpu.VMEM((heads, 2 * size, length), bf16),
+        pltpu.VMEM((heads, length, 2 * size), bf16),
         pltpu.VMEM((heads, size, length), bf16),
         pltpu.VMEM(bias.shape, f32),
         pltpu.VMEM((2, heads, TILE, TILE), f32),
@@ -362,7 +373,7 @@
     qkv_ref = [qkv_early.at[i] for i in range(parts - 1)] + [qkv_late.at[0]]
     (
         dqkv_ref, band_out,
-        qt_ref, kt_ref, vt_ref, got_ref,
+        qt_ref, kt_ref, vt_ref, got_ref, pair_ref,
         dqt_acc, dk_acc, dv_acc, delta_ref, band_ref, bias_held, bias_sem, band_sem,
     ) = refs[3 * parts + 6 :]
     heads, size, length = qt_ref.shape
@@ -385,6 +396,7 @@
             places = pl.ds(pl.multiple_of(slot_ref[i] * part_length, TILE), part_length)
             for h in every:
                 qt_ref[h, :, places] = qkv_ref[i][h]
+                pair_ref[h, :, places] = query_pair(qkv_ref[i][h])
                 kt_ref[h, :, places] = qkv_ref[i][heads + h]
                 vt_ref[h, :, places] = qkv_ref[i][2 * heads + h]
         for turn in range(parts):
@@ -402,18 +414,18 @@
     dk_acc[...] = jnp.zeros_like(dk_acc)
     dv_acc[...] = jnp.zeros_like(dv_acc)
     kt = [kt_ref[h, :, key_cols] for h in every]
-    k = [tile.T for tile in kt]
+    k = [key_pair(tile) for tile in kt]
     v = [vt_ref[h, :, key_cols].T for h in every]
 
     def step(query, masked):
         cols = pl.ds(pl.multiple_of(query * TILE, TILE), TILE)
         place = key - query + count - 1
-        scores = [dot(k[h], qt_ref[h, :, cols]) + bias_held[h, place] for h in every]
+        scores = [dot(k[h], pair_ref[h, :, cols]) + bias_held[h, place] for h in every]
         if masked:
             keep = lax.broadcasted_iota(jnp.int32, (TILE, TILE), 0) + key * TILE < end_ref[:, cols]
             scores = [jnp.where(keep, tile, MASKED) for tile in scores]
         grad_weights = [dot(v[h], got_ref[h, :, cols]) for h in every]
-        weights = [jnp.exp(scores[h] - lse_ref[h, :, cols]) for h in every]
+        weights = [jnp.exp2(scores[h] - lse_ref[h, :, cols]) for h in every]
         grad_scores = [weights[h] * (grad_weights[h] - delta_ref[h, :, cols]) for h in every]
         for h in every:
             band_ref[h, place] += grad_scores[h]
@@ -553,6 +565,7 @@
         out_shape=outs + [shape(*bias.shape, kind=f32)],
         scratch_shapes=[by_columns] * 4
         + [
+            pltpu.VMEM((heads, 2 * size, length), bf16),
             pltpu.VMEM((heads, size, length), f32),
             pltpu.VMEM((heads, size, TILE), f32),
             pltpu.VMEM((heads, size, TILE), f32),

time: 308 us -> 308 us (level)
  transfers between devices with their start and end apart: 47 -> 47, of which waited for: 21 -> 21; matrix products, arithmetic and copies ran while one was open for 11% -> 11% of each run, Pallas kernels for 34% -> 33%
where the time goes in v6:
time: 308 us; the launch traced here: 307 us
  Pallas kernels  126 us (41%)
  waiting for transfers between devices  67.1 us (22%)
  starting transfers between devices  59.3 us (19%)
  other arithmetic  26.4 us (9%)
  between operations  14.4 us (5%)
  local copies, waits for them, and re-layouts  13.3 us (4%)
    pallas_call x1, Pallas kernels, attend_backward(): pl.pallas_call(backward_kernel, grid=(length // TILE,), in_specs=[smem] *...  42.7 us
    pallas_call x1, Pallas kernels, middle(): pl.pallas_call(middle_kernel, in_specs=[smem] + [whole(a.shape) for a in...  25 us
    pallas_call x1, Pallas kernels, attend_early(): pl.pallas_call(early_kernel, grid=((parts - 1) * part_length // TILE,), i...  21.2 us
    pallas_call x1, Pallas kernels, attend_late(): pl.pallas_call(late_kernel, grid=(length // TILE,), in_specs=[smem] * 5 +...  18.6 us
    ppermute x9, starting transfers between devices, swap(): return lax.ppermute(value, 'core', SWAP)  14.7 us
    ppermute x1, waiting for transfers between devices, body(): lax.ppermute(jnp.where(lower, low, high), LINE, back(weight_routes[0]))  13.9 us
    pallas_call x1, Pallas kernels, attend_sums(): pl.pallas_call(sums_kernel, in_specs=[smem] * 2 + [whole(a.shape) for a i...  12.1 us
    ppermute x3, waiting for transfers between devices, body(): lax.ppermute(ots[r], LINE, rounds[r])  8.53 us
  transfers between devices with their start and end apart: 47, of which 21 were waited for; matrix products, arithmetic and copies ran while one was open for 11% of the time, Pallas kernels for 33%

profile of v6, /device:TPU:9, one launch (start us, length us, event | category | flops | bytes accessed | tf_op | source)
XLA Modules:
  0.0 306.9 jit_solution(7112921695937175791)
XLA Ops:
  8.0 3.2 %collective-permute-start = (bf16[512,768]{1,0:T(8,128)(2,1)}, bf16[512,768]{1,0:T(8,128)(2,1)S(1)}, u32[]{:S(2)}, u32[]{:S(2)}) collective-permute-start(bf16[512,768]{1,0:T(8,128)(2,1)} %param.18), channel_id=1, source_target_pairs={{1,0},{2,1},{3,2},{4,5},{5,6},{6,7},{9,8},{10,9},{11,10},{12,13},{... | collective-permute-start | bytes 2359304 | tf_op jit(solution)/shard_map/ppermute | solution.py:827
  21.2 4.3 %collective-permute-start.5 = (bf16[96,576]{1,0:T(8,128)(2,1)S(1)}, bf16[96,576]{1,0:T(8,128)(2,1)}, u32[]{:S(2)}, u32[]{:S(2)}) collective-permute-start(bf16[96,576]{1,0:T(8,128)(2,1)S(1)} %pad_maximum_fusion), channel_id=1, source_target_pairs={{0,0},{2,1},{4,2},{6,3},{1,4},{3,5},{5,6},{7,7},{8,8},{10,9},{12,1... | collective-permute-start | bytes 331784 | tf_op jit(solution)/shard_map/ppermute | solution.py:834
  25.6 3.9 %collective-permute-start.2 = (bf16[512,768]{1,0:T(8,128)(2,1)S(1)}, bf16[512,768]{1,0:T(8,128)(2,1)}, u32[]{:S(2)}, u32[]{:S(2)}) collective-permute-start(bf16[512,768]{1,0:T(8,128)(2,1)S(1)} %collective-permute-done), channel_id=1, source_target_pairs={{1,0},{2,1},{5,6},{6,7},{9,8},{10,9},{13,14},{14,15},{17,16},{18,1... | collective-permute-start | bytes 2359304 | tf_op jit(solution)/shard_map/ppermute | solution.py:835
  33.6 5.7 %collective-permute-done.7 = f32[32,3]{0,1:T(4,128)S(1)} collective-permute-done((f32[32,3]{0,1:T(4,128)S(1)}, f32[32,3]{0,1:T(4,128)S(1)}, u32[]{:S(2)}, u32[]{:S(2)}) %collective-permute-start.7) | collective-permute-done | bytes 416 | tf_op jit(solution)/shard_map/ppermute | solution.py:831
  40.2 6.6 %bias_tiles.1.refs_13_.refs_8_ = f32[3,10,256,256]{3,2,1,0:T(8,128)} custom-call(f32[3,1,2816]{2,1,0:T(1,128)} %mul.88.row_ref), custom_call_target="tpu_custom_call" | custom-call | flops 6000000000 | tf_op jit(solution)/shard_map/bias_tiles/pallas_call | solution.py:84
  58.2 3.6 %all-gather.5.cloned.1.call-done = bf16[384,1792]{1,0:T(8,128)(2,1)} async-done(((bf16[96,1792]{1,0:T(8,128)(2,1)}), bf16[384,1792]{1,0:T(8,128)(2,1)}) %all-gather.5.cloned.1.call-update) | async-done | bytes 1376272 | tf_op jit(solution)/shard_map/all_gather | solution.py:833
  62.8 2.1 collective-permute-done.15
  65.0 2.1 broadcast_select_fusion.2
  67.9 21.2 %attend_early.1 = (bf16[3,9,64,512]{3,2,1,0:T(8,128)(2,1)}, bf16[3,512,768]{2,1,0:T(8,128)(2,1)}, bf16[576,768]{1,0:T(8,128)(2,1)}, bf16[512,768]{1,0:T(8,128)(2...) custom-call(s32[8]{0:T(128)} %copy-done.16, s32[8]{0:T(128)} %copy-done.15, ...), custom_call_target="tpu_custom_call" | custom-call | flops 20000000000 | tf_op jit(solution)/shard_map/attend_early/pallas_call | solution.py:323
  89.0 3.0 collective-permute-start.16
  92.1 2.6 collective-permute-start.20
  95.6 18.6 %attend_late.1 = (bf16[192,512]{1,0:T(8,128)(2,1)}, bf16[192,512]{1,0:T(8,128)(2,1)}, bf16[192,512]{1,0:T(8,128)(2,1)}, bf16[192,512]{1,0:T(8,128)(2,1)}, f32[3,...) custom-call(s32[8]{0:T(128)} %copy-done.16, s32[8]{0:T(128)} %copy-done.15, ...), custom_call_target="tpu_custom_call" | custom-call | flops 15000000512 | tf_op jit(solution)/shard_map/attend_late/pallas_call | solution.py:353
  117.6 3.7 %collective-permute-done.18.refs_2_ = bf16[192,512]{1,0:T(8,128)(2,1)S(1)} collective-permute-done((bf16[192,512]{1,0:T(8,128)(2,1)}, bf16[192,512]{1,0:T(8,128)(2,1)S(1)}, u32[]{:S(2)}, u32[]{:S(2)}) %collective-permute-start.18) | collective-permute-done | bytes 196640 | tf_op jit(solution)/shard_map/ppermute | solution.py:869
  121.4 4.8 %collective-permute-done.19.refs_3_ = bf16[192,512]{1,0:T(8,128)(2,1)S(1)} collective-permute-done((bf16[192,512]{1,0:T(8,128)(2,1)}, bf16[192,512]{1,0:T(8,128)(2,1)S(1)}, u32[]{:S(2)}, u32[]{:S(2)}) %collective-permute-start.19) | collective-permute-done | bytes 196640 | tf_op jit(solution)/shard_map/ppermute | solution.py:869
  126.2 3.6 %all-gather.7.cloned.1.call-done = bf16[32,96,1792]{2,1,0:T(8,128)(2,1)} async-done(((bf16[4,96,1792]{2,1,0:T(8,128)(2,1)}), bf16[32,96,1792]{2,1,0:T(8,128)(2,1)}) %all-gather.7.cloned.1.call-update) | async-done | bytes 11010064 | tf_op jit(solution)/shard_map/all_gather | solution.py:859
  129.8 25.0 %middle.1 = (bf16[2,512,768]{2,1,0:T(8,128)(2,1)}, f32[1,768]{1,0:T(1,128)}, bf16[192,512]{1,0:T(8,128)(2,1)}, bf16[192,512]{1,0:T(8,128)(2,1)}, bf16[192,512]{1...) custom-call(s32[4]{0:T(128)} %iota_xor_fusion.turn_ref, ...), custom_call_target="tpu_custom_call" | custom-call | tf_op jit(solution)/shard_map/middle/pallas_call | solution.py:715
  158.5 3.8 %collective-permute-done.22.refs_2_ = bf16[192,512]{1,0:T(8,128)(2,1)S(1)} collective-permute-done((bf16[192,512]{1,0:T(8,128)(2,1)S(1)}, bf16[192,512]{1,0:T(8,128)(2,1)S(1)}, u32[]{:S(2)}, u32[]{:S(2)}) %collective-permute-start.22) | collective-permute-done | bytes 196640 | tf_op jit(solution)/shard_map/ppermute | solution.py:878
  162.3 4.6 %collective-permute-done.23.refs_3_ = bf16[192,512]{1,0:T(8,128)(2,1)S(1)} collective-permute-done((bf16[192,512]{1,0:T(8,128)(2,1)S(1)}, bf16[192,512]{1,0:T(8,128)(2,1)S(1)}, u32[]{:S(2)}, u32[]{:S(2)}) %collective-permute-start.23) | collective-permute-done | bytes 196640 | tf_op jit(solution)/shard_map/ppermute | solution.py:878
  166.9 4.1 %collective-permute-start.24 = (bf16[2,512,768]{2,1,0:T(8,128)(2,1)}, bf16[2,512,768]{2,1,0:T(8,128)(2,1)S(1)}, u32[]{:S(2)}, u32[]{:S(2)}) collective-permute-start(bf16[2,512,768]{2,1,0:T(8,128)(2,1)} %get-tuple-element.157), channel_id=1, source_target_pairs={{0,0},{1,2},{2,4},{3,6},{4,1},{5,3},{6,5},{7,7},{8,8},{9,10},{10,1... | collective-permute-start | bytes 4718600 | tf_op jit(solution)/shard_map/ppermute | solution.py:886
  171.1 42.7 %attend_backward.1 = (bf16[512,768]{1,0:T(8,128)(2,1)}, bf16[512,768]{1,0:T(8,128)(2,1)}, bf16[512,768]{1,0:T(8,128)(2,1)}, bf16[512,768]{1,0:T(8,128)(2,1)}, bf...) custom-call(s32[8]{0:T(128)} %convert_reduce_fusion.2.least_ref, s32[8]{0:T(128)} %convert_reduce_fusion.1.clear_ref, ...), custom_call_target="tpu_custom_call" | custom-call | flops 44999999488 | tf_op jit(solution)/shard_map/attend_backward/pallas_call | solution.py:560
  214.3 2.3 collective-permute-done.26
  216.6 2.2 add.126
  219.6 12.1 %attend_sums.1 = (f32[16,128]{1,0:T(8,128)}, bf16[2,96,576]{2,1,0:T(8,128)(2,1)}, bf16[2,96,576]{2,1,0:T(8,128)(2,1)}, bf16[2,96,576]{2,1,0:T(8,128)(2,1)}, bf16[2,96,576]{2,1,0:T(8,128)(2,1)}) custom-call(s32[1]{0:T(128)} %bitcast.5.group_ref, s32[8]{0:T(128)} %multiply_add_fusion.place_ref, bf16[4,576,512]{2,1,0:T(8,128)(2,1)} %get-tuple-element.164.refs_0_, ...), custom_call_target="tpu_custom_call" | custom-call | flops 12000000000 | tf_op jit(solution)/shard_map/attend_sums/pallas_call | solution.py:591
  231.7 7.0 %reduce-scatter.3.cloned.1.call-done = bf16[1,4,96,1792]{3,2,1,0:T(8,128)(2,1)} async-done(((bf16[8,4,96,1792]{3,2,1,0:T(8,128)(2,1)}), bf16[1,4,96,1792]{3,2,1,0:T(8,128)(2,1)}) %reduce-scatter.3.cloned.1.call-update) | async-done | bytes 1376272 | tf_op jit(solution)/shard_map/reduce_scatter | solution.py:888
  238.7 2.4 add_select_fusion
  242.6 2.8 collective-permute-start.28
  250.3 6.4 %collective-permute-start.25 = (bf16[512,768]{1,0:T(8,128)(2,1)}, bf16[512,768]{1,0:T(8,128)(2,1)}, u32[]{:S(2)}, u32[]{:S(2)}) collective-permute-start(bf16[512,768]{1,0:T(8,128)(2,1)} %get-tuple-element.159), channel_id=1, source_target_pairs={{0,4},{4,0},{1,5},{5,1},{2,6},{6,2},{3,7},{7,3},{8,12},{12,8},{9,1... | collective-permute-start | bytes 2359304 | tf_op jit(solution)/shard_map/ppermute | solution.py:821
  259.0 3.6 %collective-permute-done.36 = f32[16,128]{1,0:T(8,128)S(1)} collective-permute-done((f32[16,128]{1,0:T(8,128)S(1)}, f32[16,128]{1,0:T(8,128)S(1)}, u32[]{:S(2)}, u32[]{:S(2)}) %collective-permute-start.36) | collective-permute-done | bytes 8224 | tf_op jit(solution)/shard_map/ppermute | solution.py:901
  265.9 2.7 select_add_fusion
  272.6 4.5 %collective-permute-start.41 = (bf16[96,576]{1,0:T(8,128)(2,1)S(1)}, bf16[96,576]{1,0:T(8,128)(2,1)}, u32[]{:S(2)}, u32[]{:S(2)}) collective-permute-start(bf16[96,576]{1,0:T(8,128)(2,1)S(1)} %get-tuple-element.251), channel_id=1, source_target_pairs={{0,0},{1,2},{2,4},{3,6},{4,1},{5,3},{6,5},{7,7},{8,8},{9,10},{10,1... | collective-permute-start | bytes 331784 | tf_op jit(solution)/shard_map/ppermute | solution.py:934
  278.5 13.9 %collective-permute-done.41 = bf16[96,576]{1,0:T(8,128)(2,1)} collective-permute-done((bf16[96,576]{1,0:T(8,128)(2,1)S(1)}, bf16[96,576]{1,0:T(8,128)(2,1)}, u32[]{:S(2)}, u32[]{:S(2)}) %collective-permute-start.41) | collective-permute-done | bytes 110624 | tf_op jit(solution)/shard_map/ppermute | solution.py:934
  294.1 2.2 fusion.2
  (193 shorter events, 61.0 us)
Async XLA Ops:
  7.2 54.6 %all-gather.5.cloned.1.call-start = ((), (), s32[]{:S(2)}) async-start(), calls=%async_computation.4 | async-start | bytes 1720320 | tf_op jit(solution)/shard_map/all_gather | solution.py:833
  7.2 22.8 %collective-permute-start.3 = (bf16[512,768]{1,0:T(8,128)(2,1)}, bf16[512,768]{1,0:T(8,128)(2,1)S(1)}, u32[]{:S(2)}, u32[]{:S(2)}) collective-permute-start(bf16[512,768]{1,0:T(8,128)(2,1)} %param.18), channel_id=1, source_target_pairs={{0,4},{4,0},{1,5},{5,1},{2,6},{6,2},{3,7},{7,3},{8,12},{12,8},{9,1... | collective-permute-start | bytes 2359304 | tf_op jit(solution)/shard_map/ppermute | solution.py:821
  8.0 13.2 %collective-permute-start = (bf16[512,768]{1,0:T(8,128)(2,1)}, bf16[512,768]{1,0:T(8,128)(2,1)S(1)}, u32[]{:S(2)}, u32[]{:S(2)}) collective-permute-start(bf16[512,768]{1,0:T(8,128)(2,1)} %param.18), channel_id=1, source_target_pairs={{1,0},{2,1},{3,2},{4,5},{5,6},{6,7},{9,8},{10,9},{11,10},{12,13},{... | collective-permute-start | bytes 2359304 | tf_op jit(solution)/shard_map/ppermute | solution.py:827
  11.2 8.9 %collective-permute-start.1 = (s32[1,2048]{1,0:T(1,128)}, s32[1,2048]{1,0:T(1,128)S(1)}, u32[]{:S(2)}, u32[]{:S(2)}) collective-permute-start(s32[1,2048]{1,0:T(1,128)} %param.28), channel_id=1, source_target_pairs={{0,4},{4,0},{1,5},{5,1},{2,6},{6,2},{3,7},{7,3},{8,12},{12,8},{9,1... | collective-permute-start | bytes 24584 | tf_op jit(solution)/shard_map/ppermute | solution.py:821
  21.2 25.6 %collective-permute-start.6 = (bf16[96,576]{1,0:T(8,128)(2,1)S(1)}, bf16[96,576]{1,0:T(8,128)(2,1)S(1)}, u32[]{:S(2)}, u32[]{:S(2)}) collective-permute-start(bf16[96,576]{1,0:T(8,128)(2,1)S(1)} %pad_maximum_fusion), channel_id=1, source_target_pairs={{4,0},{6,1},{0,2},{2,3},{5,4},{7,5},{1,6},{3,7},{12,8},{14,9},{8,1... | collective-permute-start | bytes 331784 | tf_op jit(solution)/shard_map/ppermute | solution.py:834
  21.2 25.6 %collective-permute-start.5 = (bf16[96,576]{1,0:T(8,128)(2,1)S(1)}, bf16[96,576]{1,0:T(8,128)(2,1)}, u32[]{:S(2)}, u32[]{:S(2)}) collective-permute-start(bf16[96,576]{1,0:T(8,128)(2,1)S(1)} %pad_maximum_fusion), channel_id=1, source_target_pairs={{0,0},{2,1},{4,2},{6,3},{1,4},{3,5},{5,6},{7,7},{8,8},{10,9},{12,1... | collective-permute-start | bytes 331784 | tf_op jit(solution)/shard_map/ppermute | solution.py:834
  25.5 28.3 %collective-permute-start.4 = (bf16[512,768]{1,0:T(8,128)(2,1)S(1)}, bf16[512,768]{1,0:T(8,128)(2,1)S(1)}, u32[]{:S(2)}, u32[]{:S(2)}) collective-permute-start(bf16[512,768]{1,0:T(8,128)(2,1)S(1)} %collective-permute-done), channel_id=1, source_target_pairs={{0,4},{4,0},{1,5},{5,1},{2,6},{6,2},{3,7},{7,3},{8,12},{12,8},{9,1... | collective-permute-start | bytes 2359304 | tf_op jit(solution)/shard_map/ppermute | solution.py:821
  25.6 32.6 %collective-permute-start.2 = (bf16[512,768]{1,0:T(8,128)(2,1)S(1)}, bf16[512,768]{1,0:T(8,128)(2,1)}, u32[]{:S(2)}, u32[]{:S(2)}) collective-permute-start(bf16[512,768]{1,0:T(8,128)(2,1)S(1)} %collective-permute-done), channel_id=1, source_target_pairs={{1,0},{2,1},{5,6},{6,7},{9,8},{10,9},{13,14},{14,15},{17,16},{18,1... | collective-permute-start | bytes 2359304 | tf_op jit(solution)/shard_map/ppermute | solution.py:835
  29.5 100.3 %all-gather.7.cloned.1.call-start = ((), (), s32[]{:S(2)}) async-start(), calls=%async_computation.5 | async-start | bytes 12386304 | tf_op jit(solution)/shard_map/all_gather | solution.py:859
  30.0 9.3 %collective-permute-start.7 = (f32[32,3]{0,1:T(4,128)S(1)}, f32[32,3]{0,1:T(4,128)S(1)}, u32[]{:S(2)}, u32[]{:S(2)}) collective-permute-start(f32[32,3]{0,1:T(4,128)S(1)} %copy-done.30), channel_id=1, source_target_pairs={{0,0},{2,1},{4,2},{6,3},{1,4},{3,5},{5,6},{7,7},{8,8},{10,9},{12,1... | collective-permute-start | bytes 1160 | tf_op jit(solution)/shard_map/ppermute | solution.py:831
  61.8 176.9 %reduce-scatter.3.cloned.1.call-start = ((), (), s32[]{:S(2)}) async-start(), calls=%async_computation.2 | async-start | bytes 12386304 | tf_op jit(solution)/shard_map/reduce_scatter | solution.py:888
  67.1 21.9 %collective-permute-start.14 = (bf16[512,768]{1,0:T(8,128)(2,1)S(1)}, bf16[512,768]{1,0:T(8,128)(2,1)S(1)}, u32[]{:S(2)}, u32[]{:S(2)}) collective-permute-start(bf16[512,768]{1,0:T(8,128)(2,1)S(1)} %get-tuple-element.249), channel_id=1, source_target_pairs={{1,0},{0,1},{6,7},{7,6},{9,8},{8,9},{14,15},{15,14},{17,16},{16,17... | collective-permute-start | bytes 2359304 | tf_op jit(solution)/shard_map/ppermute | solution.py:857
  89.0 5.6 %collective-permute-start.16 = (bf16[512,768]{1,0:T(8,128)(2,1)S(1)}, bf16[512,768]{1,0:T(8,128)(2,1)S(1)}, u32[]{:S(2)}, u32[]{:S(2)}) collective-permute-start(bf16[512,768]{1,0:T(8,128)(2,1)S(1)} %collective-permute-done.14), channel_id=1, source_target_pairs={{0,4},{4,0},{1,5},{5,1},{2,6},{6,2},{3,7},{7,3},{8,12},{12,8},{9,1... | collective-permute-start | bytes 2359304 | tf_op jit(solution)/shard_map/ppermute | solution.py:821
  92.1 25.5 %collective-permute-start.20 = (bf16[512,768]{1,0:T(8,128)(2,1)S(1)}, bf16[512,768]{1,0:T(8,128)(2,1)S(1)}, u32[]{:S(2)}, u32[]{:S(2)}) collective-permute-start(bf16[512,768]{1,0:T(8,128)(2,1)S(1)} %copy-done.17), channel_id=1, source_target_pairs={{0,0},{2,1},{4,2},{6,3},{1,4},{3,5},{5,6},{7,7},{8,8},{10,9},{12,1... | collective-permute-start | bytes 2359304 | tf_op jit(solution)/shard_map/ppermute | solution.py:865
  114.7 6.7 %collective-permute-start.18 = (bf16[192,512]{1,0:T(8,128)(2,1)}, bf16[192,512]{1,0:T(8,128)(2,1)S(1)}, u32[]{:S(2)}, u32[]{:S(2)}) collective-permute-start(bf16[192,512]{1,0:T(8,128)(2,1)} %get-tuple-element.139.refs_6_), channel_id=1, source_target_pairs={{0,1},{1,0},{2,3},{3,2},{4,5},{5,4},{6,7},{7,6},{8,9},{9,8},{10,11... | collective-permute-start | bytes 589832 | tf_op jit(solution)/shard_map/ppermute | solution.py:869
  114.7 11.4 %collective-permute-start.19 = (bf16[192,512]{1,0:T(8,128)(2,1)}, bf16[192,512]{1,0:T(8,128)(2,1)S(1)}, u32[]{:S(2)}, u32[]{:S(2)}) collective-permute-start(bf16[192,512]{1,0:T(8,128)(2,1)} %get-tuple-element.140.refs_7_), channel_id=1, source_target_pairs={{0,5},{1,4},{2,7},{3,6},{4,1},{5,0},{6,3},{7,2},{8,13},{9,12},{10,... | collective-permute-start | bytes 589832 | tf_op jit(solution)/shard_map/ppermute | solution.py:869
  154.9 142.8 %reduce-scatter.5.cloned.1.call-start = ((), (), s32[]{:S(2)}) async-start(), calls=%async_computation.3 | async-start | bytes 1720320 | tf_op jit(solution)/shard_map/reduce_scatter | solution.py:909
  156.0 6.2 %collective-permute-start.22 = (bf16[192,512]{1,0:T(8,128)(2,1)S(1)}, bf16[192,512]{1,0:T(8,128)(2,1)S(1)}, u32[]{:S(2)}, u32[]{:S(2)}) collective-permute-start(bf16[192,512]{1,0:T(8,128)(2,1)S(1)} %copy-done.20), channel_id=1, source_target_pairs={{0,1},{1,0},{2,3},{3,2},{4,5},{5,4},{6,7},{7,6},{8,9},{9,8},{10,11... | collective-permute-start | bytes 589832 | tf_op jit(solution)/shard_map/ppermute | solution.py:878
  156.3 10.6 %collective-permute-start.23 = (bf16[192,512]{1,0:T(8,128)(2,1)S(1)}, bf16[192,512]{1,0:T(8,128)(2,1)S(1)}, u32[]{:S(2)}, u32[]{:S(2)}) collective-permute-start(bf16[192,512]{1,0:T(8,128)(2,1)S(1)} %copy-done.18), channel_id=1, source_target_pairs={{0,5},{1,4},{2,7},{3,6},{4,1},{5,0},{6,3},{7,2},{8,13},{9,12},{10,... | collective-permute-start | bytes 589832 | tf_op jit(solution)/shard_map/ppermute | solution.py:878
  166.9 46.8 %collective-permute-start.24 = (bf16[2,512,768]{2,1,0:T(8,128)(2,1)}, bf16[2,512,768]{2,1,0:T(8,128)(2,1)S(1)}, u32[]{:S(2)}, u32[]{:S(2)}) collective-permute-start(bf16[2,512,768]{2,1,0:T(8,128)(2,1)} %get-tuple-element.157), channel_id=1, source_target_pairs={{0,0},{1,2},{2,4},{3,6},{4,1},{5,3},{6,5},{7,7},{8,8},{9,10},{10,1... | collective-permute-start | bytes 4718600 | tf_op jit(solution)/shard_map/ppermute | solution.py:886
  213.8 24.9 %collective-permute-start.29 = (bf16[512,768]{1,0:T(8,128)(2,1)}, bf16[512,768]{1,0:T(8,128)(2,1)}, u32[]{:S(2)}, u32[]{:S(2)}) collective-permute-start(bf16[512,768]{1,0:T(8,128)(2,1)} %get-tuple-element.178), channel_id=1, source_target_pairs={{0,4},{4,0},{1,5},{5,1},{2,6},{6,2},{3,7},{7,3},{8,12},{12,8},{9,1... | collective-permute-start | bytes 2359304 | tf_op jit(solution)/shard_map/ppermute | solution.py:821
  218.9 12.8 %collective-permute-start.27 = (bf16[512,768]{1,0:T(8,128)(2,1)}, bf16[512,768]{1,0:T(8,128)(2,1)S(1)}, u32[]{:S(2)}, u32[]{:S(2)}) collective-permute-start(bf16[512,768]{1,0:T(8,128)(2,1)} %add.126), channel_id=1, source_target_pairs={{0,1},{1,0},{7,6},{6,7},{8,9},{9,8},{15,14},{14,15},{16,17},{17,16... | collective-permute-start | bytes 2359304 | tf_op jit(solution)/shard_map/ppermute | solution.py:896
  241.1 17.8 %collective-permute-start.30 = (bf16[512,768]{1,0:T(8,128)(2,1)}, bf16[512,768]{1,0:T(8,128)(2,1)}, u32[]{:S(2)}, u32[]{:S(2)}) collective-permute-start(bf16[512,768]{1,0:T(8,128)(2,1)} %add_select_fusion), channel_id=1, source_target_pairs={{0,1},{1,2},{6,5},{7,6},{8,9},{9,10},{14,13},{15,14},{16,17},{17,1... | collective-permute-start | bytes 2359304 | tf_op jit(solution)/shard_map/ppermute | solution.py:912
  242.6 23.2 %collective-permute-start.28 = (bf16[512,768]{1,0:T(8,128)(2,1)}, bf16[512,768]{1,0:T(8,128)(2,1)}, u32[]{:S(2)}, u32[]{:S(2)}) collective-permute-start(bf16[512,768]{1,0:T(8,128)(2,1)} %get-tuple-element.177), channel_id=1, source_target_pairs={{0,4},{4,0},{1,5},{5,1},{2,6},{6,2},{3,7},{7,3},{8,12},{12,8},{9,1... | collective-permute-start | bytes 2359304 | tf_op jit(solution)/shard_map/ppermute | solution.py:821
  245.6 11.2 %collective-permute-start.31 = (bf16[2,96,576]{2,1,0:T(8,128)(2,1)}, bf16[2,96,576]{2,1,0:T(8,128)(2,1)}, u32[]{:S(2)}, u32[]{:S(2)}) collective-permute-start(bf16[2,96,576]{2,1,0:T(8,128)(2,1)} %get-tuple-element.180), channel_id=1, source_target_pairs={{0,8},{8,0},{16,24},{24,16},{1,9},{9,1},{17,25},{25,17},{2,10},{10... | collective-permute-start | bytes 663560 | tf_op jit(solution)/shard_map/ppermute | solution.py:776
  246.6 11.3 %collective-permute-start.32 = (bf16[2,96,576]{2,1,0:T(8,128)(2,1)}, bf16[2,96,576]{2,1,0:T(8,128)(2,1)}, u32[]{:S(2)}, u32[]{:S(2)}) collective-permute-start(bf16[2,96,576]{2,1,0:T(8,128)(2,1)} %get-tuple-element.182), channel_id=1, source_target_pairs={{0,16},{8,24},{16,0},{24,8},{1,17},{9,25},{17,1},{25,9},{2,18},{10... | collective-permute-start | bytes 663560 | tf_op jit(solution)/shard_map/ppermute | solution.py:776
  250.3 43.8 %collective-permute-start.25 = (bf16[512,768]{1,0:T(8,128)(2,1)}, bf16[512,768]{1,0:T(8,128)(2,1)}, u32[]{:S(2)}, u32[]{:S(2)}) collective-permute-start(bf16[512,768]{1,0:T(8,128)(2,1)} %get-tuple-element.159), channel_id=1, source_target_pairs={{0,4},{4,0},{1,5},{5,1},{2,6},{6,2},{3,7},{7,3},{8,12},{12,8},{9,1... | collective-permute-start | bytes 2359304 | tf_op jit(solution)/shard_map/ppermute | solution.py:821
  262.9 7.7 %collective-permute-start.40 = (bf16[96,576]{1,0:T(8,128)(2,1)S(1)}, bf16[96,576]{1,0:T(8,128)(2,1)S(1)}, u32[]{:S(2)}, u32[]{:S(2)}) collective-permute-start(bf16[96,576]{1,0:T(8,128)(2,1)S(1)} %slice_bitcast_fusion.2), channel_id=1, source_target_pairs={{0,8},{8,0},{16,24},{24,16},{1,9},{9,1},{17,25},{25,17},{2,10},{10... | collective-permute-start | bytes 331784 | tf_op jit(solution)/shard_map/ppermute | solution.py:776
  264.1 6.5 %collective-permute-start.39 = (bf16[96,576]{1,0:T(8,128)(2,1)S(1)}, bf16[96,576]{1,0:T(8,128)(2,1)S(1)}, u32[]{:S(2)}, u32[]{:S(2)}) collective-permute-start(bf16[96,576]{1,0:T(8,128)(2,1)S(1)} %slice_bitcast_fusion.3), channel_id=1, source_target_pairs={{0,16},{8,24},{16,0},{24,8},{1,17},{9,25},{17,1},{25,9},{2,18},{10... | collective-permute-start | bytes 331784 | tf_op jit(solution)/shard_map/ppermute | solution.py:776
  268.5 25.5 %collective-permute-start.35 = (bf16[512,768]{1,0:T(8,128)(2,1)}, bf16[512,768]{1,0:T(8,128)(2,1)}, u32[]{:S(2)}, u32[]{:S(2)}) collective-permute-start(bf16[512,768]{1,0:T(8,128)(2,1)} %select_add_fusion), channel_id=1, source_target_pairs={{0,1},{1,2},{2,3},{5,4},{6,5},{7,6},{8,9},{9,10},{10,11},{13,12},{... | collective-permute-start | bytes 2359304 | tf_op jit(solution)/shard_map/ppermute | solution.py:922
  270.7 7.8 %collective-permute-start.42 = (bf16[96,576]{1,0:T(8,128)(2,1)S(1)}, bf16[96,576]{1,0:T(8,128)(2,1)S(1)}, u32[]{:S(2)}, u32[]{:S(2)}) collective-permute-start(bf16[96,576]{1,0:T(8,128)(2,1)S(1)} %get-tuple-element.250), channel_id=1, source_target_pairs={{0,4},{1,6},{2,0},{3,2},{4,5},{5,7},{6,1},{7,3},{8,12},{9,14},{10,... | collective-permute-start | bytes 331784 | tf_op jit(solution)/shard_map/ppermute | solution.py:935
  272.6 19.8 %collective-permute-start.41 = (bf16[96,576]{1,0:T(8,128)(2,1)S(1)}, bf16[96,576]{1,0:T(8,128)(2,1)}, u32[]{:S(2)}, u32[]{:S(2)}) collective-permute-start(bf16[96,576]{1,0:T(8,128)(2,1)S(1)} %get-tuple-element.251), channel_id=1, source_target_pairs={{0,0},{1,2},{2,4},{3,6},{4,1},{5,3},{6,5},{7,7},{8,8},{9,10},{10,1... | collective-permute-start | bytes 331784 | tf_op jit(solution)/shard_map/ppermute | solution.py:934
  (46 other events, 415.2 us)
Sparse Core Ops, SparseCore 0:
  29.6 32.1 all-gather.4
  63.6 66.0 all-gather.6
  155.1 83.6 reduce-scatter.2
  249.5 31.0 reduce-scatter.4

commit v7 on v6

--- a/solution.py
+++ b/solution.py
@@ -685,7 +685,6 @@
     rounded = grad_hidden.astype(bf16)
     out_ref[1] = rounded
     for turn in range(parts):
-        gots[turn][...] = dot(output_rows(turn), rounded, ((0,), (1,))).astype(bf16)
         grads = dot(rounded, mixes[turn][...], ((0,), (1,))).astype(bf16)
         grad_ref[turn_ref[turn], :, :, feed : feed + columns] = grads.reshape(
             *grad_ref.shape[1:3], columns
@@ -695,6 +694,8 @@
         )
     for z in range(parts):
         store(z, 0, late).start()
+    for turn in range(parts):
+        gots[turn][...] = dot(output_rows(turn), rounded, ((0,), (1,))).astype(bf16)
     for z in range(parts):
         store(z, 0, late).wait()
         store(z, 1, early).wait()

time: 308 us -> 307 us (level)
  transfers between devices with their start and end apart: 47 -> 47, of which waited for: 21 -> 21; matrix products, arithmetic and copies ran while one was open for 11% -> 11% of each run, Pallas kernels for 33% -> 34%
where the time goes in v7:
time: 307 us; the launch traced here: 306 us
  Pallas kernels  127 us (41%)
  waiting for transfers between devices  65.8 us (21%)
  starting transfers between devices  59.3 us (19%)
  other arithmetic  26.4 us (9%)
  between operations  14.4 us (5%)
  local copies, waits for them, and re-layouts  13.3 us (4%)
    pallas_call x1, Pallas kernels, attend_backward(): pl.pallas_call(backward_kernel, grid=(length // TILE,), in_specs=[smem] *...  44.2 us
    pallas_call x1, Pallas kernels, middle(): pl.pallas_call(middle_kernel, in_specs=[smem] + [whole(a.shape) for a in...  24.1 us
    pallas_call x1, Pallas kernels, attend_early(): pl.pallas_call(early_kernel, grid=((parts - 1) * part_length // TILE,), i...  21.7 us
    pallas_call x1, Pallas kernels, attend_late(): pl.pallas_call(late_kernel, grid=(length // TILE,), in_specs=[smem] * 5 +...  18.8 us
    ppermute x9, starting transfers between devices, swap(): return lax.ppermute(value, 'core', SWAP)  14.7 us
    ppermute x1, waiting for transfers between devices, body(): lax.ppermute(jnp.where(lower, low, high), LINE, back(weight_routes[0]))  13.9 us
    pallas_call x1, Pallas kernels, attend_sums(): pl.pallas_call(sums_kernel, in_specs=[smem] * 2 + [whole(a.shape) for a i...  11.3 us
    ppermute x3, waiting for transfers between devices, body(): lax.ppermute(ots[r], LINE, rounds[r])  8.64 us
  transfers between devices with their start and end apart: 47, of which 21 were waited for; matrix products, arithmetic and copies ran while one was open for 11% of the time, Pallas kernels for 34%

profile of v7, /device:TPU:9, one launch (start us, length us, event | category | flops | bytes accessed | tf_op | source)
XLA Modules:
  0.0 306.0 jit_solution(14740118993519637074)
XLA Ops:
  8.0 3.2 %collective-permute-start = (bf16[512,768]{1,0:T(8,128)(2,1)}, bf16[512,768]{1,0:T(8,128)(2,1)S(1)}, u32[]{:S(2)}, u32[]{:S(2)}) collective-permute-start(bf16[512,768]{1,0:T(8,128)(2,1)} %param.18), channel_id=1, source_target_pairs={{1,0},{2,1},{3,2},{4,5},{5,6},{6,7},{9,8},{10,9},{11,10},{12,13},{... | collective-permute-start | bytes 2359304 | tf_op jit(solution)/shard_map/ppermute | solution.py:828
  21.2 4.3 %collective-permute-start.5 = (bf16[96,576]{1,0:T(8,128)(2,1)S(1)}, bf16[96,576]{1,0:T(8,128)(2,1)}, u32[]{:S(2)}, u32[]{:S(2)}) collective-permute-start(bf16[96,576]{1,0:T(8,128)(2,1)S(1)} %pad_maximum_fusion), channel_id=1, source_target_pairs={{0,0},{2,1},{4,2},{6,3},{1,4},{3,5},{5,6},{7,7},{8,8},{10,9},{12,1... | collective-permute-start | bytes 331784 | tf_op jit(solution)/shard_map/ppermute | solution.py:835
  25.6 3.9 %collective-permute-start.2 = (bf16[512,768]{1,0:T(8,128)(2,1)S(1)}, bf16[512,768]{1,0:T(8,128)(2,1)}, u32[]{:S(2)}, u32[]{:S(2)}) collective-permute-start(bf16[512,768]{1,0:T(8,128)(2,1)S(1)} %collective-permute-done), channel_id=1, source_target_pairs={{1,0},{2,1},{5,6},{6,7},{9,8},{10,9},{13,14},{14,15},{17,16},{18,1... | collective-permute-start | bytes 2359304 | tf_op jit(solution)/shard_map/ppermute | solution.py:836
  33.6 5.7 %collective-permute-done.7 = f32[32,3]{0,1:T(4,128)S(1)} collective-permute-done((f32[32,3]{0,1:T(4,128)S(1)}, f32[32,3]{0,1:T(4,128)S(1)}, u32[]{:S(2)}, u32[]{:S(2)}) %collective-permute-start.7) | collective-permute-done | bytes 416 | tf_op jit(solution)/shard_map/ppermute | solution.py:832
  40.2 6.6 %bias_tiles.1.refs_13_.refs_8_ = f32[3,10,256,256]{3,2,1,0:T(8,128)} custom-call(f32[3,1,2816]{2,1,0:T(1,128)} %mul.88.row_ref), custom_call_target="tpu_custom_call" | custom-call | flops 6000000000 | tf_op jit(solution)/shard_map/bias_tiles/pallas_call | solution.py:84
  58.2 3.6 %all-gather.5.cloned.1.call-done = bf16[384,1792]{1,0:T(8,128)(2,1)} async-done(((bf16[96,1792]{1,0:T(8,128)(2,1)}), bf16[384,1792]{1,0:T(8,128)(2,1)}) %all-gather.5.cloned.1.call-update) | async-done | bytes 1376272 | tf_op jit(solution)/shard_map/all_gather | solution.py:834
  62.8 2.1 collective-permute-done.15
  65.0 2.1 broadcast_select_fusion.2
  67.9 21.7 %attend_early.1 = (bf16[3,9,64,512]{3,2,1,0:T(8,128)(2,1)}, bf16[3,512,768]{2,1,0:T(8,128)(2,1)}, bf16[576,768]{1,0:T(8,128)(2,1)}, bf16[512,768]{1,0:T(8,128)(2...) custom-call(s32[8]{0:T(128)} %copy-done.16, s32[8]{0:T(128)} %copy-done.15, ...), custom_call_target="tpu_custom_call" | custom-call | flops 20000000000 | tf_op jit(solution)/shard_map/attend_early/pallas_call | solution.py:323
  89.6 3.0 collective-permute-start.16
  92.7 2.4 collective-permute-start.20
  96.0 18.8 %attend_late.1 = (bf16[192,512]{1,0:T(8,128)(2,1)}, bf16[192,512]{1,0:T(8,128)(2,1)}, bf16[192,512]{1,0:T(8,128)(2,1)}, bf16[192,512]{1,0:T(8,128)(2,1)}, f32[3,...) custom-call(s32[8]{0:T(128)} %copy-done.16, s32[8]{0:T(128)} %copy-done.15, ...), custom_call_target="tpu_custom_call" | custom-call | flops 15000000512 | tf_op jit(solution)/shard_map/attend_late/pallas_call | solution.py:353
  118.3 4.0 %collective-permute-done.18.refs_2_ = bf16[192,512]{1,0:T(8,128)(2,1)S(1)} collective-permute-done((bf16[192,512]{1,0:T(8,128)(2,1)}, bf16[192,512]{1,0:T(8,128)(2,1)S(1)}, u32[]{:S(2)}, u32[]{:S(2)}) %collective-permute-start.18) | collective-permute-done | bytes 196640 | tf_op jit(solution)/shard_map/ppermute | solution.py:870
  122.2 4.7 %collective-permute-done.19.refs_3_ = bf16[192,512]{1,0:T(8,128)(2,1)S(1)} collective-permute-done((bf16[192,512]{1,0:T(8,128)(2,1)}, bf16[192,512]{1,0:T(8,128)(2,1)S(1)}, u32[]{:S(2)}, u32[]{:S(2)}) %collective-permute-start.19) | collective-permute-done | bytes 196640 | tf_op jit(solution)/shard_map/ppermute | solution.py:870
  126.9 2.9 all-gather.7.cloned.1.call-done
  129.8 24.1 %middle.1 = (bf16[2,512,768]{2,1,0:T(8,128)(2,1)}, f32[1,768]{1,0:T(1,128)}, bf16[192,512]{1,0:T(8,128)(2,1)}, bf16[192,512]{1,0:T(8,128)(2,1)}, bf16[192,512]{1...) custom-call(s32[4]{0:T(128)} %iota_xor_fusion.turn_ref, ...), custom_call_target="tpu_custom_call" | custom-call | tf_op jit(solution)/shard_map/middle/pallas_call | solution.py:716
  157.6 3.8 %collective-permute-done.22.refs_2_ = bf16[192,512]{1,0:T(8,128)(2,1)S(1)} collective-permute-done((bf16[192,512]{1,0:T(8,128)(2,1)S(1)}, bf16[192,512]{1,0:T(8,128)(2,1)S(1)}, u32[]{:S(2)}, u32[]{:S(2)}) %collective-permute-start.22) | collective-permute-done | bytes 196640 | tf_op jit(solution)/shard_map/ppermute | solution.py:879
  161.4 4.6 %collective-permute-done.23.refs_3_ = bf16[192,512]{1,0:T(8,128)(2,1)S(1)} collective-permute-done((bf16[192,512]{1,0:T(8,128)(2,1)S(1)}, bf16[192,512]{1,0:T(8,128)(2,1)S(1)}, u32[]{:S(2)}, u32[]{:S(2)}) %collective-permute-start.23) | collective-permute-done | bytes 196640 | tf_op jit(solution)/shard_map/ppermute | solution.py:879
  166.0 4.1 %collective-permute-start.24 = (bf16[2,512,768]{2,1,0:T(8,128)(2,1)}, bf16[2,512,768]{2,1,0:T(8,128)(2,1)S(1)}, u32[]{:S(2)}, u32[]{:S(2)}) collective-permute-start(bf16[2,512,768]{2,1,0:T(8,128)(2,1)} %get-tuple-element.157), channel_id=1, source_target_pairs={{0,0},{1,2},{2,4},{3,6},{4,1},{5,3},{6,5},{7,7},{8,8},{9,10},{10,1... | collective-permute-start | bytes 4718600 | tf_op jit(solution)/shard_map/ppermute | solution.py:887
  170.2 44.2 %attend_backward.1 = (bf16[512,768]{1,0:T(8,128)(2,1)}, bf16[512,768]{1,0:T(8,128)(2,1)}, bf16[512,768]{1,0:T(8,128)(2,1)}, bf16[512,768]{1,0:T(8,128)(2,1)}, bf...) custom-call(s32[8]{0:T(128)} %convert_reduce_fusion.2.least_ref, s32[8]{0:T(128)} %convert_reduce_fusion.1.clear_ref, ...), custom_call_target="tpu_custom_call" | custom-call | flops 44999999488 | tf_op jit(solution)/shard_map/attend_backward/pallas_call | solution.py:560
  214.9 2.3 collective-permute-done.26
  217.2 2.2 add.126
  220.2 11.3 %attend_sums.1 = (f32[16,128]{1,0:T(8,128)}, bf16[2,96,576]{2,1,0:T(8,128)(2,1)}, bf16[2,96,576]{2,1,0:T(8,128)(2,1)}, bf16[2,96,576]{2,1,0:T(8,128)(2,1)}, bf16[2,96,576]{2,1,0:T(8,128)(2,1)}) custom-call(s32[1]{0:T(128)} %bitcast.5.group_ref, s32[8]{0:T(128)} %multiply_add_fusion.place_ref, bf16[4,576,512]{2,1,0:T(8,128)(2,1)} %get-tuple-element.164.refs_0_, ...), custom_call_target="tpu_custom_call" | custom-call | flops 12000000000 | tf_op jit(solution)/shard_map/attend_sums/pallas_call | solution.py:591
  231.5 6.3 %reduce-scatter.3.cloned.1.call-done = bf16[1,4,96,1792]{3,2,1,0:T(8,128)(2,1)} async-done(((bf16[8,4,96,1792]{3,2,1,0:T(8,128)(2,1)}), bf16[1,4,96,1792]{3,2,1,0:T(8,128)(2,1)}) %reduce-scatter.3.cloned.1.call-update) | async-done | bytes 1376272 | tf_op jit(solution)/shard_map/reduce_scatter | solution.py:889
  237.8 2.4 add_select_fusion
  241.7 2.8 collective-permute-start.28
  249.4 6.4 %collective-permute-start.25 = (bf16[512,768]{1,0:T(8,128)(2,1)}, bf16[512,768]{1,0:T(8,128)(2,1)}, u32[]{:S(2)}, u32[]{:S(2)}) collective-permute-start(bf16[512,768]{1,0:T(8,128)(2,1)} %get-tuple-element.159), channel_id=1, source_target_pairs={{0,4},{4,0},{1,5},{5,1},{2,6},{6,2},{3,7},{7,3},{8,12},{12,8},{9,1... | collective-permute-start | bytes 2359304 | tf_op jit(solution)/shard_map/ppermute | solution.py:822
  258.1 3.6 %collective-permute-done.36 = f32[16,128]{1,0:T(8,128)S(1)} collective-permute-done((f32[16,128]{1,0:T(8,128)S(1)}, f32[16,128]{1,0:T(8,128)S(1)}, u32[]{:S(2)}, u32[]{:S(2)}) %collective-permute-start.36) | collective-permute-done | bytes 8224 | tf_op jit(solution)/shard_map/ppermute | solution.py:902
  265.0 2.7 select_add_fusion
  271.7 4.5 %collective-permute-start.41 = (bf16[96,576]{1,0:T(8,128)(2,1)S(1)}, bf16[96,576]{1,0:T(8,128)(2,1)}, u32[]{:S(2)}, u32[]{:S(2)}) collective-permute-start(bf16[96,576]{1,0:T(8,128)(2,1)S(1)} %get-tuple-element.251), channel_id=1, source_target_pairs={{0,0},{1,2},{2,4},{3,6},{4,1},{5,3},{6,5},{7,7},{8,8},{9,10},{10,1... | collective-permute-start | bytes 331784 | tf_op jit(solution)/shard_map/ppermute | solution.py:935
  277.6 13.9 %collective-permute-done.41 = bf16[96,576]{1,0:T(8,128)(2,1)} collective-permute-done((bf16[96,576]{1,0:T(8,128)(2,1)S(1)}, bf16[96,576]{1,0:T(8,128)(2,1)}, u32[]{:S(2)}, u32[]{:S(2)}) %collective-permute-start.41) | collective-permute-done | bytes 110624 | tf_op jit(solution)/shard_map/ppermute | solution.py:935
  293.2 2.2 fusion.2
  (193 shorter events, 61.1 us)
Async XLA Ops:
  7.2 54.6 %all-gather.5.cloned.1.call-start = ((), (), s32[]{:S(2)}) async-start(), calls=%async_computation.4 | async-start | bytes 1720320 | tf_op jit(solution)/shard_map/all_gather | solution.py:834
  7.2 22.8 %collective-permute-start.3 = (bf16[512,768]{1,0:T(8,128)(2,1)}, bf16[512,768]{1,0:T(8,128)(2,1)S(1)}, u32[]{:S(2)}, u32[]{:S(2)}) collective-permute-start(bf16[512,768]{1,0:T(8,128)(2,1)} %param.18), channel_id=1, source_target_pairs={{0,4},{4,0},{1,5},{5,1},{2,6},{6,2},{3,7},{7,3},{8,12},{12,8},{9,1... | collective-permute-start | bytes 2359304 | tf_op jit(solution)/shard_map/ppermute | solution.py:822
  8.0 13.2 %collective-permute-start = (bf16[512,768]{1,0:T(8,128)(2,1)}, bf16[512,768]{1,0:T(8,128)(2,1)S(1)}, u32[]{:S(2)}, u32[]{:S(2)}) collective-permute-start(bf16[512,768]{1,0:T(8,128)(2,1)} %param.18), channel_id=1, source_target_pairs={{1,0},{2,1},{3,2},{4,5},{5,6},{6,7},{9,8},{10,9},{11,10},{12,13},{... | collective-permute-start | bytes 2359304 | tf_op jit(solution)/shard_map/ppermute | solution.py:828
  11.2 8.9 %collective-permute-start.1 = (s32[1,2048]{1,0:T(1,128)}, s32[1,2048]{1,0:T(1,128)S(1)}, u32[]{:S(2)}, u32[]{:S(2)}) collective-permute-start(s32[1,2048]{1,0:T(1,128)} %param.28), channel_id=1, source_target_pairs={{0,4},{4,0},{1,5},{5,1},{2,6},{6,2},{3,7},{7,3},{8,12},{12,8},{9,1... | collective-permute-start | bytes 24584 | tf_op jit(solution)/shard_map/ppermute | solution.py:822
  21.2 25.6 %collective-permute-start.6 = (bf16[96,576]{1,0:T(8,128)(2,1)S(1)}, bf16[96,576]{1,0:T(8,128)(2,1)S(1)}, u32[]{:S(2)}, u32[]{:S(2)}) collective-permute-start(bf16[96,576]{1,0:T(8,128)(2,1)S(1)} %pad_maximum_fusion), channel_id=1, source_target_pairs={{4,0},{6,1},{0,2},{2,3},{5,4},{7,5},{1,6},{3,7},{12,8},{14,9},{8,1... | collective-permute-start | bytes 331784 | tf_op jit(solution)/shard_map/ppermute | solution.py:835
  21.2 25.6 %collective-permute-start.5 = (bf16[96,576]{1,0:T(8,128)(2,1)S(1)}, bf16[96,576]{1,0:T(8,128)(2,1)}, u32[]{:S(2)}, u32[]{:S(2)}) collective-permute-start(bf16[96,576]{1,0:T(8,128)(2,1)S(1)} %pad_maximum_fusion), channel_id=1, source_target_pairs={{0,0},{2,1},{4,2},{6,3},{1,4},{3,5},{5,6},{7,7},{8,8},{10,9},{12,1... | collective-permute-start | bytes 331784 | tf_op jit(solution)/shard_map/ppermute | solution.py:835
  25.5 28.3 %collective-permute-start.4 = (bf16[512,768]{1,0:T(8,128)(2,1)S(1)}, bf16[512,768]{1,0:T(8,128)(2,1)S(1)}, u32[]{:S(2)}, u32[]{:S(2)}) collective-permute-start(bf16[512,768]{1,0:T(8,128)(2,1)S(1)} %collective-permute-done), channel_id=1, source_target_pairs={{0,4},{4,0},{1,5},{5,1},{2,6},{6,2},{3,7},{7,3},{8,12},{12,8},{9,1... | collective-permute-start | bytes 2359304 | tf_op jit(solution)/shard_map/ppermute | solution.py:822
  25.6 32.6 %collective-permute-start.2 = (bf16[512,768]{1,0:T(8,128)(2,1)S(1)}, bf16[512,768]{1,0:T(8,128)(2,1)}, u32[]{:S(2)}, u32[]{:S(2)}) collective-permute-start(bf16[512,768]{1,0:T(8,128)(2,1)S(1)} %collective-permute-done), channel_id=1, source_target_pairs={{1,0},{2,1},{5,6},{6,7},{9,8},{10,9},{13,14},{14,15},{17,16},{18,1... | collective-permute-start | bytes 2359304 | tf_op jit(solution)/shard_map/ppermute | solution.py:836
  29.5 100.3 %all-gather.7.cloned.1.call-start = ((), (), s32[]{:S(2)}) async-start(), calls=%async_computation.5 | async-start | bytes 12386304 | tf_op jit(solution)/shard_map/all_gather | solution.py:860
  30.0 9.3 %collective-permute-start.7 = (f32[32,3]{0,1:T(4,128)S(1)}, f32[32,3]{0,1:T(4,128)S(1)}, u32[]{:S(2)}, u32[]{:S(2)}) collective-permute-start(f32[32,3]{0,1:T(4,128)S(1)} %copy-done.30), channel_id=1, source_target_pairs={{0,0},{2,1},{4,2},{6,3},{1,4},{3,5},{5,6},{7,7},{8,8},{10,9},{12,1... | collective-permute-start | bytes 1160 | tf_op jit(solution)/shard_map/ppermute | solution.py:832
  61.8 176.0 %reduce-scatter.3.cloned.1.call-start = ((), (), s32[]{:S(2)}) async-start(), calls=%async_computation.2 | async-start | bytes 12386304 | tf_op jit(solution)/shard_map/reduce_scatter | solution.py:889
  67.1 22.5 %collective-permute-start.14 = (bf16[512,768]{1,0:T(8,128)(2,1)S(1)}, bf16[512,768]{1,0:T(8,128)(2,1)S(1)}, u32[]{:S(2)}, u32[]{:S(2)}) collective-permute-start(bf16[512,768]{1,0:T(8,128)(2,1)S(1)} %get-tuple-element.249), channel_id=1, source_target_pairs={{1,0},{0,1},{6,7},{7,6},{9,8},{8,9},{14,15},{15,14},{17,16},{16,17... | collective-permute-start | bytes 2359304 | tf_op jit(solution)/shard_map/ppermute | solution.py:858
  89.6 5.4 %collective-permute-start.16 = (bf16[512,768]{1,0:T(8,128)(2,1)S(1)}, bf16[512,768]{1,0:T(8,128)(2,1)S(1)}, u32[]{:S(2)}, u32[]{:S(2)}) collective-permute-start(bf16[512,768]{1,0:T(8,128)(2,1)S(1)} %collective-permute-done.14), channel_id=1, source_target_pairs={{0,4},{4,0},{1,5},{5,1},{2,6},{6,2},{3,7},{7,3},{8,12},{12,8},{9,1... | collective-permute-start | bytes 2359304 | tf_op jit(solution)/shard_map/ppermute | solution.py:822
  92.7 25.6 %collective-permute-start.20 = (bf16[512,768]{1,0:T(8,128)(2,1)S(1)}, bf16[512,768]{1,0:T(8,128)(2,1)S(1)}, u32[]{:S(2)}, u32[]{:S(2)}) collective-permute-start(bf16[512,768]{1,0:T(8,128)(2,1)S(1)} %copy-done.17), channel_id=1, source_target_pairs={{0,0},{2,1},{4,2},{6,3},{1,4},{3,5},{5,6},{7,7},{8,8},{10,9},{12,1... | collective-permute-start | bytes 2359304 | tf_op jit(solution)/shard_map/ppermute | solution.py:866
  115.4 6.8 %collective-permute-start.18 = (bf16[192,512]{1,0:T(8,128)(2,1)}, bf16[192,512]{1,0:T(8,128)(2,1)S(1)}, u32[]{:S(2)}, u32[]{:S(2)}) collective-permute-start(bf16[192,512]{1,0:T(8,128)(2,1)} %get-tuple-element.139.refs_6_), channel_id=1, source_target_pairs={{0,1},{1,0},{2,3},{3,2},{4,5},{5,4},{6,7},{7,6},{8,9},{9,8},{10,11... | collective-permute-start | bytes 589832 | tf_op jit(solution)/shard_map/ppermute | solution.py:870
  115.4 11.5 %collective-permute-start.19 = (bf16[192,512]{1,0:T(8,128)(2,1)}, bf16[192,512]{1,0:T(8,128)(2,1)S(1)}, u32[]{:S(2)}, u32[]{:S(2)}) collective-permute-start(bf16[192,512]{1,0:T(8,128)(2,1)} %get-tuple-element.140.refs_7_), channel_id=1, source_target_pairs={{0,5},{1,4},{2,7},{3,6},{4,1},{5,0},{6,3},{7,2},{8,13},{9,12},{10,... | collective-permute-start | bytes 589832 | tf_op jit(solution)/shard_map/ppermute | solution.py:870
  154.0 142.8 %reduce-scatter.5.cloned.1.call-start = ((), (), s32[]{:S(2)}) async-start(), calls=%async_computation.3 | async-start | bytes 1720320 | tf_op jit(solution)/shard_map/reduce_scatter | solution.py:910
  155.1 6.3 %collective-permute-start.22 = (bf16[192,512]{1,0:T(8,128)(2,1)S(1)}, bf16[192,512]{1,0:T(8,128)(2,1)S(1)}, u32[]{:S(2)}, u32[]{:S(2)}) collective-permute-start(bf16[192,512]{1,0:T(8,128)(2,1)S(1)} %copy-done.20), channel_id=1, source_target_pairs={{0,1},{1,0},{2,3},{3,2},{4,5},{5,4},{6,7},{7,6},{8,9},{9,8},{10,11... | collective-permute-start | bytes 589832 | tf_op jit(solution)/shard_map/ppermute | solution.py:879
  155.4 10.6 %collective-permute-start.23 = (bf16[192,512]{1,0:T(8,128)(2,1)S(1)}, bf16[192,512]{1,0:T(8,128)(2,1)S(1)}, u32[]{:S(2)}, u32[]{:S(2)}) collective-permute-start(bf16[192,512]{1,0:T(8,128)(2,1)S(1)} %copy-done.18), channel_id=1, source_target_pairs={{0,5},{1,4},{2,7},{3,6},{4,1},{5,0},{6,3},{7,2},{8,13},{9,12},{10,... | collective-permute-start | bytes 589832 | tf_op jit(solution)/shard_map/ppermute | solution.py:879
  166.0 48.3 %collective-permute-start.24 = (bf16[2,512,768]{2,1,0:T(8,128)(2,1)}, bf16[2,512,768]{2,1,0:T(8,128)(2,1)S(1)}, u32[]{:S(2)}, u32[]{:S(2)}) collective-permute-start(bf16[2,512,768]{2,1,0:T(8,128)(2,1)} %get-tuple-element.157), channel_id=1, source_target_pairs={{0,0},{1,2},{2,4},{3,6},{4,1},{5,3},{6,5},{7,7},{8,8},{9,10},{10,1... | collective-permute-start | bytes 4718600 | tf_op jit(solution)/shard_map/ppermute | solution.py:887
  214.4 23.4 %collective-permute-start.29 = (bf16[512,768]{1,0:T(8,128)(2,1)}, bf16[512,768]{1,0:T(8,128)(2,1)}, u32[]{:S(2)}, u32[]{:S(2)}) collective-permute-start(bf16[512,768]{1,0:T(8,128)(2,1)} %get-tuple-element.178), channel_id=1, source_target_pairs={{0,4},{4,0},{1,5},{5,1},{2,6},{6,2},{3,7},{7,3},{8,12},{12,8},{9,1... | collective-permute-start | bytes 2359304 | tf_op jit(solution)/shard_map/ppermute | solution.py:822
  219.5 12.0 %collective-permute-start.27 = (bf16[512,768]{1,0:T(8,128)(2,1)}, bf16[512,768]{1,0:T(8,128)(2,1)S(1)}, u32[]{:S(2)}, u32[]{:S(2)}) collective-permute-start(bf16[512,768]{1,0:T(8,128)(2,1)} %add.126), channel_id=1, source_target_pairs={{0,1},{1,0},{7,6},{6,7},{8,9},{9,8},{15,14},{14,15},{16,17},{17,16... | collective-permute-start | bytes 2359304 | tf_op jit(solution)/shard_map/ppermute | solution.py:897
  240.2 17.8 %collective-permute-start.30 = (bf16[512,768]{1,0:T(8,128)(2,1)}, bf16[512,768]{1,0:T(8,128)(2,1)}, u32[]{:S(2)}, u32[]{:S(2)}) collective-permute-start(bf16[512,768]{1,0:T(8,128)(2,1)} %add_select_fusion), channel_id=1, source_target_pairs={{0,1},{1,2},{6,5},{7,6},{8,9},{9,10},{14,13},{15,14},{16,17},{17,1... | collective-permute-start | bytes 2359304 | tf_op jit(solution)/shard_map/ppermute | solution.py:913
  241.7 23.2 %collective-permute-start.28 = (bf16[512,768]{1,0:T(8,128)(2,1)}, bf16[512,768]{1,0:T(8,128)(2,1)}, u32[]{:S(2)}, u32[]{:S(2)}) collective-permute-start(bf16[512,768]{1,0:T(8,128)(2,1)} %get-tuple-element.177), channel_id=1, source_target_pairs={{0,4},{4,0},{1,5},{5,1},{2,6},{6,2},{3,7},{7,3},{8,12},{12,8},{9,1... | collective-permute-start | bytes 2359304 | tf_op jit(solution)/shard_map/ppermute | solution.py:822
  244.6 11.2 %collective-permute-start.31 = (bf16[2,96,576]{2,1,0:T(8,128)(2,1)}, bf16[2,96,576]{2,1,0:T(8,128)(2,1)}, u32[]{:S(2)}, u32[]{:S(2)}) collective-permute-start(bf16[2,96,576]{2,1,0:T(8,128)(2,1)} %get-tuple-element.180), channel_id=1, source_target_pairs={{0,8},{8,0},{16,24},{24,16},{1,9},{9,1},{17,25},{25,17},{2,10},{10... | collective-permute-start | bytes 663560 | tf_op jit(solution)/shard_map/ppermute | solution.py:777
  245.7 11.3 %collective-permute-start.32 = (bf16[2,96,576]{2,1,0:T(8,128)(2,1)}, bf16[2,96,576]{2,1,0:T(8,128)(2,1)}, u32[]{:S(2)}, u32[]{:S(2)}) collective-permute-start(bf16[2,96,576]{2,1,0:T(8,128)(2,1)} %get-tuple-element.182), channel_id=1, source_target_pairs={{0,16},{8,24},{16,0},{24,8},{1,17},{9,25},{17,1},{25,9},{2,18},{10... | collective-permute-start | bytes 663560 | tf_op jit(solution)/shard_map/ppermute | solution.py:777
  249.4 43.8 %collective-permute-start.25 = (bf16[512,768]{1,0:T(8,128)(2,1)}, bf16[512,768]{1,0:T(8,128)(2,1)}, u32[]{:S(2)}, u32[]{:S(2)}) collective-permute-start(bf16[512,768]{1,0:T(8,128)(2,1)} %get-tuple-element.159), channel_id=1, source_target_pairs={{0,4},{4,0},{1,5},{5,1},{2,6},{6,2},{3,7},{7,3},{8,12},{12,8},{9,1... | collective-permute-start | bytes 2359304 | tf_op jit(solution)/shard_map/ppermute | solution.py:822
  262.1 7.7 %collective-permute-start.40 = (bf16[96,576]{1,0:T(8,128)(2,1)S(1)}, bf16[96,576]{1,0:T(8,128)(2,1)S(1)}, u32[]{:S(2)}, u32[]{:S(2)}) collective-permute-start(bf16[96,576]{1,0:T(8,128)(2,1)S(1)} %slice_bitcast_fusion.2), channel_id=1, source_target_pairs={{0,8},{8,0},{16,24},{24,16},{1,9},{9,1},{17,25},{25,17},{2,10},{10... | collective-permute-start | bytes 331784 | tf_op jit(solution)/shard_map/ppermute | solution.py:777
  263.2 6.5 %collective-permute-start.39 = (bf16[96,576]{1,0:T(8,128)(2,1)S(1)}, bf16[96,576]{1,0:T(8,128)(2,1)S(1)}, u32[]{:S(2)}, u32[]{:S(2)}) collective-permute-start(bf16[96,576]{1,0:T(8,128)(2,1)S(1)} %slice_bitcast_fusion.3), channel_id=1, source_target_pairs={{0,16},{8,24},{16,0},{24,8},{1,17},{9,25},{17,1},{25,9},{2,18},{10... | collective-permute-start | bytes 331784 | tf_op jit(solution)/shard_map/ppermute | solution.py:777
  267.6 25.5 %collective-permute-start.35 = (bf16[512,768]{1,0:T(8,128)(2,1)}, bf16[512,768]{1,0:T(8,128)(2,1)}, u32[]{:S(2)}, u32[]{:S(2)}) collective-permute-start(bf16[512,768]{1,0:T(8,128)(2,1)} %select_add_fusion), channel_id=1, source_target_pairs={{0,1},{1,2},{2,3},{5,4},{6,5},{7,6},{8,9},{9,10},{10,11},{13,12},{... | collective-permute-start | bytes 2359304 | tf_op jit(solution)/shard_map/ppermute | solution.py:923
  269.8 7.8 %collective-permute-start.42 = (bf16[96,576]{1,0:T(8,128)(2,1)S(1)}, bf16[96,576]{1,0:T(8,128)(2,1)S(1)}, u32[]{:S(2)}, u32[]{:S(2)}) collective-permute-start(bf16[96,576]{1,0:T(8,128)(2,1)S(1)} %get-tuple-element.250), channel_id=1, source_target_pairs={{0,4},{1,6},{2,0},{3,2},{4,5},{5,7},{6,1},{7,3},{8,12},{9,14},{10,... | collective-permute-start | bytes 331784 | tf_op jit(solution)/shard_map/ppermute | solution.py:936
  271.7 19.7 %collective-permute-start.41 = (bf16[96,576]{1,0:T(8,128)(2,1)S(1)}, bf16[96,576]{1,0:T(8,128)(2,1)}, u32[]{:S(2)}, u32[]{:S(2)}) collective-permute-start(bf16[96,576]{1,0:T(8,128)(2,1)S(1)} %get-tuple-element.251), channel_id=1, source_target_pairs={{0,0},{1,2},{2,4},{3,6},{4,1},{5,3},{6,5},{7,7},{8,8},{9,10},{10,1... | collective-permute-start | bytes 331784 | tf_op jit(solution)/shard_map/ppermute | solution.py:935
  (46 other events, 413.3 us)
Sparse Core Ops, SparseCore 0:
  29.6 32.1 all-gather.4
  63.6 66.0 all-gather.6
  154.1 83.6 reduce-scatter.2
  248.6 31.0 reduce-scatter.4
